TPU v7x, 32 devices: a whole 2x2x4 slice. The times are simulated.
32 devices in a mesh: dp: 16 (over z, y, core), seq: 2 (over x).
Axes of the slice: x: 2, y: 2, z: 4, core: 2. Of those that a mesh axis runs over, the one named last changes fastest.
Arguments:
- inputs: bfloat16 [48, 100, 768], P('dp'), may hold values from -6 to 6
- memory: bfloat16 [48, 1024, 768], P('dp', 'seq'), may hold values from -6 to 6
- lengths: int32 [48], P('dp'), may hold values from 256 to 1024, as said below
- matched: int32 [48, 64], P('dp'), may hold values from 0 to 99, as said below
- cotangent: bfloat16 [48, 64, 768], P('dp'), may hold values from -6 to 6
- weights: bfloat16 [1, 12544, 768], P(None, ('dp', 'seq')), as said below
Outputs:
- outputs: float32 [48, 100, 768], P('dp')
- input_grads: float32 [48, 100, 768], P('dp')
- memory_grads: float32 [48, 1024, 768], P('dp', 'seq')
- weight_grads: float32 [1, 12544, 768], P(None, ('dp', 'seq'))
Inputs may be any that keep to these rules, and one draw needn't show every extreme that they name: Token j of image i is padding where j >= lengths[i]; in each group of 3 consecutive images one image, drawn from the seed, has all 1024 tokens. `matched`: each row holds 64 different query indices. `weights`: rows from 12305 on are zero.
All inputs are finite; a program needn't handle non-finite values.
Results may differ from a plain program's by a relative error of at most 0.02.
The roundings to bfloat16 on the way count: a program that leaves them out, or rounds other values in their place, can miss the bound.
Values may be sent and summed in bfloat16 or wider, within the bound.
No kernel may reach another device: no remote copies, remote signals or barrier semaphores. Data moves between devices by JAX's collectives and lax.ppermute only.
A program may use at most 192 MiB of HBM per device.

v0:
```python
from functools import partial

import jax
import jax.numpy as jnp
from jax import lax
from jax.experimental import pallas as pl
from jax.experimental.pallas import tpu as pltpu
from jax.sharding import PartitionSpec as P

D = 768
H = 12
HEAD = 64
FF = 3072
PAIRS = H // 2
LANES = 2 * HEAD
QP = 112
VEC_ROW = 8 * D + 2 * FF
VECS = 24
TAIL = 256
HEAD_ROWS = 128
QUERY_HEAD = 64
SCALE = HEAD ** (-0.5)
EPS = 1e-05
NEG = -1e30
F32 = jnp.float32
BF16 = jnp.bfloat16
MIB = 1024 * 1024


def dot_nn(a, b):
    return lax.dot_general(a, b, (((1,), (0,)), ((), ())), preferred_element_type=F32)


def dot_nt(a, b):
    return lax.dot_general(a, b, (((1,), (1,)), ((), ())), preferred_element_type=F32)


def dot_tn(a, b):
    return lax.dot_general(a, b, (((0,), (0,)), ((), ())), preferred_element_type=F32)


def norm_parts(v):
    center = v - jnp.mean(v, axis=-1, keepdims=True)
    inverse = lax.rsqrt(jnp.mean(center * center, axis=-1, keepdims=True) + EPS)
    return center * inverse, inverse


def norm_back(dy, hat, inverse, gain):
    scaled = dy * gain
    mean_one = jnp.mean(scaled, axis=-1, keepdims=True)
    mean_two = jnp.mean(scaled * hat, axis=-1, keepdims=True)
    return inverse * (scaled - mean_one - hat * mean_two)


def rowsum(v):
    return jnp.sum(v.astype(F32), axis=0, keepdims=True)


def head_masks():
    lane = lax.broadcasted_iota(jnp.int32, (1, LANES), 1)
    first = jnp.where(lane < HEAD, 1.0, 0.0)
    return first.astype(BF16), (1.0 - first).astype(BF16)


def two_heads(block, masks):
    return jnp.concatenate([block * masks[0], block * masks[1]], axis=0)


def join_heads(stacked):
    lane = lax.broadcasted_iota(jnp.int32, (QP, LANES), 1)
    return jnp.where(lane < HEAD, stacked[:QP], stacked[QP:])


def weight_block(index):
    return pl.BlockSpec((D, D), lambda *_: (index, 0))


def whole(shape):
    return pl.BlockSpec(shape, lambda *_: (0,) * len(shape))


def params(mib):
    return pltpu.CompilerParams(vmem_limit_bytes=mib * MIB)


def cost(flops, moved):
    return pl.CostEstimate(flops=flops // 1000, bytes_accessed=moved // 1000, transcendentals=0)


FIRST_BLOCKS = (0, 1, 2, 5, 6, 3, 4)
SPREAD = ((0, 0, 0), (0, 0, 1), (0, 1, 0), (1, 0, 0), (0, 1, 1), (1, 1, 0), (1, 0, 1), (1, 1, 1))
PAIR_ROWS = 784
HOLDER = (3, 1, 1, 1)


class Assembly:
    def __init__(self, flags, bufs, weights, sems, vec_low, vec_sem):
        self.core, self.x, self.y, self.z = flags[0], flags[1], flags[2], flags[3]
        self.bufs, self.weights, self.sems = bufs, weights, sems
        self.vec_low, self.vec_sem = vec_low, vec_sem
        self.ready = set()

    def buf(self, dc, dz2, spread):
        return self.bufs[dc * 16 + dz2 * 8 + SPREAD.index(spread)]

    def start_vec(self):
        first = VEC_ROW - 15 * PAIR_ROWS - 384
        for dc in (0, 1):
            for dz2 in (0, 1):
                for dz1, dy, dx in SPREAD:
                    here = (self.z ^ (2 * dz2 + dz1), self.y ^ dy, self.core ^ dc, self.x ^ dx)
                    hit = (here[0] == HOLDER[0]) & (here[1] == HOLDER[1]) & (here[2] == HOLDER[2]) & (here[3] == HOLDER[3])

                    @pl.when(hit)
                    def _(source=self.buf(dc, dz2, (dz1, dy, dx))):
                        pltpu.make_async_copy(source.at[pl.ds(first, 32)], self.vec_low, self.vec_sem).start()

    def wait_vec(self):
        pltpu.make_async_copy(self.weights.at[pl.ds(0, 32)], self.vec_low, self.vec_sem).wait()

    def start_group(self, dz2):
        def rows(start, count):
            return pl.ds(pl.multiple_of(start, 16), count)

        for dz1 in (0, 1):
            for dy in (0, 1):
                for dc in (0, 1):
                    pair = (self.z ^ (2 * dz2 + dz1)) * 4 + (self.y ^ dy) * 2 + (self.core ^ dc)
                    base, sem = pair * PAIR_ROWS, self.sems.at[pair]
                    near, far = self.buf(dc, dz2, (dz1, dy, 0)), self.buf(dc, dz2, (dz1, dy, 1))
                    for source, x in ((near, self.x), (far, 1 - self.x)):
                        target = self.weights.at[rows(base + 400 * x, 384)]
                        pltpu.make_async_copy(source.at[rows(16 * x, 384)], target, sem).start()
                    target = self.weights.at[rows(base + 384, 16)]
                    pltpu.make_async_copy(near.at[rows(384 * (1 - self.x), 16)], target, sem).start()

    def start(self):
        self.start_vec()
        for low in (True, False):

            @pl.when((self.z < 2) == low)
            def _(low=low):
                for dz2 in (0, 1) if low else (1, 0):
                    self.start_group(dz2)

    def wait(self, pair):
        if pair not in self.ready:
            self.ready.add(pair)
            rows = self.weights.at[pl.ds(pair * PAIR_ROWS, PAIR_ROWS)]
            pltpu.make_async_copy(rows, rows, self.sems.at[pair]).wait()

    def block(self, number):
        for pair in range(number * D // PAIR_ROWS, (number * D + D - 1) // PAIR_ROWS + 1):
            self.wait(pair)


class Direct:
    def __init__(self, w_hbm, weights, sems, vec_low, vec_sem):
        self.copies = {}
        for number in FIRST_BLOCKS:
            rows = pl.ds(number * D, D)
            self.copies[number] = pltpu.make_async_copy(w_hbm.at[rows], weights.at[rows], sems.at[number])
        self.vec = pltpu.make_async_copy(w_hbm.at[pl.ds(VEC_ROW, 32)], vec_low, vec_sem)
        self.ready = set()

    def start(self):
        self.vec.start()
        for number in FIRST_BLOCKS:
            self.copies[number].start()

    def wait_vec(self):
        self.vec.wait()

    def block(self, number):
        if number not in self.ready:
            self.ready.add(number)
            self.copies[number].wait()


def forward_kernel(queries, custom, left_ref, flags, xb_ref, m_hbm, *refs):
    count = 32 if custom else 1
    bufs, refs = refs[:count], refs[count:]
    qs_out, ks_out, vs_out, os_out, y1_out, qc_out, k_out, v_out, o_out, stat_ref = refs[:10]
    w_out = refs[10] if custom else None
    weights, m_ref, qs_ref, ks_ref, vs_ref, os_ref, y1_ref, qc_ref, k_ref, v_ref, o_ref, vec_low = refs[10 + custom : 22 + custom]
    w_sems, m_sems, out_sems, kv_sems, vec_sem, all_sems = refs[22 + custom :]
    images = m_ref.shape[0]
    tokens = m_ref.shape[1]
    if custom:
        feed = Assembly(flags, bufs, weights, w_sems, vec_low, vec_sem)
    else:
        feed = Direct(bufs[0], weights, w_sems, vec_low, vec_sem)

    def load_memory(image):
        return pltpu.make_async_copy(m_hbm.at[image], m_ref.at[image], m_sems.at[image])

    def matrix(block):
        feed.block(block)
        return weights[block * D : (block + 1) * D, :]

    def leave_weights(half):
        rows = pl.ds(half * 8 * PAIR_ROWS, 8 * PAIR_ROWS)
        return pltpu.make_async_copy(weights.at[rows], w_out.at[rows], all_sems.at[half])

    small = [(qs_ref, qs_out), (ks_ref, ks_out), (vs_ref, vs_out), (os_ref, os_out), (y1_ref, y1_out), (qc_ref, qc_out)]

    def leave(number):
        return pltpu.make_async_copy(*small[number], out_sems.at[number])

    def leave_image(image, number):
        source, target = [(k_ref, k_out), (v_ref, v_out), (o_ref, o_out)][number]
        return pltpu.make_async_copy(source.at[image], target.at[image], kv_sems.at[image, number])

    feed.start()
    for image in range(images):
        load_memory(image).start()
    feed.wait_vec()
    vec = vec_low[...].astype(F32)
    xb = xb_ref[...]
    qs_ref[...] = ((dot_nn(xb, matrix(0)) + vec[0:1, :]) * SCALE).astype(BF16)
    leave(0).start()
    ks_ref[...] = dot_nn(xb, matrix(1)).astype(BF16)
    leave(1).start()
    vs_ref[...] = (dot_nn(xb, matrix(2)) + vec[1:2, :]).astype(BF16)
    leave(2).start()
    masks = head_masks()
    real = lax.broadcasted_iota(jnp.int32, (2 * QP, QP), 1) < queries
    for image in range(images):
        rows = slice(image * QP, (image + 1) * QP)
        for pair in range(PAIRS):
            lanes = slice(pair * LANES, (pair + 1) * LANES)
            scores = dot_nt(two_heads(qs_ref[rows, lanes], masks), ks_ref[rows, lanes])
            scores = jnp.where(real, scores, NEG)
            probs = jnp.exp(scores - jnp.max(scores, axis=-1, keepdims=True))
            probs = probs / jnp.sum(probs, axis=-1, keepdims=True)
            os_ref[rows, lanes] = join_heads(dot_nn(probs.astype(BF16), vs_ref[rows, lanes])).astype(BF16)
    leave(3).start()
    y1 = xb.astype(F32) + (dot_nn(os_ref[...], matrix(3)) + vec[2:3, :])
    y1_ref[...] = y1
    leave(4).start()
    hat, _ = norm_parts(y1)
    x1 = hat * vec[11:12, :] + vec[12:13, :]
    qc_ref[...] = ((dot_nn(x1.astype(BF16), matrix(4)) + vec[3:4, :]) * SCALE).astype(BF16)
    leave(5).start()

    feed.block(5)
    feed.block(6)
    if custom:
        for pair in range(8):
            feed.wait(pair)
        leave_weights(0).start()
    column = lax.broadcasted_iota(jnp.int32, (2 * QP, 128), 1)
    for image in range(images):
        load_memory(image).wait()
        rows = slice(image * QP, (image + 1) * QP)
        k_ref[image] = dot_nn(m_ref[image], matrix(5)).astype(BF16)
        v_ref[image] = (dot_nn(m_ref[image], matrix(6)) + vec[4:5, :]).astype(BF16)
        leave_image(image, 0).start()
        leave_image(image, 1).start()
        valid = lax.broadcasted_iota(jnp.int32, (2 * QP, tokens), 1) < left_ref[image]
        stat = jnp.zeros((2 * QP, 128), F32)
        for pair in range(PAIRS):
            lanes = slice(pair * LANES, (pair + 1) * LANES)
            scores = dot_nt(two_heads(qc_ref[rows, lanes], masks), k_ref[image, :, lanes])
            scores = jnp.where(valid, scores, NEG)
            top = jnp.max(scores, axis=-1, keepdims=True)
            probs = jnp.exp(scores - top)
            total = jnp.sum(probs, axis=-1, keepdims=True)
            mixed = dot_nn(probs.astype(BF16), v_ref[image, :, lanes]) / total
            o_ref[image, :, lanes] = join_heads(mixed).astype(BF16)
            stat = jnp.where(column == pair, top + jnp.log(total), stat)
        stat_ref[image] = jnp.where(left_ref[image] > 0, stat.T[:8], NEG)
        leave_image(image, 2).start()
        if custom and image == 0:
            for pair in range(8, 16):
                feed.wait(pair)
            leave_weights(1).start()
    for number in range(len(small)):
        leave(number).wait()
    for image in range(images):
        for number in range(3):
            leave_image(image, number).wait()
    if custom:
        leave_weights(0).wait()
        leave_weights(1).wait()


def forward(left, flags, xb, memory, bufs, queries):
    custom = len(bufs) > 1
    rows = xb.shape[0]
    images, tokens, _ = memory.shape
    narrow = jax.ShapeDtypeStruct((rows, D), BF16)
    tall = jax.ShapeDtypeStruct(memory.shape, BF16)
    anywhere = pl.BlockSpec(memory_space=pl.ANY)
    small = pltpu.VMEM((rows, D), BF16)
    large = pltpu.VMEM(memory.shape, BF16)
    held = 16 * PAIR_ROWS if custom else 7 * D
    return pl.pallas_call(
        partial(forward_kernel, queries, custom),
        grid_spec=pltpu.PrefetchScalarGridSpec(
            num_scalar_prefetch=2,
            grid=(1,),
            in_specs=[whole((rows, D)), anywhere] + [anywhere] * len(bufs),
            out_specs=[anywhere] * 9 + [whole((images, 8, 2 * QP))] + [anywhere] * custom,
            scratch_shapes=[
                pltpu.VMEM((held, D), BF16),
                large, small, small, small, small,
                pltpu.VMEM((rows, D), F32),
                small, large, large,
                pltpu.VMEM((images, QP, D), BF16),
                pltpu.VMEM((32, D), BF16),
                pltpu.SemaphoreType.DMA((16,)),
                pltpu.SemaphoreType.DMA((images,)),
                pltpu.SemaphoreType.DMA((6,)),
                pltpu.SemaphoreType.DMA((images, 3)),
                pltpu.SemaphoreType.DMA(()),
                pltpu.SemaphoreType.DMA((2,)),
            ],
        ),
        out_shape=[
            narrow, narrow, narrow, narrow,
            jax.ShapeDtypeStruct((rows, D), F32),
            narrow, tall, tall,
            jax.ShapeDtypeStruct((images, QP, D), BF16),
            jax.ShapeDtypeStruct((images, 8, 2 * QP), F32),
        ]
        + [jax.ShapeDtypeStruct((held, D), BF16)] * custom,
        cost_estimate=cost(0, 0),
        compiler_params=params(60),
        name="forward",
    )(left, flags, xb, memory, *bufs)


def pieces(start, count, size):
    found = []
    done = 0
    while done < count:
        pair, offset = divmod(start + done, size)
        length = min(count - done, size - offset)
        found.append((done, pair, offset, length))
        done += length
    return found


class Halves:
    def __init__(self, keep, send, my_core):
        self.keep, self.send, self.my_core = keep, send, my_core

    def copy(self, target, source, pair, offset, length, sem):
        place = pair // self.cores()
        index = []
        for extent in reversed(target.shape[:-2]):
            index.insert(0, place % extent)
            place = place // extent
        return pltpu.make_async_copy(source, target.at[(*index, pl.ds(offset, length))], sem)

    def cores(self):
        return 1 if self.send is None else 2

    def start(self, source, pair, offset, length, sem):
        if self.send is None:
            self.copy(self.keep, source, pair, offset, length, sem).start()
            return

        @pl.when(self.my_core == pair % 2)
        def _():
            self.copy(self.keep, source, pair, offset, length, sem).start()

        @pl.when(self.my_core != pair % 2)
        def _():
            self.copy(self.send, source, pair, offset, length, sem).start()

    def wait(self, source, pair, offset, length, sem):
        self.copy(self.keep, source, pair, offset, length, sem).wait()


def middle_kernel(parts, split, *refs):
    flags, y1_ref = refs[:2]
    o_refs, stat_refs = refs[2 : 2 + parts], refs[2 + parts : 2 + 2 * parts]
    refs = refs[2 + 2 * parts :]
    w_hbm, vec, cot_ref, match_ref, out_hbm = refs[:5]
    halves = Halves(refs[5], refs[6] if split else None, flags[0])
    refs = refs[6 + split :]
    cross_halves = Halves(refs[0], refs[1] if split else None, flags[0])
    refs = refs[1 + split :]
    db_ref, doc_ref, tot_ref, dvec_ref = refs[:4]
    ocf, ocb, y2, x2b, u, slope, acc, e3b, staged, blank, out_ref, dco_ref, co, feed = refs[4:18]
    sems, blank_sem, out_sem, side_sems, w_sems = refs[18:]
    phase, step = pl.program_id(0), pl.program_id(1)
    steps = FF // D
    images = match_ref.shape[0]
    column = lax.broadcasted_iota(jnp.int32, (2 * QP, 128), 1)
    lane = lax.broadcasted_iota(jnp.int32, (QP, LANES), 1)
    size = halves.keep.shape[-2]
    side = cross_halves.keep.shape[-2]

    def load(block):
        target = co if block == 7 else feed.at[block - 8]
        return pltpu.make_async_copy(w_hbm.at[pl.ds(block * D, D)], target, w_sems.at[block - 7])

    def leave_out():
        return pltpu.make_async_copy(out_ref, out_hbm, out_sem)

    def leave_side(act):
        starts = [(dco_ref, 3 * D - QUERY_HEAD, D), (staged.at[0, 0], 4 * D - QUERY_HEAD, HEAD_ROWS)]
        for which, (source, start, count) in enumerate(starts):
            if (which == 0) != (act[0] == "o"):
                continue
            for number, (done, pair, offset, length) in enumerate(pieces(start, count, side)):
                piece = source.at[pl.ds(done, length)]
                getattr(cross_halves, act[1])(piece, pair, offset, length, side_sems.at[which, number])

    def leave(which, at, act):
        skip = HEAD_ROWS if which + at == 0 else 0
        start = which * FF + at * D + skip - HEAD_ROWS
        for number, (done, pair, offset, length) in enumerate(pieces(start, D - skip, size)):
            source = staged.at[at % 2, which, pl.ds(done + skip, length)]
            getattr(halves, act)(source, pair, offset, length, sems.at[at, which, number])

    def leave_blank(act):
        for _, pair, offset, length in pieces(2 * FF - HEAD_ROWS, TAIL, size):
            getattr(halves, act)(blank, pair, offset, length, blank_sem)

    def ordered(first, second):
        if parts != 2:
            return first, second
        swap = flags[1] != 0
        return jnp.where(swap, second, first), jnp.where(swap, first, second)

    @pl.when((phase == 0) & (step == 0))
    def _():
        load(7).start()
        for at in range(steps):
            load(8 + at).start()
            load(8 + steps + at).start()
        for image in range(images):
            rows = slice(image * QP, (image + 1) * QP)
            stats = [ref[image] for ref in stat_refs]
            if parts == 2:
                stats = ordered(*stats)
            top = stats[0]
            for n in range(1, parts):
                top = jnp.maximum(top, stats[n])
            mass = [jnp.exp(stats[n] - top) for n in range(parts)]
            total = mass[0]
            for n in range(1, parts):
                total = total + mass[n]
            tot_ref[image, 0:8, :] = top + jnp.log(total)
            shares = [jnp.concatenate([m / total, jnp.zeros((120, 2 * QP), F32)], axis=0).T for m in mass]
            for pair in range(PAIRS):
                lanes = slice(pair * LANES, (pair + 1) * LANES)
                values = [ref[image, :, lanes].astype(F32) for ref in o_refs]
                if parts == 2:
                    values = ordered(*values)
                mixed = jnp.zeros((QP, LANES), F32)
                for n in range(parts):
                    share = shares[n][:, pair : pair + 1]
                    mixed = mixed + values[n] * jnp.where(lane < HEAD, share[:QP], share[QP:])
                ocf[rows, lanes] = mixed
        ocb[...] = ocf[...].astype(BF16)
        hat, _ = norm_parts(y1_ref[...])
        x1 = hat * vec[11:12, :] + vec[12:13, :]
        load(7).wait()
        total = x1 + (dot_nn(ocb[...], co[...]) + vec[5:6, :])
        y2[...] = total
        hat, _ = norm_parts(total)
        x2 = hat * vec[13:14, :] + vec[14:15, :]
        x2b[...] = x2.astype(BF16)
        acc[...] = x2 + vec[6:7, :]

    for at in range(steps):

        @pl.when((phase == 0) & (step == at))
        def _(at=at):
            load(8 + at).wait()
            load(8 + steps + at).wait()

    f1, f2 = feed.at[step], feed.at[steps + step]

    @pl.when(phase == 0)
    def _():
        h = dot_nt(x2b[...], f1[...]) + vec[pl.ds(7 + step, 1), :]
        root = 0.7978845608028654
        square = h * h
        t = jnp.tanh(root * (h + 0.044715 * (h * square)))
        half = 0.5 * (1.0 + t)
        slope[step] = half + (0.5 * root) * h * (1.0 - t * t) * (1.0 + 0.134145 * square)
        active = (h * half).astype(BF16)
        u[step] = active
        acc[...] += dot_nn(active, f2[...])

    @pl.when((phase == 1) & (step == 0))
    def _():
        blank[...] = jnp.zeros_like(blank)
        leave_blank("start")
        dvec_ref[...] = jnp.zeros_like(dvec_ref)
        hat, inverse = norm_parts(acc[...])
        out = hat * vec[15:16, :] + vec[16:17, :]
        grads = []
        for image in range(images):
            out_ref[image] = out[image * QP : (image + 1) * QP]
            matched = match_ref[image]
            hit = lax.broadcasted_iota(jnp.int32, (QP, matched.shape[1]), 0) == matched
            grads.append(dot_nn(jnp.where(hit, 1.0, 0.0).astype(BF16), cot_ref[image]))
        leave_out().start()
        dy = jnp.concatenate(grads, axis=0)
        dvec_ref[15:16, :] = rowsum(dy * hat)
        dvec_ref[16:17, :] = rowsum(dy)
        dc = norm_back(dy, hat, inverse, vec[15:16, :])
        low = dc.astype(BF16)
        e3b[...] = low
        dvec_ref[6:7, :] = rowsum(low)
        acc[...] = dc

    for at in range(2, steps):

        @pl.when((phase == 1) & (step == at))
        def _(at=at):
            leave(0, at - 2, "wait")
            leave(1, at - 2, "wait")
            if at == 2:
                leave_side(("f", "wait"))

    @pl.when(phase == 1)
    def _():
        du = dot_nt(e3b[...], f2[...])
        dh = (du * slope[step]).astype(BF16)
        slot = lax.rem(step, 2)
        staged[slot, 1] = dot_tn(u[step], e3b[...]).astype(BF16)
        staged[slot, 0] = dot_tn(dh, x2b[...]).astype(BF16)

        @pl.when(step == 0)
        def _():
            leave_side(("f", "start"))

        for at in range(steps):

            @pl.when(step == at)
            def _(at=at):
                leave(0, at, "start")
                leave(1, at, "start")

        dvec_ref[pl.ds(7 + step, 1), :] = rowsum(dh)
        acc[...] += dot_nn(dh, f1[...])

    @pl.when((phase == 1) & (step == steps - 1))
    def _():
        hat, inverse = norm_parts(y2[...])
        dy = acc[...]
        dvec_ref[13:14, :] = rowsum(dy * hat)
        dvec_ref[14:15, :] = rowsum(dy)
        db = norm_back(dy, hat, inverse, vec[13:14, :])
        db_ref[...] = db
        low = db.astype(BF16)
        dvec_ref[5:6, :] = rowsum(low)
        dco_ref[...] = dot_tn(ocb[...], low).astype(BF16)
        leave_side(("o", "start"))
        doc = dot_nt(low, co[...]).astype(BF16)
        doc_ref[...] = doc
        both = doc.astype(F32) * ocf[...]
        for image in range(images):
            rows = slice(image * QP, (image + 1) * QP)
            tot = jnp.zeros((2 * QP, 128), F32)
            for pair in range(PAIRS):
                piece = both[rows, pair * LANES : (pair + 1) * LANES]
                one = jnp.sum(jnp.where(lane < HEAD, piece, 0.0), axis=-1, keepdims=True)
                two = jnp.sum(jnp.where(lane < HEAD, 0.0, piece), axis=-1, keepdims=True)
                tot = jnp.where(column == pair, jnp.concatenate([one, two], axis=0), tot)
            tot_ref[image, 8:16, :] = tot.T[:8]
        leave_blank("wait")
        leave_out().wait()
        leave_side(("o", "wait"))
        for which in (0, 1):
            leave(which, steps - 2, "wait")
            leave(which, steps - 1, "wait")


def halves_shape(shape, split):
    return [jax.ShapeDtypeStruct(shape, BF16)] * (1 + split)


def middle(flags, y1, o_parts, stat_parts, w, vec, cot, matched, far_shape, cross_shape, split):
    rows = y1.shape[0]
    images = cot.shape[0]
    steps = FF // D
    parts = len(o_parts)
    anywhere = pl.BlockSpec(memory_space=pl.ANY)
    return pl.pallas_call(
        partial(middle_kernel, parts, split),
        grid_spec=pltpu.PrefetchScalarGridSpec(
            num_scalar_prefetch=1,
            grid=(2, steps),
            in_specs=[whole(y1.shape)]
            + [whole(o_parts[0].shape)] * parts
            + [whole(stat_parts[0].shape)] * parts
            + [anywhere, whole((VECS, D)), whole(cot.shape), whole((images, 1, matched.shape[1]))],
            out_specs=[anywhere] * (3 + 2 * split)
            + [
                whole((rows, D)),
                whole((rows, D)),
                whole((images, 16, 2 * QP)),
                whole((VECS, D)),
            ],
            scratch_shapes=[
                pltpu.VMEM((rows, D), F32),
                pltpu.VMEM((rows, D), BF16),
                pltpu.VMEM((rows, D), F32),
                pltpu.VMEM((rows, D), BF16),
                pltpu.VMEM((steps, rows, D), BF16),
                pltpu.VMEM((steps, rows, D), F32),
                pltpu.VMEM((rows, D), F32),
                pltpu.VMEM((rows, D), BF16),
                pltpu.VMEM((2, 2, D, D), BF16),
                pltpu.VMEM((TAIL, D), BF16),
                pltpu.VMEM((images, QP, D), F32),
                pltpu.VMEM((D, D), BF16),
                pltpu.VMEM((D, D), BF16),
                pltpu.VMEM((2 * steps, D, D), BF16),
                pltpu.SemaphoreType.DMA((steps, 2, 2)),
                pltpu.SemaphoreType.DMA(()),
                pltpu.SemaphoreType.DMA(()),
                pltpu.SemaphoreType.DMA((2, 2)),
                pltpu.SemaphoreType.DMA((1 + 2 * steps,)),
            ],
        ),
        out_shape=[jax.ShapeDtypeStruct((images, QP, D), F32)]
        + halves_shape(far_shape, split)
        + halves_shape(cross_shape, split)
        + [
            jax.ShapeDtypeStruct((rows, D), F32),
            jax.ShapeDtypeStruct((rows, D), BF16),
            jax.ShapeDtypeStruct((images, 16, 2 * QP), F32),
            jax.ShapeDtypeStruct((VECS, D), F32),
        ],
        cost_estimate=cost(2 * rows * D * (6 * FF + 3 * D), 2 * FF * D * 6),
        compiler_params=params(60),
        name="middle",
    )(flags, y1, *o_parts, *stat_parts, w, vec, cot, matched[:, None, :])


def cross_backward_kernel(left_ref, q_ref, k_ref, v_ref, do_ref, tot_ref, dq_ref, dk_ref, dv_ref):
    tokens = k_ref.shape[1]
    masks = head_masks()
    valid = lax.broadcasted_iota(jnp.int32, (tokens, 2 * QP), 0) < left_ref[pl.program_id(0)]
    for pair in range(PAIRS):
        lanes = slice(pair * LANES, (pair + 1) * LANES)
        key, value = k_ref[0, :, lanes], v_ref[0, :, lanes]
        query = two_heads(q_ref[0, :, lanes], masks)
        dout = two_heads(do_ref[0, :, lanes], masks)
        scores = dot_nt(key, query)
        probs = jnp.where(valid, jnp.exp(scores - tot_ref[0, pair : pair + 1, :]), 0.0)
        dprobs = dot_nt(value, dout)
        dscores = (probs * (dprobs - tot_ref[0, 8 + pair : 9 + pair, :])).astype(BF16)
        dv_ref[0, :, lanes] = dot_nn(probs.astype(BF16), dout).astype(BF16)
        dk_ref[0, :, lanes] = dot_nn(dscores, query).astype(BF16)
        dq_ref[0, :, lanes] = join_heads(dot_tn(key, dscores).T).astype(BF16)


def cross_backward(left, qc, key, value, doc, tot):
    images, tokens, _ = key.shape
    q_block = pl.BlockSpec((1, QP, D), lambda i, _: (i, 0, 0))
    m_block = pl.BlockSpec((1, tokens, D), lambda i, _: (i, 0, 0))
    s_block = pl.BlockSpec((1, 16, 2 * QP), lambda i, _: (i, 0, 0))
    return pl.pallas_call(
        cross_backward_kernel,
        grid_spec=pltpu.PrefetchScalarGridSpec(
            num_scalar_prefetch=1,
            grid=(images,),
            in_specs=[q_block, m_block, m_block, q_block, s_block],
            out_specs=[q_block, m_block, m_block],
        ),
        out_shape=[
            jax.ShapeDtypeStruct((images, QP, D), BF16),
            jax.ShapeDtypeStruct(key.shape, BF16),
            jax.ShapeDtypeStruct(key.shape, BF16),
        ],
        cost_estimate=cost(4 * images * 2 * QP * tokens * D // 3, images * tokens * D * 8),
        compiler_params=params(60),
        name="cross_backward",
    )(left, qc.reshape(images, QP, D), key, value, doc.reshape(images, QP, D), tot)


def memory_weights_kernel(split, flags, *refs):
    m_ref, dk_ref, dv_ref = refs[1 + split : 4 + split]
    refs = refs[4 + split :]
    if split:
        a, b, c, d = refs[:4]
        far_out = refs[-4]
        far_out[0] = add(a[...], b[...])
        far_out[1] = add(c[...], d[...])
        refs = refs[4:-4] + refs[-3:]
    gb_ref = refs[0]
    halves = Halves(refs[1], refs[2] if split else None, flags[0])
    sums, low, sems = refs[2 + split :]
    step = pl.program_id(0)
    dv = dv_ref[0]
    more = [dot_tn(m_ref[0], dk_ref[0]), dot_tn(m_ref[0], dv)]

    @pl.when(step == 0)
    def _():
        for which in (0, 1):
            sums[which] = more[which]
        gb_ref[...] = jnp.broadcast_to(rowsum(dv), gb_ref.shape)

    @pl.when(step > 0)
    def _():
        for which in (0, 1):
            sums[which] += more[which]
        gb_ref[...] += jnp.broadcast_to(rowsum(dv), gb_ref.shape)

    def leave(which, act):
        start = (1 + which) * D - QUERY_HEAD
        for number, (done, pair, offset, length) in enumerate(pieces(start, D, halves.keep.shape[-2])):
            piece = low.at[which, pl.ds(done, length)]
            getattr(halves, act)(piece, pair, offset, length, sems.at[which, number])

    @pl.when(step == pl.num_programs(0) - 1)
    def _():
        for which in (0, 1):
            low[which] = sums[which].astype(BF16)
            leave(which, "start")
        for which in (0, 1):
            leave(which, "wait")


def memory_weights(flags, cross, memory, dk, dv, far, split):
    images, tokens, _ = memory.shape
    block = pl.BlockSpec((1, tokens, D), lambda i, _: (i, 0, 0))
    anywhere = pl.BlockSpec(memory_space=pl.ANY)
    far = [blocks_of(part) for part in far]
    part = D // images
    sources, far_specs, far_out, far_shape = [], [], [], []
    if split:
        rows = far[0].shape[-2]
        for r in (0, 1):
            for array in far:
                sources.append(array)
                far_specs.append(
                    pl.BlockSpec((None, None, None, rows, part), lambda i, f, r=r: (r, 1 - f[2], f[1], 0, i))
                )
        far_out = [pl.BlockSpec((2, rows, part), lambda i, f: (0, 0, i))]
        far_shape = [jax.ShapeDtypeStruct((2, rows, D), BF16)]
    return pl.pallas_call(
        partial(memory_weights_kernel, split),
        grid_spec=pltpu.PrefetchScalarGridSpec(
            num_scalar_prefetch=1,
            grid=(images,),
            in_specs=[anywhere] * (1 + split) + [block, block, block] + far_specs,
            out_specs=[whole((8, D))] + [anywhere] * (1 + split) + far_out,
            scratch_shapes=[
                pltpu.VMEM((2, D, D), F32),
                pltpu.VMEM((2, D, D), BF16),
                pltpu.SemaphoreType.DMA((2, 2)),
            ],
        ),
        out_shape=[jax.ShapeDtypeStruct((8, D), F32)] + halves_shape(cross[0].shape, split) + far_shape,
        input_output_aliases={1 + n: 1 + n for n in range(1 + split)},
        cost_estimate=cost(4 * images * tokens * D * D, images * tokens * D * 6),
        compiler_params=params(60),
        name="memory_weights",
    )(flags, *cross, memory, dk, dv, *sources)


def memory_grads_kernel(dk_ref, dv_ref, ck, cv, gm_ref):
    gm_ref[0] = dot_nt(dk_ref[0], ck[...]) + dot_nt(dv_ref[0], cv[...])


def memory_grads(dk, dv, w):
    images, tokens, _ = dk.shape
    block = pl.BlockSpec((1, tokens, D), lambda i: (i, 0, 0))
    return pl.pallas_call(
        memory_grads_kernel,
        grid=(images,),
        in_specs=[block, block, weight_block(5), weight_block(6)],
        out_specs=block,
        out_shape=jax.ShapeDtypeStruct(dk.shape, F32),
        cost_estimate=pl.CostEstimate(
            flops=4 * images * tokens * D * D, bytes_accessed=images * tokens * D * 8, transcendentals=0
        ),
        compiler_params=params(60),
        name="memory_grads",
    )(dk, dv, w, w)


class Loads:
    def __init__(self, pairs, sems):
        self.copies = [(pltpu.make_async_copy(source, target, sems.at[n]), target) for n, (source, target) in enumerate(pairs)]
        self.ready = set()
        for copy, _ in self.copies:
            copy.start()

    def __call__(self, number):
        copy, target = self.copies[number]
        if number not in self.ready:
            copy.wait()
            self.ready.add(number)
        return target[...]


def query_backward_kernel(parts, split, flags, *refs):
    sources, vec = refs[1 + split : 4 + split + parts], refs[4 + split + parts]
    refs = refs[5 + split + parts :]
    da_ref, gq_head_ref, dvec_ref = refs[:3]
    halves = Halves(refs[3], refs[4] if split else None, flags[0])
    refs = refs[4 + split :]
    targets, staged, load_sems, sems = refs[: 3 + parts], refs[3 + parts], refs[4 + parts], refs[5 + parts]
    w_hbm = sources[-1]
    sources = [*sources[:-1], w_hbm.at[pl.ds(4 * D, D)]]
    get = Loads(list(zip(sources, targets)), load_sems)

    def leave(act):
        for number, (done, pair, offset, length) in enumerate(pieces(0, D - QUERY_HEAD, halves.keep.shape[-2])):
            piece = staged.at[pl.ds(done + QUERY_HEAD, length)]
            getattr(halves, act)(piece, pair, offset, length, sems.at[number])

    total = get(0).astype(F32)
    for number in range(1, parts):
        total = total + get(number).astype(F32)
    dq = total.astype(BF16) * SCALE
    hat, inverse = norm_parts(get(parts))
    gain = vec[11:12, :]
    x1b = (hat * gain + vec[12:13, :]).astype(BF16)
    gcq = dot_tn(x1b, dq).astype(BF16)
    staged[...] = gcq
    leave("start")
    gq_head_ref[...] = gcq[:QUERY_HEAD]
    dvec_ref[...] = jnp.zeros_like(dvec_ref)
    dvec_ref[3:4, :] = rowsum(dq)
    dy = get(parts + 1) + dot_nt(dq, get(parts + 2))
    dvec_ref[11:12, :] = rowsum(dy * hat)
    dvec_ref[12:13, :] = rowsum(dy)
    da = norm_back(dy, hat, inverse, gain)
    da_ref[...] = da
    dvec_ref[2:3, :] = rowsum(da.astype(BF16))
    leave("wait")


def query_backward(flags, cross, y1, db, dq_parts, w, vec, split):
    rows = y1.shape[0]
    parts = len(dq_parts)
    full = whole((rows, D))
    anywhere = pl.BlockSpec(memory_space=pl.ANY)
    return pl.pallas_call(
        partial(query_backward_kernel, parts, split),
        grid_spec=pltpu.PrefetchScalarGridSpec(
            num_scalar_prefetch=1,
            grid=(1,),
            in_specs=[anywhere] * (4 + split + parts) + [whole((VECS, D))],
            out_specs=[full, whole((QUERY_HEAD, D)), whole((VECS, D))] + [anywhere] * (1 + split),
            scratch_shapes=[pltpu.VMEM((rows, D), BF16)] * parts
            + [pltpu.VMEM((rows, D), F32)] * 2
            + [pltpu.VMEM((D, D), BF16)] * 2
            + [pltpu.SemaphoreType.DMA((parts + 3,)), pltpu.SemaphoreType.DMA((2,))],
        ),
        out_shape=[
            jax.ShapeDtypeStruct((rows, D), F32),
            jax.ShapeDtypeStruct((QUERY_HEAD, D), BF16),
            jax.ShapeDtypeStruct((VECS, D), F32),
        ]
        + halves_shape(cross[0].shape, split),
        input_output_aliases={1 + n: 3 + n for n in range(1 + split)},
        cost_estimate=cost(4 * rows * D * D, rows * D * 16),
        compiler_params=params(60),
        name="query_backward",
    )(flags, *cross, *[part.reshape(rows, D) for part in dq_parts], y1, db, w, vec)


def self_backward_kernel(queries, split, *refs):
    flags, os_hbm, da_hbm, qs_hbm, ks_hbm, vs_hbm, x_hbm, w_hbm, gq_ref, gx_ref, dvec_ref, keep_ref = refs[:12]
    halves = Halves(keep_ref, refs[12] if split else None, flags[0])
    sq, sk, sv, g_ref, os_ref, da_ref, ao, qs, ks, vs, x_ref, aq, ak, av, sems, load_sems = refs[12 + split :]
    size = keep_ref.shape[-2]
    matrices = [w_hbm.at[pl.ds(block * D, D)] for block in range(4)]
    get = Loads(
        [(os_hbm, os_ref), (da_hbm, da_ref), (matrices[3], ao), (qs_hbm, qs), (ks_hbm, ks), (vs_hbm, vs)]
        + [(x_hbm, x_ref), (matrices[0], aq), (matrices[1], ak), (matrices[2], av)],
        load_sems,
    )

    def leave(pair, act):
        getattr(halves, act)(g_ref.at[pl.ds(pair * size, size)], pair, 0, size, sems.at[pair])

    pairs = g_ref.shape[0] // size
    images = x_ref.shape[0] // QP
    dvec_ref[...] = jnp.zeros_like(dvec_ref)
    os = get(0)
    da = get(1)
    low = da.astype(BF16)
    g_ref[4 * D :, :] = gq_ref[...]
    g_ref[3 * D : 4 * D, :] = dot_tn(os, low).astype(BF16)
    dos = dot_nt(low, get(2)).astype(BF16)
    for number in (3, 4, 5):
        get(number)
    masks = head_masks()
    real = lax.broadcasted_iota(jnp.int32, (QP, 2 * QP), 0) < queries
    for image in range(images):
        rows = slice(image * QP, (image + 1) * QP)
        for pair in range(PAIRS):
            lanes = slice(pair * LANES, (pair + 1) * LANES)
            key, value = ks[rows, lanes], vs[rows, lanes]
            query = two_heads(qs[rows, lanes], masks)
            dout = two_heads(dos[rows, lanes], masks)
            scores = jnp.where(real, dot_nt(key, query), NEG)
            probs = jnp.exp(scores - jnp.max(scores, axis=0, keepdims=True))
            probs = probs / jnp.sum(probs, axis=0, keepdims=True)
            dprobs = dot_nt(value, dout)
            dscores = (probs * (dprobs - jnp.sum(probs * dprobs, axis=0, keepdims=True))).astype(BF16)
            sv[rows, lanes] = dot_nn(probs.astype(BF16), dout).astype(BF16)
            sk[rows, lanes] = dot_nn(dscores, query).astype(BF16)
            sq[rows, lanes] = join_heads(dot_tn(key, dscores).T).astype(BF16) * SCALE
    dvec_ref[0:1, :] = rowsum(sq[...])
    dvec_ref[1:2, :] = rowsum(sv[...])
    xb = get(6)
    g_ref[2 * D : 3 * D, :] = dot_tn(xb, sv[...]).astype(BF16)
    for pair in range(2, pairs):
        leave(pair, "start")
    g_ref[D : 2 * D, :] = dot_tn(xb, sk[...]).astype(BF16)
    for pair in range(1, min(2, pairs)):
        leave(pair, "start")
    g_ref[0:D, :] = dot_tn(xb, sq[...]).astype(BF16)
    leave(0, "start")
    gx = da + dot_nt(sq[...], get(7)) + dot_nt(sk[...], get(8)) + dot_nt(sv[...], get(9))
    for image in range(images):
        gx_ref[image] = gx[image * QP : (image + 1) * QP]
    for pair in range(pairs):
        leave(pair, "wait")


def self_backward(flags, xb, qs, ks, vs, os, da, gq_head, w, queries, shape, split):
    rows = xb.shape[0]
    images = rows // QP
    anywhere = pl.BlockSpec(memory_space=pl.ANY)
    return pl.pallas_call(
        partial(self_backward_kernel, queries, split),
        grid_spec=pltpu.PrefetchScalarGridSpec(
            num_scalar_prefetch=1,
            grid=(1,),
            in_specs=[anywhere] * 7 + [whole((QUERY_HEAD, D))],
            out_specs=[whole((images, QP, D)), whole((VECS, D))] + [anywhere] * (1 + split),
            scratch_shapes=[pltpu.VMEM((rows, D), BF16)] * 3
            + [pltpu.VMEM((4 * D + QUERY_HEAD, D), BF16), pltpu.VMEM((rows, D), BF16), pltpu.VMEM((rows, D), F32)]
            + [pltpu.VMEM((D, D), BF16)]
            + [pltpu.VMEM((rows, D), BF16)] * 4
            + [pltpu.VMEM((D, D), BF16)] * 3
            + [pltpu.SemaphoreType.DMA((4,)), pltpu.SemaphoreType.DMA((10,))],
        ),
        out_shape=[
            jax.ShapeDtypeStruct((images, QP, D), F32),
            jax.ShapeDtypeStruct((VECS, D), F32),
        ]
        + halves_shape(shape, split),
        cost_estimate=cost(16 * rows * D * D * 2, 8 * D * D * 2),
        compiler_params=params(60),
        name="self_backward",
    )(flags, os, da, qs, ks, vs, xb, w, gq_head)


class Place:
    def __init__(self):
        place = lax.axis_index("dp")
        self.x = lax.axis_index("seq")
        self.c = lax.rem(place, 2)
        self.y = lax.rem(place // 2, 2)
        self.z = place // 4


def pick(array, index, axis):
    return lax.dynamic_index_in_dim(array, index, axis, keepdims=False)


def over_core(v):
    return lax.ppermute(v, "dp", [(i, i ^ 1) for i in range(16)])


def over_y(v):
    return lax.ppermute(v, "dp", [(i, i ^ 2) for i in range(16)])


def over_x(v):
    return lax.ppermute(v, "seq", [(0, 1), (1, 0)])


def over_z(v, hops):
    return lax.ppermute(v, "dp", [(4 * a + i, 4 * b + i) for a, b in hops for i in range(4)])


def over_far(v):
    return over_z(v, [(0, 2), (2, 0), (1, 3), (3, 1)])


def over_near(v):
    return over_z(v, SWAP_ONE)


def spread(own):
    x, y, z = over_x(own), over_y(own), over_near(own)
    xy, yz, zx = over_x(y), over_y(z), over_near(x)
    return own, x, y, z, xy, yz, zx


def gather(at, rows):
    low = at.x == 0
    edge = over_x(jnp.where(low, rows[-8:], rows[:8]))
    own = jnp.where(low, jnp.concatenate([rows, edge]), jnp.concatenate([edge, rows]))
    other = over_far(own)
    here, there = spread(own), spread(other)
    found = [*here, over_x(here[5]), *there, over_y(there[6])]
    return found + [over_core(part) for part in found]


def tie(*values):
    return lax.optimization_barrier(values)


def add(kept, came):
    return (kept.astype(F32) + came.astype(F32)).astype(BF16)


def own_half(pairs, x):
    half = pairs.shape[-2] // 2
    return pick(pairs.reshape(*pairs.shape[:-2], 2, half, D), x, pairs.ndim - 2)


def blocks_of(pairs):
    return pairs.reshape(*pairs.shape[:-2], 2, pairs.shape[-2] // 2, D)


def picked(pairs, half, x):
    return pick(pick(pairs, half, 0), x, 0)


def merge(body, flags, sources, out_rows, name):
    parts = 3
    specs = []
    for array, where in sources:
        lead = (None,) * (array.ndim - 2)
        shape = (*lead, array.shape[-2], D // parts)
        specs.append(pl.BlockSpec(shape, lambda i, f, where=where: (*where(f), 0, i)))
    return pl.pallas_call(
        body,
        grid_spec=pltpu.PrefetchScalarGridSpec(
            num_scalar_prefetch=1,
            grid=(parts,),
            in_specs=specs,
            out_specs=[
                pl.BlockSpec((*rows, D // parts), lambda i, f, n=len(rows): (*[0] * n, i)) for rows in out_rows
            ],
        ),
        out_shape=[jax.ShapeDtypeStruct((*rows, D), BF16) for rows in out_rows],
        cost_estimate=cost(0, 0),
        compiler_params=params(60),
        name=name,
    )(flags, *[array for array, _ in sources])


def core_merge_kernel(flags, *refs):
    ins, outs = refs[:14], refs[14:]
    for number in range(2):
        first, second, third = ins[3 * number : 3 * number + 3]
        outs[number][...] = (first[...].astype(F32) + second[...].astype(F32) + third[...].astype(F32)).astype(BF16)
    outs[2][...] = add(ins[6][...], ins[7][...])
    outs[3][...] = add(ins[8][...], ins[9][...])
    message = outs[4]
    block = ins[10].shape[0]
    message[:block, :] = add(ins[10][...], ins[11][...])
    spill = message.shape[0] - (block + 8)
    total = ins[12][...].astype(F32) + ins[13][...].astype(F32)
    message[block:, :] = jnp.concatenate([jnp.zeros((8, total.shape[1]), F32), total[block - spill :]]).astype(BF16)


def core_merge(flags, far, far_came, far_last, cross, cross_came):
    far, far_came, cross, cross_came = [blocks_of(v) for v in (far, far_came, cross, cross_came)]
    block = cross.shape[-2]
    spill = 2 * block - (D - QUERY_HEAD)
    sources = []
    for r in (lambda f: 1 - f[3] % 2, lambda f: f[3] % 2):
        sources += [(part, lambda f, r=r: (r(f), f[2], f[1])) for part in (far, far_came)]
        sources += [(far_last, lambda f, r=r: (r(f),))]
    chosen = [
        lambda f: (0, f[1]),
        lambda f: (1, f[1]),
        lambda f: (1 - f[0], 1 - f[1]),
        lambda f: (0, 1 - f[1]),
    ]
    for where in chosen:
        sources += [(cross, where), (cross_came, where)]
    return merge(core_merge_kernel, flags, sources, [(block,)] * 4 + [(block + 8 + spill,)], "core_merge")


def cross_second(at, mine, came):
    start = D - QUERY_HEAD
    block = mine[0].shape[-2]
    spill = 2 * block - start
    main = came[:block].astype(F32)
    tall = jnp.concatenate([jnp.zeros((block - spill, D), F32), came[block + 8 :].astype(F32)])
    ids = (at.c * 2 + at.x) * block + jnp.arange(block)[:, None]

    def half(index, y):
        part = jnp.where((at.c == 0) & (y == 0), tall, main)
        place = ids + y * 4 * block
        shared = (place >= start) & (place < start + 2 * D)
        own = jnp.where(index == 0, mine[0], mine[1]).astype(F32)
        return (own + jnp.where(shared, part, 0.0)).astype(BF16)

    return half(1 - at.y, 1 - at.y), half(at.y, at.y)


SWAP_ONE = [(0, 1), (1, 0), (2, 3), (3, 2)]
SWAP_TWO = [(0, 2), (2, 0), (1, 3), (3, 1)]


def finish(at, flags, block, far, far_last, near, near_send, cross, cross_came, vec_rows, extra):
    near_came = over_core(near_send)
    vec_came = over_core(vec_rows)
    far_out, far, low, high, message = core_merge(flags, *far, far_last, cross, cross_came)
    near_came, message, far_out, low, high, far = tie(near_came, message, far_out, low, high, far)
    came, far_came = over_x(message), over_z(far_out, SWAP_ONE)
    near, near_came = blocks_of(near), blocks_of(near_came)
    near_send = add(picked(near, 1 - at.y, at.x), picked(near_came, 1 - at.y, at.x))
    near = add(picked(near, at.y, at.x), picked(near_came, at.y, at.x))
    vec_rows = vec_rows + vec_came
    near_send, near, vec_rows, dk, dv, w = tie(near_send, near, vec_rows, *extra)
    near_came, vec_came = over_y(near_send), over_y(vec_rows)
    gm = memory_grads(dk, dv, w)
    gm, came = tie(gm, came)
    send, cross = cross_second(at, (low, high), came)
    send, near_came, far_came, cross = tie(send, near_came, far_came, cross)

    near = add(near, near_came)
    far = add(far, far_came)
    vec_rows = vec_rows + vec_came
    near, far, vec_rows, send = tie(near, far, vec_rows, send)
    cross_came, near_came = over_y(send), over_z(near, [(3, 2), (1, 0)])
    cut = block // 16 * 8
    far_top, vec_came = over_z(far[:cut], [(0, 2), (1, 3)]), over_z(vec_rows, SWAP_ONE)
    cross = add(cross, cross_came)
    near = add(near, near_came)
    vec_rows = vec_rows + vec_came
    near, cross, vec_rows, far_top, far = tie(near, cross, vec_rows, far_top, far)

    cross_came, near_came = over_z(cross, [(3, 2), (0, 1)]), over_z(near, [(2, 0)])
    far_low, vec_came = over_z(far[cut:], [(0, 2), (1, 3)]), over_z(vec_rows, SWAP_TWO)
    cross = add(cross, cross_came)
    vec_rows = vec_rows + vec_came
    near_came, cross, vec_rows, far_low = tie(near_came, cross, vec_rows, far_low)

    cross_came = over_z(cross, [(2, 1)])
    far_came = jnp.concatenate([far_top, far_low])
    kept = jnp.where(at.z >= 2, far, jnp.where(at.z == 0, near, cross))
    came = jnp.where(at.z >= 2, far_came, jnp.where(at.z == 0, near_came, cross_came))
    grad_rows = kept.astype(F32) + came.astype(F32)
    start = VEC_ROW - 31 * block
    last = jnp.concatenate([grad_rows[:start], vec_rows, jnp.zeros((block - start - VECS, D), F32)])
    is_last = (lax.axis_index("dp") == 15) & (at.x == 1)
    return jnp.where(is_last, last, grad_rows), gm


def shards(custom, inputs, memory, lengths, matched, cotangent, weights):
    axes = ("dp", "seq")
    share = 1.0 / lax.axis_size("seq")
    images, queries, _ = inputs.shape
    tokens = memory.shape[1]
    block = weights.shape[1]
    at = Place()
    left = lengths - at.x * tokens
    flags = jnp.stack([at.c if custom else 0, at.x, at.y, at.z]).astype(jnp.int32)

    def parts_of(value):
        if custom:
            return [value, over_x(value)]
        gathered = lax.all_gather(value, "seq")
        return [gathered[n] for n in range(gathered.shape[0])]

    if custom:
        bufs = gather(at, weights[0])
    else:
        bufs = [lax.all_gather(weights[0], axes, axis=0, tiled=True)]
    xb = jnp.pad(inputs, ((0, 0), (0, QP - queries), (0, 0))).reshape(images * QP, D)
    qs, ks, vs, os, y1, qc, key, value, mixed, stat, *w = forward(left, flags, xb, memory, bufs, queries)
    w = w[0] if custom else bufs[0]
    vec = w[VEC_ROW : VEC_ROW + VECS].astype(F32)
    near_rows = 4 * D + QUERY_HEAD
    far_rows = 2 * FF - HEAD_ROWS + TAIL
    cross_rows = 4 * D - QUERY_HEAD + HEAD_ROWS
    far_shape = (2, 2, 2 * block, D) if custom else (far_rows, D)
    near_shape = (2, 2 * block, D) if custom else (near_rows, D)
    cross_shape = (2, 2 * block, D) if custom else (cross_rows, D)
    out, *grads, db, doc, tot, dvec_mid = middle(
        flags, y1, parts_of(mixed), parts_of(stat), w, vec, cotangent, matched, far_shape, cross_shape, custom
    )
    far, cross = grads[: 1 + custom], grads[1 + custom :]
    if custom:
        far_came = over_core(far[1])
    dq, dk, dv = cross_backward(left, qc, key, value, doc, tot)
    dq_parts = parts_of(dq)
    if custom:
        far = [far[0], far_came]
    dcv_row, *cross = memory_weights(flags, cross, memory, dk, dv, far, custom)
    if custom:
        dcv_row = dcv_row + over_x(dcv_row)
        dq_parts[1], message = tie(dq_parts[1], cross.pop())
        far_last = over_y(message)
    da, gq_head, dvec_query, *cross = query_backward(flags, cross, y1, db, dq_parts, w, vec, custom)
    if custom:
        cross_came = over_core(cross[1])
    gq_head, dcv_row = tie(gq_head, dcv_row)
    gx, dvec_self, *near = self_backward(
        flags, xb, qs, ks, vs, os, da, gq_head, w, queries, near_shape, custom
    )
    vec_rows = (dvec_mid + dvec_query + dvec_self) * (1.0 if custom else share)
    is_value_bias = jnp.arange(VECS)[:, None] == 4
    vec_rows = jnp.where(is_value_bias, dcv_row[0:1], vec_rows)
    if custom:
        far_last, near_send = tie(far_last, near[1])
        grad_rows, gm = finish(
            at, flags, block, far, far_last, near[0], near_send, cross[0], cross_came, vec_rows, (dk, dv, w)
        )
    else:
        gm = memory_grads(dk, dv, w)
        low_share = jnp.asarray(share, BF16)
        pad = lax.axis_size(axes) * block - VEC_ROW - VECS
        last = 2 * FF - HEAD_ROWS
        memory_rows = slice(D - QUERY_HEAD, 3 * D - QUERY_HEAD)
        grads = jnp.concatenate(
            [near[0] * low_share, cross[0][: memory_rows.start] * low_share, cross[0][memory_rows]]
            + [cross[0][memory_rows.stop :] * low_share, far[0][:last] * low_share]
            + [vec_rows.astype(BF16), jnp.zeros((pad, D), BF16)]
        )
        grad_rows = lax.psum_scatter(grads, axes, scatter_dimension=0, tiled=True).astype(F32)
    return out[:, :queries], gx[:, :queries], gm, grad_rows[None]


def solution(mesh):
    placed = (
        P("dp", None, None),
        P("dp", "seq", None),
        P("dp"),
        P("dp", None),
        P("dp", None, None),
        P(None, ("dp", "seq"), None),
    )
    custom = dict(mesh.shape) == {"dp": 16, "seq": 2}
    return jax.shard_map(
        partial(shards, custom),
        mesh=mesh,
        in_specs=placed,
        out_specs=(
            P("dp", None, None),
            P("dp", None, None),
            P("dp", "seq", None),
            P(None, ("dp", "seq"), None),
        ),
        check_vma=False,
    )
```

profile of v0, /device:TPU:8, one launch (start us, length us, event | category | flops | bytes accessed | tf_op | source)
XLA Modules:
  0.0 322.9 jit_solution(15732686160632685045)
XLA Ops:
  1.4 1.5 collective-permute-start
  2.9 2.2 collective-permute-done
  6.5 1.6 collective-permute-start.2
  8.6 1.5 collective-permute-start.1
  10.1 2.6 collective-permute-start.8
  12.7 8.4 %collective-permute-done.2.refs_2_ = bf16[400,768]{1,0:T(8,128)(2,1)S(1)} collective-permute-done((bf16[400,768]{1,0:T(8,128)(2,1)S(1)}, bf16[400,768]{1,0:T(8,128)(2,1)S(1)}, u32[]{:S(2)}, u32[]{:S(2)}) %collective-permute-start.2) | collective-permute-done | bytes 614432 | tf_op jit(solution)/shard_map/ppermute | solution.py:976
  21.1 1.5 collective-permute-start.4
  22.5 9.6 %collective-permute-done.3.refs_3_ = bf16[400,768]{1,0:T(8,128)(2,1)S(1)} collective-permute-done((bf16[400,768]{1,0:T(8,128)(2,1)S(1)}, bf16[400,768]{1,0:T(8,128)(2,1)S(1)}, u32[]{:S(2)}, u32[]{:S(2)}) %collective-permute-start.3) | collective-permute-done | bytes 614432 | tf_op jit(solution)/shard_map/ppermute | solution.py:984
  32.5 2.5 collective-permute-start.6
  35.0 3.7 %collective-permute-done.8.refs_8_ = bf16[400,768]{1,0:T(8,128)(2,1)S(1)} collective-permute-done((bf16[400,768]{1,0:T(8,128)(2,1)S(1)}, bf16[400,768]{1,0:T(8,128)(2,1)S(1)}, u32[]{:S(2)}, u32[]{:S(2)}) %collective-permute-start.8) | collective-permute-done | bytes 614432 | tf_op jit(solution)/shard_map/ppermute | solution.py:984
  39.1 1.4 collective-permute-start.11
  40.5 8.4 %collective-permute-done.5.refs_5_ = bf16[400,768]{1,0:T(8,128)(2,1)S(1)} collective-permute-done((bf16[400,768]{1,0:T(8,128)(2,1)S(1)}, bf16[400,768]{1,0:T(8,128)(2,1)S(1)}, u32[]{:S(2)}, u32[]{:S(2)}) %collective-permute-start.5) | collective-permute-done | bytes 614432 | tf_op jit(solution)/shard_map/ppermute | solution.py:976
  48.9 1.9 collective-permute-done.6.refs_6_
  51.3 7.2 %collective-permute-done.10.refs_10_ = bf16[400,768]{1,0:T(8,128)(2,1)S(1)} collective-permute-done((bf16[400,768]{1,0:T(8,128)(2,1)S(1)}, bf16[400,768]{1,0:T(8,128)(2,1)S(1)}, u32[]{:S(2)}, u32[]{:S(2)}) %collective-permute-start.10) | collective-permute-done | bytes 614432 | tf_op jit(solution)/shard_map/ppermute | solution.py:976
  58.5 3.3 %collective-permute-done.11.refs_11_ = bf16[400,768]{1,0:T(8,128)(2,1)S(1)} collective-permute-done((bf16[400,768]{1,0:T(8,128)(2,1)S(1)}, bf16[400,768]{1,0:T(8,128)(2,1)S(1)}, u32[]{:S(2)}, u32[]{:S(2)}) %collective-permute-start.11) | collective-permute-done | bytes 614432 | tf_op jit(solution)/shard_map/ppermute | solution.py:984
  61.8 1.5 collective-permute-start.7
  64.4 1.7 collective-permute-start.14
  66.2 12.5 %collective-permute-done.7.refs_7_ = bf16[400,768]{1,0:T(8,128)(2,1)} collective-permute-done((bf16[400,768]{1,0:T(8,128)(2,1)S(1)}, bf16[400,768]{1,0:T(8,128)(2,1)}, u32[]{:S(2)}, u32[]{:S(2)}) %collective-permute-start.7) | collective-permute-done | bytes 614432 | tf_op jit(solution)/shard_map/ppermute | solution.py:980
  78.7 10.1 %collective-permute-done.12.refs_12_ = bf16[400,768]{1,0:T(8,128)(2,1)} collective-permute-done((bf16[400,768]{1,0:T(8,128)(2,1)S(1)}, bf16[400,768]{1,0:T(8,128)(2,1)}, u32[]{:S(2)}, u32[]{:S(2)}) %collective-permute-start.12) | collective-permute-done | bytes 614432 | tf_op jit(solution)/shard_map/ppermute | solution.py:980
  92.8 1.6 collective-permute-done.27.refs_27_
  94.5 11.6 %collective-permute-done.15.refs_15_ = bf16[400,768]{1,0:T(8,128)(2,1)} collective-permute-done((bf16[400,768]{1,0:T(8,128)(2,1)}, bf16[400,768]{1,0:T(8,128)(2,1)}, u32[]{:S(2)}, u32[]{:S(2)}) %collective-permute-start.15) | collective-permute-done | bytes 614432 | tf_op jit(solution)/shard_map/ppermute | solution.py:976
  108.7 21.6 %forward.1 = (bf16[336,768]{1,0:T(8,128)(2,1)}, bf16[336,768]{1,0:T(8,128)(2,1)}, bf16[336,768]{1,0:T(8,128)(2,1)}, bf16[336,768]{1,0:T(8,128)(2,1)}, f32[336,76...) custom-call(s32[3]{0:T(128)} %broadcast_subtract_fusion.left_ref, ...), custom_call_target="tpu_custom_call" | custom-call | tf_op jit(solution)/shard_map/forward/pallas_call | solution.py:298
  130.3 1.8 collective-permute-start.32
  133.0 1.4 slice_convert_fusion.refs_7_
  134.4 10.9 %collective-permute-done.33.refs_5_ = f32[3,8,224]{2,1,0:T(8,128)S(1)} collective-permute-done((f32[3,8,224]{2,1,0:T(8,128)}, f32[3,8,224]{2,1,0:T(8,128)S(1)}, u32[]{:S(2)}, u32[]{:S(2)}) %collective-permute-start.33) | collective-permute-done | bytes 21536 | tf_op jit(solution)/shard_map/ppermute | solution.py:980
  146.0 26.5 %middle.1 = (f32[3,112,768]{2,1,0:T(8,128)}, bf16[2,2,784,768]{3,2,1,0:T(8,128)(2,1)}, bf16[2,2,784,768]{3,2,1,0:T(8,128)(2,1)}, bf16[2,784,768]{2,1,0:T(8,128)(...) custom-call(s32[4]{0:T(128)} %pad_add_fusion.flags.refs_0_, ...), custom_call_target="tpu_custom_call" | custom-call | flops 10701766 | bytes 28311 | tf_op jit(solution)/shard_map/middle/pallas_call | solution.py:588
  172.6 10.2 %cross_backward.1 = (bf16[3,112,768]{2,1,0:T(8,128)(2,1)}, bf16[3,512,768]{2,1,0:T(8,128)(2,1)}, bf16[3,512,768]{2,1,0:T(8,128)(2,1)}) custom-call(s32[3]{0:T(128)} %broadcast_subtract_fusion.left_ref, bf16[3,112,768]{2,1,0:T(8,128)(2,1)} %bitcast.40, bf16[3,512,768]{2,1,0:T(8,128)(2,1)} %get-tuple-element.91.k_ref, ...), custom_call_target="tpu_custom_call" | custom-call | flops 352321 | bytes 9437 | tf_op jit(solution)/shard_map/cross_backward/pallas_call | solution.py:664
  182.9 1.7 collective-permute-start.35
  184.6 11.3 %memory_weights.1 = (f32[8,768]{1,0:T(8,128)}, bf16[2,784,768]{2,1,0:T(8,128)(2,1)}, bf16[2,784,768]{2,1,0:T(8,128)(2,1)}, bf16[2,392,768]{2,1,0:T(8,128)(2,1)}) custom-call(s32[4]{0:T(128)} %pad_add_fusion.flags.refs_0_, bf16[2,784,768]{2,1,0:T(8,128)(2,1)} %get-tuple-element.88.refs_0_, ...), custom_call_target="tpu_custom_call", output_to_operand_aliasing={{1}: (1, {}), {2}: (2, {})} | custom-call | flops 3623878 | bytes 7077 | tf_op jit(solution)/shard_map/memory_weights/pallas_call | solution.py:743
  198.4 1.7 collective-permute-start.36
  200.1 6.7 %query_backward.1 = (f32[336,768]{1,0:T(8,128)}, bf16[64,768]{1,0:T(8,128)(2,1)}, f32[24,768]{1,0:T(8,128)}, bf16[2,784,768]{2,1,0:T(8,128)(2,1)}, bf16[2,784,768]{2,1,0:T(8,128)(2,1)}) custom-call(s32[4]{0:T(128)} %pad_add_fusion.flags.refs_0_, bf16[2,784,768]{2,1,0:T(8,128)(2,1)} %get-tuple-element.99.refs_0_, ...), custom_call_target="tpu_custom_call", output_to_operand_aliasing={{3}: (1, {}), {4}: (2, {})} | custom-call | flops 792723 | bytes 4128 | tf_op jit(solution)/shard_map/query_backward/pallas_call | solution.py:843
  207.0 15.9 %self_backward.1 = (f32[3,112,768]{2,1,0:T(8,128)}, f32[24,768]{1,0:T(8,128)}, bf16[2,784,768]{2,1,0:T(8,128)(2,1)}, bf16[2,784,768]{2,1,0:T(8,128)(2,1)}) custom-call(s32[4]{0:T(128)} %pad_add_fusion.flags.refs_0_, bf16[336,768]{1,0:T(8,128)(2,1)} %get-tuple-element.87.refs_1_, f32[336,768]{1,0:T(8,128)} %get-tuple-element.105.refs_2_, ...), custom_call_target="tpu_custom_call" | custom-call | flops 6341787 | bytes 9437 | tf_op jit(solution)/shard_map/self_backward/pallas_call | solution.py:933
  222.9 2.8 collective-permute-done.37.refs_2_.refs_5_
  225.7 1.4 copy-done
  227.1 6.9 %core_merge.1 = (bf16[392,768]{1,0:T(8,128)(2,1)}, bf16[392,768]{1,0:T(8,128)(2,1)}, bf16[392,768]{1,0:T(8,128)(2,1)}, bf16[392,768]{1,0:T(8,128)(2,1)}, bf16[480,768]{1,0:T(8,128)(2,1)}) custom-call(s32[4]{0:T(128)} %pad_add_fusion.flags.refs_0_, bf16[2,2,2,392,768]{4,3,2,1,0:T(8,128)(2,1)} %bitcast.30, ...), custom_call_target="tpu_custom_call" | custom-call | tf_op jit(solution)/shard_map/core_merge/pallas_call | solution.py:1039
  234.1 1.8 collective-permute-start.41
  237.2 2.8 fusion.8
  243.1 8.0 %memory_grads.1 = f32[3,512,768]{2,1,0:T(8,128)} custom-call(bf16[3,512,768]{2,1,0:T(8,128)(2,1)} %get-tuple-element.130.refs_3_.dk_ref, bf16[3,512,768]{2,1,0:T(8,128)(2,1)} %get-tuple-element.131.refs_4_.dv_ref, bf16[12544,768]{1,0:T(8,128)(2,1)} %get-tuple-element.132.refs_6_.refs_7_.ck.cv, bf16[12544,768]{1,0:T(8,128)(2,1)} %get-tuple-element.132.refs_6_.refs_7_.ck.cv), custom_call_target="tpu_custom_call" | custom-call | flops 3623878656 | bytes 9437184 | tf_op jit(solution)/shard_map/memory_grads/pallas_call | solution.py:771
  251.2 6.4 %collective-permute-done.44 = f32[24,768]{1,0:T(8,128)S(1)} collective-permute-done((f32[24,768]{1,0:T(8,128)S(1)}, f32[24,768]{1,0:T(8,128)S(1)}, u32[]{:S(2)}, u32[]{:S(2)}) %collective-permute-start.44) | collective-permute-done | bytes 73760 | tf_op jit(solution)/shard_map/ppermute | solution.py:976
  259.4 3.0 collective-permute-start.45
  263.7 4.8 %collective-permute-start.48 = (bf16[192,768]{1,0:T(8,128)(2,1)S(1)}, bf16[192,768]{1,0:T(8,128)(2,1)S(1)}, u32[]{:S(2)}, u32[]{:S(2)}) collective-permute-start(bf16[192,768]{1,0:T(8,128)(2,1)S(1)} %slice.43), channel_id=1, source_target_pairs={{0,16},{2,18},{4,20},{6,22},{8,24},{10,26},{12,28},{14,30},{1,17},... | collective-permute-start | bytes 884744 | tf_op jit(solution)/shard_map/ppermute | solution.py:984
  268.5 7.8 %collective-permute-done.47 = f32[24,768]{1,0:T(8,128)S(1)} collective-permute-done((f32[24,768]{1,0:T(8,128)S(1)}, f32[24,768]{1,0:T(8,128)S(1)}, u32[]{:S(2)}, u32[]{:S(2)}) %collective-permute-start.47) | collective-permute-done | bytes 73760 | tf_op jit(solution)/shard_map/ppermute | solution.py:984
  277.2 3.1 collective-permute-done.48
  282.4 3.5 %collective-permute-start.51 = (f32[24,768]{1,0:T(8,128)S(1)}, f32[24,768]{1,0:T(8,128)S(1)}, u32[]{:S(2)}, u32[]{:S(2)}) collective-permute-start(f32[24,768]{1,0:T(8,128)S(1)} %add.154), channel_id=1, source_target_pairs={{0,16},{2,18},{4,20},{6,22},{16,0},{18,2},{20,4},{22,6},{8,24},{10... | collective-permute-start | bytes 221192 | tf_op jit(solution)/shard_map/ppermute | solution.py:984
  285.9 1.9 collective-permute-start.52
  287.8 11.4 %collective-permute-done.51 = f32[24,768]{1,0:T(8,128)S(1)} collective-permute-done((f32[24,768]{1,0:T(8,128)S(1)}, f32[24,768]{1,0:T(8,128)S(1)}, u32[]{:S(2)}, u32[]{:S(2)}) %collective-permute-start.51) | collective-permute-done | bytes 73760 | tf_op jit(solution)/shard_map/ppermute | solution.py:984
  304.1 15.7 %collective-permute-done.53 = bf16[392,768]{1,0:T(8,128)(2,1)} collective-permute-done((bf16[392,768]{1,0:T(8,128)(2,1)S(1)}, bf16[392,768]{1,0:T(8,128)(2,1)}, u32[]{:S(2)}, u32[]{:S(2)}) %collective-permute-start.53) | collective-permute-done | bytes 602144 | tf_op jit(solution)/shard_map/ppermute | solution.py:984
  319.9 1.6 convert_add_fusion
  (185 shorter events, 32.5 us)
Async XLA Ops:
  6.5 14.5 %collective-permute-start.2 = (bf16[400,768]{1,0:T(8,128)(2,1)S(1)}, bf16[400,768]{1,0:T(8,128)(2,1)S(1)}, u32[]{:S(2)}, u32[]{:S(2)}) collective-permute-start(bf16[400,768]{1,0:T(8,128)(2,1)S(1)} %maximum_select_fusion.1.refs_0_), channel_id=1, source_target_pairs={{0,4},{2,6},{4,0},{6,2},{8,12},{10,14},{12,8},{14,10},{16,20},{18,... | collective-permute-start | bytes 1843208 | tf_op jit(solution)/shard_map/ppermute | solution.py:976
  8.1 24.0 %collective-permute-start.3 = (bf16[400,768]{1,0:T(8,128)(2,1)S(1)}, bf16[400,768]{1,0:T(8,128)(2,1)S(1)}, u32[]{:S(2)}, u32[]{:S(2)}) collective-permute-start(bf16[400,768]{1,0:T(8,128)(2,1)S(1)} %maximum_select_fusion.1.refs_0_), channel_id=1, source_target_pairs={{0,8},{2,10},{4,12},{6,14},{8,0},{10,2},{12,4},{14,6},{16,24},{18,... | collective-permute-start | bytes 1843208 | tf_op jit(solution)/shard_map/ppermute | solution.py:984
  8.6 23.9 %collective-permute-start.1 = (bf16[400,768]{1,0:T(8,128)(2,1)S(1)}, bf16[400,768]{1,0:T(8,128)(2,1)S(1)}, u32[]{:S(2)}, u32[]{:S(2)}) collective-permute-start(bf16[400,768]{1,0:T(8,128)(2,1)S(1)} %maximum_select_fusion.1.refs_0_), channel_id=1, source_target_pairs={{0,1},{1,0},{2,3},{3,2},{4,5},{5,4},{6,7},{7,6},{8,9},{9,8},{10,11... | collective-permute-start | bytes 1843208 | tf_op jit(solution)/shard_map/ppermute | solution.py:980
  10.1 28.6 %collective-permute-start.8 = (bf16[400,768]{1,0:T(8,128)(2,1)S(1)}, bf16[400,768]{1,0:T(8,128)(2,1)S(1)}, u32[]{:S(2)}, u32[]{:S(2)}) collective-permute-start(bf16[400,768]{1,0:T(8,128)(2,1)S(1)} %maximum_select_fusion.1.refs_0_), channel_id=1, source_target_pairs={{0,16},{2,18},{4,20},{6,22},{16,0},{18,2},{20,4},{22,6},{8,24},{10... | collective-permute-start | bytes 1843208 | tf_op jit(solution)/shard_map/ppermute | solution.py:984
  12.7 26.0 %collective-permute-start.16 = (bf16[400,768]{1,0:T(8,128)(2,1)S(1)}, bf16[400,768]{1,0:T(8,128)(2,1)S(1)}, u32[]{:S(2)}, u32[]{:S(2)}) collective-permute-start(bf16[400,768]{1,0:T(8,128)(2,1)S(1)} %maximum_select_fusion.1.refs_0_), channel_id=1, source_target_pairs={{0,2},{2,0},{4,6},{6,4},{8,10},{10,8},{12,14},{14,12},{16,18},{18,... | collective-permute-start | bytes 1843208 | tf_op jit(solution)/shard_map/ppermute | solution.py:972
  21.1 18.0 %collective-permute-start.4 = (bf16[400,768]{1,0:T(8,128)(2,1)S(1)}, bf16[400,768]{1,0:T(8,128)(2,1)S(1)}, u32[]{:S(2)}, u32[]{:S(2)}) collective-permute-start(bf16[400,768]{1,0:T(8,128)(2,1)S(1)} %collective-permute-done.2.refs_2_), channel_id=1, source_target_pairs={{0,1},{1,0},{2,3},{3,2},{4,5},{5,4},{6,7},{7,6},{8,9},{9,8},{10,11... | collective-permute-start | bytes 1843208 | tf_op jit(solution)/shard_map/ppermute | solution.py:980
  32.1 16.8 %collective-permute-start.5 = (bf16[400,768]{1,0:T(8,128)(2,1)S(1)}, bf16[400,768]{1,0:T(8,128)(2,1)S(1)}, u32[]{:S(2)}, u32[]{:S(2)}) collective-permute-start(bf16[400,768]{1,0:T(8,128)(2,1)S(1)} %collective-permute-done.3.refs_3_), channel_id=1, source_target_pairs={{0,4},{2,6},{4,0},{6,2},{8,12},{10,14},{12,8},{14,10},{16,20},{18,... | collective-permute-start | bytes 1843208 | tf_op jit(solution)/shard_map/ppermute | solution.py:976
  32.5 18.4 %collective-permute-start.6 = (bf16[400,768]{1,0:T(8,128)(2,1)S(1)}, bf16[400,768]{1,0:T(8,128)(2,1)S(1)}, u32[]{:S(2)}, u32[]{:S(2)}) collective-permute-start(bf16[400,768]{1,0:T(8,128)(2,1)S(1)} %collective-permute-done.1.refs_1_), channel_id=1, source_target_pairs={{0,8},{2,10},{4,12},{6,14},{8,0},{10,2},{12,4},{14,6},{16,24},{18,... | collective-permute-start | bytes 1843208 | tf_op jit(solution)/shard_map/ppermute | solution.py:984
  38.6 12.2 %collective-permute-start.9 = (bf16[400,768]{1,0:T(8,128)(2,1)S(1)}, bf16[400,768]{1,0:T(8,128)(2,1)S(1)}, u32[]{:S(2)}, u32[]{:S(2)}) collective-permute-start(bf16[400,768]{1,0:T(8,128)(2,1)S(1)} %collective-permute-done.8.refs_8_), channel_id=1, source_target_pairs={{0,1},{1,0},{2,3},{3,2},{4,5},{5,4},{6,7},{7,6},{8,9},{9,8},{10,11... | collective-permute-start | bytes 1843208 | tf_op jit(solution)/shard_map/ppermute | solution.py:980
  38.6 19.9 %collective-permute-start.10 = (bf16[400,768]{1,0:T(8,128)(2,1)S(1)}, bf16[400,768]{1,0:T(8,128)(2,1)S(1)}, u32[]{:S(2)}, u32[]{:S(2)}) collective-permute-start(bf16[400,768]{1,0:T(8,128)(2,1)S(1)} %collective-permute-done.8.refs_8_), channel_id=1, source_target_pairs={{0,4},{2,6},{4,0},{6,2},{8,12},{10,14},{12,8},{14,10},{16,20},{18,... | collective-permute-start | bytes 1843208 | tf_op jit(solution)/shard_map/ppermute | solution.py:976
  39.1 22.8 %collective-permute-start.11 = (bf16[400,768]{1,0:T(8,128)(2,1)S(1)}, bf16[400,768]{1,0:T(8,128)(2,1)S(1)}, u32[]{:S(2)}, u32[]{:S(2)}) collective-permute-start(bf16[400,768]{1,0:T(8,128)(2,1)S(1)} %collective-permute-done.8.refs_8_), channel_id=1, source_target_pairs={{0,8},{2,10},{4,12},{6,14},{8,0},{10,2},{12,4},{14,6},{16,24},{18,... | collective-permute-start | bytes 1843208 | tf_op jit(solution)/shard_map/ppermute | solution.py:984
  48.9 14.4 %collective-permute-start.17 = (bf16[400,768]{1,0:T(8,128)(2,1)S(1)}, bf16[400,768]{1,0:T(8,128)(2,1)S(1)}, u32[]{:S(2)}, u32[]{:S(2)}) collective-permute-start(bf16[400,768]{1,0:T(8,128)(2,1)S(1)} %collective-permute-done.1.refs_1_), channel_id=1, source_target_pairs={{0,2},{2,0},{4,6},{6,4},{8,10},{10,8},{12,14},{14,12},{16,18},{18,... | collective-permute-start | bytes 1843208 | tf_op jit(solution)/shard_map/ppermute | solution.py:972
  50.8 13.0 %collective-permute-start.18 = (bf16[400,768]{1,0:T(8,128)(2,1)S(1)}, bf16[400,768]{1,0:T(8,128)(2,1)S(1)}, u32[]{:S(2)}, u32[]{:S(2)}) collective-permute-start(bf16[400,768]{1,0:T(8,128)(2,1)S(1)} %collective-permute-done.2.refs_2_), channel_id=1, source_target_pairs={{0,2},{2,0},{4,6},{6,4},{8,10},{10,8},{12,14},{14,12},{16,18},{18,... | collective-permute-start | bytes 1843208 | tf_op jit(solution)/shard_map/ppermute | solution.py:972
  50.9 13.5 %collective-permute-start.19 = (bf16[400,768]{1,0:T(8,128)(2,1)S(1)}, bf16[400,768]{1,0:T(8,128)(2,1)S(1)}, u32[]{:S(2)}, u32[]{:S(2)}) collective-permute-start(bf16[400,768]{1,0:T(8,128)(2,1)S(1)} %collective-permute-done.3.refs_3_), channel_id=1, source_target_pairs={{0,2},{2,0},{4,6},{6,4},{8,10},{10,8},{12,14},{14,12},{16,18},{18,... | collective-permute-start | bytes 1843208 | tf_op jit(solution)/shard_map/ppermute | solution.py:972
  58.5 7.6 %collective-permute-start.24 = (bf16[400,768]{1,0:T(8,128)(2,1)S(1)}, bf16[400,768]{1,0:T(8,128)(2,1)S(1)}, u32[]{:S(2)}, u32[]{:S(2)}) collective-permute-start(bf16[400,768]{1,0:T(8,128)(2,1)S(1)} %collective-permute-done.8.refs_8_), channel_id=1, source_target_pairs={{0,2},{2,0},{4,6},{6,4},{8,10},{10,8},{12,14},{14,12},{16,18},{18,... | collective-permute-start | bytes 1843208 | tf_op jit(solution)/shard_map/ppermute | solution.py:972
  61.8 16.9 %collective-permute-start.7 = (bf16[400,768]{1,0:T(8,128)(2,1)S(1)}, bf16[400,768]{1,0:T(8,128)(2,1)}, u32[]{:S(2)}, u32[]{:S(2)}) collective-permute-start(bf16[400,768]{1,0:T(8,128)(2,1)S(1)} %collective-permute-done.5.refs_5_), channel_id=1, source_target_pairs={{0,1},{1,0},{2,3},{3,2},{4,5},{5,4},{6,7},{7,6},{8,9},{9,8},{10,11... | collective-permute-start | bytes 1843208 | tf_op jit(solution)/shard_map/ppermute | solution.py:980
  63.3 25.5 %collective-permute-start.12 = (bf16[400,768]{1,0:T(8,128)(2,1)S(1)}, bf16[400,768]{1,0:T(8,128)(2,1)}, u32[]{:S(2)}, u32[]{:S(2)}) collective-permute-start(bf16[400,768]{1,0:T(8,128)(2,1)S(1)} %collective-permute-done.10.refs_10_), channel_id=1, source_target_pairs={{0,1},{1,0},{2,3},{3,2},{4,5},{5,4},{6,7},{7,6},{8,9},{9,8},{10,11... | collective-permute-start | bytes 1843208 | tf_op jit(solution)/shard_map/ppermute | solution.py:980
  63.9 25.0 %collective-permute-start.13 = (bf16[400,768]{1,0:T(8,128)(2,1)S(1)}, bf16[400,768]{1,0:T(8,128)(2,1)}, u32[]{:S(2)}, u32[]{:S(2)}) collective-permute-start(bf16[400,768]{1,0:T(8,128)(2,1)S(1)} %collective-permute-done.11.refs_11_), channel_id=1, source_target_pairs={{0,4},{2,6},{4,0},{6,2},{8,12},{10,14},{12,8},{14,10},{16,20},{18,... | collective-permute-start | bytes 1843208 | tf_op jit(solution)/shard_map/ppermute | solution.py:976
  64.4 25.0 %collective-permute-start.14 = (bf16[400,768]{1,0:T(8,128)(2,1)S(1)}, bf16[400,768]{1,0:T(8,128)(2,1)}, u32[]{:S(2)}, u32[]{:S(2)}) collective-permute-start(bf16[400,768]{1,0:T(8,128)(2,1)S(1)} %collective-permute-done.9.refs_9_), channel_id=1, source_target_pairs={{0,8},{2,10},{4,12},{6,14},{8,0},{10,2},{12,4},{14,6},{16,24},{18,... | collective-permute-start | bytes 1843208 | tf_op jit(solution)/shard_map/ppermute | solution.py:984
  66.1 23.3 %collective-permute-start.20 = (bf16[400,768]{1,0:T(8,128)(2,1)S(1)}, bf16[400,768]{1,0:T(8,128)(2,1)S(1)}, u32[]{:S(2)}, u32[]{:S(2)}) collective-permute-start(bf16[400,768]{1,0:T(8,128)(2,1)S(1)} %collective-permute-done.4.refs_4_), channel_id=1, source_target_pairs={{0,2},{2,0},{4,6},{6,4},{8,10},{10,8},{12,14},{14,12},{16,18},{18,... | collective-permute-start | bytes 1843208 | tf_op jit(solution)/shard_map/ppermute | solution.py:972
  78.7 11.2 %collective-permute-start.21 = (bf16[400,768]{1,0:T(8,128)(2,1)S(1)}, bf16[400,768]{1,0:T(8,128)(2,1)S(1)}, u32[]{:S(2)}, u32[]{:S(2)}) collective-permute-start(bf16[400,768]{1,0:T(8,128)(2,1)S(1)} %collective-permute-done.5.refs_5_), channel_id=1, source_target_pairs={{0,2},{2,0},{4,6},{6,4},{8,10},{10,8},{12,14},{14,12},{16,18},{18,... | collective-permute-start | bytes 1843208 | tf_op jit(solution)/shard_map/ppermute | solution.py:972
  89.4 5.0 %collective-permute-start.27 = (bf16[400,768]{1,0:T(8,128)(2,1)S(1)}, bf16[400,768]{1,0:T(8,128)(2,1)S(1)}, u32[]{:S(2)}, u32[]{:S(2)}) collective-permute-start(bf16[400,768]{1,0:T(8,128)(2,1)S(1)} %collective-permute-done.11.refs_11_), channel_id=1, source_target_pairs={{0,2},{2,0},{4,6},{6,4},{8,10},{10,8},{12,14},{14,12},{16,18},{18,... | collective-permute-start | bytes 1843208 | tf_op jit(solution)/shard_map/ppermute | solution.py:972
  89.9 16.2 %collective-permute-start.15 = (bf16[400,768]{1,0:T(8,128)(2,1)}, bf16[400,768]{1,0:T(8,128)(2,1)}, u32[]{:S(2)}, u32[]{:S(2)}) collective-permute-start(bf16[400,768]{1,0:T(8,128)(2,1)} %collective-permute-done.14.refs_14_), channel_id=1, source_target_pairs={{0,4},{2,6},{4,0},{6,2},{8,12},{10,14},{12,8},{14,10},{16,20},{18,... | collective-permute-start | bytes 1843208 | tf_op jit(solution)/shard_map/ppermute | solution.py:976
  90.9 17.4 %collective-permute-start.30 = (bf16[400,768]{1,0:T(8,128)(2,1)}, bf16[400,768]{1,0:T(8,128)(2,1)}, u32[]{:S(2)}, u32[]{:S(2)}) collective-permute-start(bf16[400,768]{1,0:T(8,128)(2,1)} %collective-permute-done.14.refs_14_), channel_id=1, source_target_pairs={{0,2},{2,0},{4,6},{6,4},{8,10},{10,8},{12,14},{14,12},{16,18},{18,... | collective-permute-start | bytes 1843208 | tf_op jit(solution)/shard_map/ppermute | solution.py:972
  91.8 16.5 %collective-permute-start.23 = (bf16[400,768]{1,0:T(8,128)(2,1)}, bf16[400,768]{1,0:T(8,128)(2,1)}, u32[]{:S(2)}, u32[]{:S(2)}) collective-permute-start(bf16[400,768]{1,0:T(8,128)(2,1)} %collective-permute-done.7.refs_7_), channel_id=1, source_target_pairs={{0,2},{2,0},{4,6},{6,4},{8,10},{10,8},{12,14},{14,12},{16,18},{18,... | collective-permute-start | bytes 1843208 | tf_op jit(solution)/shard_map/ppermute | solution.py:972
  92.6 15.6 %collective-permute-start.28 = (bf16[400,768]{1,0:T(8,128)(2,1)}, bf16[400,768]{1,0:T(8,128)(2,1)}, u32[]{:S(2)}, u32[]{:S(2)}) collective-permute-start(bf16[400,768]{1,0:T(8,128)(2,1)} %collective-permute-done.12.refs_12_), channel_id=1, source_target_pairs={{0,2},{2,0},{4,6},{6,4},{8,10},{10,8},{12,14},{14,12},{16,18},{18,... | collective-permute-start | bytes 1843208 | tf_op jit(solution)/shard_map/ppermute | solution.py:972
  94.4 13.9 %collective-permute-start.29 = (bf16[400,768]{1,0:T(8,128)(2,1)}, bf16[400,768]{1,0:T(8,128)(2,1)}, u32[]{:S(2)}, u32[]{:S(2)}) collective-permute-start(bf16[400,768]{1,0:T(8,128)(2,1)} %collective-permute-done.13.refs_13_), channel_id=1, source_target_pairs={{0,2},{2,0},{4,6},{6,4},{8,10},{10,8},{12,14},{14,12},{16,18},{18,... | collective-permute-start | bytes 1843208 | tf_op jit(solution)/shard_map/ppermute | solution.py:972
  130.3 14.9 %collective-permute-start.32 = (bf16[3,112,768]{2,1,0:T(8,128)(2,1)}, bf16[3,112,768]{2,1,0:T(8,128)(2,1)S(1)}, u32[]{:S(2)}, u32[]{:S(2)}) collective-permute-start(bf16[3,112,768]{2,1,0:T(8,128)(2,1)} %get-tuple-element.83.refs_2_), channel_id=1, source_target_pairs={{0,1},{1,0},{2,3},{3,2},{4,5},{5,4},{6,7},{7,6},{8,9},{9,8},{10,11... | collective-permute-start | bytes 1548296 | tf_op jit(solution)/shard_map/ppermute | solution.py:980
  132.6 12.6 %collective-permute-start.33 = (f32[3,8,224]{2,1,0:T(8,128)}, f32[3,8,224]{2,1,0:T(8,128)S(1)}, u32[]{:S(2)}, u32[]{:S(2)}) collective-permute-start(f32[3,8,224]{2,1,0:T(8,128)} %get-tuple-element.84.refs_4_), channel_id=1, source_target_pairs={{0,1},{1,0},{2,3},{3,2},{4,5},{5,4},{6,7},{7,6},{8,9},{9,8},{10,11... | collective-permute-start | bytes 64520 | tf_op jit(solution)/shard_map/ppermute | solution.py:980
  172.6 12.0 %collective-permute-start.34 = (bf16[2,2,784,768]{3,2,1,0:T(8,128)(2,1)}, bf16[2,2,784,768]{3,2,1,0:T(8,128)(2,1)}, u32[]{:S(2)}, u32[]{:S(2)}) collective-permute-start(bf16[2,2,784,768]{3,2,1,0:T(8,128)(2,1)} %get-tuple-element.98), channel_id=1, source_target_pairs={{0,2},{2,0},{4,6},{6,4},{8,10},{10,8},{12,14},{14,12},{16,18},{18,... | collective-permute-start | bytes 14450696 | tf_op jit(solution)/shard_map/ppermute | solution.py:972
  182.9 14.4 %collective-permute-start.35 = (bf16[3,112,768]{2,1,0:T(8,128)(2,1)}, bf16[3,112,768]{2,1,0:T(8,128)(2,1)S(1)}, u32[]{:S(2)}, u32[]{:S(2)}) collective-permute-start(bf16[3,112,768]{2,1,0:T(8,128)(2,1)} %get-tuple-element.101), channel_id=1, source_target_pairs={{0,1},{1,0},{2,3},{3,2},{4,5},{5,4},{6,7},{7,6},{8,9},{9,8},{10,11... | collective-permute-start | bytes 1548296 | tf_op jit(solution)/shard_map/ppermute | solution.py:980
  197.2 28.4 %collective-permute-start.37 = (bf16[2,392,768]{2,1,0:T(8,128)(2,1)}, bf16[2,392,768]{2,1,0:T(8,128)(2,1)}, u32[]{:S(2)}, u32[]{:S(2)}) collective-permute-start(bf16[2,392,768]{2,1,0:T(8,128)(2,1)} %get-tuple-element.114), channel_id=1, source_target_pairs={{0,4},{2,6},{4,0},{6,2},{8,12},{10,14},{12,8},{14,10},{16,20},{18,... | collective-permute-start | bytes 3612680 | tf_op jit(solution)/shard_map/ppermute | solution.py:976
  198.4 8.6 %collective-permute-start.36 = (f32[8,768]{1,0:T(8,128)}, f32[8,768]{1,0:T(8,128)S(1)}, u32[]{:S(2)}, u32[]{:S(2)}) collective-permute-start(f32[8,768]{1,0:T(8,128)} %get-tuple-element.110), channel_id=1, source_target_pairs={{0,1},{1,0},{2,3},{3,2},{4,5},{5,4},{6,7},{7,6},{8,9},{9,8},{10,11... | collective-permute-start | bytes 73736 | tf_op jit(solution)/shard_map/ppermute | solution.py:980
  206.9 18.8 %collective-permute-start.39 = (bf16[2,784,768]{2,1,0:T(8,128)(2,1)}, bf16[2,784,768]{2,1,0:T(8,128)(2,1)S(1)}, u32[]{:S(2)}, u32[]{:S(2)}) collective-permute-start(bf16[2,784,768]{2,1,0:T(8,128)(2,1)} %get-tuple-element.119), channel_id=1, source_target_pairs={{0,2},{2,0},{4,6},{6,4},{8,10},{10,8},{12,14},{14,12},{16,18},{18,... | collective-permute-start | bytes 7225352 | tf_op jit(solution)/shard_map/ppermute | solution.py:972
  225.6 8.4 %collective-permute-start.38 = (bf16[2,784,768]{2,1,0:T(8,128)(2,1)}, bf16[2,784,768]{2,1,0:T(8,128)(2,1)}, u32[]{:S(2)}, u32[]{:S(2)}) collective-permute-start(bf16[2,784,768]{2,1,0:T(8,128)(2,1)} %get-tuple-element.116), channel_id=1, source_target_pairs={{0,2},{2,0},{4,6},{6,4},{8,10},{10,8},{12,14},{14,12},{16,18},{18,... | collective-permute-start | bytes 7225352 | tf_op jit(solution)/shard_map/ppermute | solution.py:972
  234.1 23.5 %collective-permute-start.41 = (bf16[480,768]{1,0:T(8,128)(2,1)}, bf16[480,768]{1,0:T(8,128)(2,1)S(1)}, u32[]{:S(2)}, u32[]{:S(2)}) collective-permute-start(bf16[480,768]{1,0:T(8,128)(2,1)} %get-tuple-element.133), channel_id=1, source_target_pairs={{0,1},{1,0},{2,3},{3,2},{4,5},{5,4},{6,7},{7,6},{8,9},{9,8},{10,11... | collective-permute-start | bytes 2211848 | tf_op jit(solution)/shard_map/ppermute | solution.py:980
  240.0 18.1 %collective-permute-start.42 = (bf16[392,768]{1,0:T(8,128)(2,1)}, bf16[392,768]{1,0:T(8,128)(2,1)S(1)}, u32[]{:S(2)}, u32[]{:S(2)}) collective-permute-start(bf16[392,768]{1,0:T(8,128)(2,1)} %get-tuple-element.139), channel_id=1, source_target_pairs={{0,4},{2,6},{4,0},{6,2},{8,12},{10,14},{12,8},{14,10},{16,20},{18,... | collective-permute-start | bytes 1806344 | tf_op jit(solution)/shard_map/ppermute | solution.py:976
  241.2 16.9 %collective-permute-start.43 = (bf16[392,768]{1,0:T(8,128)(2,1)}, bf16[392,768]{1,0:T(8,128)(2,1)S(1)}, u32[]{:S(2)}, u32[]{:S(2)}) collective-permute-start(bf16[392,768]{1,0:T(8,128)(2,1)} %get-tuple-element.140), channel_id=1, source_target_pairs={{0,8},{2,10},{4,12},{6,14},{8,0},{10,2},{12,4},{14,6},{16,24},{18,... | collective-permute-start | bytes 1806344 | tf_op jit(solution)/shard_map/ppermute | solution.py:984
  242.3 15.2 %collective-permute-start.44 = (f32[24,768]{1,0:T(8,128)S(1)}, f32[24,768]{1,0:T(8,128)S(1)}, u32[]{:S(2)}, u32[]{:S(2)}) collective-permute-start(f32[24,768]{1,0:T(8,128)S(1)} %add.139), channel_id=1, source_target_pairs={{0,4},{2,6},{4,0},{6,2},{8,12},{10,14},{12,8},{14,10},{16,20},{18,... | collective-permute-start | bytes 221192 | tf_op jit(solution)/shard_map/ppermute | solution.py:976
  259.4 17.0 %collective-permute-start.45 = (bf16[392,768]{1,0:T(8,128)(2,1)S(1)}, bf16[392,768]{1,0:T(8,128)(2,1)S(1)}, u32[]{:S(2)}, u32[]{:S(2)}) collective-permute-start(bf16[392,768]{1,0:T(8,128)(2,1)S(1)} %add_convert_fusion.4), channel_id=1, source_target_pairs={{24,16},{26,18},{28,20},{30,22},{8,0},{10,2},{12,4},{14,6},{25,17}... | collective-permute-start | bytes 1806344 | tf_op jit(solution)/shard_map/ppermute | solution.py:984
  262.4 14.7 %collective-permute-start.46 = (bf16[392,768]{1,0:T(8,128)(2,1)S(1)}, bf16[392,768]{1,0:T(8,128)(2,1)S(1)}, u32[]{:S(2)}, u32[]{:S(2)}) collective-permute-start(bf16[392,768]{1,0:T(8,128)(2,1)S(1)} %get-tuple-element.148), channel_id=1, source_target_pairs={{0,4},{2,6},{4,0},{6,2},{8,12},{10,14},{12,8},{14,10},{16,20},{18,... | collective-permute-start | bytes 1806344 | tf_op jit(solution)/shard_map/ppermute | solution.py:976
  263.7 12.7 %collective-permute-start.47 = (f32[24,768]{1,0:T(8,128)S(1)}, f32[24,768]{1,0:T(8,128)S(1)}, u32[]{:S(2)}, u32[]{:S(2)}) collective-permute-start(f32[24,768]{1,0:T(8,128)S(1)} %add.151), channel_id=1, source_target_pairs={{0,8},{2,10},{4,12},{6,14},{8,0},{10,2},{12,4},{14,6},{16,24},{18,... | collective-permute-start | bytes 221192 | tf_op jit(solution)/shard_map/ppermute | solution.py:984
  263.7 16.7 %collective-permute-start.48 = (bf16[192,768]{1,0:T(8,128)(2,1)S(1)}, bf16[192,768]{1,0:T(8,128)(2,1)S(1)}, u32[]{:S(2)}, u32[]{:S(2)}) collective-permute-start(bf16[192,768]{1,0:T(8,128)(2,1)S(1)} %slice.43), channel_id=1, source_target_pairs={{0,16},{2,18},{4,20},{6,22},{8,24},{10,26},{12,28},{14,30},{1,17},... | collective-permute-start | bytes 884744 | tf_op jit(solution)/shard_map/ppermute | solution.py:984
  280.4 18.9 %collective-permute-start.50 = (bf16[392,768]{1,0:T(8,128)(2,1)S(1)}, bf16[392,768]{1,0:T(8,128)(2,1)S(1)}, u32[]{:S(2)}, u32[]{:S(2)}) collective-permute-start(bf16[392,768]{1,0:T(8,128)(2,1)S(1)} %add_convert_fusion.1), channel_id=1, source_target_pairs={{24,16},{26,18},{28,20},{30,22},{0,8},{2,10},{4,12},{6,14},{25,17}... | collective-permute-start | bytes 1806344 | tf_op jit(solution)/shard_map/ppermute | solution.py:984
  281.7 17.8 %collective-permute-start.49 = (bf16[392,768]{1,0:T(8,128)(2,1)S(1)}, bf16[392,768]{1,0:T(8,128)(2,1)S(1)}, u32[]{:S(2)}, u32[]{:S(2)}) collective-permute-start(bf16[392,768]{1,0:T(8,128)(2,1)S(1)} %add_convert_fusion.2), channel_id=1, source_target_pairs={{16,0},{18,2},{20,4},{22,6},{17,1},{19,3},{21,5},{23,7}} | collective-permute-start | bytes 1806344 | tf_op jit(solution)/shard_map/ppermute | solution.py:984
  282.4 16.9 %collective-permute-start.51 = (f32[24,768]{1,0:T(8,128)S(1)}, f32[24,768]{1,0:T(8,128)S(1)}, u32[]{:S(2)}, u32[]{:S(2)}) collective-permute-start(f32[24,768]{1,0:T(8,128)S(1)} %add.154), channel_id=1, source_target_pairs={{0,16},{2,18},{4,20},{6,22},{16,0},{18,2},{20,4},{22,6},{8,24},{10... | collective-permute-start | bytes 221192 | tf_op jit(solution)/shard_map/ppermute | solution.py:984
  285.9 13.6 %collective-permute-start.52 = (bf16[200,768]{1,0:T(8,128)(2,1)S(1)}, bf16[200,768]{1,0:T(8,128)(2,1)S(1)}, u32[]{:S(2)}, u32[]{:S(2)}) collective-permute-start(bf16[200,768]{1,0:T(8,128)(2,1)S(1)} %slice.44), channel_id=1, source_target_pairs={{0,16},{2,18},{4,20},{6,22},{8,24},{10,26},{12,28},{14,30},{1,17},... | collective-permute-start | bytes 921608 | tf_op jit(solution)/shard_map/ppermute | solution.py:984
  300.2 19.7 %collective-permute-start.53 = (bf16[392,768]{1,0:T(8,128)(2,1)S(1)}, bf16[392,768]{1,0:T(8,128)(2,1)}, u32[]{:S(2)}, u32[]{:S(2)}) collective-permute-start(bf16[392,768]{1,0:T(8,128)(2,1)S(1)} %add_convert_fusion), channel_id=1, source_target_pairs={{16,8},{18,10},{20,12},{22,14},{17,9},{19,11},{21,13},{23,15}} | collective-permute-start | bytes 1806344 | tf_op jit(solution)/shard_map/ppermute | solution.py:984
  (48 other events, 1289.2 us)
where the time goes:
time: 327 us; the launch traced here: 323 us
  waiting for transfers between devices  144 us (44%)
  Pallas kernels  107 us (33%)
  starting transfers between devices  50.6 us (15%)
  other arithmetic  11.7 us (4%)
  local copies, waits for them, and re-layouts  8.08 us (2%)
    ppermute x14, waiting for transfers between devices, over_z(): lax.ppermute(v, 'dp', [(4 * a + i, 4 * b + i) for a, b in hops for i in r...  56.6 us
    ppermute x9, waiting for transfers between devices, over_y(): return lax.ppermute(v, 'dp', [(i, i ^ 2) for i in range(16)])  45.2 us
    ppermute x11, waiting for transfers between devices, over_x(): return lax.ppermute(v, 'seq', [(0, 1), (1, 0)])  37 us
    pallas_call x1, Pallas kernels, middle(): pl.pallas_call(partial(middle_kernel, parts, split), grid_spec=pltpu.Pref...  26.5 us
    ppermute x14, starting transfers between devices, over_z(): lax.ppermute(v, 'dp', [(4 * a + i, 4 * b + i) for a, b in hops for i in r...  26.3 us
    pallas_call x1, Pallas kernels, forward(): pl.pallas_call(partial(forward_kernel, queries, custom), grid_spec=pltpu....  21.6 us
    pallas_call x1, Pallas kernels, self_backward(): pl.pallas_call(partial(self_backward_kernel, queries, split), grid_spec=p...  15.9 us
    ppermute x11, starting transfers between devices, over_x(): return lax.ppermute(v, 'seq', [(0, 1), (1, 0)])  13.8 us
  transfers between devices with their start and end apart: 54, of which 26 were waited for; matrix products, arithmetic and copies ran while one was open for 3% of the time, Pallas kernels for 18%

commit v1 on v0

--- a/solution.py
+++ b/solution.py
@@ -225,15 +225,20 @@
     leave(2).start()
     masks = head_masks()
     real = lax.broadcasted_iota(jnp.int32, (2 * QP, QP), 1) < queries
-    for image in range(images):
-        rows = slice(image * QP, (image + 1) * QP)
-        for pair in range(PAIRS):
-            lanes = slice(pair * LANES, (pair + 1) * LANES)
-            scores = dot_nt(two_heads(qs_ref[rows, lanes], masks), ks_ref[rows, lanes])
-            scores = jnp.where(real, scores, NEG)
-            probs = jnp.exp(scores - jnp.max(scores, axis=-1, keepdims=True))
-            probs = probs / jnp.sum(probs, axis=-1, keepdims=True)
-            os_ref[rows, lanes] = join_heads(dot_nn(probs.astype(BF16), vs_ref[rows, lanes])).astype(BF16)
+    places = [(slice(i * QP, (i + 1) * QP), slice(p * LANES, (p + 1) * LANES)) for i in range(images) for p in range(PAIRS)]
+
+    def raw_self(place):
+        return dot_nt(two_heads(qs_ref[place], masks), ks_ref[place])
+
+    following = raw_self(places[0])
+    for number, place in enumerate(places):
+        scores = following
+        if number + 1 < len(places):
+            following = raw_self(places[number + 1])
+        scores = jnp.where(real, scores, NEG)
+        probs = jnp.exp(scores - jnp.max(scores, axis=-1, keepdims=True))
+        probs = probs / jnp.sum(probs, axis=-1, keepdims=True)
+        os_ref[place] = join_heads(dot_nn(probs.astype(BF16), vs_ref[place])).astype(BF16)
     leave(3).start()
     y1 = xb.astype(F32) + (dot_nn(os_ref[...], matrix(3)) + vec[2:3, :])
     y1_ref[...] = y1
@@ -259,9 +264,16 @@
         leave_image(image, 1).start()
         valid = lax.broadcasted_iota(jnp.int32, (2 * QP, tokens), 1) < left_ref[image]
         stat = jnp.zeros((2 * QP, 128), F32)
+        def raw(pair):
+            lanes = slice(pair * LANES, (pair + 1) * LANES)
+            return dot_nt(two_heads(qc_ref[rows, lanes], masks), k_ref[image, :, lanes])
+
+        following = raw(0)
         for pair in range(PAIRS):
             lanes = slice(pair * LANES, (pair + 1) * LANES)
-            scores = dot_nt(two_heads(qc_ref[rows, lanes], masks), k_ref[image, :, lanes])
+            scores = following
+            if pair + 1 < PAIRS:
+                following = raw(pair + 1)
             scores = jnp.where(valid, scores, NEG)
             top = jnp.max(scores, axis=-1, keepdims=True)
             probs = jnp.exp(scores - top)
@@ -642,18 +654,23 @@
     tokens = k_ref.shape[1]
     masks = head_masks()
     valid = lax.broadcasted_iota(jnp.int32, (tokens, 2 * QP), 0) < left_ref[pl.program_id(0)]
+    def raw(pair):
+        lanes = slice(pair * LANES, (pair + 1) * LANES)
+        query = two_heads(q_ref[0, :, lanes], masks)
+        dout = two_heads(do_ref[0, :, lanes], masks)
+        return query, dout, dot_nt(k_ref[0, :, lanes], query), dot_nt(v_ref[0, :, lanes], dout)
+
+    following = raw(0)
     for pair in range(PAIRS):
         lanes = slice(pair * LANES, (pair + 1) * LANES)
-        key, value = k_ref[0, :, lanes], v_ref[0, :, lanes]
-        query = two_heads(q_ref[0, :, lanes], masks)
-        dout = two_heads(do_ref[0, :, lanes], masks)
-        scores = dot_nt(key, query)
+        query, dout, scores, dprobs = following
+        if pair + 1 < PAIRS:
+            following = raw(pair + 1)
         probs = jnp.where(valid, jnp.exp(scores - tot_ref[0, pair : pair + 1, :]), 0.0)
-        dprobs = dot_nt(value, dout)
         dscores = (probs * (dprobs - tot_ref[0, 8 + pair : 9 + pair, :])).astype(BF16)
         dv_ref[0, :, lanes] = dot_nn(probs.astype(BF16), dout).astype(BF16)
         dk_ref[0, :, lanes] = dot_nn(dscores, query).astype(BF16)
-        dq_ref[0, :, lanes] = join_heads(dot_tn(key, dscores).T).astype(BF16)
+        dq_ref[0, :, lanes] = join_heads(dot_tn(k_ref[0, :, lanes], dscores).T).astype(BF16)
 
 
 def cross_backward(left, qc, key, value, doc, tot):
@@ -683,12 +700,6 @@
 def memory_weights_kernel(split, flags, *refs):
     m_ref, dk_ref, dv_ref = refs[1 + split : 4 + split]
     refs = refs[4 + split :]
-    if split:
-        a, b, c, d = refs[:4]
-        far_out = refs[-4]
-        far_out[0] = add(a[...], b[...])
-        far_out[1] = add(c[...], d[...])
-        refs = refs[4:-4] + refs[-3:]
     gb_ref = refs[0]
     halves = Halves(refs[1], refs[2] if split else None, flags[0])
     sums, low, sems = refs[2 + split :]
@@ -723,42 +734,29 @@
             leave(which, "wait")
 
 
-def memory_weights(flags, cross, memory, dk, dv, far, split):
+def memory_weights(flags, cross, memory, dk, dv, split):
     images, tokens, _ = memory.shape
     block = pl.BlockSpec((1, tokens, D), lambda i, _: (i, 0, 0))
     anywhere = pl.BlockSpec(memory_space=pl.ANY)
-    far = [blocks_of(part) for part in far]
-    part = D // images
-    sources, far_specs, far_out, far_shape = [], [], [], []
-    if split:
-        rows = far[0].shape[-2]
-        for r in (0, 1):
-            for array in far:
-                sources.append(array)
-                far_specs.append(
-                    pl.BlockSpec((None, None, None, rows, part), lambda i, f, r=r: (r, 1 - f[2], f[1], 0, i))
-                )
-        far_out = [pl.BlockSpec((2, rows, part), lambda i, f: (0, 0, i))]
-        far_shape = [jax.ShapeDtypeStruct((2, rows, D), BF16)]
     return pl.pallas_call(
         partial(memory_weights_kernel, split),
         grid_spec=pltpu.PrefetchScalarGridSpec(
             num_scalar_prefetch=1,
             grid=(images,),
-            in_specs=[anywhere] * (1 + split) + [block, block, block] + far_specs,
-            out_specs=[whole((8, D))] + [anywhere] * (1 + split) + far_out,
+            in_specs=[anywhere] * (1 + split) + [block, block, block],
+            out_specs=[whole((8, D))] + [anywhere] * (1 + split),
             scratch_shapes=[
                 pltpu.VMEM((2, D, D), F32),
                 pltpu.VMEM((2, D, D), BF16),
                 pltpu.SemaphoreType.DMA((2, 2)),
             ],
         ),
-        out_shape=[jax.ShapeDtypeStruct((8, D), F32)] + halves_shape(cross[0].shape, split) + far_shape,
+        out_shape=[jax.ShapeDtypeStruct((8, D), F32)] + halves_shape(cross[0].shape, split),
         input_output_aliases={1 + n: 1 + n for n in range(1 + split)},
         cost_estimate=cost(4 * images * tokens * D * D, images * tokens * D * 6),
         compiler_params=params(60),
         name="memory_weights",
-    )(flags, *cross, memory, dk, dv, *sources)
+    )(flags, *cross, memory, dk, dv)
 
 
 def memory_grads_kernel(dk_ref, dv_ref, ck, cv, gm_ref):
@@ -893,21 +891,25 @@
         get(number)
     masks = head_masks()
     real = lax.broadcasted_iota(jnp.int32, (QP, 2 * QP), 0) < queries
-    for image in range(images):
-        rows = slice(image * QP, (image + 1) * QP)
-        for pair in range(PAIRS):
-            lanes = slice(pair * LANES, (pair + 1) * LANES)
-            key, value = ks[rows, lanes], vs[rows, lanes]
-            query = two_heads(qs[rows, lanes], masks)
-            dout = two_heads(dos[rows, lanes], masks)
-            scores = jnp.where(real, dot_nt(key, query), NEG)
-            probs = jnp.exp(scores - jnp.max(scores, axis=0, keepdims=True))
-            probs = probs / jnp.sum(probs, axis=0, keepdims=True)
-            dprobs = dot_nt(value, dout)
-            dscores = (probs * (dprobs - jnp.sum(probs * dprobs, axis=0, keepdims=True))).astype(BF16)
-            sv[rows, lanes] = dot_nn(probs.astype(BF16), dout).astype(BF16)
-            sk[rows, lanes] = dot_nn(dscores, query).astype(BF16)
-            sq[rows, lanes] = join_heads(dot_tn(key, dscores).T).astype(BF16) * SCALE
+    places = [(slice(i * QP, (i + 1) * QP), slice(p * LANES, (p + 1) * LANES)) for i in range(images) for p in range(PAIRS)]
+
+    def raw(place):
+        query = two_heads(qs[place], masks)
+        dout = two_heads(dos[place], masks)
+        return query, dout, dot_nt(ks[place], query), dot_nt(vs[place], dout)
+
+    following = raw(places[0])
+    for number, place in enumerate(places):
+        query, dout, scores, dprobs = following
+        if number + 1 < len(places):
+            following = raw(places[number + 1])
+        scores = jnp.where(real, scores, NEG)
+        probs = jnp.exp(scores - jnp.max(scores, axis=0, keepdims=True))
+        probs = probs / jnp.sum(probs, axis=0, keepdims=True)
+        dscores = (probs * (dprobs - jnp.sum(probs * dprobs, axis=0, keepdims=True))).astype(BF16)
+        sv[place] = dot_nn(probs.astype(BF16), dout).astype(BF16)
+        sk[place] = dot_nn(dscores, query).astype(BF16)
+        sq[place] = join_heads(dot_tn(ks[place], dscores).T).astype(BF16) * SCALE
     dvec_ref[0:1, :] = rowsum(sq[...])
     dvec_ref[1:2, :] = rowsum(sv[...])
     xb = get(6)
@@ -1053,6 +1055,19 @@
     )(flags, *[array for array, _ in sources])
 
 
+def far_send_kernel(flags, a, b, c, d, out):
+    out[0] = add(a[...], b[...])
+    out[1] = add(c[...], d[...])
+
+
+def far_send(flags, kept, came):
+    kept, came = blocks_of(kept), blocks_of(came)
+    sources = []
+    for r in (0, 1):
+        sources += [(part, lambda f, r=r: (r, 1 - f[2], f[1])) for part in (kept, came)]
+    return merge(far_send_kernel, flags, sources, [(2, kept.shape[-2])], "far_send")[0]
+
+
 def core_merge_kernel(flags, *refs):
     ins, outs = refs[:14], refs[14:]
     for number in range(2):
@@ -1195,11 +1210,11 @@
     dq_parts = parts_of(dq)
     if custom:
         far = [far[0], far_came]
-    dcv_row, *cross = memory_weights(flags, cross, memory, dk, dv, far, custom)
+        dk, message = tie(dk, far_send(flags, *far))
+        far_last = over_y(message)
+    dcv_row, *cross = memory_weights(flags, cross, memory, dk, dv, custom)
     if custom:
         dcv_row = dcv_row + over_x(dcv_row)
-        dq_parts[1], message = tie(dq_parts[1], cross.pop())
-        far_last = over_y(message)
     da, gq_head, dvec_query, *cross = query_backward(flags, cross, y1, db, dq_parts, w, vec, custom)
     if custom:
         cross_came = over_core(cross[1])

time: 327 us -> 322 us (0.985)
    pallas_call x1 -> x2, Pallas kernels: 6.95 us -> 11.4 us  [merge(): pl.pallas_call(body, grid_spec=pltpu.PrefetchScalarGridSpec(num_scalar_pr...]
  transfers between devices with their start and end apart: 54 -> 54, of which waited for: 26 -> 25; matrix products, arithmetic and copies ran while one was open for 3% -> 3% of each run, Pallas kernels for 18% -> 18%
where the time goes in v1:
time: 322 us; the launch traced here: 318 us
  waiting for transfers between devices  141 us (44%)
  Pallas kernels  105 us (33%)
  starting transfers between devices  49.3 us (15%)
  other arithmetic  11.8 us (4%)
  local copies, waits for them, and re-layouts  8.89 us (3%)
    ppermute x14, waiting for transfers between devices, over_z(): lax.ppermute(v, 'dp', [(4 * a + i, 4 * b + i) for a, b in hops for i in r...  56.5 us
    ppermute x9, waiting for transfers between devices, over_y(): return lax.ppermute(v, 'dp', [(i, i ^ 2) for i in range(16)])  42.4 us
    ppermute x11, waiting for transfers between devices, over_x(): return lax.ppermute(v, 'seq', [(0, 1), (1, 0)])  36.8 us
    ppermute x14, starting transfers between devices, over_z(): lax.ppermute(v, 'dp', [(4 * a + i, 4 * b + i) for a, b in hops for i in r...  26.4 us
    pallas_call x1, Pallas kernels, middle(): pl.pallas_call(partial(middle_kernel, parts, split), grid_spec=pltpu.Pref...  26.3 us
    pallas_call x1, Pallas kernels, forward(): pl.pallas_call(partial(forward_kernel, queries, custom), grid_spec=pltpu....  19 us
    pallas_call x1, Pallas kernels, self_backward(): pl.pallas_call(partial(self_backward_kernel, queries, split), grid_spec=p...  13.2 us
    ppermute x11, starting transfers between devices, over_x(): return lax.ppermute(v, 'seq', [(0, 1), (1, 0)])  12.5 us
  transfers between devices with their start and end apart: 54, of which 25 were waited for; matrix products, arithmetic and copies ran while one was open for 3% of the time, Pallas kernels for 18%

profile of v1, /device:TPU:8, one launch (start us, length us, event | category | flops | bytes accessed | tf_op | source)
XLA Modules:
  0.0 317.7 jit_solution(15470711166845853729)
XLA Ops:
  1.4 1.5 collective-permute-start
  2.9 2.2 collective-permute-done
  6.5 1.6 collective-permute-start.2
  8.6 1.5 collective-permute-start.1
  10.1 2.6 collective-permute-start.8
  12.7 8.4 %collective-permute-done.2.refs_2_ = bf16[400,768]{1,0:T(8,128)(2,1)S(1)} collective-permute-done((bf16[400,768]{1,0:T(8,128)(2,1)S(1)}, bf16[400,768]{1,0:T(8,128)(2,1)S(1)}, u32[]{:S(2)}, u32[]{:S(2)}) %collective-permute-start.2) | collective-permute-done | bytes 614432 | tf_op jit(solution)/shard_map/ppermute | solution.py:978
  21.1 1.5 collective-permute-start.4
  22.5 9.6 %collective-permute-done.3.refs_3_ = bf16[400,768]{1,0:T(8,128)(2,1)S(1)} collective-permute-done((bf16[400,768]{1,0:T(8,128)(2,1)S(1)}, bf16[400,768]{1,0:T(8,128)(2,1)S(1)}, u32[]{:S(2)}, u32[]{:S(2)}) %collective-permute-start.3) | collective-permute-done | bytes 614432 | tf_op jit(solution)/shard_map/ppermute | solution.py:986
  32.5 2.5 collective-permute-start.6
  35.0 3.7 %collective-permute-done.8.refs_8_ = bf16[400,768]{1,0:T(8,128)(2,1)S(1)} collective-permute-done((bf16[400,768]{1,0:T(8,128)(2,1)S(1)}, bf16[400,768]{1,0:T(8,128)(2,1)S(1)}, u32[]{:S(2)}, u32[]{:S(2)}) %collective-permute-start.8) | collective-permute-done | bytes 614432 | tf_op jit(solution)/shard_map/ppermute | solution.py:986
  39.1 1.4 collective-permute-start.11
  40.5 8.4 %collective-permute-done.5.refs_5_ = bf16[400,768]{1,0:T(8,128)(2,1)S(1)} collective-permute-done((bf16[400,768]{1,0:T(8,128)(2,1)S(1)}, bf16[400,768]{1,0:T(8,128)(2,1)S(1)}, u32[]{:S(2)}, u32[]{:S(2)}) %collective-permute-start.5) | collective-permute-done | bytes 614432 | tf_op jit(solution)/shard_map/ppermute | solution.py:978
  48.9 1.9 collective-permute-done.6.refs_6_
  51.3 7.2 %collective-permute-done.10.refs_10_ = bf16[400,768]{1,0:T(8,128)(2,1)S(1)} collective-permute-done((bf16[400,768]{1,0:T(8,128)(2,1)S(1)}, bf16[400,768]{1,0:T(8,128)(2,1)S(1)}, u32[]{:S(2)}, u32[]{:S(2)}) %collective-permute-start.10) | collective-permute-done | bytes 614432 | tf_op jit(solution)/shard_map/ppermute | solution.py:978
  58.5 3.3 %collective-permute-done.11.refs_11_ = bf16[400,768]{1,0:T(8,128)(2,1)S(1)} collective-permute-done((bf16[400,768]{1,0:T(8,128)(2,1)S(1)}, bf16[400,768]{1,0:T(8,128)(2,1)S(1)}, u32[]{:S(2)}, u32[]{:S(2)}) %collective-permute-start.11) | collective-permute-done | bytes 614432 | tf_op jit(solution)/shard_map/ppermute | solution.py:986
  61.8 1.5 collective-permute-start.7
  64.4 1.7 collective-permute-start.14
  66.2 12.5 %collective-permute-done.7.refs_7_ = bf16[400,768]{1,0:T(8,128)(2,1)} collective-permute-done((bf16[400,768]{1,0:T(8,128)(2,1)S(1)}, bf16[400,768]{1,0:T(8,128)(2,1)}, u32[]{:S(2)}, u32[]{:S(2)}) %collective-permute-start.7) | collective-permute-done | bytes 614432 | tf_op jit(solution)/shard_map/ppermute | solution.py:982
  78.7 10.1 %collective-permute-done.12.refs_12_ = bf16[400,768]{1,0:T(8,128)(2,1)} collective-permute-done((bf16[400,768]{1,0:T(8,128)(2,1)S(1)}, bf16[400,768]{1,0:T(8,128)(2,1)}, u32[]{:S(2)}, u32[]{:S(2)}) %collective-permute-start.12) | collective-permute-done | bytes 614432 | tf_op jit(solution)/shard_map/ppermute | solution.py:982
  92.8 1.6 collective-permute-done.27.refs_27_
  94.5 11.6 %collective-permute-done.15.refs_15_ = bf16[400,768]{1,0:T(8,128)(2,1)} collective-permute-done((bf16[400,768]{1,0:T(8,128)(2,1)}, bf16[400,768]{1,0:T(8,128)(2,1)}, u32[]{:S(2)}, u32[]{:S(2)}) %collective-permute-start.15) | collective-permute-done | bytes 614432 | tf_op jit(solution)/shard_map/ppermute | solution.py:978
  108.7 19.0 %forward.1 = (bf16[336,768]{1,0:T(8,128)(2,1)}, bf16[336,768]{1,0:T(8,128)(2,1)}, bf16[336,768]{1,0:T(8,128)(2,1)}, bf16[336,768]{1,0:T(8,128)(2,1)}, f32[336,76...) custom-call(s32[3]{0:T(128)} %broadcast_subtract_fusion.left_ref, ...), custom_call_target="tpu_custom_call" | custom-call | tf_op jit(solution)/shard_map/forward/pallas_call | solution.py:310
  127.7 1.8 collective-permute-start.32
  131.8 10.9 %collective-permute-done.33.refs_5_ = f32[3,8,224]{2,1,0:T(8,128)S(1)} collective-permute-done((f32[3,8,224]{2,1,0:T(8,128)}, f32[3,8,224]{2,1,0:T(8,128)S(1)}, u32[]{:S(2)}, u32[]{:S(2)}) %collective-permute-start.33) | collective-permute-done | bytes 21536 | tf_op jit(solution)/shard_map/ppermute | solution.py:982
  143.5 26.3 %middle.1 = (f32[3,112,768]{2,1,0:T(8,128)}, bf16[2,2,784,768]{3,2,1,0:T(8,128)(2,1)}, bf16[2,2,784,768]{3,2,1,0:T(8,128)(2,1)}, bf16[2,784,768]{2,1,0:T(8,128)(...) custom-call(s32[4]{0:T(128)} %pad_add_fusion.flags.refs_0_, ...), custom_call_target="tpu_custom_call" | custom-call | flops 10701766 | bytes 28311 | tf_op jit(solution)/shard_map/middle/pallas_call | solution.py:600
  169.9 10.0 %cross_backward.1 = (bf16[3,112,768]{2,1,0:T(8,128)(2,1)}, bf16[3,512,768]{2,1,0:T(8,128)(2,1)}, bf16[3,512,768]{2,1,0:T(8,128)(2,1)}) custom-call(s32[3]{0:T(128)} %broadcast_subtract_fusion.left_ref, bf16[3,112,768]{2,1,0:T(8,128)(2,1)} %bitcast.40, bf16[3,512,768]{2,1,0:T(8,128)(2,1)} %get-tuple-element.90.k_ref, ...), custom_call_target="tpu_custom_call" | custom-call | flops 352321 | bytes 9437 | tf_op jit(solution)/shard_map/cross_backward/pallas_call | solution.py:681
  180.0 4.5 %far_send.1 = bf16[2,392,768]{2,1,0:T(8,128)(2,1)} custom-call(s32[4]{0:T(128)} %pad_add_fusion.flags.refs_0_, bf16[2,2,2,392,768]{4,3,2,1,0:T(8,128)(2,1)} %bitcast.28, bf16[2,2,2,392,768]{4,3,2,1,0:T(8,128)(2,1)} %bitcast.10.b.d.refs_1_.refs_4_, bf16[2,2,2,392,768]{4,3,2,1,0:T(8,128)(2,1)} %bitcast.29, bf16[2,2,2,392,768]{4,3,2,1,0:T(8,128)(2,1)} %bitcast.10.b.d.refs_1_.refs_4_), custom_call_target="tpu_custom_call" | custom-call | tf_op jit(solution)/shard_map/far_send/pallas_call | solution.py:1041
  185.6 1.7 collective-permute-start.35
  187.3 10.7 %memory_weights.1 = (f32[8,768]{1,0:T(8,128)}, bf16[2,784,768]{2,1,0:T(8,128)(2,1)}, bf16[2,784,768]{2,1,0:T(8,128)(2,1)}) custom-call(s32[4]{0:T(128)} %pad_add_fusion.flags.refs_0_, bf16[2,784,768]{2,1,0:T(8,128)(2,1)} %get-tuple-element.87.refs_0_, bf16[2,784,768]{2,1,0:T(8,128)(2,1)} %get-tuple-element.88.refs_1_, ...), custom_call_target="tpu_custom_call", output_to_operand_aliasing={{1}: (1, {}), {2}: (2, {})} | custom-call | flops 3623878 | bytes 7077 | tf_op jit(solution)/shard_map/memory_weights/pallas_call | solution.py:741
  200.3 6.7 %query_backward.1 = (f32[336,768]{1,0:T(8,128)}, bf16[64,768]{1,0:T(8,128)(2,1)}, f32[24,768]{1,0:T(8,128)}, bf16[2,784,768]{2,1,0:T(8,128)(2,1)}, bf16[2,784,768]{2,1,0:T(8,128)(2,1)}) custom-call(s32[4]{0:T(128)} %pad_add_fusion.flags.refs_0_, bf16[2,784,768]{2,1,0:T(8,128)(2,1)} %get-tuple-element.99.refs_0_, ...), custom_call_target="tpu_custom_call", output_to_operand_aliasing={{3}: (1, {}), {4}: (2, {})} | custom-call | flops 792723 | bytes 4128 | tf_op jit(solution)/shard_map/query_backward/pallas_call | solution.py:841
  207.1 13.2 %self_backward.1 = (f32[3,112,768]{2,1,0:T(8,128)}, f32[24,768]{1,0:T(8,128)}, bf16[2,784,768]{2,1,0:T(8,128)(2,1)}, bf16[2,784,768]{2,1,0:T(8,128)(2,1)}) custom-call(s32[4]{0:T(128)} %pad_add_fusion.flags.refs_0_, bf16[336,768]{1,0:T(8,128)(2,1)} %get-tuple-element.86.refs_1_, f32[336,768]{1,0:T(8,128)} %get-tuple-element.103.refs_2_, ...), custom_call_target="tpu_custom_call" | custom-call | flops 6341787 | bytes 9437 | tf_op jit(solution)/shard_map/self_backward/pallas_call | solution.py:935
  220.9 1.4 copy-done
  222.4 6.9 %core_merge.1 = (bf16[392,768]{1,0:T(8,128)(2,1)}, bf16[392,768]{1,0:T(8,128)(2,1)}, bf16[392,768]{1,0:T(8,128)(2,1)}, bf16[392,768]{1,0:T(8,128)(2,1)}, bf16[480,768]{1,0:T(8,128)(2,1)}) custom-call(s32[4]{0:T(128)} %pad_add_fusion.flags.refs_0_, bf16[2,2,2,392,768]{4,3,2,1,0:T(8,128)(2,1)} %bitcast.30, ...), custom_call_target="tpu_custom_call" | custom-call | tf_op jit(solution)/shard_map/core_merge/pallas_call | solution.py:1041
  229.3 1.8 collective-permute-start.41
  232.5 2.8 fusion.8
  236.1 2.0 collective-permute-start.43
  238.5 8.0 %memory_grads.1 = f32[3,512,768]{2,1,0:T(8,128)} custom-call(bf16[3,512,768]{2,1,0:T(8,128)(2,1)} %get-tuple-element.128.refs_3_.dk_ref, bf16[3,512,768]{2,1,0:T(8,128)(2,1)} %get-tuple-element.129.refs_4_.dv_ref, bf16[12544,768]{1,0:T(8,128)(2,1)} %get-tuple-element.130.refs_6_.refs_7_.ck.cv, bf16[12544,768]{1,0:T(8,128)(2,1)} %get-tuple-element.130.refs_6_.refs_7_.ck.cv), custom_call_target="tpu_custom_call" | custom-call | flops 3623878656 | bytes 9437184 | tf_op jit(solution)/shard_map/memory_grads/pallas_call | solution.py:769
  246.5 6.3 %collective-permute-done.44 = f32[24,768]{1,0:T(8,128)S(1)} collective-permute-done((f32[24,768]{1,0:T(8,128)S(1)}, f32[24,768]{1,0:T(8,128)S(1)}, u32[]{:S(2)}, u32[]{:S(2)}) %collective-permute-start.44) | collective-permute-done | bytes 73760 | tf_op jit(solution)/shard_map/ppermute | solution.py:978
  254.6 3.1 collective-permute-start.45
  257.7 1.7 collective-permute-start.46
  259.4 3.9 %collective-permute-start.48 = (bf16[192,768]{1,0:T(8,128)(2,1)S(1)}, bf16[192,768]{1,0:T(8,128)(2,1)S(1)}, u32[]{:S(2)}, u32[]{:S(2)}) collective-permute-start(bf16[192,768]{1,0:T(8,128)(2,1)S(1)} %slice.43), channel_id=1, source_target_pairs={{0,16},{2,18},{4,20},{6,22},{8,24},{10,26},{12,28},{14,30},{1,17},... | collective-permute-start | bytes 884744 | tf_op jit(solution)/shard_map/ppermute | solution.py:986
  263.4 8.1 %collective-permute-done.47 = f32[24,768]{1,0:T(8,128)S(1)} collective-permute-done((f32[24,768]{1,0:T(8,128)S(1)}, f32[24,768]{1,0:T(8,128)S(1)}, u32[]{:S(2)}, u32[]{:S(2)}) %collective-permute-start.47) | collective-permute-done | bytes 73760 | tf_op jit(solution)/shard_map/ppermute | solution.py:986
  272.4 2.7 collective-permute-done.48
  277.1 3.5 %collective-permute-start.51 = (f32[24,768]{1,0:T(8,128)S(1)}, f32[24,768]{1,0:T(8,128)S(1)}, u32[]{:S(2)}, u32[]{:S(2)}) collective-permute-start(f32[24,768]{1,0:T(8,128)S(1)} %add.154), channel_id=1, source_target_pairs={{0,16},{2,18},{4,20},{6,22},{16,0},{18,2},{20,4},{22,6},{8,24},{10... | collective-permute-start | bytes 221192 | tf_op jit(solution)/shard_map/ppermute | solution.py:986
  280.7 1.9 collective-permute-start.52
  282.6 11.4 %collective-permute-done.51 = f32[24,768]{1,0:T(8,128)S(1)} collective-permute-done((f32[24,768]{1,0:T(8,128)S(1)}, f32[24,768]{1,0:T(8,128)S(1)}, u32[]{:S(2)}, u32[]{:S(2)}) %collective-permute-start.51) | collective-permute-done | bytes 73760 | tf_op jit(solution)/shard_map/ppermute | solution.py:986
  298.9 15.7 %collective-permute-done.53 = bf16[392,768]{1,0:T(8,128)(2,1)} collective-permute-done((bf16[392,768]{1,0:T(8,128)(2,1)S(1)}, bf16[392,768]{1,0:T(8,128)(2,1)}, u32[]{:S(2)}, u32[]{:S(2)}) %collective-permute-start.53) | collective-permute-done | bytes 602144 | tf_op jit(solution)/shard_map/ppermute | solution.py:986
  314.6 1.6 convert_add_fusion
  (188 shorter events, 32.0 us)
Async XLA Ops:
  6.5 14.5 %collective-permute-start.2 = (bf16[400,768]{1,0:T(8,128)(2,1)S(1)}, bf16[400,768]{1,0:T(8,128)(2,1)S(1)}, u32[]{:S(2)}, u32[]{:S(2)}) collective-permute-start(bf16[400,768]{1,0:T(8,128)(2,1)S(1)} %maximum_select_fusion.1.refs_0_), channel_id=1, source_target_pairs={{0,4},{2,6},{4,0},{6,2},{8,12},{10,14},{12,8},{14,10},{16,20},{18,... | collective-permute-start | bytes 1843208 | tf_op jit(solution)/shard_map/ppermute | solution.py:978
  8.1 24.0 %collective-permute-start.3 = (bf16[400,768]{1,0:T(8,128)(2,1)S(1)}, bf16[400,768]{1,0:T(8,128)(2,1)S(1)}, u32[]{:S(2)}, u32[]{:S(2)}) collective-permute-start(bf16[400,768]{1,0:T(8,128)(2,1)S(1)} %maximum_select_fusion.1.refs_0_), channel_id=1, source_target_pairs={{0,8},{2,10},{4,12},{6,14},{8,0},{10,2},{12,4},{14,6},{16,24},{18,... | collective-permute-start | bytes 1843208 | tf_op jit(solution)/shard_map/ppermute | solution.py:986
  8.6 23.9 %collective-permute-start.1 = (bf16[400,768]{1,0:T(8,128)(2,1)S(1)}, bf16[400,768]{1,0:T(8,128)(2,1)S(1)}, u32[]{:S(2)}, u32[]{:S(2)}) collective-permute-start(bf16[400,768]{1,0:T(8,128)(2,1)S(1)} %maximum_select_fusion.1.refs_0_), channel_id=1, source_target_pairs={{0,1},{1,0},{2,3},{3,2},{4,5},{5,4},{6,7},{7,6},{8,9},{9,8},{10,11... | collective-permute-start | bytes 1843208 | tf_op jit(solution)/shard_map/ppermute | solution.py:982
  10.1 28.6 %collective-permute-start.8 = (bf16[400,768]{1,0:T(8,128)(2,1)S(1)}, bf16[400,768]{1,0:T(8,128)(2,1)S(1)}, u32[]{:S(2)}, u32[]{:S(2)}) collective-permute-start(bf16[400,768]{1,0:T(8,128)(2,1)S(1)} %maximum_select_fusion.1.refs_0_), channel_id=1, source_target_pairs={{0,16},{2,18},{4,20},{6,22},{16,0},{18,2},{20,4},{22,6},{8,24},{10... | collective-permute-start | bytes 1843208 | tf_op jit(solution)/shard_map/ppermute | solution.py:986
  12.7 26.0 %collective-permute-start.16 = (bf16[400,768]{1,0:T(8,128)(2,1)S(1)}, bf16[400,768]{1,0:T(8,128)(2,1)S(1)}, u32[]{:S(2)}, u32[]{:S(2)}) collective-permute-start(bf16[400,768]{1,0:T(8,128)(2,1)S(1)} %maximum_select_fusion.1.refs_0_), channel_id=1, source_target_pairs={{0,2},{2,0},{4,6},{6,4},{8,10},{10,8},{12,14},{14,12},{16,18},{18,... | collective-permute-start | bytes 1843208 | tf_op jit(solution)/shard_map/ppermute | solution.py:974
  21.1 18.0 %collective-permute-start.4 = (bf16[400,768]{1,0:T(8,128)(2,1)S(1)}, bf16[400,768]{1,0:T(8,128)(2,1)S(1)}, u32[]{:S(2)}, u32[]{:S(2)}) collective-permute-start(bf16[400,768]{1,0:T(8,128)(2,1)S(1)} %collective-permute-done.2.refs_2_), channel_id=1, source_target_pairs={{0,1},{1,0},{2,3},{3,2},{4,5},{5,4},{6,7},{7,6},{8,9},{9,8},{10,11... | collective-permute-start | bytes 1843208 | tf_op jit(solution)/shard_map/ppermute | solution.py:982
  32.1 16.8 %collective-permute-start.5 = (bf16[400,768]{1,0:T(8,128)(2,1)S(1)}, bf16[400,768]{1,0:T(8,128)(2,1)S(1)}, u32[]{:S(2)}, u32[]{:S(2)}) collective-permute-start(bf16[400,768]{1,0:T(8,128)(2,1)S(1)} %collective-permute-done.3.refs_3_), channel_id=1, source_target_pairs={{0,4},{2,6},{4,0},{6,2},{8,12},{10,14},{12,8},{14,10},{16,20},{18,... | collective-permute-start | bytes 1843208 | tf_op jit(solution)/shard_map/ppermute | solution.py:978
  32.5 18.4 %collective-permute-start.6 = (bf16[400,768]{1,0:T(8,128)(2,1)S(1)}, bf16[400,768]{1,0:T(8,128)(2,1)S(1)}, u32[]{:S(2)}, u32[]{:S(2)}) collective-permute-start(bf16[400,768]{1,0:T(8,128)(2,1)S(1)} %collective-permute-done.1.refs_1_), channel_id=1, source_target_pairs={{0,8},{2,10},{4,12},{6,14},{8,0},{10,2},{12,4},{14,6},{16,24},{18,... | collective-permute-start | bytes 1843208 | tf_op jit(solution)/shard_map/ppermute | solution.py:986
  38.6 12.2 %collective-permute-start.9 = (bf16[400,768]{1,0:T(8,128)(2,1)S(1)}, bf16[400,768]{1,0:T(8,128)(2,1)S(1)}, u32[]{:S(2)}, u32[]{:S(2)}) collective-permute-start(bf16[400,768]{1,0:T(8,128)(2,1)S(1)} %collective-permute-done.8.refs_8_), channel_id=1, source_target_pairs={{0,1},{1,0},{2,3},{3,2},{4,5},{5,4},{6,7},{7,6},{8,9},{9,8},{10,11... | collective-permute-start | bytes 1843208 | tf_op jit(solution)/shard_map/ppermute | solution.py:982
  38.6 19.9 %collective-permute-start.10 = (bf16[400,768]{1,0:T(8,128)(2,1)S(1)}, bf16[400,768]{1,0:T(8,128)(2,1)S(1)}, u32[]{:S(2)}, u32[]{:S(2)}) collective-permute-start(bf16[400,768]{1,0:T(8,128)(2,1)S(1)} %collective-permute-done.8.refs_8_), channel_id=1, source_target_pairs={{0,4},{2,6},{4,0},{6,2},{8,12},{10,14},{12,8},{14,10},{16,20},{18,... | collective-permute-start | bytes 1843208 | tf_op jit(solution)/shard_map/ppermute | solution.py:978
  39.1 22.8 %collective-permute-start.11 = (bf16[400,768]{1,0:T(8,128)(2,1)S(1)}, bf16[400,768]{1,0:T(8,128)(2,1)S(1)}, u32[]{:S(2)}, u32[]{:S(2)}) collective-permute-start(bf16[400,768]{1,0:T(8,128)(2,1)S(1)} %collective-permute-done.8.refs_8_), channel_id=1, source_target_pairs={{0,8},{2,10},{4,12},{6,14},{8,0},{10,2},{12,4},{14,6},{16,24},{18,... | collective-permute-start | bytes 1843208 | tf_op jit(solution)/shard_map/ppermute | solution.py:986
  48.9 14.4 %collective-permute-start.17 = (bf16[400,768]{1,0:T(8,128)(2,1)S(1)}, bf16[400,768]{1,0:T(8,128)(2,1)S(1)}, u32[]{:S(2)}, u32[]{:S(2)}) collective-permute-start(bf16[400,768]{1,0:T(8,128)(2,1)S(1)} %collective-permute-done.1.refs_1_), channel_id=1, source_target_pairs={{0,2},{2,0},{4,6},{6,4},{8,10},{10,8},{12,14},{14,12},{16,18},{18,... | collective-permute-start | bytes 1843208 | tf_op jit(solution)/shard_map/ppermute | solution.py:974
  50.8 13.0 %collective-permute-start.18 = (bf16[400,768]{1,0:T(8,128)(2,1)S(1)}, bf16[400,768]{1,0:T(8,128)(2,1)S(1)}, u32[]{:S(2)}, u32[]{:S(2)}) collective-permute-start(bf16[400,768]{1,0:T(8,128)(2,1)S(1)} %collective-permute-done.2.refs_2_), channel_id=1, source_target_pairs={{0,2},{2,0},{4,6},{6,4},{8,10},{10,8},{12,14},{14,12},{16,18},{18,... | collective-permute-start | bytes 1843208 | tf_op jit(solution)/shard_map/ppermute | solution.py:974
  50.9 13.5 %collective-permute-start.19 = (bf16[400,768]{1,0:T(8,128)(2,1)S(1)}, bf16[400,768]{1,0:T(8,128)(2,1)S(1)}, u32[]{:S(2)}, u32[]{:S(2)}) collective-permute-start(bf16[400,768]{1,0:T(8,128)(2,1)S(1)} %collective-permute-done.3.refs_3_), channel_id=1, source_target_pairs={{0,2},{2,0},{4,6},{6,4},{8,10},{10,8},{12,14},{14,12},{16,18},{18,... | collective-permute-start | bytes 1843208 | tf_op jit(solution)/shard_map/ppermute | solution.py:974
  58.5 7.6 %collective-permute-start.24 = (bf16[400,768]{1,0:T(8,128)(2,1)S(1)}, bf16[400,768]{1,0:T(8,128)(2,1)S(1)}, u32[]{:S(2)}, u32[]{:S(2)}) collective-permute-start(bf16[400,768]{1,0:T(8,128)(2,1)S(1)} %collective-permute-done.8.refs_8_), channel_id=1, source_target_pairs={{0,2},{2,0},{4,6},{6,4},{8,10},{10,8},{12,14},{14,12},{16,18},{18,... | collective-permute-start | bytes 1843208 | tf_op jit(solution)/shard_map/ppermute | solution.py:974
  61.8 16.9 %collective-permute-start.7 = (bf16[400,768]{1,0:T(8,128)(2,1)S(1)}, bf16[400,768]{1,0:T(8,128)(2,1)}, u32[]{:S(2)}, u32[]{:S(2)}) collective-permute-start(bf16[400,768]{1,0:T(8,128)(2,1)S(1)} %collective-permute-done.5.refs_5_), channel_id=1, source_target_pairs={{0,1},{1,0},{2,3},{3,2},{4,5},{5,4},{6,7},{7,6},{8,9},{9,8},{10,11... | collective-permute-start | bytes 1843208 | tf_op jit(solution)/shard_map/ppermute | solution.py:982
  63.3 25.5 %collective-permute-start.12 = (bf16[400,768]{1,0:T(8,128)(2,1)S(1)}, bf16[400,768]{1,0:T(8,128)(2,1)}, u32[]{:S(2)}, u32[]{:S(2)}) collective-permute-start(bf16[400,768]{1,0:T(8,128)(2,1)S(1)} %collective-permute-done.10.refs_10_), channel_id=1, source_target_pairs={{0,1},{1,0},{2,3},{3,2},{4,5},{5,4},{6,7},{7,6},{8,9},{9,8},{10,11... | collective-permute-start | bytes 1843208 | tf_op jit(solution)/shard_map/ppermute | solution.py:982
  63.9 25.0 %collective-permute-start.13 = (bf16[400,768]{1,0:T(8,128)(2,1)S(1)}, bf16[400,768]{1,0:T(8,128)(2,1)}, u32[]{:S(2)}, u32[]{:S(2)}) collective-permute-start(bf16[400,768]{1,0:T(8,128)(2,1)S(1)} %collective-permute-done.11.refs_11_), channel_id=1, source_target_pairs={{0,4},{2,6},{4,0},{6,2},{8,12},{10,14},{12,8},{14,10},{16,20},{18,... | collective-permute-start | bytes 1843208 | tf_op jit(solution)/shard_map/ppermute | solution.py:978
  64.4 25.0 %collective-permute-start.14 = (bf16[400,768]{1,0:T(8,128)(2,1)S(1)}, bf16[400,768]{1,0:T(8,128)(2,1)}, u32[]{:S(2)}, u32[]{:S(2)}) collective-permute-start(bf16[400,768]{1,0:T(8,128)(2,1)S(1)} %collective-permute-done.9.refs_9_), channel_id=1, source_target_pairs={{0,8},{2,10},{4,12},{6,14},{8,0},{10,2},{12,4},{14,6},{16,24},{18,... | collective-permute-start | bytes 1843208 | tf_op jit(solution)/shard_map/ppermute | solution.py:986
  66.1 23.3 %collective-permute-start.20 = (bf16[400,768]{1,0:T(8,128)(2,1)S(1)}, bf16[400,768]{1,0:T(8,128)(2,1)S(1)}, u32[]{:S(2)}, u32[]{:S(2)}) collective-permute-start(bf16[400,768]{1,0:T(8,128)(2,1)S(1)} %collective-permute-done.4.refs_4_), channel_id=1, source_target_pairs={{0,2},{2,0},{4,6},{6,4},{8,10},{10,8},{12,14},{14,12},{16,18},{18,... | collective-permute-start | bytes 1843208 | tf_op jit(solution)/shard_map/ppermute | solution.py:974
  78.7 11.2 %collective-permute-start.21 = (bf16[400,768]{1,0:T(8,128)(2,1)S(1)}, bf16[400,768]{1,0:T(8,128)(2,1)S(1)}, u32[]{:S(2)}, u32[]{:S(2)}) collective-permute-start(bf16[400,768]{1,0:T(8,128)(2,1)S(1)} %collective-permute-done.5.refs_5_), channel_id=1, source_target_pairs={{0,2},{2,0},{4,6},{6,4},{8,10},{10,8},{12,14},{14,12},{16,18},{18,... | collective-permute-start | bytes 1843208 | tf_op jit(solution)/shard_map/ppermute | solution.py:974
  89.4 5.0 %collective-permute-start.27 = (bf16[400,768]{1,0:T(8,128)(2,1)S(1)}, bf16[400,768]{1,0:T(8,128)(2,1)S(1)}, u32[]{:S(2)}, u32[]{:S(2)}) collective-permute-start(bf16[400,768]{1,0:T(8,128)(2,1)S(1)} %collective-permute-done.11.refs_11_), channel_id=1, source_target_pairs={{0,2},{2,0},{4,6},{6,4},{8,10},{10,8},{12,14},{14,12},{16,18},{18,... | collective-permute-start | bytes 1843208 | tf_op jit(solution)/shard_map/ppermute | solution.py:974
  89.9 16.2 %collective-permute-start.15 = (bf16[400,768]{1,0:T(8,128)(2,1)}, bf16[400,768]{1,0:T(8,128)(2,1)}, u32[]{:S(2)}, u32[]{:S(2)}) collective-permute-start(bf16[400,768]{1,0:T(8,128)(2,1)} %collective-permute-done.14.refs_14_), channel_id=1, source_target_pairs={{0,4},{2,6},{4,0},{6,2},{8,12},{10,14},{12,8},{14,10},{16,20},{18,... | collective-permute-start | bytes 1843208 | tf_op jit(solution)/shard_map/ppermute | solution.py:978
  90.9 17.4 %collective-permute-start.30 = (bf16[400,768]{1,0:T(8,128)(2,1)}, bf16[400,768]{1,0:T(8,128)(2,1)}, u32[]{:S(2)}, u32[]{:S(2)}) collective-permute-start(bf16[400,768]{1,0:T(8,128)(2,1)} %collective-permute-done.14.refs_14_), channel_id=1, source_target_pairs={{0,2},{2,0},{4,6},{6,4},{8,10},{10,8},{12,14},{14,12},{16,18},{18,... | collective-permute-start | bytes 1843208 | tf_op jit(solution)/shard_map/ppermute | solution.py:974
  91.8 16.6 %collective-permute-start.23 = (bf16[400,768]{1,0:T(8,128)(2,1)}, bf16[400,768]{1,0:T(8,128)(2,1)}, u32[]{:S(2)}, u32[]{:S(2)}) collective-permute-start(bf16[400,768]{1,0:T(8,128)(2,1)} %collective-permute-done.7.refs_7_), channel_id=1, source_target_pairs={{0,2},{2,0},{4,6},{6,4},{8,10},{10,8},{12,14},{14,12},{16,18},{18,... | collective-permute-start | bytes 1843208 | tf_op jit(solution)/shard_map/ppermute | solution.py:974
  92.6 15.7 %collective-permute-start.28 = (bf16[400,768]{1,0:T(8,128)(2,1)}, bf16[400,768]{1,0:T(8,128)(2,1)}, u32[]{:S(2)}, u32[]{:S(2)}) collective-permute-start(bf16[400,768]{1,0:T(8,128)(2,1)} %collective-permute-done.12.refs_12_), channel_id=1, source_target_pairs={{0,2},{2,0},{4,6},{6,4},{8,10},{10,8},{12,14},{14,12},{16,18},{18,... | collective-permute-start | bytes 1843208 | tf_op jit(solution)/shard_map/ppermute | solution.py:974
  94.4 13.9 %collective-permute-start.29 = (bf16[400,768]{1,0:T(8,128)(2,1)}, bf16[400,768]{1,0:T(8,128)(2,1)}, u32[]{:S(2)}, u32[]{:S(2)}) collective-permute-start(bf16[400,768]{1,0:T(8,128)(2,1)} %collective-permute-done.13.refs_13_), channel_id=1, source_target_pairs={{0,2},{2,0},{4,6},{6,4},{8,10},{10,8},{12,14},{14,12},{16,18},{18,... | collective-permute-start | bytes 1843208 | tf_op jit(solution)/shard_map/ppermute | solution.py:974
  127.7 15.0 %collective-permute-start.32 = (bf16[3,112,768]{2,1,0:T(8,128)(2,1)}, bf16[3,112,768]{2,1,0:T(8,128)(2,1)S(1)}, u32[]{:S(2)}, u32[]{:S(2)}) collective-permute-start(bf16[3,112,768]{2,1,0:T(8,128)(2,1)} %get-tuple-element.82.refs_2_), channel_id=1, source_target_pairs={{0,1},{1,0},{2,3},{3,2},{4,5},{5,4},{6,7},{7,6},{8,9},{9,8},{10,11... | collective-permute-start | bytes 1548296 | tf_op jit(solution)/shard_map/ppermute | solution.py:982
  130.1 12.6 %collective-permute-start.33 = (f32[3,8,224]{2,1,0:T(8,128)}, f32[3,8,224]{2,1,0:T(8,128)S(1)}, u32[]{:S(2)}, u32[]{:S(2)}) collective-permute-start(f32[3,8,224]{2,1,0:T(8,128)} %get-tuple-element.83.refs_4_), channel_id=1, source_target_pairs={{0,1},{1,0},{2,3},{3,2},{4,5},{5,4},{6,7},{7,6},{8,9},{9,8},{10,11... | collective-permute-start | bytes 64520 | tf_op jit(solution)/shard_map/ppermute | solution.py:982
  169.9 10.1 %collective-permute-start.34 = (bf16[2,2,784,768]{3,2,1,0:T(8,128)(2,1)}, bf16[2,2,784,768]{3,2,1,0:T(8,128)(2,1)}, u32[]{:S(2)}, u32[]{:S(2)}) collective-permute-start(bf16[2,2,784,768]{3,2,1,0:T(8,128)(2,1)} %get-tuple-element.96), channel_id=1, source_target_pairs={{0,2},{2,0},{4,6},{6,4},{8,10},{10,8},{12,14},{14,12},{16,18},{18,... | collective-permute-start | bytes 14450696 | tf_op jit(solution)/shard_map/ppermute | solution.py:974
  184.5 35.9 %collective-permute-start.37 = (bf16[2,392,768]{2,1,0:T(8,128)(2,1)}, bf16[2,392,768]{2,1,0:T(8,128)(2,1)}, u32[]{:S(2)}, u32[]{:S(2)}) collective-permute-start(bf16[2,392,768]{2,1,0:T(8,128)(2,1)} %far_send.1), channel_id=1, source_target_pairs={{0,4},{2,6},{4,0},{6,2},{8,12},{10,14},{12,8},{14,10},{16,20},{18,... | collective-permute-start | bytes 3612680 | tf_op jit(solution)/shard_map/ppermute | solution.py:978
  185.6 13.9 %collective-permute-start.35 = (bf16[3,112,768]{2,1,0:T(8,128)(2,1)S(1)}, bf16[3,112,768]{2,1,0:T(8,128)(2,1)S(1)}, u32[]{:S(2)}, u32[]{:S(2)}) collective-permute-start(bf16[3,112,768]{2,1,0:T(8,128)(2,1)S(1)} %copy-done.28), channel_id=1, source_target_pairs={{0,1},{1,0},{2,3},{3,2},{4,5},{5,4},{6,7},{7,6},{8,9},{9,8},{10,11... | collective-permute-start | bytes 1548296 | tf_op jit(solution)/shard_map/ppermute | solution.py:982
  198.0 9.0 %collective-permute-start.36 = (f32[8,768]{1,0:T(8,128)}, f32[8,768]{1,0:T(8,128)S(1)}, u32[]{:S(2)}, u32[]{:S(2)}) collective-permute-start(f32[8,768]{1,0:T(8,128)} %get-tuple-element.108), channel_id=1, source_target_pairs={{0,1},{1,0},{2,3},{3,2},{4,5},{5,4},{6,7},{7,6},{8,9},{9,8},{10,11... | collective-permute-start | bytes 73736 | tf_op jit(solution)/shard_map/ppermute | solution.py:982
  207.0 13.9 %collective-permute-start.39 = (bf16[2,784,768]{2,1,0:T(8,128)(2,1)}, bf16[2,784,768]{2,1,0:T(8,128)(2,1)S(1)}, u32[]{:S(2)}, u32[]{:S(2)}) collective-permute-start(bf16[2,784,768]{2,1,0:T(8,128)(2,1)} %get-tuple-element.117), channel_id=1, source_target_pairs={{0,2},{2,0},{4,6},{6,4},{8,10},{10,8},{12,14},{14,12},{16,18},{18,... | collective-permute-start | bytes 7225352 | tf_op jit(solution)/shard_map/ppermute | solution.py:974
  220.3 9.0 %collective-permute-start.38 = (bf16[2,784,768]{2,1,0:T(8,128)(2,1)}, bf16[2,784,768]{2,1,0:T(8,128)(2,1)}, u32[]{:S(2)}, u32[]{:S(2)}) collective-permute-start(bf16[2,784,768]{2,1,0:T(8,128)(2,1)} %get-tuple-element.114), channel_id=1, source_target_pairs={{0,2},{2,0},{4,6},{6,4},{8,10},{10,8},{12,14},{14,12},{16,18},{18,... | collective-permute-start | bytes 7225352 | tf_op jit(solution)/shard_map/ppermute | solution.py:974
  229.3 23.4 %collective-permute-start.41 = (bf16[480,768]{1,0:T(8,128)(2,1)}, bf16[480,768]{1,0:T(8,128)(2,1)S(1)}, u32[]{:S(2)}, u32[]{:S(2)}) collective-permute-start(bf16[480,768]{1,0:T(8,128)(2,1)} %get-tuple-element.131), channel_id=1, source_target_pairs={{0,1},{1,0},{2,3},{3,2},{4,5},{5,4},{6,7},{7,6},{8,9},{9,8},{10,11... | collective-permute-start | bytes 2211848 | tf_op jit(solution)/shard_map/ppermute | solution.py:982
  235.3 18.1 %collective-permute-start.42 = (bf16[392,768]{1,0:T(8,128)(2,1)}, bf16[392,768]{1,0:T(8,128)(2,1)S(1)}, u32[]{:S(2)}, u32[]{:S(2)}) collective-permute-start(bf16[392,768]{1,0:T(8,128)(2,1)} %get-tuple-element.137), channel_id=1, source_target_pairs={{0,4},{2,6},{4,0},{6,2},{8,12},{10,14},{12,8},{14,10},{16,20},{18,... | collective-permute-start | bytes 1806344 | tf_op jit(solution)/shard_map/ppermute | solution.py:978
  236.1 17.2 %collective-permute-start.43 = (bf16[392,768]{1,0:T(8,128)(2,1)}, bf16[392,768]{1,0:T(8,128)(2,1)S(1)}, u32[]{:S(2)}, u32[]{:S(2)}) collective-permute-start(bf16[392,768]{1,0:T(8,128)(2,1)} %get-tuple-element.138), channel_id=1, source_target_pairs={{0,8},{2,10},{4,12},{6,14},{8,0},{10,2},{12,4},{14,6},{16,24},{18,... | collective-permute-start | bytes 1806344 | tf_op jit(solution)/shard_map/ppermute | solution.py:986
  238.1 14.6 %collective-permute-start.44 = (f32[24,768]{1,0:T(8,128)S(1)}, f32[24,768]{1,0:T(8,128)S(1)}, u32[]{:S(2)}, u32[]{:S(2)}) collective-permute-start(f32[24,768]{1,0:T(8,128)S(1)} %add.139), channel_id=1, source_target_pairs={{0,4},{2,6},{4,0},{6,2},{8,12},{10,14},{12,8},{14,10},{16,20},{18,... | collective-permute-start | bytes 221192 | tf_op jit(solution)/shard_map/ppermute | solution.py:978
  254.6 17.0 %collective-permute-start.45 = (bf16[392,768]{1,0:T(8,128)(2,1)S(1)}, bf16[392,768]{1,0:T(8,128)(2,1)S(1)}, u32[]{:S(2)}, u32[]{:S(2)}) collective-permute-start(bf16[392,768]{1,0:T(8,128)(2,1)S(1)} %add_convert_fusion.4), channel_id=1, source_target_pairs={{24,16},{26,18},{28,20},{30,22},{8,0},{10,2},{12,4},{14,6},{25,17}... | collective-permute-start | bytes 1806344 | tf_op jit(solution)/shard_map/ppermute | solution.py:986
  257.7 14.6 %collective-permute-start.46 = (bf16[392,768]{1,0:T(8,128)(2,1)S(1)}, bf16[392,768]{1,0:T(8,128)(2,1)S(1)}, u32[]{:S(2)}, u32[]{:S(2)}) collective-permute-start(bf16[392,768]{1,0:T(8,128)(2,1)S(1)} %get-tuple-element.146), channel_id=1, source_target_pairs={{0,4},{2,6},{4,0},{6,2},{8,12},{10,14},{12,8},{14,10},{16,20},{18,... | collective-permute-start | bytes 1806344 | tf_op jit(solution)/shard_map/ppermute | solution.py:978
  259.4 12.1 %collective-permute-start.47 = (f32[24,768]{1,0:T(8,128)S(1)}, f32[24,768]{1,0:T(8,128)S(1)}, u32[]{:S(2)}, u32[]{:S(2)}) collective-permute-start(f32[24,768]{1,0:T(8,128)S(1)} %add.151), channel_id=1, source_target_pairs={{0,8},{2,10},{4,12},{6,14},{8,0},{10,2},{12,4},{14,6},{16,24},{18,... | collective-permute-start | bytes 221192 | tf_op jit(solution)/shard_map/ppermute | solution.py:986
  259.4 15.7 %collective-permute-start.48 = (bf16[192,768]{1,0:T(8,128)(2,1)S(1)}, bf16[192,768]{1,0:T(8,128)(2,1)S(1)}, u32[]{:S(2)}, u32[]{:S(2)}) collective-permute-start(bf16[192,768]{1,0:T(8,128)(2,1)S(1)} %slice.43), channel_id=1, source_target_pairs={{0,16},{2,18},{4,20},{6,22},{8,24},{10,26},{12,28},{14,30},{1,17},... | collective-permute-start | bytes 884744 | tf_op jit(solution)/shard_map/ppermute | solution.py:986
  275.1 18.9 %collective-permute-start.50 = (bf16[392,768]{1,0:T(8,128)(2,1)S(1)}, bf16[392,768]{1,0:T(8,128)(2,1)S(1)}, u32[]{:S(2)}, u32[]{:S(2)}) collective-permute-start(bf16[392,768]{1,0:T(8,128)(2,1)S(1)} %add_convert_fusion.1), channel_id=1, source_target_pairs={{24,16},{26,18},{28,20},{30,22},{0,8},{2,10},{4,12},{6,14},{25,17}... | collective-permute-start | bytes 1806344 | tf_op jit(solution)/shard_map/ppermute | solution.py:986
  276.4 17.8 %collective-permute-start.49 = (bf16[392,768]{1,0:T(8,128)(2,1)S(1)}, bf16[392,768]{1,0:T(8,128)(2,1)S(1)}, u32[]{:S(2)}, u32[]{:S(2)}) collective-permute-start(bf16[392,768]{1,0:T(8,128)(2,1)S(1)} %add_convert_fusion.2), channel_id=1, source_target_pairs={{16,0},{18,2},{20,4},{22,6},{17,1},{19,3},{21,5},{23,7}} | collective-permute-start | bytes 1806344 | tf_op jit(solution)/shard_map/ppermute | solution.py:986
  277.1 16.9 %collective-permute-start.51 = (f32[24,768]{1,0:T(8,128)S(1)}, f32[24,768]{1,0:T(8,128)S(1)}, u32[]{:S(2)}, u32[]{:S(2)}) collective-permute-start(f32[24,768]{1,0:T(8,128)S(1)} %add.154), channel_id=1, source_target_pairs={{0,16},{2,18},{4,20},{6,22},{16,0},{18,2},{20,4},{22,6},{8,24},{10... | collective-permute-start | bytes 221192 | tf_op jit(solution)/shard_map/ppermute | solution.py:986
  280.7 13.6 %collective-permute-start.52 = (bf16[200,768]{1,0:T(8,128)(2,1)S(1)}, bf16[200,768]{1,0:T(8,128)(2,1)S(1)}, u32[]{:S(2)}, u32[]{:S(2)}) collective-permute-start(bf16[200,768]{1,0:T(8,128)(2,1)S(1)} %slice.44), channel_id=1, source_target_pairs={{0,16},{2,18},{4,20},{6,22},{8,24},{10,26},{12,28},{14,30},{1,17},... | collective-permute-start | bytes 921608 | tf_op jit(solution)/shard_map/ppermute | solution.py:986
  294.9 19.7 %collective-permute-start.53 = (bf16[392,768]{1,0:T(8,128)(2,1)S(1)}, bf16[392,768]{1,0:T(8,128)(2,1)}, u32[]{:S(2)}, u32[]{:S(2)}) collective-permute-start(bf16[392,768]{1,0:T(8,128)(2,1)S(1)} %add_convert_fusion), channel_id=1, source_target_pairs={{16,8},{18,10},{20,12},{22,14},{17,9},{19,11},{21,13},{23,15}} | collective-permute-start | bytes 1806344 | tf_op jit(solution)/shard_map/ppermute | solution.py:986
  (49 other events, 1289.7 us)

commit v2 on v1

--- a/solution.py
+++ b/solution.py
@@ -94,9 +94,9 @@
 
 
 class Assembly:
-    def __init__(self, flags, bufs, weights, sems, vec_low, vec_sem):
+    def __init__(self, flags, bufs, weights, seams, sems, vec_low, vec_sem):
         self.core, self.x, self.y, self.z = flags[0], flags[1], flags[2], flags[3]
-        self.bufs, self.weights, self.sems = bufs, weights, sems
+        self.bufs, self.weights, self.seams, self.sems = bufs, weights, seams, sems
         self.vec_low, self.vec_sem = vec_low, vec_sem
         self.ready = set()
 
@@ -104,7 +104,7 @@
         return self.bufs[dc * 16 + dz2 * 8 + SPREAD.index(spread)]
 
     def start_vec(self):
-        first = VEC_ROW - 15 * PAIR_ROWS - 384
+        first = VEC_ROW - 15 * PAIR_ROWS - 400
         for dc in (0, 1):
             for dz2 in (0, 1):
                 for dz1, dy, dx in SPREAD:
@@ -130,9 +130,8 @@
                     near, far = self.buf(dc, dz2, (dz1, dy, 0)), self.buf(dc, dz2, (dz1, dy, 1))
                     for source, x in ((near, self.x), (far, 1 - self.x)):
                         target = self.weights.at[rows(base + 400 * x, 384)]
-                        pltpu.make_async_copy(source.at[rows(16 * x, 384)], target, sem).start()
-                    target = self.weights.at[rows(base + 384, 16)]
-                    pltpu.make_async_copy(near.at[rows(384 * (1 - self.x), 16)], target, sem).start()
+                        pltpu.make_async_copy(source.at[pl.ds(0, 384)], target, sem).start()
+                        pltpu.make_async_copy(source.at[pl.ds(384, 16)], self.seams.at[pair, x], sem).start()
 
     def start(self):
         self.start_vec()
@@ -146,8 +145,11 @@
     def wait(self, pair):
         if pair not in self.ready:
             self.ready.add(pair)
-            rows = self.weights.at[pl.ds(pair * PAIR_ROWS, PAIR_ROWS)]
+            rows = self.weights.at[pl.ds(0, PAIR_ROWS + 16)]
             pltpu.make_async_copy(rows, rows, self.sems.at[pair]).wait()
+            halves = [self.seams[pair, x].astype(F32)[:8] for x in (0, 1)]
+            seam = pl.ds(pair * PAIR_ROWS + 384, 16)
+            self.weights[seam, :] = jnp.concatenate(halves, axis=0).astype(BF16)
 
     def block(self, number):
         for pair in range(number * D // PAIR_ROWS, (number * D + D - 1) // PAIR_ROWS + 1):
@@ -183,11 +185,11 @@
     qs_out, ks_out, vs_out, os_out, y1_out, qc_out, k_out, v_out, o_out, stat_ref = refs[:10]
     w_out = refs[10] if custom else None
     weights, m_ref, qs_ref, ks_ref, vs_ref, os_ref, y1_ref, qc_ref, k_ref, v_ref, o_ref, vec_low = refs[10 + custom : 22 + custom]
-    w_sems, m_sems, out_sems, kv_sems, vec_sem, all_sems = refs[22 + custom :]
+    seams, w_sems, m_sems, out_sems, kv_sems, vec_sem, all_sems = refs[22 + custom :]
     images = m_ref.shape[0]
     tokens = m_ref.shape[1]
     if custom:
-        feed = Assembly(flags, bufs, weights, w_sems, vec_low, vec_sem)
+        feed = Assembly(flags, bufs, weights, seams, w_sems, vec_low, vec_sem)
     else:
         feed = Direct(bufs[0], weights, w_sems, vec_low, vec_sem)
 
@@ -321,6 +323,7 @@
                 small, large, large,
                 pltpu.VMEM((images, QP, D), BF16),
                 pltpu.VMEM((32, D), BF16),
+                pltpu.VMEM((16, 2, 16, D), BF16),
                 pltpu.SemaphoreType.DMA((16,)),
                 pltpu.SemaphoreType.DMA((images,)),
                 pltpu.SemaphoreType.DMA((6,)),
@@ -702,51 +705,34 @@
     refs = refs[4 + split :]
     gb_ref = refs[0]
     halves = Halves(refs[1], refs[2] if split else None, flags[0])
-    sums, low, sems = refs[2 + split :]
-    step = pl.program_id(0)
-    dv = dv_ref[0]
-    more = [dot_tn(m_ref[0], dk_ref[0]), dot_tn(m_ref[0], dv)]
-
-    @pl.when(step == 0)
-    def _():
-        for which in (0, 1):
-            sums[which] = more[which]
-        gb_ref[...] = jnp.broadcast_to(rowsum(dv), gb_ref.shape)
-
-    @pl.when(step > 0)
-    def _():
-        for which in (0, 1):
-            sums[which] += more[which]
-        gb_ref[...] += jnp.broadcast_to(rowsum(dv), gb_ref.shape)
-
+    low, sems = refs[2 + split :]
     def leave(which, act):
         start = (1 + which) * D - QUERY_HEAD
         for number, (done, pair, offset, length) in enumerate(pieces(start, D, halves.keep.shape[-2])):
             piece = low.at[which, pl.ds(done, length)]
             getattr(halves, act)(piece, pair, offset, length, sems.at[which, number])
 
-    @pl.when(step == pl.num_programs(0) - 1)
-    def _():
-        for which in (0, 1):
-            low[which] = sums[which].astype(BF16)
-            leave(which, "start")
-        for which in (0, 1):
-            leave(which, "wait")
+    tall = m_ref[...].reshape(-1, D)
+    for which, ref in ((0, dk_ref), (1, dv_ref)):
+        low[which] = dot_tn(tall, ref[...].reshape(-1, D)).astype(BF16)
+        leave(which, "start")
+    gb_ref[...] = jnp.broadcast_to(rowsum(dv_ref[...].reshape(-1, D)), gb_ref.shape)
+    for which in (0, 1):
+        leave(which, "wait")
 
 
 def memory_weights(flags, cross, memory, dk, dv, split):
     images, tokens, _ = memory.shape
-    block = pl.BlockSpec((1, tokens, D), lambda i, _: (i, 0, 0))
+    block = whole(memory.shape)
     anywhere = pl.BlockSpec(memory_space=pl.ANY)
     return pl.pallas_call(
         partial(memory_weights_kernel, split),
         grid_spec=pltpu.PrefetchScalarGridSpec(
             num_scalar_prefetch=1,
-            grid=(images,),
+            grid=(1,),
             in_specs=[anywhere] * (1 + split) + [block, block, block],
             out_specs=[whole((8, D))] + [anywhere] * (1 + split),
             scratch_shapes=[
-                pltpu.VMEM((2, D, D), F32),
                 pltpu.VMEM((2, D, D), BF16),
                 pltpu.SemaphoreType.DMA((2, 2)),
             ],
@@ -1001,9 +987,8 @@
 
 
 def gather(at, rows):
-    low = at.x == 0
-    edge = over_x(jnp.where(low, rows[-8:], rows[:8]))
-    own = jnp.where(low, jnp.concatenate([rows, edge]), jnp.concatenate([edge, rows]))
+    rest = jnp.zeros((8, D), BF16)
+    own = jnp.where(at.x == 0, jnp.concatenate([rows, rest]), jnp.concatenate([rows[8:], rows[:8], rest]))
     other = over_far(own)
     here, there = spread(own), spread(other)
     found = [*here, over_x(here[5]), *there, over_y(there[6])]
@@ -1032,7 +1017,7 @@
 
 
 def merge(body, flags, sources, out_rows, name):
-    parts = 3
+    parts = 2
     specs = []
     for array, where in sources:
         lead = (None,) * (array.ndim - 2)
@@ -1124,43 +1109,46 @@
 SWAP_TWO = [(0, 2), (2, 0), (1, 3), (3, 1)]
 
 
+def with_rows(message, vec_rows):
+    return jnp.concatenate([message, vec_rows.astype(BF16)])
+
+
 def finish(at, flags, block, far, far_last, near, near_send, cross, cross_came, vec_rows, extra):
     near_came = over_core(near_send)
     vec_came = over_core(vec_rows)
     far_out, far, low, high, message = core_merge(flags, *far, far_last, cross, cross_came)
     near_came, message, far_out, low, high, far = tie(near_came, message, far_out, low, high, far)
-    came, far_came = over_x(message), over_z(far_out, SWAP_ONE)
+    came = over_x(message)
     near, near_came = blocks_of(near), blocks_of(near_came)
     near_send = add(picked(near, 1 - at.y, at.x), picked(near_came, 1 - at.y, at.x))
     near = add(picked(near, at.y, at.x), picked(near_came, at.y, at.x))
     vec_rows = vec_rows + vec_came
     near_send, near, vec_rows, dk, dv, w = tie(near_send, near, vec_rows, *extra)
-    near_came, vec_came = over_y(near_send), over_y(vec_rows)
+    near_came, far_came = over_y(near_send), over_z(with_rows(far_out, vec_rows), SWAP_ONE)
     gm = memory_grads(dk, dv, w)
     gm, came = tie(gm, came)
     send, cross = cross_second(at, (low, high), came)
     send, near_came, far_came, cross = tie(send, near_came, far_came, cross)
 
     near = add(near, near_came)
-    far = add(far, far_came)
-    vec_rows = vec_rows + vec_came
+    far = add(far, far_came[:block])
+    vec_rows = vec_rows + far_came[block:].astype(F32)
     near, far, vec_rows, send = tie(near, far, vec_rows, send)
-    cross_came, near_came = over_y(send), over_z(near, [(3, 2), (1, 0)])
+    cross_came, near_came = over_y(with_rows(send, vec_rows)), over_z(near, [(3, 2), (1, 0)])
     cut = block // 16 * 8
-    far_top, vec_came = over_z(far[:cut], [(0, 2), (1, 3)]), over_z(vec_rows, SWAP_ONE)
+    far_top = over_z(far[:cut], [(0, 2), (1, 3)])
+    cross = add(cross, cross_came[:block])
+    near = add(near, near_came)
+    vec_rows = vec_rows + cross_came[block:].astype(F32)
+    near, cross, vec_rows, far_top, far = tie(near, cross, vec_rows, far_top, far)
+
+    cross_came, near_came = over_z(cross, [(3, 2), (0, 1)]), over_z(near, [(2, 0)])
     cross = add(cross, cross_came)
-    near = add(near, near_came)
-    vec_rows = vec_rows + vec_came
-    near, cross, vec_rows, far_top, far = tie(near, cross, vec_rows, far_top, far)
-
-    cross_came, near_came = over_z(cross, [(3, 2), (0, 1)]), over_z(near, [(2, 0)])
-    far_low, vec_came = over_z(far[cut:], [(0, 2), (1, 3)]), over_z(vec_rows, SWAP_TWO)
-    cross = add(cross, cross_came)
-    vec_rows = vec_rows + vec_came
-    near_came, cross, vec_rows, far_low = tie(near_came, cross, vec_rows, far_low)
-
-    cross_came = over_z(cross, [(2, 1)])
-    far_came = jnp.concatenate([far_top, far_low])
+    near_came, cross, far, vec_rows = tie(near_came, cross, far, vec_rows)
+
+    cross_came, far_low = over_z(cross, [(2, 1)]), over_z(with_rows(far[cut:], vec_rows), [(0, 2), (1, 3)])
+    far_came = jnp.concatenate([far_top, far_low[: block - cut]])
+    vec_rows = vec_rows + far_low[block - cut :].astype(F32)
     kept = jnp.where(at.z >= 2, far, jnp.where(at.z == 0, near, cross))
     came = jnp.where(at.z >= 2, far_came, jnp.where(at.z == 0, near_came, cross_came))
     grad_rows = kept.astype(F32) + came.astype(F32)

time: 322 us -> 319 us (level)
  waiting for transfers between devices: 141 us -> 137 us
    ppermute x14 -> x12, waiting for transfers between devices: 56.5 us -> 50.8 us  [over_z(): lax.ppermute(v, 'dp', [(4 * a + i, 4 * b + i) for a, b in hops for i in r...]
    ppermute x11 -> x10, waiting for transfers between devices: 36.8 us -> 38.5 us  [over_x(): return lax.ppermute(v, 'seq', [(0, 1), (1, 0)])]
    ppermute x11 -> x10, starting transfers between devices: 12.5 us -> 11.6 us  [over_x(): return lax.ppermute(v, 'seq', [(0, 1), (1, 0)])]
    ppermute x9 -> x8, waiting for transfers between devices: 42.4 us -> 42.9 us  [over_y(): return lax.ppermute(v, 'dp', [(i, i ^ 2) for i in range(16)])]
    ppermute x14 -> x12, starting transfers between devices: 26.4 us -> 26.9 us  [over_z(): lax.ppermute(v, 'dp', [(4 * a + i, 4 * b + i) for a, b in hops for i in r...]
    ppermute x9 -> x8, starting transfers between devices: 7.49 us -> 7.09 us  [over_y(): return lax.ppermute(v, 'dp', [(i, i ^ 2) for i in range(16)])]
  transfers between devices with their start and end apart: 54 -> 50, of which waited for: 25 -> 27; matrix products, arithmetic and copies ran while one was open for 3% -> 4% of each run, Pallas kernels for 18% -> 17%
where the time goes in v2:
time: 319 us; the launch traced here: 313 us
  waiting for transfers between devices  137 us (43%)
  Pallas kernels  103 us (32%)
  starting transfers between devices  48 us (15%)
  other arithmetic  13.8 us (4%)
  local copies, waits for them, and re-layouts  10.3 us (3%)
    ppermute x12, waiting for transfers between devices, over_z(): lax.ppermute(v, 'dp', [(4 * a + i, 4 * b + i) for a, b in hops for i in r...  50.8 us
    ppermute x8, waiting for transfers between devices, over_y(): return lax.ppermute(v, 'dp', [(i, i ^ 2) for i in range(16)])  42.9 us
    ppermute x10, waiting for transfers between devices, over_x(): return lax.ppermute(v, 'seq', [(0, 1), (1, 0)])  38.5 us
    ppermute x12, starting transfers between devices, over_z(): lax.ppermute(v, 'dp', [(4 * a + i, 4 * b + i) for a, b in hops for i in r...  26.9 us
    pallas_call x1, Pallas kernels, middle(): pl.pallas_call(partial(middle_kernel, parts, split), grid_spec=pltpu.Pref...  26.3 us
    pallas_call x1, Pallas kernels, forward(): pl.pallas_call(partial(forward_kernel, queries, custom), grid_spec=pltpu....  19.1 us
    pallas_call x1, Pallas kernels, self_backward(): pl.pallas_call(partial(self_backward_kernel, queries, split), grid_spec=p...  13.4 us
    ppermute x10, starting transfers between devices, over_x(): return lax.ppermute(v, 'seq', [(0, 1), (1, 0)])  11.6 us
  transfers between devices with their start and end apart: 50, of which 27 were waited for; matrix products, arithmetic and copies ran while one was open for 4% of the time, Pallas kernels for 17%

profile of v2, /device:TPU:8, one launch (start us, length us, event | category | flops | bytes accessed | tf_op | source)
XLA Modules:
  0.0 313.3 jit_solution(5755692077395267305)
XLA Ops:
  2.9 1.6 collective-permute-start.1
  4.9 1.5 collective-permute-start
  6.4 2.6 collective-permute-start.7
  9.0 9.5 %collective-permute-done.1.refs_2_ = bf16[400,768]{1,0:T(8,128)(2,1)S(1)} collective-permute-done((bf16[400,768]{1,0:T(8,128)(2,1)S(1)}, bf16[400,768]{1,0:T(8,128)(2,1)S(1)}, u32[]{:S(2)}, u32[]{:S(2)}) %collective-permute-start.1) | collective-permute-done | bytes 614432 | tf_op jit(solution)/shard_map/ppermute | solution.py:964
  18.6 1.5 collective-permute-start.3
  20.1 9.6 %collective-permute-done.2.refs_3_ = bf16[400,768]{1,0:T(8,128)(2,1)S(1)} collective-permute-done((bf16[400,768]{1,0:T(8,128)(2,1)S(1)}, bf16[400,768]{1,0:T(8,128)(2,1)S(1)}, u32[]{:S(2)}, u32[]{:S(2)}) %collective-permute-start.2) | collective-permute-done | bytes 614432 | tf_op jit(solution)/shard_map/ppermute | solution.py:972
  30.0 2.5 collective-permute-start.5
  32.5 2.7 collective-permute-done.7.refs_8_
  36.6 1.4 collective-permute-start.10
  38.0 8.4 %collective-permute-done.4.refs_5_ = bf16[400,768]{1,0:T(8,128)(2,1)S(1)} collective-permute-done((bf16[400,768]{1,0:T(8,128)(2,1)S(1)}, bf16[400,768]{1,0:T(8,128)(2,1)S(1)}, u32[]{:S(2)}, u32[]{:S(2)}) %collective-permute-start.4) | collective-permute-done | bytes 614432 | tf_op jit(solution)/shard_map/ppermute | solution.py:964
  48.4 8.7 %collective-permute-done.9.refs_10_ = bf16[400,768]{1,0:T(8,128)(2,1)S(1)} collective-permute-done((bf16[400,768]{1,0:T(8,128)(2,1)S(1)}, bf16[400,768]{1,0:T(8,128)(2,1)S(1)}, u32[]{:S(2)}, u32[]{:S(2)}) %collective-permute-start.9) | collective-permute-done | bytes 614432 | tf_op jit(solution)/shard_map/ppermute | solution.py:964
  57.2 2.2 collective-permute-done.10.refs_11_
  59.3 1.5 collective-permute-start.6
  62.3 2.5 collective-permute-start.13
  64.9 11.4 %collective-permute-done.6.refs_7_ = bf16[400,768]{1,0:T(8,128)(2,1)} collective-permute-done((bf16[400,768]{1,0:T(8,128)(2,1)S(1)}, bf16[400,768]{1,0:T(8,128)(2,1)}, u32[]{:S(2)}, u32[]{:S(2)}) %collective-permute-start.6) | collective-permute-done | bytes 614432 | tf_op jit(solution)/shard_map/ppermute | solution.py:968
  76.2 11.2 %collective-permute-done.11.refs_12_ = bf16[400,768]{1,0:T(8,128)(2,1)} collective-permute-done((bf16[400,768]{1,0:T(8,128)(2,1)S(1)}, bf16[400,768]{1,0:T(8,128)(2,1)}, u32[]{:S(2)}, u32[]{:S(2)}) %collective-permute-start.11) | collective-permute-done | bytes 614432 | tf_op jit(solution)/shard_map/ppermute | solution.py:968
  91.4 1.6 collective-permute-done.26.refs_27_
  93.1 11.6 %collective-permute-done.14.refs_15_ = bf16[400,768]{1,0:T(8,128)(2,1)} collective-permute-done((bf16[400,768]{1,0:T(8,128)(2,1)}, bf16[400,768]{1,0:T(8,128)(2,1)}, u32[]{:S(2)}, u32[]{:S(2)}) %collective-permute-start.14) | collective-permute-done | bytes 614432 | tf_op jit(solution)/shard_map/ppermute | solution.py:964
  107.3 19.1 %forward.1 = (bf16[336,768]{1,0:T(8,128)(2,1)}, bf16[336,768]{1,0:T(8,128)(2,1)}, bf16[336,768]{1,0:T(8,128)(2,1)}, bf16[336,768]{1,0:T(8,128)(2,1)}, f32[336,76...) custom-call(s32[3]{0:T(128)} %broadcast_subtract_fusion.left_ref, ...), custom_call_target="tpu_custom_call" | custom-call | tf_op jit(solution)/shard_map/forward/pallas_call | solution.py:312
  126.4 1.8 collective-permute-start.31
  130.5 10.9 %collective-permute-done.32.refs_5_ = f32[3,8,224]{2,1,0:T(8,128)S(1)} collective-permute-done((f32[3,8,224]{2,1,0:T(8,128)}, f32[3,8,224]{2,1,0:T(8,128)S(1)}, u32[]{:S(2)}, u32[]{:S(2)}) %collective-permute-start.32) | collective-permute-done | bytes 21536 | tf_op jit(solution)/shard_map/ppermute | solution.py:968
  142.2 26.3 %middle.1 = (f32[3,112,768]{2,1,0:T(8,128)}, bf16[2,2,784,768]{3,2,1,0:T(8,128)(2,1)}, bf16[2,2,784,768]{3,2,1,0:T(8,128)(2,1)}, bf16[2,784,768]{2,1,0:T(8,128)(...) custom-call(s32[4]{0:T(128)} %pad_add_fusion.flags.refs_0_, ...), custom_call_target="tpu_custom_call" | custom-call | flops 10701766 | bytes 28311 | tf_op jit(solution)/shard_map/middle/pallas_call | solution.py:603
  168.7 10.1 %cross_backward.1 = (bf16[3,112,768]{2,1,0:T(8,128)(2,1)}, bf16[3,512,768]{2,1,0:T(8,128)(2,1)}, bf16[3,512,768]{2,1,0:T(8,128)(2,1)}) custom-call(s32[3]{0:T(128)} %broadcast_subtract_fusion.left_ref, bf16[3,112,768]{2,1,0:T(8,128)(2,1)} %bitcast.42, bf16[3,512,768]{2,1,0:T(8,128)(2,1)} %get-tuple-element.90.k_ref, ...), custom_call_target="tpu_custom_call" | custom-call | flops 352321 | bytes 9437 | tf_op jit(solution)/shard_map/cross_backward/pallas_call | solution.py:684
  178.7 3.8 %far_send.1 = bf16[2,392,768]{2,1,0:T(8,128)(2,1)} custom-call(s32[4]{0:T(128)} %pad_add_fusion.flags.refs_0_, bf16[2,2,2,392,768]{4,3,2,1,0:T(8,128)(2,1)} %bitcast.30, bf16[2,2,2,392,768]{4,3,2,1,0:T(8,128)(2,1)} %bitcast.11.b.d.refs_1_.refs_4_, bf16[2,2,2,392,768]{4,3,2,1,0:T(8,128)(2,1)} %bitcast.31, bf16[2,2,2,392,768]{4,3,2,1,0:T(8,128)(2,1)} %bitcast.11.b.d.refs_1_.refs_4_), custom_call_target="tpu_custom_call" | custom-call | tf_op jit(solution)/shard_map/far_send/pallas_call | solution.py:1026
  182.5 1.4 collective-permute-start.36
  183.9 1.6 collective-permute-start.34
  185.6 9.3 %memory_weights.1 = (f32[8,768]{1,0:T(8,128)}, bf16[2,784,768]{2,1,0:T(8,128)(2,1)}, bf16[2,784,768]{2,1,0:T(8,128)(2,1)}) custom-call(s32[4]{0:T(128)} %pad_add_fusion.flags.refs_0_, bf16[2,784,768]{2,1,0:T(8,128)(2,1)} %get-tuple-element.87.refs_0_, bf16[2,784,768]{2,1,0:T(8,128)(2,1)} %get-tuple-element.88.refs_1_, ...), custom_call_target="tpu_custom_call", output_to_operand_aliasing={{1}: (1, {}), {2}: (2, {})} | custom-call | flops 3623878 | bytes 7077 | tf_op jit(solution)/shard_map/memory_weights/pallas_call | solution.py:728
  195.3 2.6 collective-permute-done.34
  198.7 6.8 %query_backward.1 = (f32[336,768]{1,0:T(8,128)}, bf16[64,768]{1,0:T(8,128)(2,1)}, f32[24,768]{1,0:T(8,128)}, bf16[2,784,768]{2,1,0:T(8,128)(2,1)}, bf16[2,784,768]{2,1,0:T(8,128)(2,1)}) custom-call(s32[4]{0:T(128)} %pad_add_fusion.flags.refs_0_, bf16[2,784,768]{2,1,0:T(8,128)(2,1)} %get-tuple-element.99.refs_0_, ...), custom_call_target="tpu_custom_call", output_to_operand_aliasing={{3}: (1, {}), {4}: (2, {})} | custom-call | flops 792723 | bytes 4128 | tf_op jit(solution)/shard_map/query_backward/pallas_call | solution.py:827
  205.5 13.4 %self_backward.1 = (f32[3,112,768]{2,1,0:T(8,128)}, f32[24,768]{1,0:T(8,128)}, bf16[2,784,768]{2,1,0:T(8,128)(2,1)}, bf16[2,784,768]{2,1,0:T(8,128)(2,1)}) custom-call(s32[4]{0:T(128)} %pad_add_fusion.flags.refs_0_, bf16[336,768]{1,0:T(8,128)(2,1)} %get-tuple-element.86.refs_1_, f32[336,768]{1,0:T(8,128)} %get-tuple-element.103.refs_2_, ...), custom_call_target="tpu_custom_call" | custom-call | flops 6341787 | bytes 9437 | tf_op jit(solution)/shard_map/self_backward/pallas_call | solution.py:921
  219.5 1.4 copy-done
  220.9 5.9 %core_merge.1 = (bf16[392,768]{1,0:T(8,128)(2,1)}, bf16[392,768]{1,0:T(8,128)(2,1)}, bf16[392,768]{1,0:T(8,128)(2,1)}, bf16[392,768]{1,0:T(8,128)(2,1)}, bf16[480,768]{1,0:T(8,128)(2,1)}) custom-call(s32[4]{0:T(128)} %pad_add_fusion.flags.refs_0_, bf16[2,2,2,392,768]{4,3,2,1,0:T(8,128)(2,1)} %bitcast.32, ...), custom_call_target="tpu_custom_call" | custom-call | tf_op jit(solution)/shard_map/core_merge/pallas_call | solution.py:1026
  226.8 1.8 collective-permute-start.40
  230.0 2.9 fusion.8
  233.8 2.3 collective-permute-start.42
  236.1 8.0 %memory_grads.1 = f32[3,512,768]{2,1,0:T(8,128)} custom-call(bf16[3,512,768]{2,1,0:T(8,128)(2,1)} %get-tuple-element.128.refs_3_.dk_ref, bf16[3,512,768]{2,1,0:T(8,128)(2,1)} %get-tuple-element.129.refs_4_.dv_ref, bf16[12544,768]{1,0:T(8,128)(2,1)} %get-tuple-element.130.refs_6_.refs_7_.ck.cv, bf16[12544,768]{1,0:T(8,128)(2,1)} %get-tuple-element.130.refs_6_.refs_7_.ck.cv), custom_call_target="tpu_custom_call" | custom-call | flops 3623878656 | bytes 9437184 | tf_op jit(solution)/shard_map/memory_grads/pallas_call | solution.py:755
  244.2 1.4 collective-permute-done.40
  245.6 1.7 fusion.5
  247.2 1.6 collective-permute-done.41
  248.9 1.7 collective-permute-done.42
  252.0 3.7 %collective-permute-start.43 = (bf16[392,768]{1,0:T(8,128)(2,1)S(1)}, bf16[392,768]{1,0:T(8,128)(2,1)S(1)}, u32[]{:S(2)}, u32[]{:S(2)}) collective-permute-start(bf16[392,768]{1,0:T(8,128)(2,1)S(1)} %add_convert_fusion.4), channel_id=1, source_target_pairs={{24,16},{26,18},{28,20},{30,22},{8,0},{10,2},{12,4},{14,6},{25,17}... | collective-permute-start | bytes 1806344 | tf_op jit(solution)/shard_map/ppermute | solution.py:972
  256.1 4.8 %collective-permute-start.45 = (bf16[192,768]{1,0:T(8,128)(2,1)S(1)}, bf16[192,768]{1,0:T(8,128)(2,1)S(1)}, u32[]{:S(2)}, u32[]{:S(2)}) collective-permute-start(bf16[192,768]{1,0:T(8,128)(2,1)S(1)} %slice.71), channel_id=1, source_target_pairs={{0,16},{2,18},{4,20},{6,22},{8,24},{10,26},{12,28},{14,30},{1,17},... | collective-permute-start | bytes 884744 | tf_op jit(solution)/shard_map/ppermute | solution.py:972
  260.9 6.7 %collective-permute-done.43 = bf16[392,768]{1,0:T(8,128)(2,1)S(1)} collective-permute-done((bf16[392,768]{1,0:T(8,128)(2,1)S(1)}, bf16[392,768]{1,0:T(8,128)(2,1)S(1)}, u32[]{:S(2)}, u32[]{:S(2)}) %collective-permute-start.43) | collective-permute-done | bytes 602144 | tf_op jit(solution)/shard_map/ppermute | solution.py:972
  267.8 3.0 collective-permute-done.44
  273.5 15.4 %collective-permute-done.47 = bf16[392,768]{1,0:T(8,128)(2,1)S(1)} collective-permute-done((bf16[392,768]{1,0:T(8,128)(2,1)S(1)}, bf16[392,768]{1,0:T(8,128)(2,1)S(1)}, u32[]{:S(2)}, u32[]{:S(2)}) %collective-permute-start.47) | collective-permute-done | bytes 602144 | tf_op jit(solution)/shard_map/ppermute | solution.py:972
  291.2 3.4 %collective-permute-start.48 = (bf16[224,768]{1,0:T(8,128)(2,1)}, bf16[224,768]{1,0:T(8,128)(2,1)}, u32[]{:S(2)}, u32[]{:S(2)}) collective-permute-start(bf16[224,768]{1,0:T(8,128)(2,1)} %pad_maximum_fusion.2), channel_id=1, source_target_pairs={{0,16},{2,18},{4,20},{6,22},{8,24},{10,26},{12,28},{14,30},{1,17},... | collective-permute-start | bytes 1032200 | tf_op jit(solution)/shard_map/ppermute | solution.py:972
  297.2 11.3 %collective-permute-done.48 = bf16[224,768]{1,0:T(8,128)(2,1)} collective-permute-done((bf16[224,768]{1,0:T(8,128)(2,1)}, bf16[224,768]{1,0:T(8,128)(2,1)}, u32[]{:S(2)}, u32[]{:S(2)}) %collective-permute-start.48) | collective-permute-done | bytes 344096 | tf_op jit(solution)/shard_map/ppermute | solution.py:972
  310.2 1.6 convert_add_fusion
  (188 shorter events, 34.4 us)
Async XLA Ops:
  2.9 15.7 %collective-permute-start.1 = (bf16[400,768]{1,0:T(8,128)(2,1)S(1)}, bf16[400,768]{1,0:T(8,128)(2,1)S(1)}, u32[]{:S(2)}, u32[]{:S(2)}) collective-permute-start(bf16[400,768]{1,0:T(8,128)(2,1)S(1)} %maximum_select_fusion.1.refs_0_), channel_id=1, source_target_pairs={{0,4},{2,6},{4,0},{6,2},{8,12},{10,14},{12,8},{14,10},{16,20},{18,... | collective-permute-start | bytes 1843208 | tf_op jit(solution)/shard_map/ppermute | solution.py:964
  4.5 25.1 %collective-permute-start.2 = (bf16[400,768]{1,0:T(8,128)(2,1)S(1)}, bf16[400,768]{1,0:T(8,128)(2,1)S(1)}, u32[]{:S(2)}, u32[]{:S(2)}) collective-permute-start(bf16[400,768]{1,0:T(8,128)(2,1)S(1)} %maximum_select_fusion.1.refs_0_), channel_id=1, source_target_pairs={{0,8},{2,10},{4,12},{6,14},{8,0},{10,2},{12,4},{14,6},{16,24},{18,... | collective-permute-start | bytes 1843208 | tf_op jit(solution)/shard_map/ppermute | solution.py:972
  4.9 25.0 %collective-permute-start = (bf16[400,768]{1,0:T(8,128)(2,1)S(1)}, bf16[400,768]{1,0:T(8,128)(2,1)S(1)}, u32[]{:S(2)}, u32[]{:S(2)}) collective-permute-start(bf16[400,768]{1,0:T(8,128)(2,1)S(1)} %maximum_select_fusion.1.refs_0_), channel_id=1, source_target_pairs={{0,1},{1,0},{2,3},{3,2},{4,5},{5,4},{6,7},{7,6},{8,9},{9,8},{10,11... | collective-permute-start | bytes 1843208 | tf_op jit(solution)/shard_map/ppermute | solution.py:968
  6.4 28.7 %collective-permute-start.7 = (bf16[400,768]{1,0:T(8,128)(2,1)S(1)}, bf16[400,768]{1,0:T(8,128)(2,1)S(1)}, u32[]{:S(2)}, u32[]{:S(2)}) collective-permute-start(bf16[400,768]{1,0:T(8,128)(2,1)S(1)} %maximum_select_fusion.1.refs_0_), channel_id=1, source_target_pairs={{0,16},{2,18},{4,20},{6,22},{16,0},{18,2},{20,4},{22,6},{8,24},{10... | collective-permute-start | bytes 1843208 | tf_op jit(solution)/shard_map/ppermute | solution.py:972
  9.0 26.7 %collective-permute-start.15 = (bf16[400,768]{1,0:T(8,128)(2,1)S(1)}, bf16[400,768]{1,0:T(8,128)(2,1)S(1)}, u32[]{:S(2)}, u32[]{:S(2)}) collective-permute-start(bf16[400,768]{1,0:T(8,128)(2,1)S(1)} %maximum_select_fusion.1.refs_0_), channel_id=1, source_target_pairs={{0,2},{2,0},{4,6},{6,4},{8,10},{10,8},{12,14},{14,12},{16,18},{18,... | collective-permute-start | bytes 1843208 | tf_op jit(solution)/shard_map/ppermute | solution.py:960
  18.6 18.0 %collective-permute-start.3 = (bf16[400,768]{1,0:T(8,128)(2,1)S(1)}, bf16[400,768]{1,0:T(8,128)(2,1)S(1)}, u32[]{:S(2)}, u32[]{:S(2)}) collective-permute-start(bf16[400,768]{1,0:T(8,128)(2,1)S(1)} %collective-permute-done.1.refs_2_), channel_id=1, source_target_pairs={{0,1},{1,0},{2,3},{3,2},{4,5},{5,4},{6,7},{7,6},{8,9},{9,8},{10,11... | collective-permute-start | bytes 1843208 | tf_op jit(solution)/shard_map/ppermute | solution.py:968
  29.6 16.8 %collective-permute-start.4 = (bf16[400,768]{1,0:T(8,128)(2,1)S(1)}, bf16[400,768]{1,0:T(8,128)(2,1)S(1)}, u32[]{:S(2)}, u32[]{:S(2)}) collective-permute-start(bf16[400,768]{1,0:T(8,128)(2,1)S(1)} %collective-permute-done.2.refs_3_), channel_id=1, source_target_pairs={{0,4},{2,6},{4,0},{6,2},{8,12},{10,14},{12,8},{14,10},{16,20},{18,... | collective-permute-start | bytes 1843208 | tf_op jit(solution)/shard_map/ppermute | solution.py:964
  30.0 17.3 %collective-permute-start.5 = (bf16[400,768]{1,0:T(8,128)(2,1)S(1)}, bf16[400,768]{1,0:T(8,128)(2,1)S(1)}, u32[]{:S(2)}, u32[]{:S(2)}) collective-permute-start(bf16[400,768]{1,0:T(8,128)(2,1)S(1)} %collective-permute-done.refs_1_), channel_id=1, source_target_pairs={{0,8},{2,10},{4,12},{6,14},{8,0},{10,2},{12,4},{14,6},{16,24},{18,... | collective-permute-start | bytes 1843208 | tf_op jit(solution)/shard_map/ppermute | solution.py:972
  35.2 13.3 %collective-permute-start.8 = (bf16[400,768]{1,0:T(8,128)(2,1)S(1)}, bf16[400,768]{1,0:T(8,128)(2,1)S(1)}, u32[]{:S(2)}, u32[]{:S(2)}) collective-permute-start(bf16[400,768]{1,0:T(8,128)(2,1)S(1)} %collective-permute-done.7.refs_8_), channel_id=1, source_target_pairs={{0,1},{1,0},{2,3},{3,2},{4,5},{5,4},{6,7},{7,6},{8,9},{9,8},{10,11... | collective-permute-start | bytes 1843208 | tf_op jit(solution)/shard_map/ppermute | solution.py:968
  35.7 21.5 %collective-permute-start.9 = (bf16[400,768]{1,0:T(8,128)(2,1)S(1)}, bf16[400,768]{1,0:T(8,128)(2,1)S(1)}, u32[]{:S(2)}, u32[]{:S(2)}) collective-permute-start(bf16[400,768]{1,0:T(8,128)(2,1)S(1)} %collective-permute-done.7.refs_8_), channel_id=1, source_target_pairs={{0,4},{2,6},{4,0},{6,2},{8,12},{10,14},{12,8},{14,10},{16,20},{18,... | collective-permute-start | bytes 1843208 | tf_op jit(solution)/shard_map/ppermute | solution.py:964
  36.6 22.8 %collective-permute-start.10 = (bf16[400,768]{1,0:T(8,128)(2,1)S(1)}, bf16[400,768]{1,0:T(8,128)(2,1)S(1)}, u32[]{:S(2)}, u32[]{:S(2)}) collective-permute-start(bf16[400,768]{1,0:T(8,128)(2,1)S(1)} %collective-permute-done.7.refs_8_), channel_id=1, source_target_pairs={{0,8},{2,10},{4,12},{6,14},{8,0},{10,2},{12,4},{14,6},{16,24},{18,... | collective-permute-start | bytes 1843208 | tf_op jit(solution)/shard_map/ppermute | solution.py:972
  46.4 14.4 %collective-permute-start.16 = (bf16[400,768]{1,0:T(8,128)(2,1)S(1)}, bf16[400,768]{1,0:T(8,128)(2,1)S(1)}, u32[]{:S(2)}, u32[]{:S(2)}) collective-permute-start(bf16[400,768]{1,0:T(8,128)(2,1)S(1)} %collective-permute-done.refs_1_), channel_id=1, source_target_pairs={{0,2},{2,0},{4,6},{6,4},{8,10},{10,8},{12,14},{14,12},{16,18},{18,... | collective-permute-start | bytes 1843208 | tf_op jit(solution)/shard_map/ppermute | solution.py:960
  47.3 14.1 %collective-permute-start.17 = (bf16[400,768]{1,0:T(8,128)(2,1)S(1)}, bf16[400,768]{1,0:T(8,128)(2,1)S(1)}, u32[]{:S(2)}, u32[]{:S(2)}) collective-permute-start(bf16[400,768]{1,0:T(8,128)(2,1)S(1)} %collective-permute-done.1.refs_2_), channel_id=1, source_target_pairs={{0,2},{2,0},{4,6},{6,4},{8,10},{10,8},{12,14},{14,12},{16,18},{18,... | collective-permute-start | bytes 1843208 | tf_op jit(solution)/shard_map/ppermute | solution.py:960
  48.4 13.9 %collective-permute-start.18 = (bf16[400,768]{1,0:T(8,128)(2,1)S(1)}, bf16[400,768]{1,0:T(8,128)(2,1)S(1)}, u32[]{:S(2)}, u32[]{:S(2)}) collective-permute-start(bf16[400,768]{1,0:T(8,128)(2,1)S(1)} %collective-permute-done.2.refs_3_), channel_id=1, source_target_pairs={{0,2},{2,0},{4,6},{6,4},{8,10},{10,8},{12,14},{14,12},{16,18},{18,... | collective-permute-start | bytes 1843208 | tf_op jit(solution)/shard_map/ppermute | solution.py:960
  57.2 7.6 %collective-permute-start.23 = (bf16[400,768]{1,0:T(8,128)(2,1)S(1)}, bf16[400,768]{1,0:T(8,128)(2,1)S(1)}, u32[]{:S(2)}, u32[]{:S(2)}) collective-permute-start(bf16[400,768]{1,0:T(8,128)(2,1)S(1)} %collective-permute-done.7.refs_8_), channel_id=1, source_target_pairs={{0,2},{2,0},{4,6},{6,4},{8,10},{10,8},{12,14},{14,12},{16,18},{18,... | collective-permute-start | bytes 1843208 | tf_op jit(solution)/shard_map/ppermute | solution.py:960
  59.3 16.9 %collective-permute-start.6 = (bf16[400,768]{1,0:T(8,128)(2,1)S(1)}, bf16[400,768]{1,0:T(8,128)(2,1)}, u32[]{:S(2)}, u32[]{:S(2)}) collective-permute-start(bf16[400,768]{1,0:T(8,128)(2,1)S(1)} %collective-permute-done.4.refs_5_), channel_id=1, source_target_pairs={{0,1},{1,0},{2,3},{3,2},{4,5},{5,4},{6,7},{7,6},{8,9},{9,8},{10,11... | collective-permute-start | bytes 1843208 | tf_op jit(solution)/shard_map/ppermute | solution.py:968
  60.8 26.6 %collective-permute-start.11 = (bf16[400,768]{1,0:T(8,128)(2,1)S(1)}, bf16[400,768]{1,0:T(8,128)(2,1)}, u32[]{:S(2)}, u32[]{:S(2)}) collective-permute-start(bf16[400,768]{1,0:T(8,128)(2,1)S(1)} %collective-permute-done.9.refs_10_), channel_id=1, source_target_pairs={{0,1},{1,0},{2,3},{3,2},{4,5},{5,4},{6,7},{7,6},{8,9},{9,8},{10,11... | collective-permute-start | bytes 1843208 | tf_op jit(solution)/shard_map/ppermute | solution.py:968
  61.4 26.1 %collective-permute-start.12 = (bf16[400,768]{1,0:T(8,128)(2,1)S(1)}, bf16[400,768]{1,0:T(8,128)(2,1)}, u32[]{:S(2)}, u32[]{:S(2)}) collective-permute-start(bf16[400,768]{1,0:T(8,128)(2,1)S(1)} %collective-permute-done.10.refs_11_), channel_id=1, source_target_pairs={{0,4},{2,6},{4,0},{6,2},{8,12},{10,14},{12,8},{14,10},{16,20},{18,... | collective-permute-start | bytes 1843208 | tf_op jit(solution)/shard_map/ppermute | solution.py:964
  62.3 25.7 %collective-permute-start.13 = (bf16[400,768]{1,0:T(8,128)(2,1)S(1)}, bf16[400,768]{1,0:T(8,128)(2,1)}, u32[]{:S(2)}, u32[]{:S(2)}) collective-permute-start(bf16[400,768]{1,0:T(8,128)(2,1)S(1)} %collective-permute-done.8.refs_9_), channel_id=1, source_target_pairs={{0,8},{2,10},{4,12},{6,14},{8,0},{10,2},{12,4},{14,6},{16,24},{18,... | collective-permute-start | bytes 1843208 | tf_op jit(solution)/shard_map/ppermute | solution.py:972
  64.8 23.2 %collective-permute-start.19 = (bf16[400,768]{1,0:T(8,128)(2,1)S(1)}, bf16[400,768]{1,0:T(8,128)(2,1)S(1)}, u32[]{:S(2)}, u32[]{:S(2)}) collective-permute-start(bf16[400,768]{1,0:T(8,128)(2,1)S(1)} %collective-permute-done.3.refs_4_), channel_id=1, source_target_pairs={{0,2},{2,0},{4,6},{6,4},{8,10},{10,8},{12,14},{14,12},{16,18},{18,... | collective-permute-start | bytes 1843208 | tf_op jit(solution)/shard_map/ppermute | solution.py:960
  76.2 12.3 %collective-permute-start.20 = (bf16[400,768]{1,0:T(8,128)(2,1)S(1)}, bf16[400,768]{1,0:T(8,128)(2,1)S(1)}, u32[]{:S(2)}, u32[]{:S(2)}) collective-permute-start(bf16[400,768]{1,0:T(8,128)(2,1)S(1)} %collective-permute-done.4.refs_5_), channel_id=1, source_target_pairs={{0,2},{2,0},{4,6},{6,4},{8,10},{10,8},{12,14},{14,12},{16,18},{18,... | collective-permute-start | bytes 1843208 | tf_op jit(solution)/shard_map/ppermute | solution.py:960
  87.4 2.9 collective-permute-start.24
  88.0 3.3 %collective-permute-start.25 = (bf16[400,768]{1,0:T(8,128)(2,1)S(1)}, bf16[400,768]{1,0:T(8,128)(2,1)S(1)}, u32[]{:S(2)}, u32[]{:S(2)}) collective-permute-start(bf16[400,768]{1,0:T(8,128)(2,1)S(1)} %collective-permute-done.9.refs_10_), channel_id=1, source_target_pairs={{0,2},{2,0},{4,6},{6,4},{8,10},{10,8},{12,14},{14,12},{16,18},{18,... | collective-permute-start | bytes 1843208 | tf_op jit(solution)/shard_map/ppermute | solution.py:960
  88.0 5.0 %collective-permute-start.26 = (bf16[400,768]{1,0:T(8,128)(2,1)S(1)}, bf16[400,768]{1,0:T(8,128)(2,1)S(1)}, u32[]{:S(2)}, u32[]{:S(2)}) collective-permute-start(bf16[400,768]{1,0:T(8,128)(2,1)S(1)} %collective-permute-done.10.refs_11_), channel_id=1, source_target_pairs={{0,2},{2,0},{4,6},{6,4},{8,10},{10,8},{12,14},{14,12},{16,18},{18,... | collective-permute-start | bytes 1843208 | tf_op jit(solution)/shard_map/ppermute | solution.py:960
  88.5 16.2 %collective-permute-start.14 = (bf16[400,768]{1,0:T(8,128)(2,1)}, bf16[400,768]{1,0:T(8,128)(2,1)}, u32[]{:S(2)}, u32[]{:S(2)}) collective-permute-start(bf16[400,768]{1,0:T(8,128)(2,1)} %collective-permute-done.13.refs_14_), channel_id=1, source_target_pairs={{0,4},{2,6},{4,0},{6,2},{8,12},{10,14},{12,8},{14,10},{16,20},{18,... | collective-permute-start | bytes 1843208 | tf_op jit(solution)/shard_map/ppermute | solution.py:964
  89.5 17.5 %collective-permute-start.29 = (bf16[400,768]{1,0:T(8,128)(2,1)}, bf16[400,768]{1,0:T(8,128)(2,1)}, u32[]{:S(2)}, u32[]{:S(2)}) collective-permute-start(bf16[400,768]{1,0:T(8,128)(2,1)} %collective-permute-done.13.refs_14_), channel_id=1, source_target_pairs={{0,2},{2,0},{4,6},{6,4},{8,10},{10,8},{12,14},{14,12},{16,18},{18,... | collective-permute-start | bytes 1843208 | tf_op jit(solution)/shard_map/ppermute | solution.py:960
  90.4 16.6 %collective-permute-start.22 = (bf16[400,768]{1,0:T(8,128)(2,1)}, bf16[400,768]{1,0:T(8,128)(2,1)}, u32[]{:S(2)}, u32[]{:S(2)}) collective-permute-start(bf16[400,768]{1,0:T(8,128)(2,1)} %collective-permute-done.6.refs_7_), channel_id=1, source_target_pairs={{0,2},{2,0},{4,6},{6,4},{8,10},{10,8},{12,14},{14,12},{16,18},{18,... | collective-permute-start | bytes 1843208 | tf_op jit(solution)/shard_map/ppermute | solution.py:960
  91.2 15.7 %collective-permute-start.27 = (bf16[400,768]{1,0:T(8,128)(2,1)}, bf16[400,768]{1,0:T(8,128)(2,1)}, u32[]{:S(2)}, u32[]{:S(2)}) collective-permute-start(bf16[400,768]{1,0:T(8,128)(2,1)} %collective-permute-done.11.refs_12_), channel_id=1, source_target_pairs={{0,2},{2,0},{4,6},{6,4},{8,10},{10,8},{12,14},{14,12},{16,18},{18,... | collective-permute-start | bytes 1843208 | tf_op jit(solution)/shard_map/ppermute | solution.py:960
  93.0 14.0 %collective-permute-start.28 = (bf16[400,768]{1,0:T(8,128)(2,1)}, bf16[400,768]{1,0:T(8,128)(2,1)}, u32[]{:S(2)}, u32[]{:S(2)}) collective-permute-start(bf16[400,768]{1,0:T(8,128)(2,1)} %collective-permute-done.12.refs_13_), channel_id=1, source_target_pairs={{0,2},{2,0},{4,6},{6,4},{8,10},{10,8},{12,14},{14,12},{16,18},{18,... | collective-permute-start | bytes 1843208 | tf_op jit(solution)/shard_map/ppermute | solution.py:960
  104.8 2.4 collective-permute-start.30
  126.4 15.0 %collective-permute-start.31 = (bf16[3,112,768]{2,1,0:T(8,128)(2,1)}, bf16[3,112,768]{2,1,0:T(8,128)(2,1)S(1)}, u32[]{:S(2)}, u32[]{:S(2)}) collective-permute-start(bf16[3,112,768]{2,1,0:T(8,128)(2,1)} %get-tuple-element.82.refs_2_), channel_id=1, source_target_pairs={{0,1},{1,0},{2,3},{3,2},{4,5},{5,4},{6,7},{7,6},{8,9},{9,8},{10,11... | collective-permute-start | bytes 1548296 | tf_op jit(solution)/shard_map/ppermute | solution.py:968
  128.8 12.6 %collective-permute-start.32 = (f32[3,8,224]{2,1,0:T(8,128)}, f32[3,8,224]{2,1,0:T(8,128)S(1)}, u32[]{:S(2)}, u32[]{:S(2)}) collective-permute-start(f32[3,8,224]{2,1,0:T(8,128)} %get-tuple-element.83.refs_4_), channel_id=1, source_target_pairs={{0,1},{1,0},{2,3},{3,2},{4,5},{5,4},{6,7},{7,6},{8,9},{9,8},{10,11... | collective-permute-start | bytes 64520 | tf_op jit(solution)/shard_map/ppermute | solution.py:968
  168.6 10.1 %collective-permute-start.33 = (bf16[2,2,784,768]{3,2,1,0:T(8,128)(2,1)}, bf16[2,2,784,768]{3,2,1,0:T(8,128)(2,1)}, u32[]{:S(2)}, u32[]{:S(2)}) collective-permute-start(bf16[2,2,784,768]{3,2,1,0:T(8,128)(2,1)} %get-tuple-element.96), channel_id=1, source_target_pairs={{0,2},{2,0},{4,6},{6,4},{8,10},{10,8},{12,14},{14,12},{16,18},{18,... | collective-permute-start | bytes 14450696 | tf_op jit(solution)/shard_map/ppermute | solution.py:960
  182.5 36.4 %collective-permute-start.36 = (bf16[2,392,768]{2,1,0:T(8,128)(2,1)}, bf16[2,392,768]{2,1,0:T(8,128)(2,1)}, u32[]{:S(2)}, u32[]{:S(2)}) collective-permute-start(bf16[2,392,768]{2,1,0:T(8,128)(2,1)} %far_send.1), channel_id=1, source_target_pairs={{0,4},{2,6},{4,0},{6,2},{8,12},{10,14},{12,8},{14,10},{16,20},{18,... | collective-permute-start | bytes 3612680 | tf_op jit(solution)/shard_map/ppermute | solution.py:964
  183.9 13.9 %collective-permute-start.34 = (bf16[3,112,768]{2,1,0:T(8,128)(2,1)S(1)}, bf16[3,112,768]{2,1,0:T(8,128)(2,1)S(1)}, u32[]{:S(2)}, u32[]{:S(2)}) collective-permute-start(bf16[3,112,768]{2,1,0:T(8,128)(2,1)S(1)} %copy-done.29), channel_id=1, source_target_pairs={{0,1},{1,0},{2,3},{3,2},{4,5},{5,4},{6,7},{7,6},{8,9},{9,8},{10,11... | collective-permute-start | bytes 1548296 | tf_op jit(solution)/shard_map/ppermute | solution.py:968
  194.8 10.7 %collective-permute-start.35 = (f32[8,768]{1,0:T(8,128)}, f32[8,768]{1,0:T(8,128)S(1)}, u32[]{:S(2)}, u32[]{:S(2)}) collective-permute-start(f32[8,768]{1,0:T(8,128)} %get-tuple-element.108), channel_id=1, source_target_pairs={{0,1},{1,0},{2,3},{3,2},{4,5},{5,4},{6,7},{7,6},{8,9},{9,8},{10,11... | collective-permute-start | bytes 73736 | tf_op jit(solution)/shard_map/ppermute | solution.py:968
  205.4 14.1 %collective-permute-start.38 = (bf16[2,784,768]{2,1,0:T(8,128)(2,1)}, bf16[2,784,768]{2,1,0:T(8,128)(2,1)S(1)}, u32[]{:S(2)}, u32[]{:S(2)}) collective-permute-start(bf16[2,784,768]{2,1,0:T(8,128)(2,1)} %get-tuple-element.117), channel_id=1, source_target_pairs={{0,2},{2,0},{4,6},{6,4},{8,10},{10,8},{12,14},{14,12},{16,18},{18,... | collective-permute-start | bytes 7225352 | tf_op jit(solution)/shard_map/ppermute | solution.py:960
  218.9 7.9 %collective-permute-start.37 = (bf16[2,784,768]{2,1,0:T(8,128)(2,1)}, bf16[2,784,768]{2,1,0:T(8,128)(2,1)}, u32[]{:S(2)}, u32[]{:S(2)}) collective-permute-start(bf16[2,784,768]{2,1,0:T(8,128)(2,1)} %get-tuple-element.114), channel_id=1, source_target_pairs={{0,2},{2,0},{4,6},{6,4},{8,10},{10,8},{12,14},{14,12},{16,18},{18,... | collective-permute-start | bytes 7225352 | tf_op jit(solution)/shard_map/ppermute | solution.py:960
  226.8 18.8 %collective-permute-start.40 = (bf16[480,768]{1,0:T(8,128)(2,1)}, bf16[480,768]{1,0:T(8,128)(2,1)S(1)}, u32[]{:S(2)}, u32[]{:S(2)}) collective-permute-start(bf16[480,768]{1,0:T(8,128)(2,1)} %get-tuple-element.131), channel_id=1, source_target_pairs={{0,1},{1,0},{2,3},{3,2},{4,5},{5,4},{6,7},{7,6},{8,9},{9,8},{10,11... | collective-permute-start | bytes 2211848 | tf_op jit(solution)/shard_map/ppermute | solution.py:968
  232.9 16.0 %collective-permute-start.41 = (bf16[392,768]{1,0:T(8,128)(2,1)}, bf16[392,768]{1,0:T(8,128)(2,1)}, u32[]{:S(2)}, u32[]{:S(2)}) collective-permute-start(bf16[392,768]{1,0:T(8,128)(2,1)} %get-tuple-element.137), channel_id=1, source_target_pairs={{0,4},{2,6},{4,0},{6,2},{8,12},{10,14},{12,8},{14,10},{16,20},{18,... | collective-permute-start | bytes 1806344 | tf_op jit(solution)/shard_map/ppermute | solution.py:964
  233.8 16.7 %collective-permute-start.42 = (bf16[416,768]{1,0:T(8,128)(2,1)S(1)}, bf16[416,768]{1,0:T(8,128)(2,1)S(1)}, u32[]{:S(2)}, u32[]{:S(2)}) collective-permute-start(bf16[416,768]{1,0:T(8,128)(2,1)S(1)} %pad_maximum_fusion), channel_id=1, source_target_pairs={{0,8},{2,10},{4,12},{6,14},{8,0},{10,2},{12,4},{14,6},{16,24},{18,... | collective-permute-start | bytes 1916936 | tf_op jit(solution)/shard_map/ppermute | solution.py:972
  252.0 15.7 %collective-permute-start.43 = (bf16[392,768]{1,0:T(8,128)(2,1)S(1)}, bf16[392,768]{1,0:T(8,128)(2,1)S(1)}, u32[]{:S(2)}, u32[]{:S(2)}) collective-permute-start(bf16[392,768]{1,0:T(8,128)(2,1)S(1)} %add_convert_fusion.4), channel_id=1, source_target_pairs={{24,16},{26,18},{28,20},{30,22},{8,0},{10,2},{12,4},{14,6},{25,17}... | collective-permute-start | bytes 1806344 | tf_op jit(solution)/shard_map/ppermute | solution.py:972
  255.7 15.1 %collective-permute-start.44 = (bf16[416,768]{1,0:T(8,128)(2,1)S(1)}, bf16[416,768]{1,0:T(8,128)(2,1)S(1)}, u32[]{:S(2)}, u32[]{:S(2)}) collective-permute-start(bf16[416,768]{1,0:T(8,128)(2,1)S(1)} %pad_maximum_fusion.1), channel_id=1, source_target_pairs={{0,4},{2,6},{4,0},{6,2},{8,12},{10,14},{12,8},{14,10},{16,20},{18,... | collective-permute-start | bytes 1916936 | tf_op jit(solution)/shard_map/ppermute | solution.py:964
  256.1 15.4 %collective-permute-start.45 = (bf16[192,768]{1,0:T(8,128)(2,1)S(1)}, bf16[192,768]{1,0:T(8,128)(2,1)S(1)}, u32[]{:S(2)}, u32[]{:S(2)}) collective-permute-start(bf16[192,768]{1,0:T(8,128)(2,1)S(1)} %slice.71), channel_id=1, source_target_pairs={{0,16},{2,18},{4,20},{6,22},{8,24},{10,26},{12,28},{14,30},{1,17},... | collective-permute-start | bytes 884744 | tf_op jit(solution)/shard_map/ppermute | solution.py:972
  271.5 17.4 %collective-permute-start.47 = (bf16[392,768]{1,0:T(8,128)(2,1)S(1)}, bf16[392,768]{1,0:T(8,128)(2,1)S(1)}, u32[]{:S(2)}, u32[]{:S(2)}) collective-permute-start(bf16[392,768]{1,0:T(8,128)(2,1)S(1)} %add_convert_fusion.1), channel_id=1, source_target_pairs={{24,16},{26,18},{28,20},{30,22},{0,8},{2,10},{4,12},{6,14},{25,17}... | collective-permute-start | bytes 1806344 | tf_op jit(solution)/shard_map/ppermute | solution.py:972
  272.8 16.3 %collective-permute-start.46 = (bf16[392,768]{1,0:T(8,128)(2,1)S(1)}, bf16[392,768]{1,0:T(8,128)(2,1)S(1)}, u32[]{:S(2)}, u32[]{:S(2)}) collective-permute-start(bf16[392,768]{1,0:T(8,128)(2,1)S(1)} %add_convert_fusion.2), channel_id=1, source_target_pairs={{16,0},{18,2},{20,4},{22,6},{17,1},{19,3},{21,5},{23,7}} | collective-permute-start | bytes 1806344 | tf_op jit(solution)/shard_map/ppermute | solution.py:972
  289.1 21.1 %collective-permute-start.49 = (bf16[392,768]{1,0:T(8,128)(2,1)S(1)}, bf16[392,768]{1,0:T(8,128)(2,1)}, u32[]{:S(2)}, u32[]{:S(2)}) collective-permute-start(bf16[392,768]{1,0:T(8,128)(2,1)S(1)} %add_convert_fusion), channel_id=1, source_target_pairs={{16,8},{18,10},{20,12},{22,14},{17,9},{19,11},{21,13},{23,15}} | collective-permute-start | bytes 1806344 | tf_op jit(solution)/shard_map/ppermute | solution.py:972
  291.2 17.3 %collective-permute-start.48 = (bf16[224,768]{1,0:T(8,128)(2,1)}, bf16[224,768]{1,0:T(8,128)(2,1)}, u32[]{:S(2)}, u32[]{:S(2)}) collective-permute-start(bf16[224,768]{1,0:T(8,128)(2,1)} %pad_maximum_fusion.2), channel_id=1, source_target_pairs={{0,16},{2,18},{4,20},{6,22},{8,24},{10,26},{12,28},{14,30},{1,17},... | collective-permute-start | bytes 1032200 | tf_op jit(solution)/shard_map/ppermute | solution.py:972
  (44 other events, 1233.9 us)

commit v3 on v2

--- a/solution.py
+++ b/solution.py
@@ -1053,38 +1053,48 @@
     return merge(far_send_kernel, flags, sources, [(2, kept.shape[-2])], "far_send")[0]
 
 
-def core_merge_kernel(flags, *refs):
-    ins, outs = refs[:14], refs[14:]
-    for number in range(2):
-        first, second, third = ins[3 * number : 3 * number + 3]
-        outs[number][...] = (first[...].astype(F32) + second[...].astype(F32) + third[...].astype(F32)).astype(BF16)
-    outs[2][...] = add(ins[6][...], ins[7][...])
-    outs[3][...] = add(ins[8][...], ins[9][...])
-    message = outs[4]
-    block = ins[10].shape[0]
-    message[:block, :] = add(ins[10][...], ins[11][...])
+def cross_merge_kernel(flags, *refs):
+    ins, outs = refs[:8], refs[8:]
+    outs[0][...] = add(ins[0][...], ins[1][...])
+    outs[1][...] = add(ins[2][...], ins[3][...])
+    message = outs[2]
+    block = ins[4].shape[0]
+    message[:block, :] = add(ins[4][...], ins[5][...])
     spill = message.shape[0] - (block + 8)
-    total = ins[12][...].astype(F32) + ins[13][...].astype(F32)
+    total = ins[6][...].astype(F32) + ins[7][...].astype(F32)
     message[block:, :] = jnp.concatenate([jnp.zeros((8, total.shape[1]), F32), total[block - spill :]]).astype(BF16)
 
 
-def core_merge(flags, far, far_came, far_last, cross, cross_came):
-    far, far_came, cross, cross_came = [blocks_of(v) for v in (far, far_came, cross, cross_came)]
+def cross_merge(flags, cross, cross_came):
+    cross, cross_came = blocks_of(cross), blocks_of(cross_came)
     block = cross.shape[-2]
     spill = 2 * block - (D - QUERY_HEAD)
-    sources = []
-    for r in (lambda f: 1 - f[3] % 2, lambda f: f[3] % 2):
-        sources += [(part, lambda f, r=r: (r(f), f[2], f[1])) for part in (far, far_came)]
-        sources += [(far_last, lambda f, r=r: (r(f),))]
     chosen = [
         lambda f: (0, f[1]),
         lambda f: (1, f[1]),
         lambda f: (1 - f[0], 1 - f[1]),
         lambda f: (0, 1 - f[1]),
     ]
+    sources = []
     for where in chosen:
         sources += [(cross, where), (cross_came, where)]
-    return merge(core_merge_kernel, flags, sources, [(block,)] * 4 + [(block + 8 + spill,)], "core_merge")
+    return merge(cross_merge_kernel, flags, sources, [(block,)] * 2 + [(block + 8 + spill,)], "cross_merge")
+
+
+def far_merge_kernel(flags, *refs):
+    ins, outs = refs[:6], refs[6:]
+    for number in range(2):
+        first, second, third = ins[3 * number : 3 * number + 3]
+        outs[number][...] = (first[...].astype(F32) + second[...].astype(F32) + third[...].astype(F32)).astype(BF16)
+
+
+def far_merge(flags, far, far_came, far_last):
+    far, far_came = blocks_of(far), blocks_of(far_came)
+    sources = []
+    for r in (lambda f: 1 - f[3] % 2, lambda f: f[3] % 2):
+        sources += [(part, lambda f, r=r: (r(f), f[2], f[1])) for part in (far, far_came)]
+        sources += [(far_last, lambda f, r=r: (r(f),))]
+    return merge(far_merge_kernel, flags, sources, [(far.shape[-2],)] * 2, "far_merge")
 
 
 def cross_second(at, mine, came):
@@ -1116,35 +1126,36 @@
 def finish(at, flags, block, far, far_last, near, near_send, cross, cross_came, vec_rows, extra):
     near_came = over_core(near_send)
     vec_came = over_core(vec_rows)
-    far_out, far, low, high, message = core_merge(flags, *far, far_last, cross, cross_came)
-    near_came, message, far_out, low, high, far = tie(near_came, message, far_out, low, high, far)
+    low, high, message = cross_merge(flags, cross, cross_came)
+    near_came, message, low, high = tie(near_came, message, low, high)
     came = over_x(message)
     near, near_came = blocks_of(near), blocks_of(near_came)
     near_send = add(picked(near, 1 - at.y, at.x), picked(near_came, 1 - at.y, at.x))
     near = add(picked(near, at.y, at.x), picked(near_came, at.y, at.x))
     vec_rows = vec_rows + vec_came
-    near_send, near, vec_rows, dk, dv, w = tie(near_send, near, vec_rows, *extra)
-    near_came, far_came = over_y(near_send), over_z(with_rows(far_out, vec_rows), SWAP_ONE)
+    near_send, near, dk, dv, w, far_last = tie(near_send, near, *extra, far_last)
+    far_out, far = far_merge(flags, *far, far_last)
+    near_came, far_came, vec_came = over_y(near_send), over_z(far_out, SWAP_ONE), over_y(vec_rows)
     gm = memory_grads(dk, dv, w)
     gm, came = tie(gm, came)
     send, cross = cross_second(at, (low, high), came)
-    send, near_came, far_came, cross = tie(send, near_came, far_came, cross)
+    send, near_came, vec_came, cross = tie(send, near_came, vec_came, cross)
 
     near = add(near, near_came)
-    far = add(far, far_came[:block])
-    vec_rows = vec_rows + far_came[block:].astype(F32)
-    near, far, vec_rows, send = tie(near, far, vec_rows, send)
-    cross_came, near_came = over_y(with_rows(send, vec_rows)), over_z(near, [(3, 2), (1, 0)])
+    vec_rows = vec_rows + vec_came
+    near, vec_rows, send = tie(near, vec_rows, send)
+    cross_came, near_came, vec_came = over_y(send), over_z(near, [(3, 2), (1, 0)]), over_z(vec_rows, SWAP_ONE)
+    cross = add(cross, cross_came)
+    near = add(near, near_came)
+    far = add(far, far_came)
+    vec_rows = vec_rows + vec_came
+    near, cross, vec_rows, far = tie(near, cross, vec_rows, far)
+
     cut = block // 16 * 8
+    cross_came, near_came = over_z(cross, [(3, 2), (0, 1)]), over_z(near, [(2, 0)])
     far_top = over_z(far[:cut], [(0, 2), (1, 3)])
-    cross = add(cross, cross_came[:block])
-    near = add(near, near_came)
-    vec_rows = vec_rows + cross_came[block:].astype(F32)
-    near, cross, vec_rows, far_top, far = tie(near, cross, vec_rows, far_top, far)
-
-    cross_came, near_came = over_z(cross, [(3, 2), (0, 1)]), over_z(near, [(2, 0)])
     cross = add(cross, cross_came)
-    near_came, cross, far, vec_rows = tie(near_came, cross, far, vec_rows)
+    near_came, cross, far, vec_rows, far_top = tie(near_came, cross, far, vec_rows, far_top)
 
     cross_came, far_low = over_z(cross, [(2, 1)]), over_z(with_rows(far[cut:], vec_rows), [(0, 2), (1, 3)])
     far_came = jnp.concatenate([far_top, far_low[: block - cut]])

time: 319 us -> 314 us (0.984)
  waiting for transfers between devices: 137 us -> 129 us
    ppermute x12 -> x13, waiting for transfers between devices: 50.8 us -> 47 us  [over_z(): lax.ppermute(v, 'dp', [(4 * a + i, 4 * b + i) for a, b in hops for i in r...]
    ppermute x8 -> x9, waiting for transfers between devices: 42.9 us -> 39.6 us  [over_y(): return lax.ppermute(v, 'dp', [(i, i ^ 2) for i in range(16)])]
    pallas_call x2 -> x3, Pallas kernels: 9.63 us -> 11.6 us  [merge(): pl.pallas_call(body, grid_spec=pltpu.PrefetchScalarGridSpec(num_scalar_pr...]
    ppermute x8 -> x9, starting transfers between devices: 7.09 us -> 8.38 us  [over_y(): return lax.ppermute(v, 'dp', [(i, i ^ 2) for i in range(16)])]
    ppermute x12 -> x13, starting transfers between devices: 26.9 us -> 27.9 us  [over_z(): lax.ppermute(v, 'dp', [(4 * a + i, 4 * b + i) for a, b in hops for i in r...]
  transfers between devices with their start and end apart: 50 -> 52, of which waited for: 27 -> 24; matrix products, arithmetic and copies ran while one was open for 4% -> 4% of each run, Pallas kernels for 17% -> 18%
where the time goes in v3:
time: 314 us; the launch traced here: 308 us
  waiting for transfers between devices  129 us (41%)
  Pallas kernels  105 us (33%)
  starting transfers between devices  50.4 us (16%)
  other arithmetic  12.4 us (4%)
  local copies, waits for them, and re-layouts  10.3 us (3%)
    ppermute x13, waiting for transfers between devices, over_z(): lax.ppermute(v, 'dp', [(4 * a + i, 4 * b + i) for a, b in hops for i in r...  47 us
    ppermute x9, waiting for transfers between devices, over_y(): return lax.ppermute(v, 'dp', [(i, i ^ 2) for i in range(16)])  39.6 us
    ppermute x10, waiting for transfers between devices, over_x(): return lax.ppermute(v, 'seq', [(0, 1), (1, 0)])  37.1 us
    ppermute x13, starting transfers between devices, over_z(): lax.ppermute(v, 'dp', [(4 * a + i, 4 * b + i) for a, b in hops for i in r...  27.9 us
    pallas_call x1, Pallas kernels, middle(): pl.pallas_call(partial(middle_kernel, parts, split), grid_spec=pltpu.Pref...  26.3 us
    pallas_call x1, Pallas kernels, forward(): pl.pallas_call(partial(forward_kernel, queries, custom), grid_spec=pltpu....  19.1 us
    pallas_call x1, Pallas kernels, self_backward(): pl.pallas_call(partial(self_backward_kernel, queries, split), grid_spec=p...  13.4 us
    ppermute x10, starting transfers between devices, over_x(): return lax.ppermute(v, 'seq', [(0, 1), (1, 0)])  11.6 us
  transfers between devices with their start and end apart: 52, of which 24 were waited for; matrix products, arithmetic and copies ran while one was open for 4% of the time, Pallas kernels for 18%

profile of v3, /device:TPU:8, one launch (start us, length us, event | category | flops | bytes accessed | tf_op | source)
XLA Modules:
  0.0 307.8 jit_solution(18394224599625706696)
XLA Ops:
  2.9 1.6 collective-permute-start.1
  4.9 1.5 collective-permute-start
  6.4 2.6 collective-permute-start.7
  9.0 9.5 %collective-permute-done.1.refs_2_ = bf16[400,768]{1,0:T(8,128)(2,1)S(1)} collective-permute-done((bf16[400,768]{1,0:T(8,128)(2,1)S(1)}, bf16[400,768]{1,0:T(8,128)(2,1)S(1)}, u32[]{:S(2)}, u32[]{:S(2)}) %collective-permute-start.1) | collective-permute-done | bytes 614432 | tf_op jit(solution)/shard_map/ppermute | solution.py:964
  18.6 1.5 collective-permute-start.3
  20.1 9.6 %collective-permute-done.2.refs_3_ = bf16[400,768]{1,0:T(8,128)(2,1)S(1)} collective-permute-done((bf16[400,768]{1,0:T(8,128)(2,1)S(1)}, bf16[400,768]{1,0:T(8,128)(2,1)S(1)}, u32[]{:S(2)}, u32[]{:S(2)}) %collective-permute-start.2) | collective-permute-done | bytes 614432 | tf_op jit(solution)/shard_map/ppermute | solution.py:972
  30.0 2.5 collective-permute-start.5
  32.5 2.7 collective-permute-done.7.refs_8_
  36.6 1.4 collective-permute-start.10
  38.0 8.4 %collective-permute-done.4.refs_5_ = bf16[400,768]{1,0:T(8,128)(2,1)S(1)} collective-permute-done((bf16[400,768]{1,0:T(8,128)(2,1)S(1)}, bf16[400,768]{1,0:T(8,128)(2,1)S(1)}, u32[]{:S(2)}, u32[]{:S(2)}) %collective-permute-start.4) | collective-permute-done | bytes 614432 | tf_op jit(solution)/shard_map/ppermute | solution.py:964
  48.4 8.7 %collective-permute-done.9.refs_10_ = bf16[400,768]{1,0:T(8,128)(2,1)S(1)} collective-permute-done((bf16[400,768]{1,0:T(8,128)(2,1)S(1)}, bf16[400,768]{1,0:T(8,128)(2,1)S(1)}, u32[]{:S(2)}, u32[]{:S(2)}) %collective-permute-start.9) | collective-permute-done | bytes 614432 | tf_op jit(solution)/shard_map/ppermute | solution.py:964
  57.2 2.2 collective-permute-done.10.refs_11_
  59.3 1.5 collective-permute-start.6
  62.3 2.5 collective-permute-start.13
  64.9 11.4 %collective-permute-done.6.refs_7_ = bf16[400,768]{1,0:T(8,128)(2,1)} collective-permute-done((bf16[400,768]{1,0:T(8,128)(2,1)S(1)}, bf16[400,768]{1,0:T(8,128)(2,1)}, u32[]{:S(2)}, u32[]{:S(2)}) %collective-permute-start.6) | collective-permute-done | bytes 614432 | tf_op jit(solution)/shard_map/ppermute | solution.py:968
  76.2 11.2 %collective-permute-done.11.refs_12_ = bf16[400,768]{1,0:T(8,128)(2,1)} collective-permute-done((bf16[400,768]{1,0:T(8,128)(2,1)S(1)}, bf16[400,768]{1,0:T(8,128)(2,1)}, u32[]{:S(2)}, u32[]{:S(2)}) %collective-permute-start.11) | collective-permute-done | bytes 614432 | tf_op jit(solution)/shard_map/ppermute | solution.py:968
  91.4 1.6 collective-permute-done.26.refs_27_
  93.1 11.6 %collective-permute-done.14.refs_15_ = bf16[400,768]{1,0:T(8,128)(2,1)} collective-permute-done((bf16[400,768]{1,0:T(8,128)(2,1)}, bf16[400,768]{1,0:T(8,128)(2,1)}, u32[]{:S(2)}, u32[]{:S(2)}) %collective-permute-start.14) | collective-permute-done | bytes 614432 | tf_op jit(solution)/shard_map/ppermute | solution.py:964
  107.3 19.1 %forward.1 = (bf16[336,768]{1,0:T(8,128)(2,1)}, bf16[336,768]{1,0:T(8,128)(2,1)}, bf16[336,768]{1,0:T(8,128)(2,1)}, bf16[336,768]{1,0:T(8,128)(2,1)}, f32[336,76...) custom-call(s32[3]{0:T(128)} %broadcast_subtract_fusion.left_ref, ...), custom_call_target="tpu_custom_call" | custom-call | tf_op jit(solution)/shard_map/forward/pallas_call | solution.py:312
  126.5 1.8 collective-permute-start.31
  129.1 1.4 slice_convert_fusion.refs_7_
  130.5 10.9 %collective-permute-done.32.refs_5_ = f32[3,8,224]{2,1,0:T(8,128)S(1)} collective-permute-done((f32[3,8,224]{2,1,0:T(8,128)}, f32[3,8,224]{2,1,0:T(8,128)S(1)}, u32[]{:S(2)}, u32[]{:S(2)}) %collective-permute-start.32) | collective-permute-done | bytes 21536 | tf_op jit(solution)/shard_map/ppermute | solution.py:968
  142.2 26.3 %middle.1 = (f32[3,112,768]{2,1,0:T(8,128)}, bf16[2,2,784,768]{3,2,1,0:T(8,128)(2,1)}, bf16[2,2,784,768]{3,2,1,0:T(8,128)(2,1)}, bf16[2,784,768]{2,1,0:T(8,128)(...) custom-call(s32[4]{0:T(128)} %pad_add_fusion.flags.refs_0_, ...), custom_call_target="tpu_custom_call" | custom-call | flops 10701766 | bytes 28311 | tf_op jit(solution)/shard_map/middle/pallas_call | solution.py:603
  168.7 10.0 %cross_backward.1 = (bf16[3,112,768]{2,1,0:T(8,128)(2,1)}, bf16[3,512,768]{2,1,0:T(8,128)(2,1)}, bf16[3,512,768]{2,1,0:T(8,128)(2,1)}) custom-call(s32[3]{0:T(128)} %broadcast_subtract_fusion.left_ref, bf16[3,112,768]{2,1,0:T(8,128)(2,1)} %bitcast.42, bf16[3,512,768]{2,1,0:T(8,128)(2,1)} %get-tuple-element.87.k_ref, ...), custom_call_target="tpu_custom_call" | custom-call | flops 352321 | bytes 9437 | tf_op jit(solution)/shard_map/cross_backward/pallas_call | solution.py:684
  178.7 3.8 %far_send.1 = bf16[2,392,768]{2,1,0:T(8,128)(2,1)} custom-call(s32[4]{0:T(128)} %pad_add_fusion.flags.refs_0_, bf16[2,2,2,392,768]{4,3,2,1,0:T(8,128)(2,1)} %bitcast.30, bf16[2,2,2,392,768]{4,3,2,1,0:T(8,128)(2,1)} %bitcast.11.b.d.refs_1_.refs_4_, bf16[2,2,2,392,768]{4,3,2,1,0:T(8,128)(2,1)} %bitcast.31, bf16[2,2,2,392,768]{4,3,2,1,0:T(8,128)(2,1)} %bitcast.11.b.d.refs_1_.refs_4_), custom_call_target="tpu_custom_call" | custom-call | tf_op jit(solution)/shard_map/far_send/pallas_call | solution.py:1026
  182.5 1.4 collective-permute-start.36
  183.9 1.6 collective-permute-start.34
  185.5 9.3 %memory_weights.1 = (f32[8,768]{1,0:T(8,128)}, bf16[2,784,768]{2,1,0:T(8,128)(2,1)}, bf16[2,784,768]{2,1,0:T(8,128)(2,1)}) custom-call(s32[4]{0:T(128)} %pad_add_fusion.flags.refs_0_, bf16[2,784,768]{2,1,0:T(8,128)(2,1)} %get-tuple-element.84.refs_0_, bf16[2,784,768]{2,1,0:T(8,128)(2,1)} %get-tuple-element.85.refs_1_, ...), custom_call_target="tpu_custom_call", output_to_operand_aliasing={{1}: (1, {}), {2}: (2, {})} | custom-call | flops 3623878 | bytes 7077 | tf_op jit(solution)/shard_map/memory_weights/pallas_call | solution.py:728
  195.3 2.5 collective-permute-done.34
  198.6 6.7 %query_backward.1 = (f32[336,768]{1,0:T(8,128)}, bf16[64,768]{1,0:T(8,128)(2,1)}, f32[24,768]{1,0:T(8,128)}, bf16[2,784,768]{2,1,0:T(8,128)(2,1)}, bf16[2,784,768]{2,1,0:T(8,128)(2,1)}) custom-call(s32[4]{0:T(128)} %pad_add_fusion.flags.refs_0_, bf16[2,784,768]{2,1,0:T(8,128)(2,1)} %get-tuple-element.96.refs_0_, ...), custom_call_target="tpu_custom_call", output_to_operand_aliasing={{3}: (1, {}), {4}: (2, {})} | custom-call | flops 792723 | bytes 4128 | tf_op jit(solution)/shard_map/query_backward/pallas_call | solution.py:827
  205.4 13.4 %self_backward.1 = (f32[3,112,768]{2,1,0:T(8,128)}, f32[24,768]{1,0:T(8,128)}, bf16[2,784,768]{2,1,0:T(8,128)(2,1)}, bf16[2,784,768]{2,1,0:T(8,128)(2,1)}) custom-call(s32[4]{0:T(128)} %pad_add_fusion.flags.refs_0_, bf16[336,768]{1,0:T(8,128)(2,1)} %get-tuple-element.83.refs_1_, f32[336,768]{1,0:T(8,128)} %get-tuple-element.100.refs_2_, ...), custom_call_target="tpu_custom_call" | custom-call | flops 6341787 | bytes 9437 | tf_op jit(solution)/shard_map/self_backward/pallas_call | solution.py:921
  219.4 1.5 copy-done
  220.9 4.2 %cross_merge.1 = (bf16[392,768]{1,0:T(8,128)(2,1)}, bf16[392,768]{1,0:T(8,128)(2,1)}, bf16[480,768]{1,0:T(8,128)(2,1)}) custom-call(s32[4]{0:T(128)} %pad_add_fusion.flags.refs_0_, bf16[2,2,392,768]{3,2,1,0:T(8,128)(2,1)} %bitcast.26, bf16[2,2,392,768]{3,2,1,0:T(8,128)(2,1)} %bitcast.34, bf16[2,2,392,768]{3,2,1,0:T(8,128)(2,1)} %bitcast.27, ...), custom_call_target="tpu_custom_call" | custom-call | tf_op jit(solution)/shard_map/cross_merge/pallas_call | solution.py:1026
  225.1 1.9 collective-permute-start.39
  229.2 2.7 fusion.8
  233.2 3.6 %far_merge.1 = (bf16[392,768]{1,0:T(8,128)(2,1)}, bf16[392,768]{1,0:T(8,128)(2,1)}) custom-call(s32[4]{0:T(128)} %pad_add_fusion.flags.refs_0_, bf16[2,2,2,392,768]{4,3,2,1,0:T(8,128)(2,1)} %bitcast.32, bf16[2,2,2,392,768]{4,3,2,1,0:T(8,128)(2,1)} %bitcast.11.b.d.refs_1_.refs_4_, bf16[2,392,768]{2,1,0:T(8,128)(2,1)} %collective-permute-done.36.refs_2_.refs_5_, ...), custom_call_target="tpu_custom_call" | custom-call | tf_op jit(solution)/shard_map/far_merge/pallas_call | solution.py:1026
  236.8 1.4 collective-permute-start.46
  238.3 8.0 %memory_grads.1 = f32[3,512,768]{2,1,0:T(8,128)} custom-call(bf16[3,512,768]{2,1,0:T(8,128)(2,1)} %get-tuple-element.119.refs_3_.dk_ref, bf16[3,512,768]{2,1,0:T(8,128)(2,1)} %get-tuple-element.120.refs_4_.dv_ref, bf16[12544,768]{1,0:T(8,128)(2,1)} %get-tuple-element.121.refs_6_.refs_7_.ck.cv, bf16[12544,768]{1,0:T(8,128)(2,1)} %get-tuple-element.121.refs_6_.refs_7_.ck.cv), custom_call_target="tpu_custom_call" | custom-call | flops 3623878656 | bytes 9437184 | tf_op jit(solution)/shard_map/memory_grads/pallas_call | solution.py:755
  247.7 1.2 add_convert_fusion.4
  248.9 4.2 %collective-permute-start.43 = (bf16[392,768]{1,0:T(8,128)(2,1)S(1)}, bf16[392,768]{1,0:T(8,128)(2,1)S(1)}, u32[]{:S(2)}, u32[]{:S(2)}) collective-permute-start(bf16[392,768]{1,0:T(8,128)(2,1)S(1)} %add_convert_fusion.4), channel_id=1, source_target_pairs={{24,16},{26,18},{28,20},{30,22},{8,0},{10,2},{12,4},{14,6},{25,17}... | collective-permute-start | bytes 1806344 | tf_op jit(solution)/shard_map/ppermute | solution.py:972
  253.7 12.9 %collective-permute-done.45 = f32[24,768]{1,0:T(8,128)S(1)} collective-permute-done((f32[24,768]{1,0:T(8,128)S(1)}, f32[24,768]{1,0:T(8,128)S(1)}, u32[]{:S(2)}, u32[]{:S(2)}) %collective-permute-start.45) | collective-permute-done | bytes 73760 | tf_op jit(solution)/shard_map/ppermute | solution.py:972
  267.5 1.3 collective-permute-start.48
  269.6 6.6 %collective-permute-start.49 = (bf16[192,768]{1,0:T(8,128)(2,1)S(1)}, bf16[192,768]{1,0:T(8,128)(2,1)S(1)}, u32[]{:S(2)}, u32[]{:S(2)}) collective-permute-start(bf16[192,768]{1,0:T(8,128)(2,1)S(1)} %slice.55), channel_id=1, source_target_pairs={{0,16},{2,18},{4,20},{6,22},{8,24},{10,26},{12,28},{14,30},{1,17},... | collective-permute-start | bytes 884744 | tf_op jit(solution)/shard_map/ppermute | solution.py:972
  276.2 9.7 %collective-permute-done.48 = bf16[392,768]{1,0:T(8,128)(2,1)S(1)} collective-permute-done((bf16[392,768]{1,0:T(8,128)(2,1)S(1)}, bf16[392,768]{1,0:T(8,128)(2,1)S(1)}, u32[]{:S(2)}, u32[]{:S(2)}) %collective-permute-start.48) | collective-permute-done | bytes 602144 | tf_op jit(solution)/shard_map/ppermute | solution.py:972
  286.1 1.3 collective-permute-start.51
  288.2 3.0 collective-permute-start.50
  293.9 9.1 %collective-permute-done.50 = bf16[224,768]{1,0:T(8,128)(2,1)} collective-permute-done((bf16[224,768]{1,0:T(8,128)(2,1)}, bf16[224,768]{1,0:T(8,128)(2,1)}, u32[]{:S(2)}, u32[]{:S(2)}) %collective-permute-start.50) | collective-permute-done | bytes 344096 | tf_op jit(solution)/shard_map/ppermute | solution.py:972
  304.7 1.6 convert_add_fusion
  (189 shorter events, 31.8 us)
Async XLA Ops:
  2.9 15.7 %collective-permute-start.1 = (bf16[400,768]{1,0:T(8,128)(2,1)S(1)}, bf16[400,768]{1,0:T(8,128)(2,1)S(1)}, u32[]{:S(2)}, u32[]{:S(2)}) collective-permute-start(bf16[400,768]{1,0:T(8,128)(2,1)S(1)} %maximum_select_fusion.1.refs_0_), channel_id=1, source_target_pairs={{0,4},{2,6},{4,0},{6,2},{8,12},{10,14},{12,8},{14,10},{16,20},{18,... | collective-permute-start | bytes 1843208 | tf_op jit(solution)/shard_map/ppermute | solution.py:964
  4.5 25.1 %collective-permute-start.2 = (bf16[400,768]{1,0:T(8,128)(2,1)S(1)}, bf16[400,768]{1,0:T(8,128)(2,1)S(1)}, u32[]{:S(2)}, u32[]{:S(2)}) collective-permute-start(bf16[400,768]{1,0:T(8,128)(2,1)S(1)} %maximum_select_fusion.1.refs_0_), channel_id=1, source_target_pairs={{0,8},{2,10},{4,12},{6,14},{8,0},{10,2},{12,4},{14,6},{16,24},{18,... | collective-permute-start | bytes 1843208 | tf_op jit(solution)/shard_map/ppermute | solution.py:972
  4.9 25.0 %collective-permute-start = (bf16[400,768]{1,0:T(8,128)(2,1)S(1)}, bf16[400,768]{1,0:T(8,128)(2,1)S(1)}, u32[]{:S(2)}, u32[]{:S(2)}) collective-permute-start(bf16[400,768]{1,0:T(8,128)(2,1)S(1)} %maximum_select_fusion.1.refs_0_), channel_id=1, source_target_pairs={{0,1},{1,0},{2,3},{3,2},{4,5},{5,4},{6,7},{7,6},{8,9},{9,8},{10,11... | collective-permute-start | bytes 1843208 | tf_op jit(solution)/shard_map/ppermute | solution.py:968
  6.4 28.7 %collective-permute-start.7 = (bf16[400,768]{1,0:T(8,128)(2,1)S(1)}, bf16[400,768]{1,0:T(8,128)(2,1)S(1)}, u32[]{:S(2)}, u32[]{:S(2)}) collective-permute-start(bf16[400,768]{1,0:T(8,128)(2,1)S(1)} %maximum_select_fusion.1.refs_0_), channel_id=1, source_target_pairs={{0,16},{2,18},{4,20},{6,22},{16,0},{18,2},{20,4},{22,6},{8,24},{10... | collective-permute-start | bytes 1843208 | tf_op jit(solution)/shard_map/ppermute | solution.py:972
  9.0 26.7 %collective-permute-start.15 = (bf16[400,768]{1,0:T(8,128)(2,1)S(1)}, bf16[400,768]{1,0:T(8,128)(2,1)S(1)}, u32[]{:S(2)}, u32[]{:S(2)}) collective-permute-start(bf16[400,768]{1,0:T(8,128)(2,1)S(1)} %maximum_select_fusion.1.refs_0_), channel_id=1, source_target_pairs={{0,2},{2,0},{4,6},{6,4},{8,10},{10,8},{12,14},{14,12},{16,18},{18,... | collective-permute-start | bytes 1843208 | tf_op jit(solution)/shard_map/ppermute | solution.py:960
  18.6 18.0 %collective-permute-start.3 = (bf16[400,768]{1,0:T(8,128)(2,1)S(1)}, bf16[400,768]{1,0:T(8,128)(2,1)S(1)}, u32[]{:S(2)}, u32[]{:S(2)}) collective-permute-start(bf16[400,768]{1,0:T(8,128)(2,1)S(1)} %collective-permute-done.1.refs_2_), channel_id=1, source_target_pairs={{0,1},{1,0},{2,3},{3,2},{4,5},{5,4},{6,7},{7,6},{8,9},{9,8},{10,11... | collective-permute-start | bytes 1843208 | tf_op jit(solution)/shard_map/ppermute | solution.py:968
  29.6 16.8 %collective-permute-start.4 = (bf16[400,768]{1,0:T(8,128)(2,1)S(1)}, bf16[400,768]{1,0:T(8,128)(2,1)S(1)}, u32[]{:S(2)}, u32[]{:S(2)}) collective-permute-start(bf16[400,768]{1,0:T(8,128)(2,1)S(1)} %collective-permute-done.2.refs_3_), channel_id=1, source_target_pairs={{0,4},{2,6},{4,0},{6,2},{8,12},{10,14},{12,8},{14,10},{16,20},{18,... | collective-permute-start | bytes 1843208 | tf_op jit(solution)/shard_map/ppermute | solution.py:964
  30.0 17.3 %collective-permute-start.5 = (bf16[400,768]{1,0:T(8,128)(2,1)S(1)}, bf16[400,768]{1,0:T(8,128)(2,1)S(1)}, u32[]{:S(2)}, u32[]{:S(2)}) collective-permute-start(bf16[400,768]{1,0:T(8,128)(2,1)S(1)} %collective-permute-done.refs_1_), channel_id=1, source_target_pairs={{0,8},{2,10},{4,12},{6,14},{8,0},{10,2},{12,4},{14,6},{16,24},{18,... | collective-permute-start | bytes 1843208 | tf_op jit(solution)/shard_map/ppermute | solution.py:972
  35.2 13.3 %collective-permute-start.8 = (bf16[400,768]{1,0:T(8,128)(2,1)S(1)}, bf16[400,768]{1,0:T(8,128)(2,1)S(1)}, u32[]{:S(2)}, u32[]{:S(2)}) collective-permute-start(bf16[400,768]{1,0:T(8,128)(2,1)S(1)} %collective-permute-done.7.refs_8_), channel_id=1, source_target_pairs={{0,1},{1,0},{2,3},{3,2},{4,5},{5,4},{6,7},{7,6},{8,9},{9,8},{10,11... | collective-permute-start | bytes 1843208 | tf_op jit(solution)/shard_map/ppermute | solution.py:968
  35.7 21.5 %collective-permute-start.9 = (bf16[400,768]{1,0:T(8,128)(2,1)S(1)}, bf16[400,768]{1,0:T(8,128)(2,1)S(1)}, u32[]{:S(2)}, u32[]{:S(2)}) collective-permute-start(bf16[400,768]{1,0:T(8,128)(2,1)S(1)} %collective-permute-done.7.refs_8_), channel_id=1, source_target_pairs={{0,4},{2,6},{4,0},{6,2},{8,12},{10,14},{12,8},{14,10},{16,20},{18,... | collective-permute-start | bytes 1843208 | tf_op jit(solution)/shard_map/ppermute | solution.py:964
  36.6 22.8 %collective-permute-start.10 = (bf16[400,768]{1,0:T(8,128)(2,1)S(1)}, bf16[400,768]{1,0:T(8,128)(2,1)S(1)}, u32[]{:S(2)}, u32[]{:S(2)}) collective-permute-start(bf16[400,768]{1,0:T(8,128)(2,1)S(1)} %collective-permute-done.7.refs_8_), channel_id=1, source_target_pairs={{0,8},{2,10},{4,12},{6,14},{8,0},{10,2},{12,4},{14,6},{16,24},{18,... | collective-permute-start | bytes 1843208 | tf_op jit(solution)/shard_map/ppermute | solution.py:972
  46.4 14.4 %collective-permute-start.16 = (bf16[400,768]{1,0:T(8,128)(2,1)S(1)}, bf16[400,768]{1,0:T(8,128)(2,1)S(1)}, u32[]{:S(2)}, u32[]{:S(2)}) collective-permute-start(bf16[400,768]{1,0:T(8,128)(2,1)S(1)} %collective-permute-done.refs_1_), channel_id=1, source_target_pairs={{0,2},{2,0},{4,6},{6,4},{8,10},{10,8},{12,14},{14,12},{16,18},{18,... | collective-permute-start | bytes 1843208 | tf_op jit(solution)/shard_map/ppermute | solution.py:960
  47.3 14.1 %collective-permute-start.17 = (bf16[400,768]{1,0:T(8,128)(2,1)S(1)}, bf16[400,768]{1,0:T(8,128)(2,1)S(1)}, u32[]{:S(2)}, u32[]{:S(2)}) collective-permute-start(bf16[400,768]{1,0:T(8,128)(2,1)S(1)} %collective-permute-done.1.refs_2_), channel_id=1, source_target_pairs={{0,2},{2,0},{4,6},{6,4},{8,10},{10,8},{12,14},{14,12},{16,18},{18,... | collective-permute-start | bytes 1843208 | tf_op jit(solution)/shard_map/ppermute | solution.py:960
  48.4 13.9 %collective-permute-start.18 = (bf16[400,768]{1,0:T(8,128)(2,1)S(1)}, bf16[400,768]{1,0:T(8,128)(2,1)S(1)}, u32[]{:S(2)}, u32[]{:S(2)}) collective-permute-start(bf16[400,768]{1,0:T(8,128)(2,1)S(1)} %collective-permute-done.2.refs_3_), channel_id=1, source_target_pairs={{0,2},{2,0},{4,6},{6,4},{8,10},{10,8},{12,14},{14,12},{16,18},{18,... | collective-permute-start | bytes 1843208 | tf_op jit(solution)/shard_map/ppermute | solution.py:960
  57.2 7.6 %collective-permute-start.23 = (bf16[400,768]{1,0:T(8,128)(2,1)S(1)}, bf16[400,768]{1,0:T(8,128)(2,1)S(1)}, u32[]{:S(2)}, u32[]{:S(2)}) collective-permute-start(bf16[400,768]{1,0:T(8,128)(2,1)S(1)} %collective-permute-done.7.refs_8_), channel_id=1, source_target_pairs={{0,2},{2,0},{4,6},{6,4},{8,10},{10,8},{12,14},{14,12},{16,18},{18,... | collective-permute-start | bytes 1843208 | tf_op jit(solution)/shard_map/ppermute | solution.py:960
  59.3 16.9 %collective-permute-start.6 = (bf16[400,768]{1,0:T(8,128)(2,1)S(1)}, bf16[400,768]{1,0:T(8,128)(2,1)}, u32[]{:S(2)}, u32[]{:S(2)}) collective-permute-start(bf16[400,768]{1,0:T(8,128)(2,1)S(1)} %collective-permute-done.4.refs_5_), channel_id=1, source_target_pairs={{0,1},{1,0},{2,3},{3,2},{4,5},{5,4},{6,7},{7,6},{8,9},{9,8},{10,11... | collective-permute-start | bytes 1843208 | tf_op jit(solution)/shard_map/ppermute | solution.py:968
  60.8 26.6 %collective-permute-start.11 = (bf16[400,768]{1,0:T(8,128)(2,1)S(1)}, bf16[400,768]{1,0:T(8,128)(2,1)}, u32[]{:S(2)}, u32[]{:S(2)}) collective-permute-start(bf16[400,768]{1,0:T(8,128)(2,1)S(1)} %collective-permute-done.9.refs_10_), channel_id=1, source_target_pairs={{0,1},{1,0},{2,3},{3,2},{4,5},{5,4},{6,7},{7,6},{8,9},{9,8},{10,11... | collective-permute-start | bytes 1843208 | tf_op jit(solution)/shard_map/ppermute | solution.py:968
  61.4 26.1 %collective-permute-start.12 = (bf16[400,768]{1,0:T(8,128)(2,1)S(1)}, bf16[400,768]{1,0:T(8,128)(2,1)}, u32[]{:S(2)}, u32[]{:S(2)}) collective-permute-start(bf16[400,768]{1,0:T(8,128)(2,1)S(1)} %collective-permute-done.10.refs_11_), channel_id=1, source_target_pairs={{0,4},{2,6},{4,0},{6,2},{8,12},{10,14},{12,8},{14,10},{16,20},{18,... | collective-permute-start | bytes 1843208 | tf_op jit(solution)/shard_map/ppermute | solution.py:964
  62.3 25.7 %collective-permute-start.13 = (bf16[400,768]{1,0:T(8,128)(2,1)S(1)}, bf16[400,768]{1,0:T(8,128)(2,1)}, u32[]{:S(2)}, u32[]{:S(2)}) collective-permute-start(bf16[400,768]{1,0:T(8,128)(2,1)S(1)} %collective-permute-done.8.refs_9_), channel_id=1, source_target_pairs={{0,8},{2,10},{4,12},{6,14},{8,0},{10,2},{12,4},{14,6},{16,24},{18,... | collective-permute-start | bytes 1843208 | tf_op jit(solution)/shard_map/ppermute | solution.py:972
  64.8 23.2 %collective-permute-start.19 = (bf16[400,768]{1,0:T(8,128)(2,1)S(1)}, bf16[400,768]{1,0:T(8,128)(2,1)S(1)}, u32[]{:S(2)}, u32[]{:S(2)}) collective-permute-start(bf16[400,768]{1,0:T(8,128)(2,1)S(1)} %collective-permute-done.3.refs_4_), channel_id=1, source_target_pairs={{0,2},{2,0},{4,6},{6,4},{8,10},{10,8},{12,14},{14,12},{16,18},{18,... | collective-permute-start | bytes 1843208 | tf_op jit(solution)/shard_map/ppermute | solution.py:960
  76.2 12.3 %collective-permute-start.20 = (bf16[400,768]{1,0:T(8,128)(2,1)S(1)}, bf16[400,768]{1,0:T(8,128)(2,1)S(1)}, u32[]{:S(2)}, u32[]{:S(2)}) collective-permute-start(bf16[400,768]{1,0:T(8,128)(2,1)S(1)} %collective-permute-done.4.refs_5_), channel_id=1, source_target_pairs={{0,2},{2,0},{4,6},{6,4},{8,10},{10,8},{12,14},{14,12},{16,18},{18,... | collective-permute-start | bytes 1843208 | tf_op jit(solution)/shard_map/ppermute | solution.py:960
  88.0 3.3 %collective-permute-start.25 = (bf16[400,768]{1,0:T(8,128)(2,1)S(1)}, bf16[400,768]{1,0:T(8,128)(2,1)S(1)}, u32[]{:S(2)}, u32[]{:S(2)}) collective-permute-start(bf16[400,768]{1,0:T(8,128)(2,1)S(1)} %collective-permute-done.9.refs_10_), channel_id=1, source_target_pairs={{0,2},{2,0},{4,6},{6,4},{8,10},{10,8},{12,14},{14,12},{16,18},{18,... | collective-permute-start | bytes 1843208 | tf_op jit(solution)/shard_map/ppermute | solution.py:960
  88.0 5.0 %collective-permute-start.26 = (bf16[400,768]{1,0:T(8,128)(2,1)S(1)}, bf16[400,768]{1,0:T(8,128)(2,1)S(1)}, u32[]{:S(2)}, u32[]{:S(2)}) collective-permute-start(bf16[400,768]{1,0:T(8,128)(2,1)S(1)} %collective-permute-done.10.refs_11_), channel_id=1, source_target_pairs={{0,2},{2,0},{4,6},{6,4},{8,10},{10,8},{12,14},{14,12},{16,18},{18,... | collective-permute-start | bytes 1843208 | tf_op jit(solution)/shard_map/ppermute | solution.py:960
  88.5 16.2 %collective-permute-start.14 = (bf16[400,768]{1,0:T(8,128)(2,1)}, bf16[400,768]{1,0:T(8,128)(2,1)}, u32[]{:S(2)}, u32[]{:S(2)}) collective-permute-start(bf16[400,768]{1,0:T(8,128)(2,1)} %collective-permute-done.13.refs_14_), channel_id=1, source_target_pairs={{0,4},{2,6},{4,0},{6,2},{8,12},{10,14},{12,8},{14,10},{16,20},{18,... | collective-permute-start | bytes 1843208 | tf_op jit(solution)/shard_map/ppermute | solution.py:964
  89.5 17.4 %collective-permute-start.29 = (bf16[400,768]{1,0:T(8,128)(2,1)}, bf16[400,768]{1,0:T(8,128)(2,1)}, u32[]{:S(2)}, u32[]{:S(2)}) collective-permute-start(bf16[400,768]{1,0:T(8,128)(2,1)} %collective-permute-done.13.refs_14_), channel_id=1, source_target_pairs={{0,2},{2,0},{4,6},{6,4},{8,10},{10,8},{12,14},{14,12},{16,18},{18,... | collective-permute-start | bytes 1843208 | tf_op jit(solution)/shard_map/ppermute | solution.py:960
  90.4 16.5 %collective-permute-start.22 = (bf16[400,768]{1,0:T(8,128)(2,1)}, bf16[400,768]{1,0:T(8,128)(2,1)}, u32[]{:S(2)}, u32[]{:S(2)}) collective-permute-start(bf16[400,768]{1,0:T(8,128)(2,1)} %collective-permute-done.6.refs_7_), channel_id=1, source_target_pairs={{0,2},{2,0},{4,6},{6,4},{8,10},{10,8},{12,14},{14,12},{16,18},{18,... | collective-permute-start | bytes 1843208 | tf_op jit(solution)/shard_map/ppermute | solution.py:960
  91.2 15.7 %collective-permute-start.27 = (bf16[400,768]{1,0:T(8,128)(2,1)}, bf16[400,768]{1,0:T(8,128)(2,1)}, u32[]{:S(2)}, u32[]{:S(2)}) collective-permute-start(bf16[400,768]{1,0:T(8,128)(2,1)} %collective-permute-done.11.refs_12_), channel_id=1, source_target_pairs={{0,2},{2,0},{4,6},{6,4},{8,10},{10,8},{12,14},{14,12},{16,18},{18,... | collective-permute-start | bytes 1843208 | tf_op jit(solution)/shard_map/ppermute | solution.py:960
  93.0 13.9 %collective-permute-start.28 = (bf16[400,768]{1,0:T(8,128)(2,1)}, bf16[400,768]{1,0:T(8,128)(2,1)}, u32[]{:S(2)}, u32[]{:S(2)}) collective-permute-start(bf16[400,768]{1,0:T(8,128)(2,1)} %collective-permute-done.12.refs_13_), channel_id=1, source_target_pairs={{0,2},{2,0},{4,6},{6,4},{8,10},{10,8},{12,14},{14,12},{16,18},{18,... | collective-permute-start | bytes 1843208 | tf_op jit(solution)/shard_map/ppermute | solution.py:960
  126.5 15.0 %collective-permute-start.31 = (bf16[3,112,768]{2,1,0:T(8,128)(2,1)}, bf16[3,112,768]{2,1,0:T(8,128)(2,1)S(1)}, u32[]{:S(2)}, u32[]{:S(2)}) collective-permute-start(bf16[3,112,768]{2,1,0:T(8,128)(2,1)} %get-tuple-element.79.refs_2_), channel_id=1, source_target_pairs={{0,1},{1,0},{2,3},{3,2},{4,5},{5,4},{6,7},{7,6},{8,9},{9,8},{10,11... | collective-permute-start | bytes 1548296 | tf_op jit(solution)/shard_map/ppermute | solution.py:968
  128.9 12.6 %collective-permute-start.32 = (f32[3,8,224]{2,1,0:T(8,128)}, f32[3,8,224]{2,1,0:T(8,128)S(1)}, u32[]{:S(2)}, u32[]{:S(2)}) collective-permute-start(f32[3,8,224]{2,1,0:T(8,128)} %get-tuple-element.80.refs_4_), channel_id=1, source_target_pairs={{0,1},{1,0},{2,3},{3,2},{4,5},{5,4},{6,7},{7,6},{8,9},{9,8},{10,11... | collective-permute-start | bytes 64520 | tf_op jit(solution)/shard_map/ppermute | solution.py:968
  168.6 10.1 %collective-permute-start.33 = (bf16[2,2,784,768]{3,2,1,0:T(8,128)(2,1)}, bf16[2,2,784,768]{3,2,1,0:T(8,128)(2,1)}, u32[]{:S(2)}, u32[]{:S(2)}) collective-permute-start(bf16[2,2,784,768]{3,2,1,0:T(8,128)(2,1)} %get-tuple-element.93), channel_id=1, source_target_pairs={{0,2},{2,0},{4,6},{6,4},{8,10},{10,8},{12,14},{14,12},{16,18},{18,... | collective-permute-start | bytes 14450696 | tf_op jit(solution)/shard_map/ppermute | solution.py:960
  182.5 36.3 %collective-permute-start.36 = (bf16[2,392,768]{2,1,0:T(8,128)(2,1)}, bf16[2,392,768]{2,1,0:T(8,128)(2,1)}, u32[]{:S(2)}, u32[]{:S(2)}) collective-permute-start(bf16[2,392,768]{2,1,0:T(8,128)(2,1)} %far_send.1), channel_id=1, source_target_pairs={{0,4},{2,6},{4,0},{6,2},{8,12},{10,14},{12,8},{14,10},{16,20},{18,... | collective-permute-start | bytes 3612680 | tf_op jit(solution)/shard_map/ppermute | solution.py:964
  183.9 13.9 %collective-permute-start.34 = (bf16[3,112,768]{2,1,0:T(8,128)(2,1)S(1)}, bf16[3,112,768]{2,1,0:T(8,128)(2,1)S(1)}, u32[]{:S(2)}, u32[]{:S(2)}) collective-permute-start(bf16[3,112,768]{2,1,0:T(8,128)(2,1)S(1)} %copy-done.29), channel_id=1, source_target_pairs={{0,1},{1,0},{2,3},{3,2},{4,5},{5,4},{6,7},{7,6},{8,9},{9,8},{10,11... | collective-permute-start | bytes 1548296 | tf_op jit(solution)/shard_map/ppermute | solution.py:968
  194.8 10.6 %collective-permute-start.35 = (f32[8,768]{1,0:T(8,128)}, f32[8,768]{1,0:T(8,128)S(1)}, u32[]{:S(2)}, u32[]{:S(2)}) collective-permute-start(f32[8,768]{1,0:T(8,128)} %get-tuple-element.105), channel_id=1, source_target_pairs={{0,1},{1,0},{2,3},{3,2},{4,5},{5,4},{6,7},{7,6},{8,9},{9,8},{10,11... | collective-permute-start | bytes 73736 | tf_op jit(solution)/shard_map/ppermute | solution.py:968
  205.3 14.1 %collective-permute-start.38 = (bf16[2,784,768]{2,1,0:T(8,128)(2,1)}, bf16[2,784,768]{2,1,0:T(8,128)(2,1)S(1)}, u32[]{:S(2)}, u32[]{:S(2)}) collective-permute-start(bf16[2,784,768]{2,1,0:T(8,128)(2,1)} %get-tuple-element.113), channel_id=1, source_target_pairs={{0,2},{2,0},{4,6},{6,4},{8,10},{10,8},{12,14},{14,12},{16,18},{18,... | collective-permute-start | bytes 7225352 | tf_op jit(solution)/shard_map/ppermute | solution.py:960
  218.8 6.3 %collective-permute-start.37 = (bf16[2,784,768]{2,1,0:T(8,128)(2,1)}, bf16[2,784,768]{2,1,0:T(8,128)(2,1)}, u32[]{:S(2)}, u32[]{:S(2)}) collective-permute-start(bf16[2,784,768]{2,1,0:T(8,128)(2,1)} %get-tuple-element.111), channel_id=1, source_target_pairs={{0,2},{2,0},{4,6},{6,4},{8,10},{10,8},{12,14},{14,12},{16,18},{18,... | collective-permute-start | bytes 7225352 | tf_op jit(solution)/shard_map/ppermute | solution.py:960
  225.1 21.2 %collective-permute-start.39 = (bf16[480,768]{1,0:T(8,128)(2,1)}, bf16[480,768]{1,0:T(8,128)(2,1)S(1)}, u32[]{:S(2)}, u32[]{:S(2)}) collective-permute-start(bf16[480,768]{1,0:T(8,128)(2,1)} %get-tuple-element.122), channel_id=1, source_target_pairs={{0,1},{1,0},{2,3},{3,2},{4,5},{5,4},{6,7},{7,6},{8,9},{9,8},{10,11... | collective-permute-start | bytes 2211848 | tf_op jit(solution)/shard_map/ppermute | solution.py:968
  228.4 18.5 %collective-permute-start.42 = (f32[24,768]{1,0:T(8,128)S(1)}, f32[24,768]{1,0:T(8,128)S(1)}, u32[]{:S(2)}, u32[]{:S(2)}) collective-permute-start(f32[24,768]{1,0:T(8,128)S(1)} %add.147), channel_id=1, source_target_pairs={{0,4},{2,6},{4,0},{6,2},{8,12},{10,14},{12,8},{14,10},{16,20},{18,... | collective-permute-start | bytes 221192 | tf_op jit(solution)/shard_map/ppermute | solution.py:964
  232.0 15.7 %collective-permute-start.40 = (bf16[392,768]{1,0:T(8,128)(2,1)}, bf16[392,768]{1,0:T(8,128)(2,1)}, u32[]{:S(2)}, u32[]{:S(2)}) collective-permute-start(bf16[392,768]{1,0:T(8,128)(2,1)} %get-tuple-element.128), channel_id=1, source_target_pairs={{0,4},{2,6},{4,0},{6,2},{8,12},{10,14},{12,8},{14,10},{16,20},{18,... | collective-permute-start | bytes 1806344 | tf_op jit(solution)/shard_map/ppermute | solution.py:964
  236.8 16.7 %collective-permute-start.46 = (bf16[392,768]{1,0:T(8,128)(2,1)}, bf16[392,768]{1,0:T(8,128)(2,1)S(1)}, u32[]{:S(2)}, u32[]{:S(2)}) collective-permute-start(bf16[392,768]{1,0:T(8,128)(2,1)} %get-tuple-element.142), channel_id=1, source_target_pairs={{0,8},{2,10},{4,12},{6,14},{8,0},{10,2},{12,4},{14,6},{16,24},{18,... | collective-permute-start | bytes 1806344 | tf_op jit(solution)/shard_map/ppermute | solution.py:972
  248.9 17.7 %collective-permute-start.43 = (bf16[392,768]{1,0:T(8,128)(2,1)S(1)}, bf16[392,768]{1,0:T(8,128)(2,1)S(1)}, u32[]{:S(2)}, u32[]{:S(2)}) collective-permute-start(bf16[392,768]{1,0:T(8,128)(2,1)S(1)} %add_convert_fusion.4), channel_id=1, source_target_pairs={{24,16},{26,18},{28,20},{30,22},{8,0},{10,2},{12,4},{14,6},{25,17}... | collective-permute-start | bytes 1806344 | tf_op jit(solution)/shard_map/ppermute | solution.py:972
  253.1 14.3 %collective-permute-start.44 = (bf16[392,768]{1,0:T(8,128)(2,1)S(1)}, bf16[392,768]{1,0:T(8,128)(2,1)S(1)}, u32[]{:S(2)}, u32[]{:S(2)}) collective-permute-start(bf16[392,768]{1,0:T(8,128)(2,1)S(1)} %get-tuple-element.138), channel_id=1, source_target_pairs={{0,4},{2,6},{4,0},{6,2},{8,12},{10,14},{12,8},{14,10},{16,20},{18,... | collective-permute-start | bytes 1806344 | tf_op jit(solution)/shard_map/ppermute | solution.py:964
  253.5 13.1 %collective-permute-start.45 = (f32[24,768]{1,0:T(8,128)S(1)}, f32[24,768]{1,0:T(8,128)S(1)}, u32[]{:S(2)}, u32[]{:S(2)}) collective-permute-start(f32[24,768]{1,0:T(8,128)S(1)} %add.152), channel_id=1, source_target_pairs={{0,8},{2,10},{4,12},{6,14},{8,0},{10,2},{12,4},{14,6},{16,24},{18,... | collective-permute-start | bytes 221192 | tf_op jit(solution)/shard_map/ppermute | solution.py:972
  267.5 18.4 %collective-permute-start.48 = (bf16[392,768]{1,0:T(8,128)(2,1)S(1)}, bf16[392,768]{1,0:T(8,128)(2,1)S(1)}, u32[]{:S(2)}, u32[]{:S(2)}) collective-permute-start(bf16[392,768]{1,0:T(8,128)(2,1)S(1)} %add_convert_fusion.2), channel_id=1, source_target_pairs={{24,16},{26,18},{28,20},{30,22},{0,8},{2,10},{4,12},{6,14},{25,17}... | collective-permute-start | bytes 1806344 | tf_op jit(solution)/shard_map/ppermute | solution.py:972
  268.8 17.2 %collective-permute-start.47 = (bf16[392,768]{1,0:T(8,128)(2,1)S(1)}, bf16[392,768]{1,0:T(8,128)(2,1)S(1)}, u32[]{:S(2)}, u32[]{:S(2)}) collective-permute-start(bf16[392,768]{1,0:T(8,128)(2,1)S(1)} %add_convert_fusion.3), channel_id=1, source_target_pairs={{16,0},{18,2},{20,4},{22,6},{17,1},{19,3},{21,5},{23,7}} | collective-permute-start | bytes 1806344 | tf_op jit(solution)/shard_map/ppermute | solution.py:972
  269.6 16.5 %collective-permute-start.49 = (bf16[192,768]{1,0:T(8,128)(2,1)S(1)}, bf16[192,768]{1,0:T(8,128)(2,1)S(1)}, u32[]{:S(2)}, u32[]{:S(2)}) collective-permute-start(bf16[192,768]{1,0:T(8,128)(2,1)S(1)} %slice.55), channel_id=1, source_target_pairs={{0,16},{2,18},{4,20},{6,22},{8,24},{10,26},{12,28},{14,30},{1,17},... | collective-permute-start | bytes 884744 | tf_op jit(solution)/shard_map/ppermute | solution.py:972
  286.1 18.6 %collective-permute-start.51 = (bf16[392,768]{1,0:T(8,128)(2,1)S(1)}, bf16[392,768]{1,0:T(8,128)(2,1)}, u32[]{:S(2)}, u32[]{:S(2)}) collective-permute-start(bf16[392,768]{1,0:T(8,128)(2,1)S(1)} %add_convert_fusion), channel_id=1, source_target_pairs={{16,8},{18,10},{20,12},{22,14},{17,9},{19,11},{21,13},{23,15}} | collective-permute-start | bytes 1806344 | tf_op jit(solution)/shard_map/ppermute | solution.py:972
  288.2 14.7 %collective-permute-start.50 = (bf16[224,768]{1,0:T(8,128)(2,1)}, bf16[224,768]{1,0:T(8,128)(2,1)}, u32[]{:S(2)}, u32[]{:S(2)}) collective-permute-start(bf16[224,768]{1,0:T(8,128)(2,1)} %pad_maximum_fusion), channel_id=1, source_target_pairs={{0,16},{2,18},{4,20},{6,22},{8,24},{10,26},{12,28},{14,30},{1,17},... | collective-permute-start | bytes 1032200 | tf_op jit(solution)/shard_map/ppermute | solution.py:972
  (46 other events, 1235.7 us)

commit v4 on v3

--- a/solution.py
+++ b/solution.py
@@ -1059,10 +1059,11 @@
     outs[1][...] = add(ins[2][...], ins[3][...])
     message = outs[2]
     block = ins[4].shape[0]
-    message[:block, :] = add(ins[4][...], ins[5][...])
     spill = message.shape[0] - (block + 8)
+    main = ins[4][...].astype(F32) + ins[5][...].astype(F32)
     total = ins[6][...].astype(F32) + ins[7][...].astype(F32)
-    message[block:, :] = jnp.concatenate([jnp.zeros((8, total.shape[1]), F32), total[block - spill :]]).astype(BF16)
+    gap = jnp.zeros((8, total.shape[1]), F32)
+    message[...] = jnp.concatenate([main, gap, total[block - spill :]], axis=0).astype(BF16)
 
 
 def cross_merge(flags, cross, cross_came):

time: 314 us -> 314 us (level)
  no operation moved by 1% of the time
where the time goes in v4:
time: 314 us; the launch traced here: 308 us
  waiting for transfers between devices  129 us (41%)
  Pallas kernels  105 us (33%)
  starting transfers between devices  50.4 us (16%)
  other arithmetic  12.4 us (4%)
  local copies, waits for them, and re-layouts  10.3 us (3%)
    ppermute x13, waiting for transfers between devices, over_z(): lax.ppermute(v, 'dp', [(4 * a + i, 4 * b + i) for a, b in hops for i in r...  47 us
    ppermute x9, waiting for transfers between devices, over_y(): return lax.ppermute(v, 'dp', [(i, i ^ 2) for i in range(16)])  39.6 us
    ppermute x10, waiting for transfers between devices, over_x(): return lax.ppermute(v, 'seq', [(0, 1), (1, 0)])  37.1 us
    ppermute x13, starting transfers between devices, over_z(): lax.ppermute(v, 'dp', [(4 * a + i, 4 * b + i) for a, b in hops for i in r...  27.9 us
    pallas_call x1, Pallas kernels, middle(): pl.pallas_call(partial(middle_kernel, parts, split), grid_spec=pltpu.Pref...  26.3 us
    pallas_call x1, Pallas kernels, forward(): pl.pallas_call(partial(forward_kernel, queries, custom), grid_spec=pltpu....  19.1 us
    pallas_call x1, Pallas kernels, self_backward(): pl.pallas_call(partial(self_backward_kernel, queries, split), grid_spec=p...  13.4 us
    ppermute x10, starting transfers between devices, over_x(): return lax.ppermute(v, 'seq', [(0, 1), (1, 0)])  11.6 us
  transfers between devices with their start and end apart: 52, of which 24 were waited for; matrix products, arithmetic and copies ran while one was open for 4% of the time, Pallas kernels for 18%

profile of v4, /device:TPU:8, one launch (start us, length us, event | category | flops | bytes accessed | tf_op | source)
XLA Modules:
  0.0 307.8 jit_solution(18394224599625706696)
XLA Ops:
  2.9 1.6 collective-permute-start.1
  4.9 1.5 collective-permute-start
  6.4 2.6 collective-permute-start.7
  9.0 9.5 %collective-permute-done.1.refs_2_ = bf16[400,768]{1,0:T(8,128)(2,1)S(1)} collective-permute-done((bf16[400,768]{1,0:T(8,128)(2,1)S(1)}, bf16[400,768]{1,0:T(8,128)(2,1)S(1)}, u32[]{:S(2)}, u32[]{:S(2)}) %collective-permute-start.1) | collective-permute-done | bytes 614432 | tf_op jit(solution)/shard_map/ppermute | solution.py:964
  18.6 1.5 collective-permute-start.3
  20.1 9.6 %collective-permute-done.2.refs_3_ = bf16[400,768]{1,0:T(8,128)(2,1)S(1)} collective-permute-done((bf16[400,768]{1,0:T(8,128)(2,1)S(1)}, bf16[400,768]{1,0:T(8,128)(2,1)S(1)}, u32[]{:S(2)}, u32[]{:S(2)}) %collective-permute-start.2) | collective-permute-done | bytes 614432 | tf_op jit(solution)/shard_map/ppermute | solution.py:972
  30.0 2.5 collective-permute-start.5
  32.5 2.7 collective-permute-done.7.refs_8_
  36.6 1.4 collective-permute-start.10
  38.0 8.4 %collective-permute-done.4.refs_5_ = bf16[400,768]{1,0:T(8,128)(2,1)S(1)} collective-permute-done((bf16[400,768]{1,0:T(8,128)(2,1)S(1)}, bf16[400,768]{1,0:T(8,128)(2,1)S(1)}, u32[]{:S(2)}, u32[]{:S(2)}) %collective-permute-start.4) | collective-permute-done | bytes 614432 | tf_op jit(solution)/shard_map/ppermute | solution.py:964
  48.4 8.7 %collective-permute-done.9.refs_10_ = bf16[400,768]{1,0:T(8,128)(2,1)S(1)} collective-permute-done((bf16[400,768]{1,0:T(8,128)(2,1)S(1)}, bf16[400,768]{1,0:T(8,128)(2,1)S(1)}, u32[]{:S(2)}, u32[]{:S(2)}) %collective-permute-start.9) | collective-permute-done | bytes 614432 | tf_op jit(solution)/shard_map/ppermute | solution.py:964
  57.2 2.2 collective-permute-done.10.refs_11_
  59.3 1.5 collective-permute-start.6
  62.3 2.5 collective-permute-start.13
  64.9 11.4 %collective-permute-done.6.refs_7_ = bf16[400,768]{1,0:T(8,128)(2,1)} collective-permute-done((bf16[400,768]{1,0:T(8,128)(2,1)S(1)}, bf16[400,768]{1,0:T(8,128)(2,1)}, u32[]{:S(2)}, u32[]{:S(2)}) %collective-permute-start.6) | collective-permute-done | bytes 614432 | tf_op jit(solution)/shard_map/ppermute | solution.py:968
  76.2 11.2 %collective-permute-done.11.refs_12_ = bf16[400,768]{1,0:T(8,128)(2,1)} collective-permute-done((bf16[400,768]{1,0:T(8,128)(2,1)S(1)}, bf16[400,768]{1,0:T(8,128)(2,1)}, u32[]{:S(2)}, u32[]{:S(2)}) %collective-permute-start.11) | collective-permute-done | bytes 614432 | tf_op jit(solution)/shard_map/ppermute | solution.py:968
  91.4 1.6 collective-permute-done.26.refs_27_
  93.1 11.6 %collective-permute-done.14.refs_15_ = bf16[400,768]{1,0:T(8,128)(2,1)} collective-permute-done((bf16[400,768]{1,0:T(8,128)(2,1)}, bf16[400,768]{1,0:T(8,128)(2,1)}, u32[]{:S(2)}, u32[]{:S(2)}) %collective-permute-start.14) | collective-permute-done | bytes 614432 | tf_op jit(solution)/shard_map/ppermute | solution.py:964
  107.3 19.1 %forward.1 = (bf16[336,768]{1,0:T(8,128)(2,1)}, bf16[336,768]{1,0:T(8,128)(2,1)}, bf16[336,768]{1,0:T(8,128)(2,1)}, bf16[336,768]{1,0:T(8,128)(2,1)}, f32[336,76...) custom-call(s32[3]{0:T(128)} %broadcast_subtract_fusion.left_ref, ...), custom_call_target="tpu_custom_call" | custom-call | tf_op jit(solution)/shard_map/forward/pallas_call | solution.py:312
  126.5 1.8 collective-permute-start.31
  129.1 1.4 slice_convert_fusion.refs_7_
  130.5 10.9 %collective-permute-done.32.refs_5_ = f32[3,8,224]{2,1,0:T(8,128)S(1)} collective-permute-done((f32[3,8,224]{2,1,0:T(8,128)}, f32[3,8,224]{2,1,0:T(8,128)S(1)}, u32[]{:S(2)}, u32[]{:S(2)}) %collective-permute-start.32) | collective-permute-done | bytes 21536 | tf_op jit(solution)/shard_map/ppermute | solution.py:968
  142.2 26.3 %middle.1 = (f32[3,112,768]{2,1,0:T(8,128)}, bf16[2,2,784,768]{3,2,1,0:T(8,128)(2,1)}, bf16[2,2,784,768]{3,2,1,0:T(8,128)(2,1)}, bf16[2,784,768]{2,1,0:T(8,128)(...) custom-call(s32[4]{0:T(128)} %pad_add_fusion.flags.refs_0_, ...), custom_call_target="tpu_custom_call" | custom-call | flops 10701766 | bytes 28311 | tf_op jit(solution)/shard_map/middle/pallas_call | solution.py:603
  168.7 10.0 %cross_backward.1 = (bf16[3,112,768]{2,1,0:T(8,128)(2,1)}, bf16[3,512,768]{2,1,0:T(8,128)(2,1)}, bf16[3,512,768]{2,1,0:T(8,128)(2,1)}) custom-call(s32[3]{0:T(128)} %broadcast_subtract_fusion.left_ref, bf16[3,112,768]{2,1,0:T(8,128)(2,1)} %bitcast.42, bf16[3,512,768]{2,1,0:T(8,128)(2,1)} %get-tuple-element.87.k_ref, ...), custom_call_target="tpu_custom_call" | custom-call | flops 352321 | bytes 9437 | tf_op jit(solution)/shard_map/cross_backward/pallas_call | solution.py:684
  178.7 3.8 %far_send.1 = bf16[2,392,768]{2,1,0:T(8,128)(2,1)} custom-call(s32[4]{0:T(128)} %pad_add_fusion.flags.refs_0_, bf16[2,2,2,392,768]{4,3,2,1,0:T(8,128)(2,1)} %bitcast.30, bf16[2,2,2,392,768]{4,3,2,1,0:T(8,128)(2,1)} %bitcast.11.b.d.refs_1_.refs_4_, bf16[2,2,2,392,768]{4,3,2,1,0:T(8,128)(2,1)} %bitcast.31, bf16[2,2,2,392,768]{4,3,2,1,0:T(8,128)(2,1)} %bitcast.11.b.d.refs_1_.refs_4_), custom_call_target="tpu_custom_call" | custom-call | tf_op jit(solution)/shard_map/far_send/pallas_call | solution.py:1026
  182.5 1.4 collective-permute-start.36
  183.9 1.6 collective-permute-start.34
  185.5 9.3 %memory_weights.1 = (f32[8,768]{1,0:T(8,128)}, bf16[2,784,768]{2,1,0:T(8,128)(2,1)}, bf16[2,784,768]{2,1,0:T(8,128)(2,1)}) custom-call(s32[4]{0:T(128)} %pad_add_fusion.flags.refs_0_, bf16[2,784,768]{2,1,0:T(8,128)(2,1)} %get-tuple-element.84.refs_0_, bf16[2,784,768]{2,1,0:T(8,128)(2,1)} %get-tuple-element.85.refs_1_, ...), custom_call_target="tpu_custom_call", output_to_operand_aliasing={{1}: (1, {}), {2}: (2, {})} | custom-call | flops 3623878 | bytes 7077 | tf_op jit(solution)/shard_map/memory_weights/pallas_call | solution.py:728
  195.3 2.5 collective-permute-done.34
  198.6 6.7 %query_backward.1 = (f32[336,768]{1,0:T(8,128)}, bf16[64,768]{1,0:T(8,128)(2,1)}, f32[24,768]{1,0:T(8,128)}, bf16[2,784,768]{2,1,0:T(8,128)(2,1)}, bf16[2,784,768]{2,1,0:T(8,128)(2,1)}) custom-call(s32[4]{0:T(128)} %pad_add_fusion.flags.refs_0_, bf16[2,784,768]{2,1,0:T(8,128)(2,1)} %get-tuple-element.96.refs_0_, ...), custom_call_target="tpu_custom_call", output_to_operand_aliasing={{3}: (1, {}), {4}: (2, {})} | custom-call | flops 792723 | bytes 4128 | tf_op jit(solution)/shard_map/query_backward/pallas_call | solution.py:827
  205.4 13.4 %self_backward.1 = (f32[3,112,768]{2,1,0:T(8,128)}, f32[24,768]{1,0:T(8,128)}, bf16[2,784,768]{2,1,0:T(8,128)(2,1)}, bf16[2,784,768]{2,1,0:T(8,128)(2,1)}) custom-call(s32[4]{0:T(128)} %pad_add_fusion.flags.refs_0_, bf16[336,768]{1,0:T(8,128)(2,1)} %get-tuple-element.83.refs_1_, f32[336,768]{1,0:T(8,128)} %get-tuple-element.100.refs_2_, ...), custom_call_target="tpu_custom_call" | custom-call | flops 6341787 | bytes 9437 | tf_op jit(solution)/shard_map/self_backward/pallas_call | solution.py:921
  219.4 1.5 copy-done
  220.9 4.2 %cross_merge.1 = (bf16[392,768]{1,0:T(8,128)(2,1)}, bf16[392,768]{1,0:T(8,128)(2,1)}, bf16[480,768]{1,0:T(8,128)(2,1)}) custom-call(s32[4]{0:T(128)} %pad_add_fusion.flags.refs_0_, bf16[2,2,392,768]{3,2,1,0:T(8,128)(2,1)} %bitcast.26, bf16[2,2,392,768]{3,2,1,0:T(8,128)(2,1)} %bitcast.34, bf16[2,2,392,768]{3,2,1,0:T(8,128)(2,1)} %bitcast.27, ...), custom_call_target="tpu_custom_call" | custom-call | tf_op jit(solution)/shard_map/cross_merge/pallas_call | solution.py:1026
  225.1 1.9 collective-permute-start.39
  229.2 2.7 fusion.8
  233.2 3.6 %far_merge.1 = (bf16[392,768]{1,0:T(8,128)(2,1)}, bf16[392,768]{1,0:T(8,128)(2,1)}) custom-call(s32[4]{0:T(128)} %pad_add_fusion.flags.refs_0_, bf16[2,2,2,392,768]{4,3,2,1,0:T(8,128)(2,1)} %bitcast.32, bf16[2,2,2,392,768]{4,3,2,1,0:T(8,128)(2,1)} %bitcast.11.b.d.refs_1_.refs_4_, bf16[2,392,768]{2,1,0:T(8,128)(2,1)} %collective-permute-done.36.refs_2_.refs_5_, ...), custom_call_target="tpu_custom_call" | custom-call | tf_op jit(solution)/shard_map/far_merge/pallas_call | solution.py:1026
  236.8 1.4 collective-permute-start.46
  238.3 8.0 %memory_grads.1 = f32[3,512,768]{2,1,0:T(8,128)} custom-call(bf16[3,512,768]{2,1,0:T(8,128)(2,1)} %get-tuple-element.119.refs_3_.dk_ref, bf16[3,512,768]{2,1,0:T(8,128)(2,1)} %get-tuple-element.120.refs_4_.dv_ref, bf16[12544,768]{1,0:T(8,128)(2,1)} %get-tuple-element.121.refs_6_.refs_7_.ck.cv, bf16[12544,768]{1,0:T(8,128)(2,1)} %get-tuple-element.121.refs_6_.refs_7_.ck.cv), custom_call_target="tpu_custom_call" | custom-call | flops 3623878656 | bytes 9437184 | tf_op jit(solution)/shard_map/memory_grads/pallas_call | solution.py:755
  247.7 1.2 add_convert_fusion.4
  248.9 4.2 %collective-permute-start.43 = (bf16[392,768]{1,0:T(8,128)(2,1)S(1)}, bf16[392,768]{1,0:T(8,128)(2,1)S(1)}, u32[]{:S(2)}, u32[]{:S(2)}) collective-permute-start(bf16[392,768]{1,0:T(8,128)(2,1)S(1)} %add_convert_fusion.4), channel_id=1, source_target_pairs={{24,16},{26,18},{28,20},{30,22},{8,0},{10,2},{12,4},{14,6},{25,17}... | collective-permute-start | bytes 1806344 | tf_op jit(solution)/shard_map/ppermute | solution.py:972
  253.7 12.9 %collective-permute-done.45 = f32[24,768]{1,0:T(8,128)S(1)} collective-permute-done((f32[24,768]{1,0:T(8,128)S(1)}, f32[24,768]{1,0:T(8,128)S(1)}, u32[]{:S(2)}, u32[]{:S(2)}) %collective-permute-start.45) | collective-permute-done | bytes 73760 | tf_op jit(solution)/shard_map/ppermute | solution.py:972
  267.5 1.3 collective-permute-start.48
  269.6 6.6 %collective-permute-start.49 = (bf16[192,768]{1,0:T(8,128)(2,1)S(1)}, bf16[192,768]{1,0:T(8,128)(2,1)S(1)}, u32[]{:S(2)}, u32[]{:S(2)}) collective-permute-start(bf16[192,768]{1,0:T(8,128)(2,1)S(1)} %slice.55), channel_id=1, source_target_pairs={{0,16},{2,18},{4,20},{6,22},{8,24},{10,26},{12,28},{14,30},{1,17},... | collective-permute-start | bytes 884744 | tf_op jit(solution)/shard_map/ppermute | solution.py:972
  276.2 9.7 %collective-permute-done.48 = bf16[392,768]{1,0:T(8,128)(2,1)S(1)} collective-permute-done((bf16[392,768]{1,0:T(8,128)(2,1)S(1)}, bf16[392,768]{1,0:T(8,128)(2,1)S(1)}, u32[]{:S(2)}, u32[]{:S(2)}) %collective-permute-start.48) | collective-permute-done | bytes 602144 | tf_op jit(solution)/shard_map/ppermute | solution.py:972
  286.1 1.3 collective-permute-start.51
  288.2 3.0 collective-permute-start.50
  293.9 9.1 %collective-permute-done.50 = bf16[224,768]{1,0:T(8,128)(2,1)} collective-permute-done((bf16[224,768]{1,0:T(8,128)(2,1)}, bf16[224,768]{1,0:T(8,128)(2,1)}, u32[]{:S(2)}, u32[]{:S(2)}) %collective-permute-start.50) | collective-permute-done | bytes 344096 | tf_op jit(solution)/shard_map/ppermute | solution.py:972
  304.7 1.6 convert_add_fusion
  (189 shorter events, 31.8 us)
Async XLA Ops:
  2.9 15.7 %collective-permute-start.1 = (bf16[400,768]{1,0:T(8,128)(2,1)S(1)}, bf16[400,768]{1,0:T(8,128)(2,1)S(1)}, u32[]{:S(2)}, u32[]{:S(2)}) collective-permute-start(bf16[400,768]{1,0:T(8,128)(2,1)S(1)} %maximum_select_fusion.1.refs_0_), channel_id=1, source_target_pairs={{0,4},{2,6},{4,0},{6,2},{8,12},{10,14},{12,8},{14,10},{16,20},{18,... | collective-permute-start | bytes 1843208 | tf_op jit(solution)/shard_map/ppermute | solution.py:964
  4.5 25.1 %collective-permute-start.2 = (bf16[400,768]{1,0:T(8,128)(2,1)S(1)}, bf16[400,768]{1,0:T(8,128)(2,1)S(1)}, u32[]{:S(2)}, u32[]{:S(2)}) collective-permute-start(bf16[400,768]{1,0:T(8,128)(2,1)S(1)} %maximum_select_fusion.1.refs_0_), channel_id=1, source_target_pairs={{0,8},{2,10},{4,12},{6,14},{8,0},{10,2},{12,4},{14,6},{16,24},{18,... | collective-permute-start | bytes 1843208 | tf_op jit(solution)/shard_map/ppermute | solution.py:972
  4.9 25.0 %collective-permute-start = (bf16[400,768]{1,0:T(8,128)(2,1)S(1)}, bf16[400,768]{1,0:T(8,128)(2,1)S(1)}, u32[]{:S(2)}, u32[]{:S(2)}) collective-permute-start(bf16[400,768]{1,0:T(8,128)(2,1)S(1)} %maximum_select_fusion.1.refs_0_), channel_id=1, source_target_pairs={{0,1},{1,0},{2,3},{3,2},{4,5},{5,4},{6,7},{7,6},{8,9},{9,8},{10,11... | collective-permute-start | bytes 1843208 | tf_op jit(solution)/shard_map/ppermute | solution.py:968
  6.4 28.7 %collective-permute-start.7 = (bf16[400,768]{1,0:T(8,128)(2,1)S(1)}, bf16[400,768]{1,0:T(8,128)(2,1)S(1)}, u32[]{:S(2)}, u32[]{:S(2)}) collective-permute-start(bf16[400,768]{1,0:T(8,128)(2,1)S(1)} %maximum_select_fusion.1.refs_0_), channel_id=1, source_target_pairs={{0,16},{2,18},{4,20},{6,22},{16,0},{18,2},{20,4},{22,6},{8,24},{10... | collective-permute-start | bytes 1843208 | tf_op jit(solution)/shard_map/ppermute | solution.py:972
  9.0 26.7 %collective-permute-start.15 = (bf16[400,768]{1,0:T(8,128)(2,1)S(1)}, bf16[400,768]{1,0:T(8,128)(2,1)S(1)}, u32[]{:S(2)}, u32[]{:S(2)}) collective-permute-start(bf16[400,768]{1,0:T(8,128)(2,1)S(1)} %maximum_select_fusion.1.refs_0_), channel_id=1, source_target_pairs={{0,2},{2,0},{4,6},{6,4},{8,10},{10,8},{12,14},{14,12},{16,18},{18,... | collective-permute-start | bytes 1843208 | tf_op jit(solution)/shard_map/ppermute | solution.py:960
  18.6 18.0 %collective-permute-start.3 = (bf16[400,768]{1,0:T(8,128)(2,1)S(1)}, bf16[400,768]{1,0:T(8,128)(2,1)S(1)}, u32[]{:S(2)}, u32[]{:S(2)}) collective-permute-start(bf16[400,768]{1,0:T(8,128)(2,1)S(1)} %collective-permute-done.1.refs_2_), channel_id=1, source_target_pairs={{0,1},{1,0},{2,3},{3,2},{4,5},{5,4},{6,7},{7,6},{8,9},{9,8},{10,11... | collective-permute-start | bytes 1843208 | tf_op jit(solution)/shard_map/ppermute | solution.py:968
  29.6 16.8 %collective-permute-start.4 = (bf16[400,768]{1,0:T(8,128)(2,1)S(1)}, bf16[400,768]{1,0:T(8,128)(2,1)S(1)}, u32[]{:S(2)}, u32[]{:S(2)}) collective-permute-start(bf16[400,768]{1,0:T(8,128)(2,1)S(1)} %collective-permute-done.2.refs_3_), channel_id=1, source_target_pairs={{0,4},{2,6},{4,0},{6,2},{8,12},{10,14},{12,8},{14,10},{16,20},{18,... | collective-permute-start | bytes 1843208 | tf_op jit(solution)/shard_map/ppermute | solution.py:964
  30.0 17.3 %collective-permute-start.5 = (bf16[400,768]{1,0:T(8,128)(2,1)S(1)}, bf16[400,768]{1,0:T(8,128)(2,1)S(1)}, u32[]{:S(2)}, u32[]{:S(2)}) collective-permute-start(bf16[400,768]{1,0:T(8,128)(2,1)S(1)} %collective-permute-done.refs_1_), channel_id=1, source_target_pairs={{0,8},{2,10},{4,12},{6,14},{8,0},{10,2},{12,4},{14,6},{16,24},{18,... | collective-permute-start | bytes 1843208 | tf_op jit(solution)/shard_map/ppermute | solution.py:972
  35.2 13.3 %collective-permute-start.8 = (bf16[400,768]{1,0:T(8,128)(2,1)S(1)}, bf16[400,768]{1,0:T(8,128)(2,1)S(1)}, u32[]{:S(2)}, u32[]{:S(2)}) collective-permute-start(bf16[400,768]{1,0:T(8,128)(2,1)S(1)} %collective-permute-done.7.refs_8_), channel_id=1, source_target_pairs={{0,1},{1,0},{2,3},{3,2},{4,5},{5,4},{6,7},{7,6},{8,9},{9,8},{10,11... | collective-permute-start | bytes 1843208 | tf_op jit(solution)/shard_map/ppermute | solution.py:968
  35.7 21.5 %collective-permute-start.9 = (bf16[400,768]{1,0:T(8,128)(2,1)S(1)}, bf16[400,768]{1,0:T(8,128)(2,1)S(1)}, u32[]{:S(2)}, u32[]{:S(2)}) collective-permute-start(bf16[400,768]{1,0:T(8,128)(2,1)S(1)} %collective-permute-done.7.refs_8_), channel_id=1, source_target_pairs={{0,4},{2,6},{4,0},{6,2},{8,12},{10,14},{12,8},{14,10},{16,20},{18,... | collective-permute-start | bytes 1843208 | tf_op jit(solution)/shard_map/ppermute | solution.py:964
  36.6 22.8 %collective-permute-start.10 = (bf16[400,768]{1,0:T(8,128)(2,1)S(1)}, bf16[400,768]{1,0:T(8,128)(2,1)S(1)}, u32[]{:S(2)}, u32[]{:S(2)}) collective-permute-start(bf16[400,768]{1,0:T(8,128)(2,1)S(1)} %collective-permute-done.7.refs_8_), channel_id=1, source_target_pairs={{0,8},{2,10},{4,12},{6,14},{8,0},{10,2},{12,4},{14,6},{16,24},{18,... | collective-permute-start | bytes 1843208 | tf_op jit(solution)/shard_map/ppermute | solution.py:972
  46.4 14.4 %collective-permute-start.16 = (bf16[400,768]{1,0:T(8,128)(2,1)S(1)}, bf16[400,768]{1,0:T(8,128)(2,1)S(1)}, u32[]{:S(2)}, u32[]{:S(2)}) collective-permute-start(bf16[400,768]{1,0:T(8,128)(2,1)S(1)} %collective-permute-done.refs_1_), channel_id=1, source_target_pairs={{0,2},{2,0},{4,6},{6,4},{8,10},{10,8},{12,14},{14,12},{16,18},{18,... | collective-permute-start | bytes 1843208 | tf_op jit(solution)/shard_map/ppermute | solution.py:960
  47.3 14.1 %collective-permute-start.17 = (bf16[400,768]{1,0:T(8,128)(2,1)S(1)}, bf16[400,768]{1,0:T(8,128)(2,1)S(1)}, u32[]{:S(2)}, u32[]{:S(2)}) collective-permute-start(bf16[400,768]{1,0:T(8,128)(2,1)S(1)} %collective-permute-done.1.refs_2_), channel_id=1, source_target_pairs={{0,2},{2,0},{4,6},{6,4},{8,10},{10,8},{12,14},{14,12},{16,18},{18,... | collective-permute-start | bytes 1843208 | tf_op jit(solution)/shard_map/ppermute | solution.py:960
  48.4 13.9 %collective-permute-start.18 = (bf16[400,768]{1,0:T(8,128)(2,1)S(1)}, bf16[400,768]{1,0:T(8,128)(2,1)S(1)}, u32[]{:S(2)}, u32[]{:S(2)}) collective-permute-start(bf16[400,768]{1,0:T(8,128)(2,1)S(1)} %collective-permute-done.2.refs_3_), channel_id=1, source_target_pairs={{0,2},{2,0},{4,6},{6,4},{8,10},{10,8},{12,14},{14,12},{16,18},{18,... | collective-permute-start | bytes 1843208 | tf_op jit(solution)/shard_map/ppermute | solution.py:960
  57.2 7.6 %collective-permute-start.23 = (bf16[400,768]{1,0:T(8,128)(2,1)S(1)}, bf16[400,768]{1,0:T(8,128)(2,1)S(1)}, u32[]{:S(2)}, u32[]{:S(2)}) collective-permute-start(bf16[400,768]{1,0:T(8,128)(2,1)S(1)} %collective-permute-done.7.refs_8_), channel_id=1, source_target_pairs={{0,2},{2,0},{4,6},{6,4},{8,10},{10,8},{12,14},{14,12},{16,18},{18,... | collective-permute-start | bytes 1843208 | tf_op jit(solution)/shard_map/ppermute | solution.py:960
  59.3 16.9 %collective-permute-start.6 = (bf16[400,768]{1,0:T(8,128)(2,1)S(1)}, bf16[400,768]{1,0:T(8,128)(2,1)}, u32[]{:S(2)}, u32[]{:S(2)}) collective-permute-start(bf16[400,768]{1,0:T(8,128)(2,1)S(1)} %collective-permute-done.4.refs_5_), channel_id=1, source_target_pairs={{0,1},{1,0},{2,3},{3,2},{4,5},{5,4},{6,7},{7,6},{8,9},{9,8},{10,11... | collective-permute-start | bytes 1843208 | tf_op jit(solution)/shard_map/ppermute | solution.py:968
  60.8 26.6 %collective-permute-start.11 = (bf16[400,768]{1,0:T(8,128)(2,1)S(1)}, bf16[400,768]{1,0:T(8,128)(2,1)}, u32[]{:S(2)}, u32[]{:S(2)}) collective-permute-start(bf16[400,768]{1,0:T(8,128)(2,1)S(1)} %collective-permute-done.9.refs_10_), channel_id=1, source_target_pairs={{0,1},{1,0},{2,3},{3,2},{4,5},{5,4},{6,7},{7,6},{8,9},{9,8},{10,11... | collective-permute-start | bytes 1843208 | tf_op jit(solution)/shard_map/ppermute | solution.py:968
  61.4 26.1 %collective-permute-start.12 = (bf16[400,768]{1,0:T(8,128)(2,1)S(1)}, bf16[400,768]{1,0:T(8,128)(2,1)}, u32[]{:S(2)}, u32[]{:S(2)}) collective-permute-start(bf16[400,768]{1,0:T(8,128)(2,1)S(1)} %collective-permute-done.10.refs_11_), channel_id=1, source_target_pairs={{0,4},{2,6},{4,0},{6,2},{8,12},{10,14},{12,8},{14,10},{16,20},{18,... | collective-permute-start | bytes 1843208 | tf_op jit(solution)/shard_map/ppermute | solution.py:964
  62.3 25.7 %collective-permute-start.13 = (bf16[400,768]{1,0:T(8,128)(2,1)S(1)}, bf16[400,768]{1,0:T(8,128)(2,1)}, u32[]{:S(2)}, u32[]{:S(2)}) collective-permute-start(bf16[400,768]{1,0:T(8,128)(2,1)S(1)} %collective-permute-done.8.refs_9_), channel_id=1, source_target_pairs={{0,8},{2,10},{4,12},{6,14},{8,0},{10,2},{12,4},{14,6},{16,24},{18,... | collective-permute-start | bytes 1843208 | tf_op jit(solution)/shard_map/ppermute | solution.py:972
  64.8 23.2 %collective-permute-start.19 = (bf16[400,768]{1,0:T(8,128)(2,1)S(1)}, bf16[400,768]{1,0:T(8,128)(2,1)S(1)}, u32[]{:S(2)}, u32[]{:S(2)}) collective-permute-start(bf16[400,768]{1,0:T(8,128)(2,1)S(1)} %collective-permute-done.3.refs_4_), channel_id=1, source_target_pairs={{0,2},{2,0},{4,6},{6,4},{8,10},{10,8},{12,14},{14,12},{16,18},{18,... | collective-permute-start | bytes 1843208 | tf_op jit(solution)/shard_map/ppermute | solution.py:960
  76.2 12.3 %collective-permute-start.20 = (bf16[400,768]{1,0:T(8,128)(2,1)S(1)}, bf16[400,768]{1,0:T(8,128)(2,1)S(1)}, u32[]{:S(2)}, u32[]{:S(2)}) collective-permute-start(bf16[400,768]{1,0:T(8,128)(2,1)S(1)} %collective-permute-done.4.refs_5_), channel_id=1, source_target_pairs={{0,2},{2,0},{4,6},{6,4},{8,10},{10,8},{12,14},{14,12},{16,18},{18,... | collective-permute-start | bytes 1843208 | tf_op jit(solution)/shard_map/ppermute | solution.py:960
  88.0 3.3 %collective-permute-start.25 = (bf16[400,768]{1,0:T(8,128)(2,1)S(1)}, bf16[400,768]{1,0:T(8,128)(2,1)S(1)}, u32[]{:S(2)}, u32[]{:S(2)}) collective-permute-start(bf16[400,768]{1,0:T(8,128)(2,1)S(1)} %collective-permute-done.9.refs_10_), channel_id=1, source_target_pairs={{0,2},{2,0},{4,6},{6,4},{8,10},{10,8},{12,14},{14,12},{16,18},{18,... | collective-permute-start | bytes 1843208 | tf_op jit(solution)/shard_map/ppermute | solution.py:960
  88.0 5.0 %collective-permute-start.26 = (bf16[400,768]{1,0:T(8,128)(2,1)S(1)}, bf16[400,768]{1,0:T(8,128)(2,1)S(1)}, u32[]{:S(2)}, u32[]{:S(2)}) collective-permute-start(bf16[400,768]{1,0:T(8,128)(2,1)S(1)} %collective-permute-done.10.refs_11_), channel_id=1, source_target_pairs={{0,2},{2,0},{4,6},{6,4},{8,10},{10,8},{12,14},{14,12},{16,18},{18,... | collective-permute-start | bytes 1843208 | tf_op jit(solution)/shard_map/ppermute | solution.py:960
  88.5 16.2 %collective-permute-start.14 = (bf16[400,768]{1,0:T(8,128)(2,1)}, bf16[400,768]{1,0:T(8,128)(2,1)}, u32[]{:S(2)}, u32[]{:S(2)}) collective-permute-start(bf16[400,768]{1,0:T(8,128)(2,1)} %collective-permute-done.13.refs_14_), channel_id=1, source_target_pairs={{0,4},{2,6},{4,0},{6,2},{8,12},{10,14},{12,8},{14,10},{16,20},{18,... | collective-permute-start | bytes 1843208 | tf_op jit(solution)/shard_map/ppermute | solution.py:964
  89.5 17.4 %collective-permute-start.29 = (bf16[400,768]{1,0:T(8,128)(2,1)}, bf16[400,768]{1,0:T(8,128)(2,1)}, u32[]{:S(2)}, u32[]{:S(2)}) collective-permute-start(bf16[400,768]{1,0:T(8,128)(2,1)} %collective-permute-done.13.refs_14_), channel_id=1, source_target_pairs={{0,2},{2,0},{4,6},{6,4},{8,10},{10,8},{12,14},{14,12},{16,18},{18,... | collective-permute-start | bytes 1843208 | tf_op jit(solution)/shard_map/ppermute | solution.py:960
  90.4 16.5 %collective-permute-start.22 = (bf16[400,768]{1,0:T(8,128)(2,1)}, bf16[400,768]{1,0:T(8,128)(2,1)}, u32[]{:S(2)}, u32[]{:S(2)}) collective-permute-start(bf16[400,768]{1,0:T(8,128)(2,1)} %collective-permute-done.6.refs_7_), channel_id=1, source_target_pairs={{0,2},{2,0},{4,6},{6,4},{8,10},{10,8},{12,14},{14,12},{16,18},{18,... | collective-permute-start | bytes 1843208 | tf_op jit(solution)/shard_map/ppermute | solution.py:960
  91.2 15.7 %collective-permute-start.27 = (bf16[400,768]{1,0:T(8,128)(2,1)}, bf16[400,768]{1,0:T(8,128)(2,1)}, u32[]{:S(2)}, u32[]{:S(2)}) collective-permute-start(bf16[400,768]{1,0:T(8,128)(2,1)} %collective-permute-done.11.refs_12_), channel_id=1, source_target_pairs={{0,2},{2,0},{4,6},{6,4},{8,10},{10,8},{12,14},{14,12},{16,18},{18,... | collective-permute-start | bytes 1843208 | tf_op jit(solution)/shard_map/ppermute | solution.py:960
  93.0 13.9 %collective-permute-start.28 = (bf16[400,768]{1,0:T(8,128)(2,1)}, bf16[400,768]{1,0:T(8,128)(2,1)}, u32[]{:S(2)}, u32[]{:S(2)}) collective-permute-start(bf16[400,768]{1,0:T(8,128)(2,1)} %collective-permute-done.12.refs_13_), channel_id=1, source_target_pairs={{0,2},{2,0},{4,6},{6,4},{8,10},{10,8},{12,14},{14,12},{16,18},{18,... | collective-permute-start | bytes 1843208 | tf_op jit(solution)/shard_map/ppermute | solution.py:960
  126.5 15.0 %collective-permute-start.31 = (bf16[3,112,768]{2,1,0:T(8,128)(2,1)}, bf16[3,112,768]{2,1,0:T(8,128)(2,1)S(1)}, u32[]{:S(2)}, u32[]{:S(2)}) collective-permute-start(bf16[3,112,768]{2,1,0:T(8,128)(2,1)} %get-tuple-element.79.refs_2_), channel_id=1, source_target_pairs={{0,1},{1,0},{2,3},{3,2},{4,5},{5,4},{6,7},{7,6},{8,9},{9,8},{10,11... | collective-permute-start | bytes 1548296 | tf_op jit(solution)/shard_map/ppermute | solution.py:968
  128.9 12.6 %collective-permute-start.32 = (f32[3,8,224]{2,1,0:T(8,128)}, f32[3,8,224]{2,1,0:T(8,128)S(1)}, u32[]{:S(2)}, u32[]{:S(2)}) collective-permute-start(f32[3,8,224]{2,1,0:T(8,128)} %get-tuple-element.80.refs_4_), channel_id=1, source_target_pairs={{0,1},{1,0},{2,3},{3,2},{4,5},{5,4},{6,7},{7,6},{8,9},{9,8},{10,11... | collective-permute-start | bytes 64520 | tf_op jit(solution)/shard_map/ppermute | solution.py:968
  168.6 10.1 %collective-permute-start.33 = (bf16[2,2,784,768]{3,2,1,0:T(8,128)(2,1)}, bf16[2,2,784,768]{3,2,1,0:T(8,128)(2,1)}, u32[]{:S(2)}, u32[]{:S(2)}) collective-permute-start(bf16[2,2,784,768]{3,2,1,0:T(8,128)(2,1)} %get-tuple-element.93), channel_id=1, source_target_pairs={{0,2},{2,0},{4,6},{6,4},{8,10},{10,8},{12,14},{14,12},{16,18},{18,... | collective-permute-start | bytes 14450696 | tf_op jit(solution)/shard_map/ppermute | solution.py:960
  182.5 36.3 %collective-permute-start.36 = (bf16[2,392,768]{2,1,0:T(8,128)(2,1)}, bf16[2,392,768]{2,1,0:T(8,128)(2,1)}, u32[]{:S(2)}, u32[]{:S(2)}) collective-permute-start(bf16[2,392,768]{2,1,0:T(8,128)(2,1)} %far_send.1), channel_id=1, source_target_pairs={{0,4},{2,6},{4,0},{6,2},{8,12},{10,14},{12,8},{14,10},{16,20},{18,... | collective-permute-start | bytes 3612680 | tf_op jit(solution)/shard_map/ppermute | solution.py:964
  183.9 13.9 %collective-permute-start.34 = (bf16[3,112,768]{2,1,0:T(8,128)(2,1)S(1)}, bf16[3,112,768]{2,1,0:T(8,128)(2,1)S(1)}, u32[]{:S(2)}, u32[]{:S(2)}) collective-permute-start(bf16[3,112,768]{2,1,0:T(8,128)(2,1)S(1)} %copy-done.29), channel_id=1, source_target_pairs={{0,1},{1,0},{2,3},{3,2},{4,5},{5,4},{6,7},{7,6},{8,9},{9,8},{10,11... | collective-permute-start | bytes 1548296 | tf_op jit(solution)/shard_map/ppermute | solution.py:968
  194.8 10.6 %collective-permute-start.35 = (f32[8,768]{1,0:T(8,128)}, f32[8,768]{1,0:T(8,128)S(1)}, u32[]{:S(2)}, u32[]{:S(2)}) collective-permute-start(f32[8,768]{1,0:T(8,128)} %get-tuple-element.105), channel_id=1, source_target_pairs={{0,1},{1,0},{2,3},{3,2},{4,5},{5,4},{6,7},{7,6},{8,9},{9,8},{10,11... | collective-permute-start | bytes 73736 | tf_op jit(solution)/shard_map/ppermute | solution.py:968
  205.3 14.1 %collective-permute-start.38 = (bf16[2,784,768]{2,1,0:T(8,128)(2,1)}, bf16[2,784,768]{2,1,0:T(8,128)(2,1)S(1)}, u32[]{:S(2)}, u32[]{:S(2)}) collective-permute-start(bf16[2,784,768]{2,1,0:T(8,128)(2,1)} %get-tuple-element.113), channel_id=1, source_target_pairs={{0,2},{2,0},{4,6},{6,4},{8,10},{10,8},{12,14},{14,12},{16,18},{18,... | collective-permute-start | bytes 7225352 | tf_op jit(solution)/shard_map/ppermute | solution.py:960
  218.8 6.3 %collective-permute-start.37 = (bf16[2,784,768]{2,1,0:T(8,128)(2,1)}, bf16[2,784,768]{2,1,0:T(8,128)(2,1)}, u32[]{:S(2)}, u32[]{:S(2)}) collective-permute-start(bf16[2,784,768]{2,1,0:T(8,128)(2,1)} %get-tuple-element.111), channel_id=1, source_target_pairs={{0,2},{2,0},{4,6},{6,4},{8,10},{10,8},{12,14},{14,12},{16,18},{18,... | collective-permute-start | bytes 7225352 | tf_op jit(solution)/shard_map/ppermute | solution.py:960
  225.1 21.2 %collective-permute-start.39 = (bf16[480,768]{1,0:T(8,128)(2,1)}, bf16[480,768]{1,0:T(8,128)(2,1)S(1)}, u32[]{:S(2)}, u32[]{:S(2)}) collective-permute-start(bf16[480,768]{1,0:T(8,128)(2,1)} %get-tuple-element.122), channel_id=1, source_target_pairs={{0,1},{1,0},{2,3},{3,2},{4,5},{5,4},{6,7},{7,6},{8,9},{9,8},{10,11... | collective-permute-start | bytes 2211848 | tf_op jit(solution)/shard_map/ppermute | solution.py:968
  228.4 18.5 %collective-permute-start.42 = (f32[24,768]{1,0:T(8,128)S(1)}, f32[24,768]{1,0:T(8,128)S(1)}, u32[]{:S(2)}, u32[]{:S(2)}) collective-permute-start(f32[24,768]{1,0:T(8,128)S(1)} %add.147), channel_id=1, source_target_pairs={{0,4},{2,6},{4,0},{6,2},{8,12},{10,14},{12,8},{14,10},{16,20},{18,... | collective-permute-start | bytes 221192 | tf_op jit(solution)/shard_map/ppermute | solution.py:964
  232.0 15.7 %collective-permute-start.40 = (bf16[392,768]{1,0:T(8,128)(2,1)}, bf16[392,768]{1,0:T(8,128)(2,1)}, u32[]{:S(2)}, u32[]{:S(2)}) collective-permute-start(bf16[392,768]{1,0:T(8,128)(2,1)} %get-tuple-element.128), channel_id=1, source_target_pairs={{0,4},{2,6},{4,0},{6,2},{8,12},{10,14},{12,8},{14,10},{16,20},{18,... | collective-permute-start | bytes 1806344 | tf_op jit(solution)/shard_map/ppermute | solution.py:964
  236.8 16.7 %collective-permute-start.46 = (bf16[392,768]{1,0:T(8,128)(2,1)}, bf16[392,768]{1,0:T(8,128)(2,1)S(1)}, u32[]{:S(2)}, u32[]{:S(2)}) collective-permute-start(bf16[392,768]{1,0:T(8,128)(2,1)} %get-tuple-element.142), channel_id=1, source_target_pairs={{0,8},{2,10},{4,12},{6,14},{8,0},{10,2},{12,4},{14,6},{16,24},{18,... | collective-permute-start | bytes 1806344 | tf_op jit(solution)/shard_map/ppermute | solution.py:972
  248.9 17.7 %collective-permute-start.43 = (bf16[392,768]{1,0:T(8,128)(2,1)S(1)}, bf16[392,768]{1,0:T(8,128)(2,1)S(1)}, u32[]{:S(2)}, u32[]{:S(2)}) collective-permute-start(bf16[392,768]{1,0:T(8,128)(2,1)S(1)} %add_convert_fusion.4), channel_id=1, source_target_pairs={{24,16},{26,18},{28,20},{30,22},{8,0},{10,2},{12,4},{14,6},{25,17}... | collective-permute-start | bytes 1806344 | tf_op jit(solution)/shard_map/ppermute | solution.py:972
  253.1 14.3 %collective-permute-start.44 = (bf16[392,768]{1,0:T(8,128)(2,1)S(1)}, bf16[392,768]{1,0:T(8,128)(2,1)S(1)}, u32[]{:S(2)}, u32[]{:S(2)}) collective-permute-start(bf16[392,768]{1,0:T(8,128)(2,1)S(1)} %get-tuple-element.138), channel_id=1, source_target_pairs={{0,4},{2,6},{4,0},{6,2},{8,12},{10,14},{12,8},{14,10},{16,20},{18,... | collective-permute-start | bytes 1806344 | tf_op jit(solution)/shard_map/ppermute | solution.py:964
  253.5 13.1 %collective-permute-start.45 = (f32[24,768]{1,0:T(8,128)S(1)}, f32[24,768]{1,0:T(8,128)S(1)}, u32[]{:S(2)}, u32[]{:S(2)}) collective-permute-start(f32[24,768]{1,0:T(8,128)S(1)} %add.152), channel_id=1, source_target_pairs={{0,8},{2,10},{4,12},{6,14},{8,0},{10,2},{12,4},{14,6},{16,24},{18,... | collective-permute-start | bytes 221192 | tf_op jit(solution)/shard_map/ppermute | solution.py:972
  267.5 18.4 %collective-permute-start.48 = (bf16[392,768]{1,0:T(8,128)(2,1)S(1)}, bf16[392,768]{1,0:T(8,128)(2,1)S(1)}, u32[]{:S(2)}, u32[]{:S(2)}) collective-permute-start(bf16[392,768]{1,0:T(8,128)(2,1)S(1)} %add_convert_fusion.2), channel_id=1, source_target_pairs={{24,16},{26,18},{28,20},{30,22},{0,8},{2,10},{4,12},{6,14},{25,17}... | collective-permute-start | bytes 1806344 | tf_op jit(solution)/shard_map/ppermute | solution.py:972
  268.8 17.2 %collective-permute-start.47 = (bf16[392,768]{1,0:T(8,128)(2,1)S(1)}, bf16[392,768]{1,0:T(8,128)(2,1)S(1)}, u32[]{:S(2)}, u32[]{:S(2)}) collective-permute-start(bf16[392,768]{1,0:T(8,128)(2,1)S(1)} %add_convert_fusion.3), channel_id=1, source_target_pairs={{16,0},{18,2},{20,4},{22,6},{17,1},{19,3},{21,5},{23,7}} | collective-permute-start | bytes 1806344 | tf_op jit(solution)/shard_map/ppermute | solution.py:972
  269.6 16.5 %collective-permute-start.49 = (bf16[192,768]{1,0:T(8,128)(2,1)S(1)}, bf16[192,768]{1,0:T(8,128)(2,1)S(1)}, u32[]{:S(2)}, u32[]{:S(2)}) collective-permute-start(bf16[192,768]{1,0:T(8,128)(2,1)S(1)} %slice.55), channel_id=1, source_target_pairs={{0,16},{2,18},{4,20},{6,22},{8,24},{10,26},{12,28},{14,30},{1,17},... | collective-permute-start | bytes 884744 | tf_op jit(solution)/shard_map/ppermute | solution.py:972
  286.1 18.6 %collective-permute-start.51 = (bf16[392,768]{1,0:T(8,128)(2,1)S(1)}, bf16[392,768]{1,0:T(8,128)(2,1)}, u32[]{:S(2)}, u32[]{:S(2)}) collective-permute-start(bf16[392,768]{1,0:T(8,128)(2,1)S(1)} %add_convert_fusion), channel_id=1, source_target_pairs={{16,8},{18,10},{20,12},{22,14},{17,9},{19,11},{21,13},{23,15}} | collective-permute-start | bytes 1806344 | tf_op jit(solution)/shard_map/ppermute | solution.py:972
  288.2 14.7 %collective-permute-start.50 = (bf16[224,768]{1,0:T(8,128)(2,1)}, bf16[224,768]{1,0:T(8,128)(2,1)}, u32[]{:S(2)}, u32[]{:S(2)}) collective-permute-start(bf16[224,768]{1,0:T(8,128)(2,1)} %pad_maximum_fusion), channel_id=1, source_target_pairs={{0,16},{2,18},{4,20},{6,22},{8,24},{10,26},{12,28},{14,30},{1,17},... | collective-permute-start | bytes 1032200 | tf_op jit(solution)/shard_map/ppermute | solution.py:972
  (46 other events, 1235.7 us)

commit v5 on v4

--- a/solution.py
+++ b/solution.py
@@ -1132,9 +1132,8 @@
     came = over_x(message)
     near, near_came = blocks_of(near), blocks_of(near_came)
     near_send = add(picked(near, 1 - at.y, at.x), picked(near_came, 1 - at.y, at.x))
-    near = add(picked(near, at.y, at.x), picked(near_came, at.y, at.x))
     vec_rows = vec_rows + vec_came
-    near_send, near, dk, dv, w, far_last = tie(near_send, near, *extra, far_last)
+    near_send, near, near_kept, dk, dv, w, far_last = tie(near_send, near, near_came, *extra, far_last)
     far_out, far = far_merge(flags, *far, far_last)
     near_came, far_came, vec_came = over_y(near_send), over_z(far_out, SWAP_ONE), over_y(vec_rows)
     gm = memory_grads(dk, dv, w)
@@ -1142,7 +1141,8 @@
     send, cross = cross_second(at, (low, high), came)
     send, near_came, vec_came, cross = tie(send, near_came, vec_came, cross)
 
-    near = add(near, near_came)
+    near = picked(near, at.y, at.x).astype(F32) + picked(near_kept, at.y, at.x).astype(F32)
+    near = (near + near_came.astype(F32)).astype(BF16)
     vec_rows = vec_rows + vec_came
     near, vec_rows, send = tie(near, vec_rows, send)
     cross_came, near_came, vec_came = over_y(send), over_z(near, [(3, 2), (1, 0)]), over_z(vec_rows, SWAP_ONE)

time: 314 us -> 313 us (level)
  no operation moved by 1% of the time
where the time goes in v5:
time: 313 us; the launch traced here: 307 us
  waiting for transfers between devices  128 us (41%)
  Pallas kernels  105 us (34%)
  starting transfers between devices  51 us (16%)
  other arithmetic  11.5 us (4%)
  local copies, waits for them, and re-layouts  10.3 us (3%)
    ppermute x13, waiting for transfers between devices, over_z(): lax.ppermute(v, 'dp', [(4 * a + i, 4 * b + i) for a, b in hops for i in r...  46.9 us
    ppermute x9, waiting for transfers between devices, over_y(): return lax.ppermute(v, 'dp', [(i, i ^ 2) for i in range(16)])  39.4 us
    ppermute x10, waiting for transfers between devices, over_x(): return lax.ppermute(v, 'seq', [(0, 1), (1, 0)])  37.1 us
    ppermute x13, starting transfers between devices, over_z(): lax.ppermute(v, 'dp', [(4 * a + i, 4 * b + i) for a, b in hops for i in r...  28.4 us
    pallas_call x1, Pallas kernels, middle(): pl.pallas_call(partial(middle_kernel, parts, split), grid_spec=pltpu.Pref...  26.3 us
    pallas_call x1, Pallas kernels, forward(): pl.pallas_call(partial(forward_kernel, queries, custom), grid_spec=pltpu....  19.1 us
    pallas_call x1, Pallas kernels, self_backward(): pl.pallas_call(partial(self_backward_kernel, queries, split), grid_spec=p...  13.3 us
    ppermute x10, starting transfers between devices, over_x(): return lax.ppermute(v, 'seq', [(0, 1), (1, 0)])  11.6 us
  transfers between devices with their start and end apart: 52, of which 24 were waited for; matrix products, arithmetic and copies ran while one was open for 4% of the time, Pallas kernels for 18%

profile of v5, /device:TPU:8, one launch (start us, length us, event | category | flops | bytes accessed | tf_op | source)
XLA Modules:
  0.0 307.0 jit_solution(18058992667337278426)
XLA Ops:
  2.9 1.6 collective-permute-start.1
  4.9 1.5 collective-permute-start
  6.4 2.6 collective-permute-start.7
  9.0 9.5 %collective-permute-done.1.refs_2_ = bf16[400,768]{1,0:T(8,128)(2,1)S(1)} collective-permute-done((bf16[400,768]{1,0:T(8,128)(2,1)S(1)}, bf16[400,768]{1,0:T(8,128)(2,1)S(1)}, u32[]{:S(2)}, u32[]{:S(2)}) %collective-permute-start.1) | collective-permute-done | bytes 614432 | tf_op jit(solution)/shard_map/ppermute | solution.py:964
  18.6 1.5 collective-permute-start.3
  20.1 9.6 %collective-permute-done.2.refs_3_ = bf16[400,768]{1,0:T(8,128)(2,1)S(1)} collective-permute-done((bf16[400,768]{1,0:T(8,128)(2,1)S(1)}, bf16[400,768]{1,0:T(8,128)(2,1)S(1)}, u32[]{:S(2)}, u32[]{:S(2)}) %collective-permute-start.2) | collective-permute-done | bytes 614432 | tf_op jit(solution)/shard_map/ppermute | solution.py:972
  30.0 2.5 collective-permute-start.5
  32.5 2.7 collective-permute-done.7.refs_8_
  36.6 1.4 collective-permute-start.10
  38.0 8.4 %collective-permute-done.4.refs_5_ = bf16[400,768]{1,0:T(8,128)(2,1)S(1)} collective-permute-done((bf16[400,768]{1,0:T(8,128)(2,1)S(1)}, bf16[400,768]{1,0:T(8,128)(2,1)S(1)}, u32[]{:S(2)}, u32[]{:S(2)}) %collective-permute-start.4) | collective-permute-done | bytes 614432 | tf_op jit(solution)/shard_map/ppermute | solution.py:964
  48.4 8.7 %collective-permute-done.9.refs_10_ = bf16[400,768]{1,0:T(8,128)(2,1)S(1)} collective-permute-done((bf16[400,768]{1,0:T(8,128)(2,1)S(1)}, bf16[400,768]{1,0:T(8,128)(2,1)S(1)}, u32[]{:S(2)}, u32[]{:S(2)}) %collective-permute-start.9) | collective-permute-done | bytes 614432 | tf_op jit(solution)/shard_map/ppermute | solution.py:964
  57.2 2.2 collective-permute-done.10.refs_11_
  59.3 1.5 collective-permute-start.6
  62.3 2.5 collective-permute-start.13
  64.9 11.4 %collective-permute-done.6.refs_7_ = bf16[400,768]{1,0:T(8,128)(2,1)} collective-permute-done((bf16[400,768]{1,0:T(8,128)(2,1)S(1)}, bf16[400,768]{1,0:T(8,128)(2,1)}, u32[]{:S(2)}, u32[]{:S(2)}) %collective-permute-start.6) | collective-permute-done | bytes 614432 | tf_op jit(solution)/shard_map/ppermute | solution.py:968
  76.2 11.2 %collective-permute-done.11.refs_12_ = bf16[400,768]{1,0:T(8,128)(2,1)} collective-permute-done((bf16[400,768]{1,0:T(8,128)(2,1)S(1)}, bf16[400,768]{1,0:T(8,128)(2,1)}, u32[]{:S(2)}, u32[]{:S(2)}) %collective-permute-start.11) | collective-permute-done | bytes 614432 | tf_op jit(solution)/shard_map/ppermute | solution.py:968
  91.4 1.6 collective-permute-done.26.refs_27_
  93.1 11.6 %collective-permute-done.14.refs_15_ = bf16[400,768]{1,0:T(8,128)(2,1)} collective-permute-done((bf16[400,768]{1,0:T(8,128)(2,1)}, bf16[400,768]{1,0:T(8,128)(2,1)}, u32[]{:S(2)}, u32[]{:S(2)}) %collective-permute-start.14) | collective-permute-done | bytes 614432 | tf_op jit(solution)/shard_map/ppermute | solution.py:964
  107.3 19.1 %forward.1 = (bf16[336,768]{1,0:T(8,128)(2,1)}, bf16[336,768]{1,0:T(8,128)(2,1)}, bf16[336,768]{1,0:T(8,128)(2,1)}, bf16[336,768]{1,0:T(8,128)(2,1)}, f32[336,76...) custom-call(s32[3]{0:T(128)} %broadcast_subtract_fusion.left_ref, ...), custom_call_target="tpu_custom_call" | custom-call | tf_op jit(solution)/shard_map/forward/pallas_call | solution.py:312
  126.5 1.8 collective-permute-start.31
  129.1 1.4 slice_convert_fusion.refs_7_
  130.5 10.9 %collective-permute-done.32.refs_5_ = f32[3,8,224]{2,1,0:T(8,128)S(1)} collective-permute-done((f32[3,8,224]{2,1,0:T(8,128)}, f32[3,8,224]{2,1,0:T(8,128)S(1)}, u32[]{:S(2)}, u32[]{:S(2)}) %collective-permute-start.32) | collective-permute-done | bytes 21536 | tf_op jit(solution)/shard_map/ppermute | solution.py:968
  142.2 26.3 %middle.1 = (f32[3,112,768]{2,1,0:T(8,128)}, bf16[2,2,784,768]{3,2,1,0:T(8,128)(2,1)}, bf16[2,2,784,768]{3,2,1,0:T(8,128)(2,1)}, bf16[2,784,768]{2,1,0:T(8,128)(...) custom-call(s32[4]{0:T(128)} %pad_add_fusion.flags.refs_0_, ...), custom_call_target="tpu_custom_call" | custom-call | flops 10701766 | bytes 28311 | tf_op jit(solution)/shard_map/middle/pallas_call | solution.py:603
  168.7 10.0 %cross_backward.1 = (bf16[3,112,768]{2,1,0:T(8,128)(2,1)}, bf16[3,512,768]{2,1,0:T(8,128)(2,1)}, bf16[3,512,768]{2,1,0:T(8,128)(2,1)}) custom-call(s32[3]{0:T(128)} %broadcast_subtract_fusion.left_ref, bf16[3,112,768]{2,1,0:T(8,128)(2,1)} %bitcast.45, bf16[3,512,768]{2,1,0:T(8,128)(2,1)} %get-tuple-element.88.k_ref, ...), custom_call_target="tpu_custom_call" | custom-call | flops 352321 | bytes 9437 | tf_op jit(solution)/shard_map/cross_backward/pallas_call | solution.py:684
  178.7 3.8 %far_send.1 = bf16[2,392,768]{2,1,0:T(8,128)(2,1)} custom-call(s32[4]{0:T(128)} %pad_add_fusion.flags.refs_0_, bf16[2,2,2,392,768]{4,3,2,1,0:T(8,128)(2,1)} %bitcast.32, bf16[2,2,2,392,768]{4,3,2,1,0:T(8,128)(2,1)} %bitcast.11.b.d.refs_1_.refs_4_, bf16[2,2,2,392,768]{4,3,2,1,0:T(8,128)(2,1)} %bitcast.33, bf16[2,2,2,392,768]{4,3,2,1,0:T(8,128)(2,1)} %bitcast.11.b.d.refs_1_.refs_4_), custom_call_target="tpu_custom_call" | custom-call | tf_op jit(solution)/shard_map/far_send/pallas_call | solution.py:1026
  182.5 1.4 collective-permute-start.36
  183.9 1.6 collective-permute-start.34
  185.5 9.3 %memory_weights.1 = (f32[8,768]{1,0:T(8,128)}, bf16[2,784,768]{2,1,0:T(8,128)(2,1)}, bf16[2,784,768]{2,1,0:T(8,128)(2,1)}) custom-call(s32[4]{0:T(128)} %pad_add_fusion.flags.refs_0_, bf16[2,784,768]{2,1,0:T(8,128)(2,1)} %get-tuple-element.85.refs_0_, bf16[2,784,768]{2,1,0:T(8,128)(2,1)} %get-tuple-element.86.refs_1_, ...), custom_call_target="tpu_custom_call", output_to_operand_aliasing={{1}: (1, {}), {2}: (2, {})} | custom-call | flops 3623878 | bytes 7077 | tf_op jit(solution)/shard_map/memory_weights/pallas_call | solution.py:728
  195.3 2.5 collective-permute-done.34
  198.6 6.7 %query_backward.1 = (f32[336,768]{1,0:T(8,128)}, bf16[64,768]{1,0:T(8,128)(2,1)}, f32[24,768]{1,0:T(8,128)}, bf16[2,784,768]{2,1,0:T(8,128)(2,1)}, bf16[2,784,768]{2,1,0:T(8,128)(2,1)}) custom-call(s32[4]{0:T(128)} %pad_add_fusion.flags.refs_0_, bf16[2,784,768]{2,1,0:T(8,128)(2,1)} %get-tuple-element.97.refs_0_, ...), custom_call_target="tpu_custom_call", output_to_operand_aliasing={{3}: (1, {}), {4}: (2, {})} | custom-call | flops 792723 | bytes 4128 | tf_op jit(solution)/shard_map/query_backward/pallas_call | solution.py:827
  205.5 13.3 %self_backward.1 = (f32[3,112,768]{2,1,0:T(8,128)}, f32[24,768]{1,0:T(8,128)}, bf16[2,784,768]{2,1,0:T(8,128)(2,1)}, bf16[2,784,768]{2,1,0:T(8,128)(2,1)}) custom-call(s32[4]{0:T(128)} %pad_add_fusion.flags.refs_0_, bf16[336,768]{1,0:T(8,128)(2,1)} %get-tuple-element.84.refs_1_, f32[336,768]{1,0:T(8,128)} %get-tuple-element.101.refs_2_, ...), custom_call_target="tpu_custom_call" | custom-call | flops 6341787 | bytes 9437 | tf_op jit(solution)/shard_map/self_backward/pallas_call | solution.py:921
  219.4 1.5 copy-done
  220.9 4.2 %cross_merge.1 = (bf16[392,768]{1,0:T(8,128)(2,1)}, bf16[392,768]{1,0:T(8,128)(2,1)}, bf16[480,768]{1,0:T(8,128)(2,1)}) custom-call(s32[4]{0:T(128)} %pad_add_fusion.flags.refs_0_, bf16[2,2,392,768]{3,2,1,0:T(8,128)(2,1)} %bitcast.28, bf16[2,2,392,768]{3,2,1,0:T(8,128)(2,1)} %bitcast.36, bf16[2,2,392,768]{3,2,1,0:T(8,128)(2,1)} %bitcast.29, ...), custom_call_target="tpu_custom_call" | custom-call | tf_op jit(solution)/shard_map/cross_merge/pallas_call | solution.py:1026
  225.1 1.9 collective-permute-start.39
  229.3 1.4 fusion.8
  231.9 3.6 %far_merge.1 = (bf16[392,768]{1,0:T(8,128)(2,1)}, bf16[392,768]{1,0:T(8,128)(2,1)}) custom-call(s32[4]{0:T(128)} %pad_add_fusion.flags.refs_0_, bf16[2,2,2,392,768]{4,3,2,1,0:T(8,128)(2,1)} %bitcast.34, bf16[2,2,2,392,768]{4,3,2,1,0:T(8,128)(2,1)} %bitcast.11.b.d.refs_1_.refs_4_, bf16[2,392,768]{2,1,0:T(8,128)(2,1)} %collective-permute-done.36.refs_2_.refs_5_, ...), custom_call_target="tpu_custom_call" | custom-call | tf_op jit(solution)/shard_map/far_merge/pallas_call | solution.py:1026
  235.6 1.5 collective-permute-start.46
  237.0 8.0 %memory_grads.1 = f32[3,512,768]{2,1,0:T(8,128)} custom-call(bf16[3,512,768]{2,1,0:T(8,128)(2,1)} %get-tuple-element.120.refs_3_.dk_ref, bf16[3,512,768]{2,1,0:T(8,128)(2,1)} %get-tuple-element.121.refs_4_.dv_ref, bf16[12544,768]{1,0:T(8,128)(2,1)} %get-tuple-element.122.refs_6_.refs_7_.ck.cv, bf16[12544,768]{1,0:T(8,128)(2,1)} %get-tuple-element.122.refs_6_.refs_7_.ck.cv), custom_call_target="tpu_custom_call" | custom-call | flops 3623878656 | bytes 9437184 | tf_op jit(solution)/shard_map/memory_grads/pallas_call | solution.py:755
  246.2 1.7 fusion.7
  247.9 4.2 %collective-permute-start.43 = (bf16[392,768]{1,0:T(8,128)(2,1)S(1)}, bf16[392,768]{1,0:T(8,128)(2,1)S(1)}, u32[]{:S(2)}, u32[]{:S(2)}) collective-permute-start(bf16[392,768]{1,0:T(8,128)(2,1)S(1)} %fusion.7), channel_id=1, source_target_pairs={{24,16},{26,18},{28,20},{30,22},{8,0},{10,2},{12,4},{14,6},{25,17}... | collective-permute-start | bytes 1806344 | tf_op jit(solution)/shard_map/ppermute | solution.py:972
  252.8 12.9 %collective-permute-done.45 = f32[24,768]{1,0:T(8,128)S(1)} collective-permute-done((f32[24,768]{1,0:T(8,128)S(1)}, f32[24,768]{1,0:T(8,128)S(1)}, u32[]{:S(2)}, u32[]{:S(2)}) %collective-permute-start.45) | collective-permute-done | bytes 73760 | tf_op jit(solution)/shard_map/ppermute | solution.py:972
  266.6 1.3 collective-permute-start.48
  268.6 6.7 %collective-permute-start.49 = (bf16[192,768]{1,0:T(8,128)(2,1)S(1)}, bf16[192,768]{1,0:T(8,128)(2,1)S(1)}, u32[]{:S(2)}, u32[]{:S(2)}) collective-permute-start(bf16[192,768]{1,0:T(8,128)(2,1)S(1)} %slice.55), channel_id=1, source_target_pairs={{0,16},{2,18},{4,20},{6,22},{8,24},{10,26},{12,28},{14,30},{1,17},... | collective-permute-start | bytes 884744 | tf_op jit(solution)/shard_map/ppermute | solution.py:972
  275.3 9.6 %collective-permute-done.48 = bf16[392,768]{1,0:T(8,128)(2,1)S(1)} collective-permute-done((bf16[392,768]{1,0:T(8,128)(2,1)S(1)}, bf16[392,768]{1,0:T(8,128)(2,1)S(1)}, u32[]{:S(2)}, u32[]{:S(2)}) %collective-permute-start.48) | collective-permute-done | bytes 602144 | tf_op jit(solution)/shard_map/ppermute | solution.py:972
  285.2 1.3 collective-permute-start.51
  287.2 3.3 %collective-permute-start.50 = (bf16[224,768]{1,0:T(8,128)(2,1)}, bf16[224,768]{1,0:T(8,128)(2,1)}, u32[]{:S(2)}, u32[]{:S(2)}) collective-permute-start(bf16[224,768]{1,0:T(8,128)(2,1)} %pad_maximum_fusion), channel_id=1, source_target_pairs={{0,16},{2,18},{4,20},{6,22},{8,24},{10,26},{12,28},{14,30},{1,17},... | collective-permute-start | bytes 1032200 | tf_op jit(solution)/shard_map/ppermute | solution.py:972
  293.1 9.1 %collective-permute-done.50 = bf16[224,768]{1,0:T(8,128)(2,1)} collective-permute-done((bf16[224,768]{1,0:T(8,128)(2,1)}, bf16[224,768]{1,0:T(8,128)(2,1)}, u32[]{:S(2)}, u32[]{:S(2)}) %collective-permute-start.50) | collective-permute-done | bytes 344096 | tf_op jit(solution)/shard_map/ppermute | solution.py:972
  304.0 1.6 convert_add_fusion
  (189 shorter events, 31.6 us)
Async XLA Ops:
  2.9 15.7 %collective-permute-start.1 = (bf16[400,768]{1,0:T(8,128)(2,1)S(1)}, bf16[400,768]{1,0:T(8,128)(2,1)S(1)}, u32[]{:S(2)}, u32[]{:S(2)}) collective-permute-start(bf16[400,768]{1,0:T(8,128)(2,1)S(1)} %maximum_select_fusion.1.refs_0_), channel_id=1, source_target_pairs={{0,4},{2,6},{4,0},{6,2},{8,12},{10,14},{12,8},{14,10},{16,20},{18,... | collective-permute-start | bytes 1843208 | tf_op jit(solution)/shard_map/ppermute | solution.py:964
  4.5 25.1 %collective-permute-start.2 = (bf16[400,768]{1,0:T(8,128)(2,1)S(1)}, bf16[400,768]{1,0:T(8,128)(2,1)S(1)}, u32[]{:S(2)}, u32[]{:S(2)}) collective-permute-start(bf16[400,768]{1,0:T(8,128)(2,1)S(1)} %maximum_select_fusion.1.refs_0_), channel_id=1, source_target_pairs={{0,8},{2,10},{4,12},{6,14},{8,0},{10,2},{12,4},{14,6},{16,24},{18,... | collective-permute-start | bytes 1843208 | tf_op jit(solution)/shard_map/ppermute | solution.py:972
  4.9 25.0 %collective-permute-start = (bf16[400,768]{1,0:T(8,128)(2,1)S(1)}, bf16[400,768]{1,0:T(8,128)(2,1)S(1)}, u32[]{:S(2)}, u32[]{:S(2)}) collective-permute-start(bf16[400,768]{1,0:T(8,128)(2,1)S(1)} %maximum_select_fusion.1.refs_0_), channel_id=1, source_target_pairs={{0,1},{1,0},{2,3},{3,2},{4,5},{5,4},{6,7},{7,6},{8,9},{9,8},{10,11... | collective-permute-start | bytes 1843208 | tf_op jit(solution)/shard_map/ppermute | solution.py:968
  6.4 28.7 %collective-permute-start.7 = (bf16[400,768]{1,0:T(8,128)(2,1)S(1)}, bf16[400,768]{1,0:T(8,128)(2,1)S(1)}, u32[]{:S(2)}, u32[]{:S(2)}) collective-permute-start(bf16[400,768]{1,0:T(8,128)(2,1)S(1)} %maximum_select_fusion.1.refs_0_), channel_id=1, source_target_pairs={{0,16},{2,18},{4,20},{6,22},{16,0},{18,2},{20,4},{22,6},{8,24},{10... | collective-permute-start | bytes 1843208 | tf_op jit(solution)/shard_map/ppermute | solution.py:972
  9.0 26.7 %collective-permute-start.15 = (bf16[400,768]{1,0:T(8,128)(2,1)S(1)}, bf16[400,768]{1,0:T(8,128)(2,1)S(1)}, u32[]{:S(2)}, u32[]{:S(2)}) collective-permute-start(bf16[400,768]{1,0:T(8,128)(2,1)S(1)} %maximum_select_fusion.1.refs_0_), channel_id=1, source_target_pairs={{0,2},{2,0},{4,6},{6,4},{8,10},{10,8},{12,14},{14,12},{16,18},{18,... | collective-permute-start | bytes 1843208 | tf_op jit(solution)/shard_map/ppermute | solution.py:960
  18.6 18.0 %collective-permute-start.3 = (bf16[400,768]{1,0:T(8,128)(2,1)S(1)}, bf16[400,768]{1,0:T(8,128)(2,1)S(1)}, u32[]{:S(2)}, u32[]{:S(2)}) collective-permute-start(bf16[400,768]{1,0:T(8,128)(2,1)S(1)} %collective-permute-done.1.refs_2_), channel_id=1, source_target_pairs={{0,1},{1,0},{2,3},{3,2},{4,5},{5,4},{6,7},{7,6},{8,9},{9,8},{10,11... | collective-permute-start | bytes 1843208 | tf_op jit(solution)/shard_map/ppermute | solution.py:968
  29.6 16.8 %collective-permute-start.4 = (bf16[400,768]{1,0:T(8,128)(2,1)S(1)}, bf16[400,768]{1,0:T(8,128)(2,1)S(1)}, u32[]{:S(2)}, u32[]{:S(2)}) collective-permute-start(bf16[400,768]{1,0:T(8,128)(2,1)S(1)} %collective-permute-done.2.refs_3_), channel_id=1, source_target_pairs={{0,4},{2,6},{4,0},{6,2},{8,12},{10,14},{12,8},{14,10},{16,20},{18,... | collective-permute-start | bytes 1843208 | tf_op jit(solution)/shard_map/ppermute | solution.py:964
  30.0 17.3 %collective-permute-start.5 = (bf16[400,768]{1,0:T(8,128)(2,1)S(1)}, bf16[400,768]{1,0:T(8,128)(2,1)S(1)}, u32[]{:S(2)}, u32[]{:S(2)}) collective-permute-start(bf16[400,768]{1,0:T(8,128)(2,1)S(1)} %collective-permute-done.refs_1_), channel_id=1, source_target_pairs={{0,8},{2,10},{4,12},{6,14},{8,0},{10,2},{12,4},{14,6},{16,24},{18,... | collective-permute-start | bytes 1843208 | tf_op jit(solution)/shard_map/ppermute | solution.py:972
  35.2 13.3 %collective-permute-start.8 = (bf16[400,768]{1,0:T(8,128)(2,1)S(1)}, bf16[400,768]{1,0:T(8,128)(2,1)S(1)}, u32[]{:S(2)}, u32[]{:S(2)}) collective-permute-start(bf16[400,768]{1,0:T(8,128)(2,1)S(1)} %collective-permute-done.7.refs_8_), channel_id=1, source_target_pairs={{0,1},{1,0},{2,3},{3,2},{4,5},{5,4},{6,7},{7,6},{8,9},{9,8},{10,11... | collective-permute-start | bytes 1843208 | tf_op jit(solution)/shard_map/ppermute | solution.py:968
  35.7 21.5 %collective-permute-start.9 = (bf16[400,768]{1,0:T(8,128)(2,1)S(1)}, bf16[400,768]{1,0:T(8,128)(2,1)S(1)}, u32[]{:S(2)}, u32[]{:S(2)}) collective-permute-start(bf16[400,768]{1,0:T(8,128)(2,1)S(1)} %collective-permute-done.7.refs_8_), channel_id=1, source_target_pairs={{0,4},{2,6},{4,0},{6,2},{8,12},{10,14},{12,8},{14,10},{16,20},{18,... | collective-permute-start | bytes 1843208 | tf_op jit(solution)/shard_map/ppermute | solution.py:964
  36.6 22.8 %collective-permute-start.10 = (bf16[400,768]{1,0:T(8,128)(2,1)S(1)}, bf16[400,768]{1,0:T(8,128)(2,1)S(1)}, u32[]{:S(2)}, u32[]{:S(2)}) collective-permute-start(bf16[400,768]{1,0:T(8,128)(2,1)S(1)} %collective-permute-done.7.refs_8_), channel_id=1, source_target_pairs={{0,8},{2,10},{4,12},{6,14},{8,0},{10,2},{12,4},{14,6},{16,24},{18,... | collective-permute-start | bytes 1843208 | tf_op jit(solution)/shard_map/ppermute | solution.py:972
  46.4 14.4 %collective-permute-start.16 = (bf16[400,768]{1,0:T(8,128)(2,1)S(1)}, bf16[400,768]{1,0:T(8,128)(2,1)S(1)}, u32[]{:S(2)}, u32[]{:S(2)}) collective-permute-start(bf16[400,768]{1,0:T(8,128)(2,1)S(1)} %collective-permute-done.refs_1_), channel_id=1, source_target_pairs={{0,2},{2,0},{4,6},{6,4},{8,10},{10,8},{12,14},{14,12},{16,18},{18,... | collective-permute-start | bytes 1843208 | tf_op jit(solution)/shard_map/ppermute | solution.py:960
  47.3 14.1 %collective-permute-start.17 = (bf16[400,768]{1,0:T(8,128)(2,1)S(1)}, bf16[400,768]{1,0:T(8,128)(2,1)S(1)}, u32[]{:S(2)}, u32[]{:S(2)}) collective-permute-start(bf16[400,768]{1,0:T(8,128)(2,1)S(1)} %collective-permute-done.1.refs_2_), channel_id=1, source_target_pairs={{0,2},{2,0},{4,6},{6,4},{8,10},{10,8},{12,14},{14,12},{16,18},{18,... | collective-permute-start | bytes 1843208 | tf_op jit(solution)/shard_map/ppermute | solution.py:960
  48.4 13.9 %collective-permute-start.18 = (bf16[400,768]{1,0:T(8,128)(2,1)S(1)}, bf16[400,768]{1,0:T(8,128)(2,1)S(1)}, u32[]{:S(2)}, u32[]{:S(2)}) collective-permute-start(bf16[400,768]{1,0:T(8,128)(2,1)S(1)} %collective-permute-done.2.refs_3_), channel_id=1, source_target_pairs={{0,2},{2,0},{4,6},{6,4},{8,10},{10,8},{12,14},{14,12},{16,18},{18,... | collective-permute-start | bytes 1843208 | tf_op jit(solution)/shard_map/ppermute | solution.py:960
  57.2 7.6 %collective-permute-start.23 = (bf16[400,768]{1,0:T(8,128)(2,1)S(1)}, bf16[400,768]{1,0:T(8,128)(2,1)S(1)}, u32[]{:S(2)}, u32[]{:S(2)}) collective-permute-start(bf16[400,768]{1,0:T(8,128)(2,1)S(1)} %collective-permute-done.7.refs_8_), channel_id=1, source_target_pairs={{0,2},{2,0},{4,6},{6,4},{8,10},{10,8},{12,14},{14,12},{16,18},{18,... | collective-permute-start | bytes 1843208 | tf_op jit(solution)/shard_map/ppermute | solution.py:960
  59.3 16.9 %collective-permute-start.6 = (bf16[400,768]{1,0:T(8,128)(2,1)S(1)}, bf16[400,768]{1,0:T(8,128)(2,1)}, u32[]{:S(2)}, u32[]{:S(2)}) collective-permute-start(bf16[400,768]{1,0:T(8,128)(2,1)S(1)} %collective-permute-done.4.refs_5_), channel_id=1, source_target_pairs={{0,1},{1,0},{2,3},{3,2},{4,5},{5,4},{6,7},{7,6},{8,9},{9,8},{10,11... | collective-permute-start | bytes 1843208 | tf_op jit(solution)/shard_map/ppermute | solution.py:968
  60.8 26.6 %collective-permute-start.11 = (bf16[400,768]{1,0:T(8,128)(2,1)S(1)}, bf16[400,768]{1,0:T(8,128)(2,1)}, u32[]{:S(2)}, u32[]{:S(2)}) collective-permute-start(bf16[400,768]{1,0:T(8,128)(2,1)S(1)} %collective-permute-done.9.refs_10_), channel_id=1, source_target_pairs={{0,1},{1,0},{2,3},{3,2},{4,5},{5,4},{6,7},{7,6},{8,9},{9,8},{10,11... | collective-permute-start | bytes 1843208 | tf_op jit(solution)/shard_map/ppermute | solution.py:968
  61.4 26.1 %collective-permute-start.12 = (bf16[400,768]{1,0:T(8,128)(2,1)S(1)}, bf16[400,768]{1,0:T(8,128)(2,1)}, u32[]{:S(2)}, u32[]{:S(2)}) collective-permute-start(bf16[400,768]{1,0:T(8,128)(2,1)S(1)} %collective-permute-done.10.refs_11_), channel_id=1, source_target_pairs={{0,4},{2,6},{4,0},{6,2},{8,12},{10,14},{12,8},{14,10},{16,20},{18,... | collective-permute-start | bytes 1843208 | tf_op jit(solution)/shard_map/ppermute | solution.py:964
  62.3 25.7 %collective-permute-start.13 = (bf16[400,768]{1,0:T(8,128)(2,1)S(1)}, bf16[400,768]{1,0:T(8,128)(2,1)}, u32[]{:S(2)}, u32[]{:S(2)}) collective-permute-start(bf16[400,768]{1,0:T(8,128)(2,1)S(1)} %collective-permute-done.8.refs_9_), channel_id=1, source_target_pairs={{0,8},{2,10},{4,12},{6,14},{8,0},{10,2},{12,4},{14,6},{16,24},{18,... | collective-permute-start | bytes 1843208 | tf_op jit(solution)/shard_map/ppermute | solution.py:972
  64.8 23.2 %collective-permute-start.19 = (bf16[400,768]{1,0:T(8,128)(2,1)S(1)}, bf16[400,768]{1,0:T(8,128)(2,1)S(1)}, u32[]{:S(2)}, u32[]{:S(2)}) collective-permute-start(bf16[400,768]{1,0:T(8,128)(2,1)S(1)} %collective-permute-done.3.refs_4_), channel_id=1, source_target_pairs={{0,2},{2,0},{4,6},{6,4},{8,10},{10,8},{12,14},{14,12},{16,18},{18,... | collective-permute-start | bytes 1843208 | tf_op jit(solution)/shard_map/ppermute | solution.py:960
  76.2 12.3 %collective-permute-start.20 = (bf16[400,768]{1,0:T(8,128)(2,1)S(1)}, bf16[400,768]{1,0:T(8,128)(2,1)S(1)}, u32[]{:S(2)}, u32[]{:S(2)}) collective-permute-start(bf16[400,768]{1,0:T(8,128)(2,1)S(1)} %collective-permute-done.4.refs_5_), channel_id=1, source_target_pairs={{0,2},{2,0},{4,6},{6,4},{8,10},{10,8},{12,14},{14,12},{16,18},{18,... | collective-permute-start | bytes 1843208 | tf_op jit(solution)/shard_map/ppermute | solution.py:960
  88.0 3.3 %collective-permute-start.25 = (bf16[400,768]{1,0:T(8,128)(2,1)S(1)}, bf16[400,768]{1,0:T(8,128)(2,1)S(1)}, u32[]{:S(2)}, u32[]{:S(2)}) collective-permute-start(bf16[400,768]{1,0:T(8,128)(2,1)S(1)} %collective-permute-done.9.refs_10_), channel_id=1, source_target_pairs={{0,2},{2,0},{4,6},{6,4},{8,10},{10,8},{12,14},{14,12},{16,18},{18,... | collective-permute-start | bytes 1843208 | tf_op jit(solution)/shard_map/ppermute | solution.py:960
  88.0 5.0 %collective-permute-start.26 = (bf16[400,768]{1,0:T(8,128)(2,1)S(1)}, bf16[400,768]{1,0:T(8,128)(2,1)S(1)}, u32[]{:S(2)}, u32[]{:S(2)}) collective-permute-start(bf16[400,768]{1,0:T(8,128)(2,1)S(1)} %collective-permute-done.10.refs_11_), channel_id=1, source_target_pairs={{0,2},{2,0},{4,6},{6,4},{8,10},{10,8},{12,14},{14,12},{16,18},{18,... | collective-permute-start | bytes 1843208 | tf_op jit(solution)/shard_map/ppermute | solution.py:960
  88.5 16.2 %collective-permute-start.14 = (bf16[400,768]{1,0:T(8,128)(2,1)}, bf16[400,768]{1,0:T(8,128)(2,1)}, u32[]{:S(2)}, u32[]{:S(2)}) collective-permute-start(bf16[400,768]{1,0:T(8,128)(2,1)} %collective-permute-done.13.refs_14_), channel_id=1, source_target_pairs={{0,4},{2,6},{4,0},{6,2},{8,12},{10,14},{12,8},{14,10},{16,20},{18,... | collective-permute-start | bytes 1843208 | tf_op jit(solution)/shard_map/ppermute | solution.py:964
  89.5 17.4 %collective-permute-start.29 = (bf16[400,768]{1,0:T(8,128)(2,1)}, bf16[400,768]{1,0:T(8,128)(2,1)}, u32[]{:S(2)}, u32[]{:S(2)}) collective-permute-start(bf16[400,768]{1,0:T(8,128)(2,1)} %collective-permute-done.13.refs_14_), channel_id=1, source_target_pairs={{0,2},{2,0},{4,6},{6,4},{8,10},{10,8},{12,14},{14,12},{16,18},{18,... | collective-permute-start | bytes 1843208 | tf_op jit(solution)/shard_map/ppermute | solution.py:960
  90.4 16.6 %collective-permute-start.22 = (bf16[400,768]{1,0:T(8,128)(2,1)}, bf16[400,768]{1,0:T(8,128)(2,1)}, u32[]{:S(2)}, u32[]{:S(2)}) collective-permute-start(bf16[400,768]{1,0:T(8,128)(2,1)} %collective-permute-done.6.refs_7_), channel_id=1, source_target_pairs={{0,2},{2,0},{4,6},{6,4},{8,10},{10,8},{12,14},{14,12},{16,18},{18,... | collective-permute-start | bytes 1843208 | tf_op jit(solution)/shard_map/ppermute | solution.py:960
  91.2 15.7 %collective-permute-start.27 = (bf16[400,768]{1,0:T(8,128)(2,1)}, bf16[400,768]{1,0:T(8,128)(2,1)}, u32[]{:S(2)}, u32[]{:S(2)}) collective-permute-start(bf16[400,768]{1,0:T(8,128)(2,1)} %collective-permute-done.11.refs_12_), channel_id=1, source_target_pairs={{0,2},{2,0},{4,6},{6,4},{8,10},{10,8},{12,14},{14,12},{16,18},{18,... | collective-permute-start | bytes 1843208 | tf_op jit(solution)/shard_map/ppermute | solution.py:960
  93.0 13.9 %collective-permute-start.28 = (bf16[400,768]{1,0:T(8,128)(2,1)}, bf16[400,768]{1,0:T(8,128)(2,1)}, u32[]{:S(2)}, u32[]{:S(2)}) collective-permute-start(bf16[400,768]{1,0:T(8,128)(2,1)} %collective-permute-done.12.refs_13_), channel_id=1, source_target_pairs={{0,2},{2,0},{4,6},{6,4},{8,10},{10,8},{12,14},{14,12},{16,18},{18,... | collective-permute-start | bytes 1843208 | tf_op jit(solution)/shard_map/ppermute | solution.py:960
  126.5 15.0 %collective-permute-start.31 = (bf16[3,112,768]{2,1,0:T(8,128)(2,1)}, bf16[3,112,768]{2,1,0:T(8,128)(2,1)S(1)}, u32[]{:S(2)}, u32[]{:S(2)}) collective-permute-start(bf16[3,112,768]{2,1,0:T(8,128)(2,1)} %get-tuple-element.80.refs_2_), channel_id=1, source_target_pairs={{0,1},{1,0},{2,3},{3,2},{4,5},{5,4},{6,7},{7,6},{8,9},{9,8},{10,11... | collective-permute-start | bytes 1548296 | tf_op jit(solution)/shard_map/ppermute | solution.py:968
  128.8 12.6 %collective-permute-start.32 = (f32[3,8,224]{2,1,0:T(8,128)}, f32[3,8,224]{2,1,0:T(8,128)S(1)}, u32[]{:S(2)}, u32[]{:S(2)}) collective-permute-start(f32[3,8,224]{2,1,0:T(8,128)} %get-tuple-element.81.refs_4_), channel_id=1, source_target_pairs={{0,1},{1,0},{2,3},{3,2},{4,5},{5,4},{6,7},{7,6},{8,9},{9,8},{10,11... | collective-permute-start | bytes 64520 | tf_op jit(solution)/shard_map/ppermute | solution.py:968
  168.6 10.1 %collective-permute-start.33 = (bf16[2,2,784,768]{3,2,1,0:T(8,128)(2,1)}, bf16[2,2,784,768]{3,2,1,0:T(8,128)(2,1)}, u32[]{:S(2)}, u32[]{:S(2)}) collective-permute-start(bf16[2,2,784,768]{3,2,1,0:T(8,128)(2,1)} %get-tuple-element.94), channel_id=1, source_target_pairs={{0,2},{2,0},{4,6},{6,4},{8,10},{10,8},{12,14},{14,12},{16,18},{18,... | collective-permute-start | bytes 14450696 | tf_op jit(solution)/shard_map/ppermute | solution.py:960
  182.5 36.3 %collective-permute-start.36 = (bf16[2,392,768]{2,1,0:T(8,128)(2,1)}, bf16[2,392,768]{2,1,0:T(8,128)(2,1)}, u32[]{:S(2)}, u32[]{:S(2)}) collective-permute-start(bf16[2,392,768]{2,1,0:T(8,128)(2,1)} %far_send.1), channel_id=1, source_target_pairs={{0,4},{2,6},{4,0},{6,2},{8,12},{10,14},{12,8},{14,10},{16,20},{18,... | collective-permute-start | bytes 3612680 | tf_op jit(solution)/shard_map/ppermute | solution.py:964
  183.9 13.9 %collective-permute-start.34 = (bf16[3,112,768]{2,1,0:T(8,128)(2,1)S(1)}, bf16[3,112,768]{2,1,0:T(8,128)(2,1)S(1)}, u32[]{:S(2)}, u32[]{:S(2)}) collective-permute-start(bf16[3,112,768]{2,1,0:T(8,128)(2,1)S(1)} %copy-done.29), channel_id=1, source_target_pairs={{0,1},{1,0},{2,3},{3,2},{4,5},{5,4},{6,7},{7,6},{8,9},{9,8},{10,11... | collective-permute-start | bytes 1548296 | tf_op jit(solution)/shard_map/ppermute | solution.py:968
  194.8 10.6 %collective-permute-start.35 = (f32[8,768]{1,0:T(8,128)}, f32[8,768]{1,0:T(8,128)S(1)}, u32[]{:S(2)}, u32[]{:S(2)}) collective-permute-start(f32[8,768]{1,0:T(8,128)} %get-tuple-element.106), channel_id=1, source_target_pairs={{0,1},{1,0},{2,3},{3,2},{4,5},{5,4},{6,7},{7,6},{8,9},{9,8},{10,11... | collective-permute-start | bytes 73736 | tf_op jit(solution)/shard_map/ppermute | solution.py:968
  205.3 14.0 %collective-permute-start.38 = (bf16[2,784,768]{2,1,0:T(8,128)(2,1)}, bf16[2,784,768]{2,1,0:T(8,128)(2,1)S(1)}, u32[]{:S(2)}, u32[]{:S(2)}) collective-permute-start(bf16[2,784,768]{2,1,0:T(8,128)(2,1)} %get-tuple-element.114), channel_id=1, source_target_pairs={{0,2},{2,0},{4,6},{6,4},{8,10},{10,8},{12,14},{14,12},{16,18},{18,... | collective-permute-start | bytes 7225352 | tf_op jit(solution)/shard_map/ppermute | solution.py:960
  218.8 6.3 %collective-permute-start.37 = (bf16[2,784,768]{2,1,0:T(8,128)(2,1)}, bf16[2,784,768]{2,1,0:T(8,128)(2,1)}, u32[]{:S(2)}, u32[]{:S(2)}) collective-permute-start(bf16[2,784,768]{2,1,0:T(8,128)(2,1)} %get-tuple-element.112), channel_id=1, source_target_pairs={{0,2},{2,0},{4,6},{6,4},{8,10},{10,8},{12,14},{14,12},{16,18},{18,... | collective-permute-start | bytes 7225352 | tf_op jit(solution)/shard_map/ppermute | solution.py:960
  225.1 20.0 %collective-permute-start.39 = (bf16[480,768]{1,0:T(8,128)(2,1)}, bf16[480,768]{1,0:T(8,128)(2,1)S(1)}, u32[]{:S(2)}, u32[]{:S(2)}) collective-permute-start(bf16[480,768]{1,0:T(8,128)(2,1)} %get-tuple-element.123), channel_id=1, source_target_pairs={{0,1},{1,0},{2,3},{3,2},{4,5},{5,4},{6,7},{7,6},{8,9},{9,8},{10,11... | collective-permute-start | bytes 2211848 | tf_op jit(solution)/shard_map/ppermute | solution.py:968
  228.4 17.3 %collective-permute-start.42 = (f32[24,768]{1,0:T(8,128)S(1)}, f32[24,768]{1,0:T(8,128)S(1)}, u32[]{:S(2)}, u32[]{:S(2)}) collective-permute-start(f32[24,768]{1,0:T(8,128)S(1)} %add.150), channel_id=1, source_target_pairs={{0,4},{2,6},{4,0},{6,2},{8,12},{10,14},{12,8},{14,10},{16,20},{18,... | collective-permute-start | bytes 221192 | tf_op jit(solution)/shard_map/ppermute | solution.py:964
  230.7 15.5 %collective-permute-start.40 = (bf16[392,768]{1,0:T(8,128)(2,1)S(1)}, bf16[392,768]{1,0:T(8,128)(2,1)}, u32[]{:S(2)}, u32[]{:S(2)}) collective-permute-start(bf16[392,768]{1,0:T(8,128)(2,1)S(1)} %fusion.8), channel_id=1, source_target_pairs={{0,4},{2,6},{4,0},{6,2},{8,12},{10,14},{12,8},{14,10},{16,20},{18,... | collective-permute-start | bytes 1806344 | tf_op jit(solution)/shard_map/ppermute | solution.py:964
  235.6 17.1 %collective-permute-start.46 = (bf16[392,768]{1,0:T(8,128)(2,1)}, bf16[392,768]{1,0:T(8,128)(2,1)S(1)}, u32[]{:S(2)}, u32[]{:S(2)}) collective-permute-start(bf16[392,768]{1,0:T(8,128)(2,1)} %get-tuple-element.144), channel_id=1, source_target_pairs={{0,8},{2,10},{4,12},{6,14},{8,0},{10,2},{12,4},{14,6},{16,24},{18,... | collective-permute-start | bytes 1806344 | tf_op jit(solution)/shard_map/ppermute | solution.py:972
  247.9 17.7 %collective-permute-start.43 = (bf16[392,768]{1,0:T(8,128)(2,1)S(1)}, bf16[392,768]{1,0:T(8,128)(2,1)S(1)}, u32[]{:S(2)}, u32[]{:S(2)}) collective-permute-start(bf16[392,768]{1,0:T(8,128)(2,1)S(1)} %fusion.7), channel_id=1, source_target_pairs={{24,16},{26,18},{28,20},{30,22},{8,0},{10,2},{12,4},{14,6},{25,17}... | collective-permute-start | bytes 1806344 | tf_op jit(solution)/shard_map/ppermute | solution.py:972
  252.1 14.3 %collective-permute-start.44 = (bf16[392,768]{1,0:T(8,128)(2,1)S(1)}, bf16[392,768]{1,0:T(8,128)(2,1)S(1)}, u32[]{:S(2)}, u32[]{:S(2)}) collective-permute-start(bf16[392,768]{1,0:T(8,128)(2,1)S(1)} %get-tuple-element.140), channel_id=1, source_target_pairs={{0,4},{2,6},{4,0},{6,2},{8,12},{10,14},{12,8},{14,10},{16,20},{18,... | collective-permute-start | bytes 1806344 | tf_op jit(solution)/shard_map/ppermute | solution.py:964
  252.6 13.1 %collective-permute-start.45 = (f32[24,768]{1,0:T(8,128)S(1)}, f32[24,768]{1,0:T(8,128)S(1)}, u32[]{:S(2)}, u32[]{:S(2)}) collective-permute-start(f32[24,768]{1,0:T(8,128)S(1)} %add.155), channel_id=1, source_target_pairs={{0,8},{2,10},{4,12},{6,14},{8,0},{10,2},{12,4},{14,6},{16,24},{18,... | collective-permute-start | bytes 221192 | tf_op jit(solution)/shard_map/ppermute | solution.py:972
  266.6 18.4 %collective-permute-start.48 = (bf16[392,768]{1,0:T(8,128)(2,1)S(1)}, bf16[392,768]{1,0:T(8,128)(2,1)S(1)}, u32[]{:S(2)}, u32[]{:S(2)}) collective-permute-start(bf16[392,768]{1,0:T(8,128)(2,1)S(1)} %add_convert_fusion.2), channel_id=1, source_target_pairs={{24,16},{26,18},{28,20},{30,22},{0,8},{2,10},{4,12},{6,14},{25,17}... | collective-permute-start | bytes 1806344 | tf_op jit(solution)/shard_map/ppermute | solution.py:972
  267.9 17.2 %collective-permute-start.47 = (bf16[392,768]{1,0:T(8,128)(2,1)S(1)}, bf16[392,768]{1,0:T(8,128)(2,1)S(1)}, u32[]{:S(2)}, u32[]{:S(2)}) collective-permute-start(bf16[392,768]{1,0:T(8,128)(2,1)S(1)} %add_convert_fusion.3), channel_id=1, source_target_pairs={{16,0},{18,2},{20,4},{22,6},{17,1},{19,3},{21,5},{23,7}} | collective-permute-start | bytes 1806344 | tf_op jit(solution)/shard_map/ppermute | solution.py:972
  268.6 16.5 %collective-permute-start.49 = (bf16[192,768]{1,0:T(8,128)(2,1)S(1)}, bf16[192,768]{1,0:T(8,128)(2,1)S(1)}, u32[]{:S(2)}, u32[]{:S(2)}) collective-permute-start(bf16[192,768]{1,0:T(8,128)(2,1)S(1)} %slice.55), channel_id=1, source_target_pairs={{0,16},{2,18},{4,20},{6,22},{8,24},{10,26},{12,28},{14,30},{1,17},... | collective-permute-start | bytes 884744 | tf_op jit(solution)/shard_map/ppermute | solution.py:972
  285.2 18.8 %collective-permute-start.51 = (bf16[392,768]{1,0:T(8,128)(2,1)S(1)}, bf16[392,768]{1,0:T(8,128)(2,1)}, u32[]{:S(2)}, u32[]{:S(2)}) collective-permute-start(bf16[392,768]{1,0:T(8,128)(2,1)S(1)} %add_convert_fusion), channel_id=1, source_target_pairs={{16,8},{18,10},{20,12},{22,14},{17,9},{19,11},{21,13},{23,15}} | collective-permute-start | bytes 1806344 | tf_op jit(solution)/shard_map/ppermute | solution.py:972
  287.2 15.0 %collective-permute-start.50 = (bf16[224,768]{1,0:T(8,128)(2,1)}, bf16[224,768]{1,0:T(8,128)(2,1)}, u32[]{:S(2)}, u32[]{:S(2)}) collective-permute-start(bf16[224,768]{1,0:T(8,128)(2,1)} %pad_maximum_fusion), channel_id=1, source_target_pairs={{0,16},{2,18},{4,20},{6,22},{8,24},{10,26},{12,28},{14,30},{1,17},... | collective-permute-start | bytes 1032200 | tf_op jit(solution)/shard_map/ppermute | solution.py:972
  (46 other events, 1235.8 us)

commit v6 on v5

--- a/solution.py
+++ b/solution.py
@@ -988,7 +988,7 @@
 
 def gather(at, rows):
     rest = jnp.zeros((8, D), BF16)
-    own = jnp.where(at.x == 0, jnp.concatenate([rows, rest]), jnp.concatenate([rows[8:], rows[:8], rest]))
+    own = lax.dynamic_slice_in_dim(jnp.concatenate([rows, rows[:8], rest]), 8 * at.x, rows.shape[0] + 8)
     other = over_far(own)
     here, there = spread(own), spread(other)
     found = [*here, over_x(here[5]), *there, over_y(there[6])]

time: 313 us -> 313 us (level)
  no operation moved by 1% of the time
where the time goes in v6:
time: 313 us; the launch traced here: 307 us
  waiting for transfers between devices  128 us (41%)
  Pallas kernels  105 us (34%)
  starting transfers between devices  51 us (16%)
  other arithmetic  12.6 us (4%)
  local copies, waits for them, and re-layouts  9.15 us (3%)
    ppermute x13, waiting for transfers between devices, over_z(): lax.ppermute(v, 'dp', [(4 * a + i, 4 * b + i) for a, b in hops for i in r...  46.8 us
    ppermute x9, waiting for transfers between devices, over_y(): return lax.ppermute(v, 'dp', [(i, i ^ 2) for i in range(16)])  39.4 us
    ppermute x10, waiting for transfers between devices, over_x(): return lax.ppermute(v, 'seq', [(0, 1), (1, 0)])  37.2 us
    ppermute x13, starting transfers between devices, over_z(): lax.ppermute(v, 'dp', [(4 * a + i, 4 * b + i) for a, b in hops for i in r...  28.5 us
    pallas_call x1, Pallas kernels, middle(): pl.pallas_call(partial(middle_kernel, parts, split), grid_spec=pltpu.Pref...  26.3 us
    pallas_call x1, Pallas kernels, forward(): pl.pallas_call(partial(forward_kernel, queries, custom), grid_spec=pltpu....  19.2 us
    pallas_call x1, Pallas kernels, self_backward(): pl.pallas_call(partial(self_backward_kernel, queries, split), grid_spec=p...  13.4 us
    ppermute x10, starting transfers between devices, over_x(): return lax.ppermute(v, 'seq', [(0, 1), (1, 0)])  11.6 us
  transfers between devices with their start and end apart: 52, of which 24 were waited for; matrix products, arithmetic and copies ran while one was open for 4% of the time, Pallas kernels for 18%

profile of v6, /device:TPU:8, one launch (start us, length us, event | category | flops | bytes accessed | tf_op | source)
XLA Modules:
  0.0 307.1 jit_solution(4786440875437021648)
XLA Ops:
  2.8 1.6 collective-permute-start.1
  4.8 1.5 collective-permute-start
  6.3 2.6 collective-permute-start.7
  8.9 9.5 %collective-permute-done.1.refs_2_ = bf16[400,768]{1,0:T(8,128)(2,1)S(1)} collective-permute-done((bf16[400,768]{1,0:T(8,128)(2,1)S(1)}, bf16[400,768]{1,0:T(8,128)(2,1)S(1)}, u32[]{:S(2)}, u32[]{:S(2)}) %collective-permute-start.1) | collective-permute-done | bytes 614432 | tf_op jit(solution)/shard_map/ppermute | solution.py:964
  18.4 1.5 collective-permute-start.3
  19.9 9.6 %collective-permute-done.2.refs_3_ = bf16[400,768]{1,0:T(8,128)(2,1)S(1)} collective-permute-done((bf16[400,768]{1,0:T(8,128)(2,1)S(1)}, bf16[400,768]{1,0:T(8,128)(2,1)S(1)}, u32[]{:S(2)}, u32[]{:S(2)}) %collective-permute-start.2) | collective-permute-done | bytes 614432 | tf_op jit(solution)/shard_map/ppermute | solution.py:972
  29.9 2.5 collective-permute-start.5
  32.3 2.7 collective-permute-done.7.refs_8_
  36.5 1.4 collective-permute-start.10
  37.9 8.4 %collective-permute-done.4.refs_5_ = bf16[400,768]{1,0:T(8,128)(2,1)S(1)} collective-permute-done((bf16[400,768]{1,0:T(8,128)(2,1)S(1)}, bf16[400,768]{1,0:T(8,128)(2,1)S(1)}, u32[]{:S(2)}, u32[]{:S(2)}) %collective-permute-start.4) | collective-permute-done | bytes 614432 | tf_op jit(solution)/shard_map/ppermute | solution.py:964
  48.3 8.7 %collective-permute-done.9.refs_10_ = bf16[400,768]{1,0:T(8,128)(2,1)S(1)} collective-permute-done((bf16[400,768]{1,0:T(8,128)(2,1)S(1)}, bf16[400,768]{1,0:T(8,128)(2,1)S(1)}, u32[]{:S(2)}, u32[]{:S(2)}) %collective-permute-start.9) | collective-permute-done | bytes 614432 | tf_op jit(solution)/shard_map/ppermute | solution.py:964
  57.1 2.2 collective-permute-done.10.refs_11_
  59.2 1.5 collective-permute-start.6
  62.2 2.5 collective-permute-start.13
  64.8 11.4 %collective-permute-done.6.refs_7_ = bf16[400,768]{1,0:T(8,128)(2,1)} collective-permute-done((bf16[400,768]{1,0:T(8,128)(2,1)S(1)}, bf16[400,768]{1,0:T(8,128)(2,1)}, u32[]{:S(2)}, u32[]{:S(2)}) %collective-permute-start.6) | collective-permute-done | bytes 614432 | tf_op jit(solution)/shard_map/ppermute | solution.py:968
  76.1 11.2 %collective-permute-done.11.refs_12_ = bf16[400,768]{1,0:T(8,128)(2,1)} collective-permute-done((bf16[400,768]{1,0:T(8,128)(2,1)S(1)}, bf16[400,768]{1,0:T(8,128)(2,1)}, u32[]{:S(2)}, u32[]{:S(2)}) %collective-permute-start.11) | collective-permute-done | bytes 614432 | tf_op jit(solution)/shard_map/ppermute | solution.py:968
  91.3 1.6 collective-permute-done.26.refs_27_
  93.0 11.6 %collective-permute-done.14.refs_15_ = bf16[400,768]{1,0:T(8,128)(2,1)} collective-permute-done((bf16[400,768]{1,0:T(8,128)(2,1)}, bf16[400,768]{1,0:T(8,128)(2,1)}, u32[]{:S(2)}, u32[]{:S(2)}) %collective-permute-start.14) | collective-permute-done | bytes 614432 | tf_op jit(solution)/shard_map/ppermute | solution.py:964
  107.2 19.2 %forward.1 = (bf16[336,768]{1,0:T(8,128)(2,1)}, bf16[336,768]{1,0:T(8,128)(2,1)}, bf16[336,768]{1,0:T(8,128)(2,1)}, bf16[336,768]{1,0:T(8,128)(2,1)}, f32[336,76...) custom-call(s32[3]{0:T(128)} %broadcast_subtract_fusion.left_ref, ...), custom_call_target="tpu_custom_call" | custom-call | tf_op jit(solution)/shard_map/forward/pallas_call | solution.py:312
  126.4 1.8 collective-permute-start.31
  129.0 1.4 slice_convert_fusion.refs_7_
  130.4 11.0 %collective-permute-done.32.refs_5_ = f32[3,8,224]{2,1,0:T(8,128)S(1)} collective-permute-done((f32[3,8,224]{2,1,0:T(8,128)}, f32[3,8,224]{2,1,0:T(8,128)S(1)}, u32[]{:S(2)}, u32[]{:S(2)}) %collective-permute-start.32) | collective-permute-done | bytes 21536 | tf_op jit(solution)/shard_map/ppermute | solution.py:968
  142.2 26.3 %middle.1 = (f32[3,112,768]{2,1,0:T(8,128)}, bf16[2,2,784,768]{3,2,1,0:T(8,128)(2,1)}, bf16[2,2,784,768]{3,2,1,0:T(8,128)(2,1)}, bf16[2,784,768]{2,1,0:T(8,128)(...) custom-call(s32[4]{0:T(128)} %pad_add_fusion.flags.refs_0_, ...), custom_call_target="tpu_custom_call" | custom-call | flops 10701766 | bytes 28311 | tf_op jit(solution)/shard_map/middle/pallas_call | solution.py:603
  168.6 10.0 %cross_backward.1 = (bf16[3,112,768]{2,1,0:T(8,128)(2,1)}, bf16[3,512,768]{2,1,0:T(8,128)(2,1)}, bf16[3,512,768]{2,1,0:T(8,128)(2,1)}) custom-call(s32[3]{0:T(128)} %broadcast_subtract_fusion.left_ref, bf16[3,112,768]{2,1,0:T(8,128)(2,1)} %bitcast.43, bf16[3,512,768]{2,1,0:T(8,128)(2,1)} %get-tuple-element.88.k_ref, ...), custom_call_target="tpu_custom_call" | custom-call | flops 352321 | bytes 9437 | tf_op jit(solution)/shard_map/cross_backward/pallas_call | solution.py:684
  178.7 3.8 %far_send.1 = bf16[2,392,768]{2,1,0:T(8,128)(2,1)} custom-call(s32[4]{0:T(128)} %pad_add_fusion.flags.refs_0_, bf16[2,2,2,392,768]{4,3,2,1,0:T(8,128)(2,1)} %bitcast.30, bf16[2,2,2,392,768]{4,3,2,1,0:T(8,128)(2,1)} %bitcast.10.b.d.refs_1_.refs_4_, bf16[2,2,2,392,768]{4,3,2,1,0:T(8,128)(2,1)} %bitcast.31, bf16[2,2,2,392,768]{4,3,2,1,0:T(8,128)(2,1)} %bitcast.10.b.d.refs_1_.refs_4_), custom_call_target="tpu_custom_call" | custom-call | tf_op jit(solution)/shard_map/far_send/pallas_call | solution.py:1026
  182.5 1.4 collective-permute-start.36
  183.9 1.6 collective-permute-start.34
  185.5 9.3 %memory_weights.1 = (f32[8,768]{1,0:T(8,128)}, bf16[2,784,768]{2,1,0:T(8,128)(2,1)}, bf16[2,784,768]{2,1,0:T(8,128)(2,1)}) custom-call(s32[4]{0:T(128)} %pad_add_fusion.flags.refs_0_, bf16[2,784,768]{2,1,0:T(8,128)(2,1)} %get-tuple-element.85.refs_0_, bf16[2,784,768]{2,1,0:T(8,128)(2,1)} %get-tuple-element.86.refs_1_, ...), custom_call_target="tpu_custom_call", output_to_operand_aliasing={{1}: (1, {}), {2}: (2, {})} | custom-call | flops 3623878 | bytes 7077 | tf_op jit(solution)/shard_map/memory_weights/pallas_call | solution.py:728
  195.3 2.5 collective-permute-done.34
  198.6 6.8 %query_backward.1 = (f32[336,768]{1,0:T(8,128)}, bf16[64,768]{1,0:T(8,128)(2,1)}, f32[24,768]{1,0:T(8,128)}, bf16[2,784,768]{2,1,0:T(8,128)(2,1)}, bf16[2,784,768]{2,1,0:T(8,128)(2,1)}) custom-call(s32[4]{0:T(128)} %pad_add_fusion.flags.refs_0_, bf16[2,784,768]{2,1,0:T(8,128)(2,1)} %get-tuple-element.97.refs_0_, ...), custom_call_target="tpu_custom_call", output_to_operand_aliasing={{3}: (1, {}), {4}: (2, {})} | custom-call | flops 792723 | bytes 4128 | tf_op jit(solution)/shard_map/query_backward/pallas_call | solution.py:827
  205.5 13.4 %self_backward.1 = (f32[3,112,768]{2,1,0:T(8,128)}, f32[24,768]{1,0:T(8,128)}, bf16[2,784,768]{2,1,0:T(8,128)(2,1)}, bf16[2,784,768]{2,1,0:T(8,128)(2,1)}) custom-call(s32[4]{0:T(128)} %pad_add_fusion.flags.refs_0_, bf16[336,768]{1,0:T(8,128)(2,1)} %get-tuple-element.84.refs_1_, f32[336,768]{1,0:T(8,128)} %get-tuple-element.101.refs_2_, ...), custom_call_target="tpu_custom_call" | custom-call | flops 6341787 | bytes 9437 | tf_op jit(solution)/shard_map/self_backward/pallas_call | solution.py:921
  219.4 1.5 copy-done
  220.9 4.2 %cross_merge.1 = (bf16[392,768]{1,0:T(8,128)(2,1)}, bf16[392,768]{1,0:T(8,128)(2,1)}, bf16[480,768]{1,0:T(8,128)(2,1)}) custom-call(s32[4]{0:T(128)} %pad_add_fusion.flags.refs_0_, bf16[2,2,392,768]{3,2,1,0:T(8,128)(2,1)} %bitcast.26, bf16[2,2,392,768]{3,2,1,0:T(8,128)(2,1)} %bitcast.34, bf16[2,2,392,768]{3,2,1,0:T(8,128)(2,1)} %bitcast.27, ...), custom_call_target="tpu_custom_call" | custom-call | tf_op jit(solution)/shard_map/cross_merge/pallas_call | solution.py:1026
  225.1 1.9 collective-permute-start.39
  229.3 1.4 fusion.10
  231.9 3.6 %far_merge.1 = (bf16[392,768]{1,0:T(8,128)(2,1)}, bf16[392,768]{1,0:T(8,128)(2,1)}) custom-call(s32[4]{0:T(128)} %pad_add_fusion.flags.refs_0_, bf16[2,2,2,392,768]{4,3,2,1,0:T(8,128)(2,1)} %bitcast.32, bf16[2,2,2,392,768]{4,3,2,1,0:T(8,128)(2,1)} %bitcast.10.b.d.refs_1_.refs_4_, bf16[2,392,768]{2,1,0:T(8,128)(2,1)} %collective-permute-done.36.refs_2_.refs_5_, ...), custom_call_target="tpu_custom_call" | custom-call | tf_op jit(solution)/shard_map/far_merge/pallas_call | solution.py:1026
  235.6 1.4 collective-permute-start.46
  237.0 8.0 %memory_grads.1 = f32[3,512,768]{2,1,0:T(8,128)} custom-call(bf16[3,512,768]{2,1,0:T(8,128)(2,1)} %get-tuple-element.120.refs_3_.dk_ref, bf16[3,512,768]{2,1,0:T(8,128)(2,1)} %get-tuple-element.121.refs_4_.dv_ref, bf16[12544,768]{1,0:T(8,128)(2,1)} %get-tuple-element.122.refs_6_.refs_7_.ck.cv, bf16[12544,768]{1,0:T(8,128)(2,1)} %get-tuple-element.122.refs_6_.refs_7_.ck.cv), custom_call_target="tpu_custom_call" | custom-call | flops 3623878656 | bytes 9437184 | tf_op jit(solution)/shard_map/memory_grads/pallas_call | solution.py:755
  246.2 1.7 fusion.7
  247.9 4.1 %collective-permute-start.43 = (bf16[392,768]{1,0:T(8,128)(2,1)S(1)}, bf16[392,768]{1,0:T(8,128)(2,1)S(1)}, u32[]{:S(2)}, u32[]{:S(2)}) collective-permute-start(bf16[392,768]{1,0:T(8,128)(2,1)S(1)} %fusion.7), channel_id=1, source_target_pairs={{24,16},{26,18},{28,20},{30,22},{8,0},{10,2},{12,4},{14,6},{25,17}... | collective-permute-start | bytes 1806344 | tf_op jit(solution)/shard_map/ppermute | solution.py:972
  252.7 12.9 %collective-permute-done.45 = f32[24,768]{1,0:T(8,128)S(1)} collective-permute-done((f32[24,768]{1,0:T(8,128)S(1)}, f32[24,768]{1,0:T(8,128)S(1)}, u32[]{:S(2)}, u32[]{:S(2)}) %collective-permute-start.45) | collective-permute-done | bytes 73760 | tf_op jit(solution)/shard_map/ppermute | solution.py:972
  266.5 1.3 collective-permute-start.48
  268.5 6.8 %collective-permute-start.49 = (bf16[192,768]{1,0:T(8,128)(2,1)S(1)}, bf16[192,768]{1,0:T(8,128)(2,1)S(1)}, u32[]{:S(2)}, u32[]{:S(2)}) collective-permute-start(bf16[192,768]{1,0:T(8,128)(2,1)S(1)} %slice.47), channel_id=1, source_target_pairs={{0,16},{2,18},{4,20},{6,22},{8,24},{10,26},{12,28},{14,30},{1,17},... | collective-permute-start | bytes 884744 | tf_op jit(solution)/shard_map/ppermute | solution.py:972
  275.4 9.5 %collective-permute-done.48 = bf16[392,768]{1,0:T(8,128)(2,1)S(1)} collective-permute-done((bf16[392,768]{1,0:T(8,128)(2,1)S(1)}, bf16[392,768]{1,0:T(8,128)(2,1)S(1)}, u32[]{:S(2)}, u32[]{:S(2)}) %collective-permute-start.48) | collective-permute-done | bytes 602144 | tf_op jit(solution)/shard_map/ppermute | solution.py:972
  285.1 1.3 collective-permute-start.51
  287.2 3.4 %collective-permute-start.50 = (bf16[224,768]{1,0:T(8,128)(2,1)}, bf16[224,768]{1,0:T(8,128)(2,1)}, u32[]{:S(2)}, u32[]{:S(2)}) collective-permute-start(bf16[224,768]{1,0:T(8,128)(2,1)} %pad_maximum_fusion), channel_id=1, source_target_pairs={{0,16},{2,18},{4,20},{6,22},{8,24},{10,26},{12,28},{14,30},{1,17},... | collective-permute-start | bytes 1032200 | tf_op jit(solution)/shard_map/ppermute | solution.py:972
  293.2 9.1 %collective-permute-done.50 = bf16[224,768]{1,0:T(8,128)(2,1)} collective-permute-done((bf16[224,768]{1,0:T(8,128)(2,1)}, bf16[224,768]{1,0:T(8,128)(2,1)}, u32[]{:S(2)}, u32[]{:S(2)}) %collective-permute-start.50) | collective-permute-done | bytes 344096 | tf_op jit(solution)/shard_map/ppermute | solution.py:972
  304.1 1.6 convert_add_fusion
  (186 shorter events, 31.6 us)
Async XLA Ops:
  2.8 15.7 %collective-permute-start.1 = (bf16[400,768]{1,0:T(8,128)(2,1)S(1)}, bf16[400,768]{1,0:T(8,128)(2,1)S(1)}, u32[]{:S(2)}, u32[]{:S(2)}) collective-permute-start(bf16[400,768]{1,0:T(8,128)(2,1)S(1)} %fusion.9.refs_0_), channel_id=1, source_target_pairs={{0,4},{2,6},{4,0},{6,2},{8,12},{10,14},{12,8},{14,10},{16,20},{18,... | collective-permute-start | bytes 1843208 | tf_op jit(solution)/shard_map/ppermute | solution.py:964
  4.4 25.1 %collective-permute-start.2 = (bf16[400,768]{1,0:T(8,128)(2,1)S(1)}, bf16[400,768]{1,0:T(8,128)(2,1)S(1)}, u32[]{:S(2)}, u32[]{:S(2)}) collective-permute-start(bf16[400,768]{1,0:T(8,128)(2,1)S(1)} %fusion.9.refs_0_), channel_id=1, source_target_pairs={{0,8},{2,10},{4,12},{6,14},{8,0},{10,2},{12,4},{14,6},{16,24},{18,... | collective-permute-start | bytes 1843208 | tf_op jit(solution)/shard_map/ppermute | solution.py:972
  4.8 25.0 %collective-permute-start = (bf16[400,768]{1,0:T(8,128)(2,1)S(1)}, bf16[400,768]{1,0:T(8,128)(2,1)S(1)}, u32[]{:S(2)}, u32[]{:S(2)}) collective-permute-start(bf16[400,768]{1,0:T(8,128)(2,1)S(1)} %fusion.9.refs_0_), channel_id=1, source_target_pairs={{0,1},{1,0},{2,3},{3,2},{4,5},{5,4},{6,7},{7,6},{8,9},{9,8},{10,11... | collective-permute-start | bytes 1843208 | tf_op jit(solution)/shard_map/ppermute | solution.py:968
  6.3 28.7 %collective-permute-start.7 = (bf16[400,768]{1,0:T(8,128)(2,1)S(1)}, bf16[400,768]{1,0:T(8,128)(2,1)S(1)}, u32[]{:S(2)}, u32[]{:S(2)}) collective-permute-start(bf16[400,768]{1,0:T(8,128)(2,1)S(1)} %fusion.9.refs_0_), channel_id=1, source_target_pairs={{0,16},{2,18},{4,20},{6,22},{16,0},{18,2},{20,4},{22,6},{8,24},{10... | collective-permute-start | bytes 1843208 | tf_op jit(solution)/shard_map/ppermute | solution.py:972
  8.9 26.7 %collective-permute-start.15 = (bf16[400,768]{1,0:T(8,128)(2,1)S(1)}, bf16[400,768]{1,0:T(8,128)(2,1)S(1)}, u32[]{:S(2)}, u32[]{:S(2)}) collective-permute-start(bf16[400,768]{1,0:T(8,128)(2,1)S(1)} %fusion.9.refs_0_), channel_id=1, source_target_pairs={{0,2},{2,0},{4,6},{6,4},{8,10},{10,8},{12,14},{14,12},{16,18},{18,... | collective-permute-start | bytes 1843208 | tf_op jit(solution)/shard_map/ppermute | solution.py:960
  18.4 18.0 %collective-permute-start.3 = (bf16[400,768]{1,0:T(8,128)(2,1)S(1)}, bf16[400,768]{1,0:T(8,128)(2,1)S(1)}, u32[]{:S(2)}, u32[]{:S(2)}) collective-permute-start(bf16[400,768]{1,0:T(8,128)(2,1)S(1)} %collective-permute-done.1.refs_2_), channel_id=1, source_target_pairs={{0,1},{1,0},{2,3},{3,2},{4,5},{5,4},{6,7},{7,6},{8,9},{9,8},{10,11... | collective-permute-start | bytes 1843208 | tf_op jit(solution)/shard_map/ppermute | solution.py:968
  29.5 16.8 %collective-permute-start.4 = (bf16[400,768]{1,0:T(8,128)(2,1)S(1)}, bf16[400,768]{1,0:T(8,128)(2,1)S(1)}, u32[]{:S(2)}, u32[]{:S(2)}) collective-permute-start(bf16[400,768]{1,0:T(8,128)(2,1)S(1)} %collective-permute-done.2.refs_3_), channel_id=1, source_target_pairs={{0,4},{2,6},{4,0},{6,2},{8,12},{10,14},{12,8},{14,10},{16,20},{18,... | collective-permute-start | bytes 1843208 | tf_op jit(solution)/shard_map/ppermute | solution.py:964
  29.9 17.3 %collective-permute-start.5 = (bf16[400,768]{1,0:T(8,128)(2,1)S(1)}, bf16[400,768]{1,0:T(8,128)(2,1)S(1)}, u32[]{:S(2)}, u32[]{:S(2)}) collective-permute-start(bf16[400,768]{1,0:T(8,128)(2,1)S(1)} %collective-permute-done.refs_1_), channel_id=1, source_target_pairs={{0,8},{2,10},{4,12},{6,14},{8,0},{10,2},{12,4},{14,6},{16,24},{18,... | collective-permute-start | bytes 1843208 | tf_op jit(solution)/shard_map/ppermute | solution.py:972
  35.0 13.3 %collective-permute-start.8 = (bf16[400,768]{1,0:T(8,128)(2,1)S(1)}, bf16[400,768]{1,0:T(8,128)(2,1)S(1)}, u32[]{:S(2)}, u32[]{:S(2)}) collective-permute-start(bf16[400,768]{1,0:T(8,128)(2,1)S(1)} %collective-permute-done.7.refs_8_), channel_id=1, source_target_pairs={{0,1},{1,0},{2,3},{3,2},{4,5},{5,4},{6,7},{7,6},{8,9},{9,8},{10,11... | collective-permute-start | bytes 1843208 | tf_op jit(solution)/shard_map/ppermute | solution.py:968
  35.6 21.5 %collective-permute-start.9 = (bf16[400,768]{1,0:T(8,128)(2,1)S(1)}, bf16[400,768]{1,0:T(8,128)(2,1)S(1)}, u32[]{:S(2)}, u32[]{:S(2)}) collective-permute-start(bf16[400,768]{1,0:T(8,128)(2,1)S(1)} %collective-permute-done.7.refs_8_), channel_id=1, source_target_pairs={{0,4},{2,6},{4,0},{6,2},{8,12},{10,14},{12,8},{14,10},{16,20},{18,... | collective-permute-start | bytes 1843208 | tf_op jit(solution)/shard_map/ppermute | solution.py:964
  36.5 22.8 %collective-permute-start.10 = (bf16[400,768]{1,0:T(8,128)(2,1)S(1)}, bf16[400,768]{1,0:T(8,128)(2,1)S(1)}, u32[]{:S(2)}, u32[]{:S(2)}) collective-permute-start(bf16[400,768]{1,0:T(8,128)(2,1)S(1)} %collective-permute-done.7.refs_8_), channel_id=1, source_target_pairs={{0,8},{2,10},{4,12},{6,14},{8,0},{10,2},{12,4},{14,6},{16,24},{18,... | collective-permute-start | bytes 1843208 | tf_op jit(solution)/shard_map/ppermute | solution.py:972
  46.3 14.4 %collective-permute-start.16 = (bf16[400,768]{1,0:T(8,128)(2,1)S(1)}, bf16[400,768]{1,0:T(8,128)(2,1)S(1)}, u32[]{:S(2)}, u32[]{:S(2)}) collective-permute-start(bf16[400,768]{1,0:T(8,128)(2,1)S(1)} %collective-permute-done.refs_1_), channel_id=1, source_target_pairs={{0,2},{2,0},{4,6},{6,4},{8,10},{10,8},{12,14},{14,12},{16,18},{18,... | collective-permute-start | bytes 1843208 | tf_op jit(solution)/shard_map/ppermute | solution.py:960
  47.2 14.1 %collective-permute-start.17 = (bf16[400,768]{1,0:T(8,128)(2,1)S(1)}, bf16[400,768]{1,0:T(8,128)(2,1)S(1)}, u32[]{:S(2)}, u32[]{:S(2)}) collective-permute-start(bf16[400,768]{1,0:T(8,128)(2,1)S(1)} %collective-permute-done.1.refs_2_), channel_id=1, source_target_pairs={{0,2},{2,0},{4,6},{6,4},{8,10},{10,8},{12,14},{14,12},{16,18},{18,... | collective-permute-start | bytes 1843208 | tf_op jit(solution)/shard_map/ppermute | solution.py:960
  48.3 13.9 %collective-permute-start.18 = (bf16[400,768]{1,0:T(8,128)(2,1)S(1)}, bf16[400,768]{1,0:T(8,128)(2,1)S(1)}, u32[]{:S(2)}, u32[]{:S(2)}) collective-permute-start(bf16[400,768]{1,0:T(8,128)(2,1)S(1)} %collective-permute-done.2.refs_3_), channel_id=1, source_target_pairs={{0,2},{2,0},{4,6},{6,4},{8,10},{10,8},{12,14},{14,12},{16,18},{18,... | collective-permute-start | bytes 1843208 | tf_op jit(solution)/shard_map/ppermute | solution.py:960
  57.1 7.6 %collective-permute-start.23 = (bf16[400,768]{1,0:T(8,128)(2,1)S(1)}, bf16[400,768]{1,0:T(8,128)(2,1)S(1)}, u32[]{:S(2)}, u32[]{:S(2)}) collective-permute-start(bf16[400,768]{1,0:T(8,128)(2,1)S(1)} %collective-permute-done.7.refs_8_), channel_id=1, source_target_pairs={{0,2},{2,0},{4,6},{6,4},{8,10},{10,8},{12,14},{14,12},{16,18},{18,... | collective-permute-start | bytes 1843208 | tf_op jit(solution)/shard_map/ppermute | solution.py:960
  59.2 16.9 %collective-permute-start.6 = (bf16[400,768]{1,0:T(8,128)(2,1)S(1)}, bf16[400,768]{1,0:T(8,128)(2,1)}, u32[]{:S(2)}, u32[]{:S(2)}) collective-permute-start(bf16[400,768]{1,0:T(8,128)(2,1)S(1)} %collective-permute-done.4.refs_5_), channel_id=1, source_target_pairs={{0,1},{1,0},{2,3},{3,2},{4,5},{5,4},{6,7},{7,6},{8,9},{9,8},{10,11... | collective-permute-start | bytes 1843208 | tf_op jit(solution)/shard_map/ppermute | solution.py:968
  60.7 26.6 %collective-permute-start.11 = (bf16[400,768]{1,0:T(8,128)(2,1)S(1)}, bf16[400,768]{1,0:T(8,128)(2,1)}, u32[]{:S(2)}, u32[]{:S(2)}) collective-permute-start(bf16[400,768]{1,0:T(8,128)(2,1)S(1)} %collective-permute-done.9.refs_10_), channel_id=1, source_target_pairs={{0,1},{1,0},{2,3},{3,2},{4,5},{5,4},{6,7},{7,6},{8,9},{9,8},{10,11... | collective-permute-start | bytes 1843208 | tf_op jit(solution)/shard_map/ppermute | solution.py:968
  61.3 26.1 %collective-permute-start.12 = (bf16[400,768]{1,0:T(8,128)(2,1)S(1)}, bf16[400,768]{1,0:T(8,128)(2,1)}, u32[]{:S(2)}, u32[]{:S(2)}) collective-permute-start(bf16[400,768]{1,0:T(8,128)(2,1)S(1)} %collective-permute-done.10.refs_11_), channel_id=1, source_target_pairs={{0,4},{2,6},{4,0},{6,2},{8,12},{10,14},{12,8},{14,10},{16,20},{18,... | collective-permute-start | bytes 1843208 | tf_op jit(solution)/shard_map/ppermute | solution.py:964
  62.2 25.6 %collective-permute-start.13 = (bf16[400,768]{1,0:T(8,128)(2,1)S(1)}, bf16[400,768]{1,0:T(8,128)(2,1)}, u32[]{:S(2)}, u32[]{:S(2)}) collective-permute-start(bf16[400,768]{1,0:T(8,128)(2,1)S(1)} %collective-permute-done.8.refs_9_), channel_id=1, source_target_pairs={{0,8},{2,10},{4,12},{6,14},{8,0},{10,2},{12,4},{14,6},{16,24},{18,... | collective-permute-start | bytes 1843208 | tf_op jit(solution)/shard_map/ppermute | solution.py:972
  64.7 23.2 %collective-permute-start.19 = (bf16[400,768]{1,0:T(8,128)(2,1)S(1)}, bf16[400,768]{1,0:T(8,128)(2,1)S(1)}, u32[]{:S(2)}, u32[]{:S(2)}) collective-permute-start(bf16[400,768]{1,0:T(8,128)(2,1)S(1)} %collective-permute-done.3.refs_4_), channel_id=1, source_target_pairs={{0,2},{2,0},{4,6},{6,4},{8,10},{10,8},{12,14},{14,12},{16,18},{18,... | collective-permute-start | bytes 1843208 | tf_op jit(solution)/shard_map/ppermute | solution.py:960
  76.1 12.3 %collective-permute-start.20 = (bf16[400,768]{1,0:T(8,128)(2,1)S(1)}, bf16[400,768]{1,0:T(8,128)(2,1)S(1)}, u32[]{:S(2)}, u32[]{:S(2)}) collective-permute-start(bf16[400,768]{1,0:T(8,128)(2,1)S(1)} %collective-permute-done.4.refs_5_), channel_id=1, source_target_pairs={{0,2},{2,0},{4,6},{6,4},{8,10},{10,8},{12,14},{14,12},{16,18},{18,... | collective-permute-start | bytes 1843208 | tf_op jit(solution)/shard_map/ppermute | solution.py:960
  87.8 3.3 %collective-permute-start.25 = (bf16[400,768]{1,0:T(8,128)(2,1)S(1)}, bf16[400,768]{1,0:T(8,128)(2,1)S(1)}, u32[]{:S(2)}, u32[]{:S(2)}) collective-permute-start(bf16[400,768]{1,0:T(8,128)(2,1)S(1)} %collective-permute-done.9.refs_10_), channel_id=1, source_target_pairs={{0,2},{2,0},{4,6},{6,4},{8,10},{10,8},{12,14},{14,12},{16,18},{18,... | collective-permute-start | bytes 1843208 | tf_op jit(solution)/shard_map/ppermute | solution.py:960
  87.9 5.0 %collective-permute-start.26 = (bf16[400,768]{1,0:T(8,128)(2,1)S(1)}, bf16[400,768]{1,0:T(8,128)(2,1)S(1)}, u32[]{:S(2)}, u32[]{:S(2)}) collective-permute-start(bf16[400,768]{1,0:T(8,128)(2,1)S(1)} %collective-permute-done.10.refs_11_), channel_id=1, source_target_pairs={{0,2},{2,0},{4,6},{6,4},{8,10},{10,8},{12,14},{14,12},{16,18},{18,... | collective-permute-start | bytes 1843208 | tf_op jit(solution)/shard_map/ppermute | solution.py:960
  88.4 16.2 %collective-permute-start.14 = (bf16[400,768]{1,0:T(8,128)(2,1)}, bf16[400,768]{1,0:T(8,128)(2,1)}, u32[]{:S(2)}, u32[]{:S(2)}) collective-permute-start(bf16[400,768]{1,0:T(8,128)(2,1)} %collective-permute-done.13.refs_14_), channel_id=1, source_target_pairs={{0,4},{2,6},{4,0},{6,2},{8,12},{10,14},{12,8},{14,10},{16,20},{18,... | collective-permute-start | bytes 1843208 | tf_op jit(solution)/shard_map/ppermute | solution.py:964
  89.4 17.5 %collective-permute-start.29 = (bf16[400,768]{1,0:T(8,128)(2,1)}, bf16[400,768]{1,0:T(8,128)(2,1)}, u32[]{:S(2)}, u32[]{:S(2)}) collective-permute-start(bf16[400,768]{1,0:T(8,128)(2,1)} %collective-permute-done.13.refs_14_), channel_id=1, source_target_pairs={{0,2},{2,0},{4,6},{6,4},{8,10},{10,8},{12,14},{14,12},{16,18},{18,... | collective-permute-start | bytes 1843208 | tf_op jit(solution)/shard_map/ppermute | solution.py:960
  90.2 16.6 %collective-permute-start.22 = (bf16[400,768]{1,0:T(8,128)(2,1)}, bf16[400,768]{1,0:T(8,128)(2,1)}, u32[]{:S(2)}, u32[]{:S(2)}) collective-permute-start(bf16[400,768]{1,0:T(8,128)(2,1)} %collective-permute-done.6.refs_7_), channel_id=1, source_target_pairs={{0,2},{2,0},{4,6},{6,4},{8,10},{10,8},{12,14},{14,12},{16,18},{18,... | collective-permute-start | bytes 1843208 | tf_op jit(solution)/shard_map/ppermute | solution.py:960
  91.1 15.7 %collective-permute-start.27 = (bf16[400,768]{1,0:T(8,128)(2,1)}, bf16[400,768]{1,0:T(8,128)(2,1)}, u32[]{:S(2)}, u32[]{:S(2)}) collective-permute-start(bf16[400,768]{1,0:T(8,128)(2,1)} %collective-permute-done.11.refs_12_), channel_id=1, source_target_pairs={{0,2},{2,0},{4,6},{6,4},{8,10},{10,8},{12,14},{14,12},{16,18},{18,... | collective-permute-start | bytes 1843208 | tf_op jit(solution)/shard_map/ppermute | solution.py:960
  92.9 14.0 %collective-permute-start.28 = (bf16[400,768]{1,0:T(8,128)(2,1)}, bf16[400,768]{1,0:T(8,128)(2,1)}, u32[]{:S(2)}, u32[]{:S(2)}) collective-permute-start(bf16[400,768]{1,0:T(8,128)(2,1)} %collective-permute-done.12.refs_13_), channel_id=1, source_target_pairs={{0,2},{2,0},{4,6},{6,4},{8,10},{10,8},{12,14},{14,12},{16,18},{18,... | collective-permute-start | bytes 1843208 | tf_op jit(solution)/shard_map/ppermute | solution.py:960
  126.4 15.1 %collective-permute-start.31 = (bf16[3,112,768]{2,1,0:T(8,128)(2,1)}, bf16[3,112,768]{2,1,0:T(8,128)(2,1)S(1)}, u32[]{:S(2)}, u32[]{:S(2)}) collective-permute-start(bf16[3,112,768]{2,1,0:T(8,128)(2,1)} %get-tuple-element.80.refs_2_), channel_id=1, source_target_pairs={{0,1},{1,0},{2,3},{3,2},{4,5},{5,4},{6,7},{7,6},{8,9},{9,8},{10,11... | collective-permute-start | bytes 1548296 | tf_op jit(solution)/shard_map/ppermute | solution.py:968
  128.7 12.7 %collective-permute-start.32 = (f32[3,8,224]{2,1,0:T(8,128)}, f32[3,8,224]{2,1,0:T(8,128)S(1)}, u32[]{:S(2)}, u32[]{:S(2)}) collective-permute-start(f32[3,8,224]{2,1,0:T(8,128)} %get-tuple-element.81.refs_4_), channel_id=1, source_target_pairs={{0,1},{1,0},{2,3},{3,2},{4,5},{5,4},{6,7},{7,6},{8,9},{9,8},{10,11... | collective-permute-start | bytes 64520 | tf_op jit(solution)/shard_map/ppermute | solution.py:968
  168.6 10.1 %collective-permute-start.33 = (bf16[2,2,784,768]{3,2,1,0:T(8,128)(2,1)}, bf16[2,2,784,768]{3,2,1,0:T(8,128)(2,1)}, u32[]{:S(2)}, u32[]{:S(2)}) collective-permute-start(bf16[2,2,784,768]{3,2,1,0:T(8,128)(2,1)} %get-tuple-element.94), channel_id=1, source_target_pairs={{0,2},{2,0},{4,6},{6,4},{8,10},{10,8},{12,14},{14,12},{16,18},{18,... | collective-permute-start | bytes 14450696 | tf_op jit(solution)/shard_map/ppermute | solution.py:960
  182.5 36.3 %collective-permute-start.36 = (bf16[2,392,768]{2,1,0:T(8,128)(2,1)}, bf16[2,392,768]{2,1,0:T(8,128)(2,1)}, u32[]{:S(2)}, u32[]{:S(2)}) collective-permute-start(bf16[2,392,768]{2,1,0:T(8,128)(2,1)} %far_send.1), channel_id=1, source_target_pairs={{0,4},{2,6},{4,0},{6,2},{8,12},{10,14},{12,8},{14,10},{16,20},{18,... | collective-permute-start | bytes 3612680 | tf_op jit(solution)/shard_map/ppermute | solution.py:964
  183.9 13.9 %collective-permute-start.34 = (bf16[3,112,768]{2,1,0:T(8,128)(2,1)S(1)}, bf16[3,112,768]{2,1,0:T(8,128)(2,1)S(1)}, u32[]{:S(2)}, u32[]{:S(2)}) collective-permute-start(bf16[3,112,768]{2,1,0:T(8,128)(2,1)S(1)} %copy-done.28), channel_id=1, source_target_pairs={{0,1},{1,0},{2,3},{3,2},{4,5},{5,4},{6,7},{7,6},{8,9},{9,8},{10,11... | collective-permute-start | bytes 1548296 | tf_op jit(solution)/shard_map/ppermute | solution.py:968
  194.8 10.6 %collective-permute-start.35 = (f32[8,768]{1,0:T(8,128)}, f32[8,768]{1,0:T(8,128)S(1)}, u32[]{:S(2)}, u32[]{:S(2)}) collective-permute-start(f32[8,768]{1,0:T(8,128)} %get-tuple-element.106), channel_id=1, source_target_pairs={{0,1},{1,0},{2,3},{3,2},{4,5},{5,4},{6,7},{7,6},{8,9},{9,8},{10,11... | collective-permute-start | bytes 73736 | tf_op jit(solution)/shard_map/ppermute | solution.py:968
  205.3 14.0 %collective-permute-start.38 = (bf16[2,784,768]{2,1,0:T(8,128)(2,1)}, bf16[2,784,768]{2,1,0:T(8,128)(2,1)S(1)}, u32[]{:S(2)}, u32[]{:S(2)}) collective-permute-start(bf16[2,784,768]{2,1,0:T(8,128)(2,1)} %get-tuple-element.114), channel_id=1, source_target_pairs={{0,2},{2,0},{4,6},{6,4},{8,10},{10,8},{12,14},{14,12},{16,18},{18,... | collective-permute-start | bytes 7225352 | tf_op jit(solution)/shard_map/ppermute | solution.py:960
  218.8 6.3 %collective-permute-start.37 = (bf16[2,784,768]{2,1,0:T(8,128)(2,1)}, bf16[2,784,768]{2,1,0:T(8,128)(2,1)}, u32[]{:S(2)}, u32[]{:S(2)}) collective-permute-start(bf16[2,784,768]{2,1,0:T(8,128)(2,1)} %get-tuple-element.112), channel_id=1, source_target_pairs={{0,2},{2,0},{4,6},{6,4},{8,10},{10,8},{12,14},{14,12},{16,18},{18,... | collective-permute-start | bytes 7225352 | tf_op jit(solution)/shard_map/ppermute | solution.py:960
  225.1 19.9 %collective-permute-start.39 = (bf16[480,768]{1,0:T(8,128)(2,1)}, bf16[480,768]{1,0:T(8,128)(2,1)S(1)}, u32[]{:S(2)}, u32[]{:S(2)}) collective-permute-start(bf16[480,768]{1,0:T(8,128)(2,1)} %get-tuple-element.123), channel_id=1, source_target_pairs={{0,1},{1,0},{2,3},{3,2},{4,5},{5,4},{6,7},{7,6},{8,9},{9,8},{10,11... | collective-permute-start | bytes 2211848 | tf_op jit(solution)/shard_map/ppermute | solution.py:968
  228.4 17.2 %collective-permute-start.42 = (f32[24,768]{1,0:T(8,128)S(1)}, f32[24,768]{1,0:T(8,128)S(1)}, u32[]{:S(2)}, u32[]{:S(2)}) collective-permute-start(f32[24,768]{1,0:T(8,128)S(1)} %add.152), channel_id=1, source_target_pairs={{0,4},{2,6},{4,0},{6,2},{8,12},{10,14},{12,8},{14,10},{16,20},{18,... | collective-permute-start | bytes 221192 | tf_op jit(solution)/shard_map/ppermute | solution.py:964
  230.7 15.5 %collective-permute-start.40 = (bf16[392,768]{1,0:T(8,128)(2,1)S(1)}, bf16[392,768]{1,0:T(8,128)(2,1)}, u32[]{:S(2)}, u32[]{:S(2)}) collective-permute-start(bf16[392,768]{1,0:T(8,128)(2,1)S(1)} %fusion.10), channel_id=1, source_target_pairs={{0,4},{2,6},{4,0},{6,2},{8,12},{10,14},{12,8},{14,10},{16,20},{18,... | collective-permute-start | bytes 1806344 | tf_op jit(solution)/shard_map/ppermute | solution.py:964
  235.6 17.0 %collective-permute-start.46 = (bf16[392,768]{1,0:T(8,128)(2,1)}, bf16[392,768]{1,0:T(8,128)(2,1)S(1)}, u32[]{:S(2)}, u32[]{:S(2)}) collective-permute-start(bf16[392,768]{1,0:T(8,128)(2,1)} %get-tuple-element.144), channel_id=1, source_target_pairs={{0,8},{2,10},{4,12},{6,14},{8,0},{10,2},{12,4},{14,6},{16,24},{18,... | collective-permute-start | bytes 1806344 | tf_op jit(solution)/shard_map/ppermute | solution.py:972
  247.9 17.7 %collective-permute-start.43 = (bf16[392,768]{1,0:T(8,128)(2,1)S(1)}, bf16[392,768]{1,0:T(8,128)(2,1)S(1)}, u32[]{:S(2)}, u32[]{:S(2)}) collective-permute-start(bf16[392,768]{1,0:T(8,128)(2,1)S(1)} %fusion.7), channel_id=1, source_target_pairs={{24,16},{26,18},{28,20},{30,22},{8,0},{10,2},{12,4},{14,6},{25,17}... | collective-permute-start | bytes 1806344 | tf_op jit(solution)/shard_map/ppermute | solution.py:972
  252.1 14.3 %collective-permute-start.44 = (bf16[392,768]{1,0:T(8,128)(2,1)S(1)}, bf16[392,768]{1,0:T(8,128)(2,1)S(1)}, u32[]{:S(2)}, u32[]{:S(2)}) collective-permute-start(bf16[392,768]{1,0:T(8,128)(2,1)S(1)} %get-tuple-element.140), channel_id=1, source_target_pairs={{0,4},{2,6},{4,0},{6,2},{8,12},{10,14},{12,8},{14,10},{16,20},{18,... | collective-permute-start | bytes 1806344 | tf_op jit(solution)/shard_map/ppermute | solution.py:964
  252.6 13.1 %collective-permute-start.45 = (f32[24,768]{1,0:T(8,128)S(1)}, f32[24,768]{1,0:T(8,128)S(1)}, u32[]{:S(2)}, u32[]{:S(2)}) collective-permute-start(f32[24,768]{1,0:T(8,128)S(1)} %add.157), channel_id=1, source_target_pairs={{0,8},{2,10},{4,12},{6,14},{8,0},{10,2},{12,4},{14,6},{16,24},{18,... | collective-permute-start | bytes 221192 | tf_op jit(solution)/shard_map/ppermute | solution.py:972
  266.5 18.4 %collective-permute-start.48 = (bf16[392,768]{1,0:T(8,128)(2,1)S(1)}, bf16[392,768]{1,0:T(8,128)(2,1)S(1)}, u32[]{:S(2)}, u32[]{:S(2)}) collective-permute-start(bf16[392,768]{1,0:T(8,128)(2,1)S(1)} %add_convert_fusion.2), channel_id=1, source_target_pairs={{24,16},{26,18},{28,20},{30,22},{0,8},{2,10},{4,12},{6,14},{25,17}... | collective-permute-start | bytes 1806344 | tf_op jit(solution)/shard_map/ppermute | solution.py:972
  267.8 17.2 %collective-permute-start.47 = (bf16[392,768]{1,0:T(8,128)(2,1)S(1)}, bf16[392,768]{1,0:T(8,128)(2,1)S(1)}, u32[]{:S(2)}, u32[]{:S(2)}) collective-permute-start(bf16[392,768]{1,0:T(8,128)(2,1)S(1)} %add_convert_fusion.3), channel_id=1, source_target_pairs={{16,0},{18,2},{20,4},{22,6},{17,1},{19,3},{21,5},{23,7}} | collective-permute-start | bytes 1806344 | tf_op jit(solution)/shard_map/ppermute | solution.py:972
  268.5 16.5 %collective-permute-start.49 = (bf16[192,768]{1,0:T(8,128)(2,1)S(1)}, bf16[192,768]{1,0:T(8,128)(2,1)S(1)}, u32[]{:S(2)}, u32[]{:S(2)}) collective-permute-start(bf16[192,768]{1,0:T(8,128)(2,1)S(1)} %slice.47), channel_id=1, source_target_pairs={{0,16},{2,18},{4,20},{6,22},{8,24},{10,26},{12,28},{14,30},{1,17},... | collective-permute-start | bytes 884744 | tf_op jit(solution)/shard_map/ppermute | solution.py:972
  285.1 19.0 %collective-permute-start.51 = (bf16[392,768]{1,0:T(8,128)(2,1)S(1)}, bf16[392,768]{1,0:T(8,128)(2,1)}, u32[]{:S(2)}, u32[]{:S(2)}) collective-permute-start(bf16[392,768]{1,0:T(8,128)(2,1)S(1)} %add_convert_fusion), channel_id=1, source_target_pairs={{16,8},{18,10},{20,12},{22,14},{17,9},{19,11},{21,13},{23,15}} | collective-permute-start | bytes 1806344 | tf_op jit(solution)/shard_map/ppermute | solution.py:972
  287.2 15.1 %collective-permute-start.50 = (bf16[224,768]{1,0:T(8,128)(2,1)}, bf16[224,768]{1,0:T(8,128)(2,1)}, u32[]{:S(2)}, u32[]{:S(2)}) collective-permute-start(bf16[224,768]{1,0:T(8,128)(2,1)} %pad_maximum_fusion), channel_id=1, source_target_pairs={{0,16},{2,18},{4,20},{6,22},{8,24},{10,26},{12,28},{14,30},{1,17},... | collective-permute-start | bytes 1032200 | tf_op jit(solution)/shard_map/ppermute | solution.py:972
  (45 other events, 1237.4 us)
